TPU v7x, 32 devices: a whole 2x2x4 slice. The times are simulated.
32 devices in a mesh: dp: 8 (over z, y), tensor: 4 (over x, core).
Axes of the slice: x: 2, y: 2, z: 4, core: 2. Of those that a mesh axis runs over, the one named last changes fastest.
Arguments:
- layer_input: bfloat16 [8192, 2048], P(('dp', 'tensor')), may hold values from -6 to 6
- cotangent: bfloat16 [8192, 2048], P(('dp', 'tensor')), may hold values from -6 to 6
- starts: int32 [8, 2], P('dp'), may hold values from 0 to 768, as said below
- pieces: int32 [8192], P('dp'), may hold values from -1 to 1, as said below
- norm_attn: float32 [2048], replicated, may hold values from 0.5 to 1.5
- w_query: bfloat16 [2048, 2048], P(None, 'tensor'), may hold values from -0.125 to 0.125
- w_key: bfloat16 [2048, 256], P(None, 'tensor'), may hold values from -0.125 to 0.125
- w_value: bfloat16 [2048, 256], P(None, 'tensor'), may hold values from -0.125 to 0.125
- w_out: bfloat16 [2048, 2048], P('tensor'), may hold values from -0.75 to 0.75
- norm_mlp: float32 [2048], replicated, may hold values from 0.5 to 1.5
- w_gate: bfloat16 [2048, 5632], P(None, 'tensor'), may hold values from -0.125 to 0.125
- w_up: bfloat16 [2048, 5632], P(None, 'tensor'), may hold values from -0.125 to 0.125
- w_down: bfloat16 [5632, 2048], P('tensor'), may hold values from -0.078125 to 0.078125
Outputs:
- block_out: bfloat16 [8192, 2048], P(('dp', 'tensor'))
- x_grad: float32 [8192, 2048], P(('dp', 'tensor'))
- norm_attn_grad: float32 [2048], P(('dp', 'tensor'))
- w_query_grad: float32 [2048, 2048], P('dp', 'tensor')
- w_key_grad: float32 [2048, 256], P('dp', 'tensor')
- w_value_grad: float32 [2048, 256], P('dp', 'tensor')
- w_out_grad: float32 [2048, 2048], P('tensor', 'dp')
- norm_mlp_grad: float32 [2048], P(('dp', 'tensor'))
- w_gate_grad: float32 [2048, 5632], P('dp', 'tensor')
- w_up_grad: float32 [2048, 5632], P('dp', 'tensor')
- w_down_grad: float32 [5632, 2048], P('tensor', 'dp')
Inputs may be any that keep to these rules, and one draw needn't show every extreme that they name: `starts`: pictures of a sequence don't intersect and lie inside it. pieces of a token is the k with starts[its sequence, k] <= its position < starts[its sequence, k] + 256, or -1 outside every picture.
All inputs are finite; a program needn't handle non-finite values.
Results may differ from a plain program's by a relative error of at most 0.02.
Values may be sent and summed in bfloat16 or wider, within the bound.
No kernel may reach another device: no remote copies, remote signals or barrier semaphores. Data moves between devices by JAX's collectives and lax.ppermute only.
A program may use at most 384 MiB of HBM per device.

v0:
```python
import jax
import jax.numpy as jnp
from jax import lax
from jax.sharding import PartitionSpec as P

HD = 64
SEQ = 1024
PIECE = 256


EPSILON = 1e-05
ROPE_BASE = 10000.0
MASKED = -1e30


def contract_rows(left, right):
    return lax.dot_general(
        left, right, (((0,), (0,)), ((), ())), preferred_element_type=jnp.float32
    )


def contract_cols(left, right):
    return lax.dot_general(
        left, right, (((1,), (1,)), ((), ())), preferred_element_type=jnp.float32
    )


def rope_tables(count, head_dim, seq_len):
    half_dim = head_dim // 2
    positions = (jnp.arange(count, dtype=jnp.int32) % seq_len).astype(jnp.float32)
    inverse = jnp.power(ROPE_BASE, -(jnp.arange(half_dim).astype(jnp.float32) * 2.0) / head_dim)
    angles = positions[:, None] * inverse[None, :]
    return (jnp.cos(angles)[:, None, :], jnp.sin(angles)[:, None, :])


def rotate(value, cos_tab, sin_tab):
    half_dim = value.shape[-1] // 2
    first = value[..., :half_dim]
    second = value[..., half_dim:]
    return jnp.concatenate(
        [first * cos_tab - second * sin_tab, second * cos_tab + first * sin_tab], axis=-1
    )


def rotate_back(grad, cos_tab, sin_tab):
    half_dim = grad.shape[-1] // 2
    first = grad[..., :half_dim]
    second = grad[..., half_dim:]
    return jnp.concatenate(
        [first * cos_tab + second * sin_tab, second * cos_tab - first * sin_tab], axis=-1
    )


def visible(row_pos, row_piece, seq_starts, length, piece_len):
    numbers = jnp.arange(seq_starts.shape[0], dtype=jnp.int32)
    hit = row_piece[:, None] == numbers[None, :]
    begin = jnp.sum(jnp.where(hit, seq_starts[None, :], 0), axis=1)
    inside = row_piece >= 0
    low_end = jnp.where(inside, begin, 0)
    high_end = jnp.where(inside, begin + piece_len, 0)
    columns = jnp.arange(length, dtype=jnp.int32)
    return (columns[None, :] <= row_pos[:, None]) | (columns[None, :] >= low_end[:, None]) & (
        columns[None, :] < high_end[:, None]
    )


def rms_inverse(resid):
    return lax.rsqrt(jnp.mean(resid * resid, axis=-1, keepdims=True) + EPSILON)


def norm_back(d_norm, resid, inverse, gain):
    scaled = d_norm * gain
    return inverse * scaled - resid * (inverse * inverse * inverse) * jnp.mean(
        scaled * resid, axis=-1, keepdims=True
    )


def gain_part(d_norm, resid, inverse):
    return jnp.sum(d_norm * resid * inverse, axis=0)


def masked_scores(q_blk, key_seq, row_piece, seq_starts, offset, seq_len):
    row_pos = jnp.arange(q_blk.shape[0], dtype=jnp.int32) + offset
    mask = visible(row_pos, row_piece, seq_starts, seq_len, PIECE)
    scores = jnp.einsum("qkrd,skd->krqs", q_blk, key_seq, preferred_element_type=jnp.float32)
    return jnp.where(mask[None, None], scores, MASKED)


def attend_forward(q_low, k_low, v_low, pieces, starts, seq_len):
    block = min(512, seq_len)
    outputs = []
    row_stats = []
    for blk_idx in range(seq_len // block):
        first_row = blk_idx * block
        masked = masked_scores(
            q_low[first_row : first_row + block],
            k_low,
            pieces[first_row : first_row + block],
            starts[0],
            blk_idx * block,
            seq_len,
        )
        row_max = jnp.max(masked, axis=-1, keepdims=True)
        exp_terms = jnp.exp(masked - row_max)
        row_sum = jnp.sum(exp_terms, axis=-1, keepdims=True)
        p_low = (exp_terms / row_sum).astype(jnp.bfloat16)
        outputs.append(
            jnp.einsum("krqs,skd->qkrd", p_low, v_low, preferred_element_type=jnp.float32)
        )
        row_stats.append((row_max, row_sum))
    return (jnp.concatenate(outputs, axis=0), row_stats)


def attend_backward(q_low, k_low, v_low, d_attn, pieces, starts, row_stats, seq_len):
    block = min(512, seq_len)
    d_query_parts = []
    d_key_seq = jnp.zeros(k_low.shape, jnp.float32)
    d_val_seq = jnp.zeros(v_low.shape, jnp.float32)
    for blk_idx in range(seq_len // block):
        first_row = blk_idx * block
        q_blk = q_low[first_row : first_row + block]
        d_out_blk = d_attn[first_row : first_row + block]
        row_max, row_sum = row_stats[blk_idx]
        masked = masked_scores(
            q_blk, k_low, pieces[first_row : first_row + block], starts[0], blk_idx * block, seq_len
        )
        p_float = jnp.exp(masked - row_max) / row_sum
        p_low = p_float.astype(jnp.bfloat16)
        dp_val = jnp.einsum("qkrd,skd->krqs", d_out_blk, v_low, preferred_element_type=jnp.float32)
        delta = jnp.sum(p_float * dp_val, axis=-1, keepdims=True)
        d_scores = (p_float * (dp_val - delta)).astype(jnp.bfloat16)
        d_query_parts.append(
            jnp.einsum("krqs,skd->qkrd", d_scores, k_low, preferred_element_type=jnp.float32)
        )
        d_key_seq = d_key_seq + jnp.einsum(
            "krqs,qkrd->skd", d_scores, q_blk, preferred_element_type=jnp.float32
        )
        d_val_seq = d_val_seq + jnp.einsum(
            "krqs,qkrd->skd", p_low, d_out_blk, preferred_element_type=jnp.float32
        )
    return (jnp.concatenate(d_query_parts, axis=0), d_key_seq, d_val_seq)


def per_device(
    layer_input,
    cotangent,
    starts,
    pieces,
    norm_attn,
    w_query,
    w_key,
    w_value,
    w_out,
    norm_mlp,
    w_gate,
    w_up,
    w_down,
):
    rows_own = layer_input.shape[0]
    group_rows = pieces.shape[0]
    head_dim = HD
    seq_len = SEQ
    kv_local = w_key.shape[1] // head_dim
    heads_local = w_query.shape[1] // head_dim
    ratio = heads_local // kv_local
    scale = head_dim ** (-0.5)
    first_own = lax.axis_index("tensor") * rows_own
    cos_tab, sin_tab = rope_tables(group_rows, head_dim, seq_len)
    x_group, cot_group = (
        lax.all_gather(layer_input, "tensor", axis=0, tiled=True),
        lax.all_gather(cotangent, "tensor", axis=0, tiled=True),
    )
    resid_in = x_group.astype(jnp.float32)
    inv_attn = rms_inverse(resid_in)
    normed_attn = (resid_in * inv_attn * norm_attn).astype(jnp.bfloat16)
    query_f = jnp.dot(normed_attn, w_query, preferred_element_type=jnp.float32).reshape(
        group_rows, heads_local, head_dim
    )
    key_f = jnp.dot(normed_attn, w_key, preferred_element_type=jnp.float32).reshape(
        group_rows, kv_local, head_dim
    )
    q_low = (
        (rotate(query_f, cos_tab, sin_tab) * scale)
        .astype(jnp.bfloat16)
        .reshape(group_rows, kv_local, ratio, head_dim)
    )
    k_low = rotate(key_f, cos_tab, sin_tab).astype(jnp.bfloat16)
    v_low = (
        jnp.dot(normed_attn, w_value, preferred_element_type=jnp.float32)
        .astype(jnp.bfloat16)
        .reshape(group_rows, kv_local, head_dim)
    )
    attn_vals, row_stats = attend_forward(q_low, k_low, v_low, pieces, starts, seq_len)
    attn_low = attn_vals.reshape(group_rows, heads_local * head_dim).astype(jnp.bfloat16)
    attn_part = jnp.dot(attn_low, w_out, preferred_element_type=jnp.float32)
    attn_total = lax.psum(attn_part.astype(jnp.bfloat16), "tensor").astype(jnp.float32)
    resid_mid = resid_in + attn_total
    inv_mlp = rms_inverse(resid_mid)
    normed_mlp = (resid_mid * inv_mlp * norm_mlp).astype(jnp.bfloat16)
    gate_val = jnp.dot(normed_mlp, w_gate, preferred_element_type=jnp.float32)
    up_val = jnp.dot(normed_mlp, w_up, preferred_element_type=jnp.float32)
    gate_sig = jax.nn.sigmoid(gate_val)
    hidden = (gate_val * gate_sig * up_val).astype(jnp.bfloat16)
    mlp_part = jnp.dot(hidden, w_down, preferred_element_type=jnp.float32)
    mlp_total = lax.psum(mlp_part.astype(jnp.bfloat16), "tensor").astype(jnp.float32)
    block_out = lax.dynamic_slice_in_dim(resid_mid + mlp_total, first_own, rows_own, 0).astype(
        jnp.bfloat16
    )
    d_hidden = contract_cols(cot_group, w_down)
    grad_down = contract_rows(hidden, cot_group)
    d_gate = (d_hidden * up_val * (gate_sig * (1.0 + gate_val * (1.0 - gate_sig)))).astype(
        jnp.bfloat16
    )
    d_up = (d_hidden * gate_val * gate_sig).astype(jnp.bfloat16)
    grad_gate = contract_rows(normed_mlp, d_gate)
    grad_up = contract_rows(normed_mlp, d_up)
    d_norm_part = contract_cols(d_gate, w_gate) + contract_cols(d_up, w_up)
    d_norm_mid = lax.psum(d_norm_part.astype(jnp.bfloat16), "tensor").astype(jnp.float32)
    d_mid_group = cot_group.astype(jnp.float32) + norm_back(
        d_norm_mid, resid_mid, inv_mlp, norm_mlp
    )
    d_attn_out = d_mid_group.astype(jnp.bfloat16)
    d_mid = lax.dynamic_slice_in_dim(d_mid_group, first_own, rows_own, 0)
    gain_mlp_part = gain_part(
        lax.dynamic_slice_in_dim(d_norm_mid, first_own, rows_own, 0),
        lax.dynamic_slice_in_dim(resid_mid, first_own, rows_own, 0),
        lax.dynamic_slice_in_dim(inv_mlp, first_own, rows_own, 0),
    )
    grad_out = contract_rows(attn_low, d_attn_out)
    d_attn = (
        contract_cols(d_attn_out, w_out)
        .astype(jnp.bfloat16)
        .reshape(group_rows, kv_local, ratio, head_dim)
    )
    d_q, d_k, d_v = attend_backward(q_low, k_low, v_low, d_attn, pieces, starts, row_stats, seq_len)
    d_query = rotate_back(d_q.reshape(group_rows, heads_local, head_dim) * scale, cos_tab, sin_tab)
    d_query = d_query.astype(jnp.bfloat16).reshape(group_rows, heads_local * head_dim)
    d_key = (
        rotate_back(d_k, cos_tab, sin_tab)
        .astype(jnp.bfloat16)
        .reshape(group_rows, kv_local * head_dim)
    )
    d_value = d_v.astype(jnp.bfloat16).reshape(group_rows, kv_local * head_dim)
    grad_query = contract_rows(normed_attn, d_query)
    grad_key = contract_rows(normed_attn, d_key)
    grad_value = contract_rows(normed_attn, d_value)
    d_norm_part_in = (
        contract_cols(d_query, w_query)
        + contract_cols(d_key, w_key)
        + contract_cols(d_value, w_value)
    )
    d_norm_total = lax.psum(d_norm_part_in.astype(jnp.bfloat16), "tensor").astype(jnp.float32)
    d_norm_in = lax.dynamic_slice_in_dim(d_norm_total, first_own, rows_own, 0)
    resid_own = lax.dynamic_slice_in_dim(resid_in, first_own, rows_own, 0)
    inv_own = lax.dynamic_slice_in_dim(inv_attn, first_own, rows_own, 0)
    x_grad = d_mid + norm_back(d_norm_in, resid_own, inv_own, norm_attn)
    gain_attn_part = gain_part(d_norm_in, resid_own, inv_own)
    summed = (
        lax.psum_scatter(
            grad_query.astype(jnp.bfloat16), "dp", scatter_dimension=0, tiled=True
        ).astype(jnp.float32),
        lax.psum_scatter(
            grad_key.astype(jnp.bfloat16), "dp", scatter_dimension=0, tiled=True
        ).astype(jnp.float32),
        lax.psum_scatter(
            grad_value.astype(jnp.bfloat16), "dp", scatter_dimension=0, tiled=True
        ).astype(jnp.float32),
        lax.psum_scatter(
            grad_out.astype(jnp.bfloat16), "dp", scatter_dimension=1, tiled=True
        ).astype(jnp.float32),
        lax.psum_scatter(
            grad_gate.astype(jnp.bfloat16), "dp", scatter_dimension=0, tiled=True
        ).astype(jnp.float32),
        lax.psum_scatter(
            grad_up.astype(jnp.bfloat16), "dp", scatter_dimension=0, tiled=True
        ).astype(jnp.float32),
        lax.psum_scatter(
            grad_down.astype(jnp.bfloat16), "dp", scatter_dimension=1, tiled=True
        ).astype(jnp.float32),
    )
    gains = (
        lax.psum_scatter(gain_attn_part, ("dp", "tensor"), scatter_dimension=0, tiled=True),
        lax.psum_scatter(gain_mlp_part, ("dp", "tensor"), scatter_dimension=0, tiled=True),
    )
    return (
        block_out,
        x_grad,
        gains[0],
        summed[0],
        summed[1],
        summed[2],
        summed[3],
        gains[1],
        summed[4],
        summed[5],
        summed[6],
    )


def solution(mesh):
    in_specs = (
        P(("dp", "tensor"), None),
        P(("dp", "tensor"), None),
        P("dp", None),
        P("dp"),
        P(),
        P(None, "tensor"),
        P(None, "tensor"),
        P(None, "tensor"),
        P("tensor", None),
        P(),
        P(None, "tensor"),
        P(None, "tensor"),
        P("tensor", None),
    )
    out_specs = (
        P(("dp", "tensor"), None),
        P(("dp", "tensor"), None),
        P(("dp", "tensor")),
        P("dp", "tensor"),
        P("dp", "tensor"),
        P("dp", "tensor"),
        P("tensor", "dp"),
        P(("dp", "tensor")),
        P("dp", "tensor"),
        P("dp", "tensor"),
        P("tensor", "dp"),
    )
    return jax.shard_map(
        per_device, mesh=mesh, in_specs=in_specs, out_specs=out_specs, check_vma=False
    )
```

profile of v0, /device:TPU:9, one launch (start us, length us, event | category | flops | bytes accessed | tf_op | source)
XLA Modules:
  0.0 1246.2 jit_solution(15837001171085388941)
XLA Ops:
  12.1 33.6 %all-gather.3.cloned.1.call-done = bf16[1024,2048]{1,0:T(8,128)(2,1)} async-done(((bf16[256,2048]{1,0:T(8,128)(2,1)}), bf16[1024,2048]{1,0:T(8,128)(2,1)}) %all-gather.3.cloned.1.call-update) | async-done | bytes 4194320 | tf_op jit(solution)/shard_map/all_gather | solution.py:170
  57.0 8.3 fusion.7
  65.3 20.0 %fusion.6 = (f32[8,512]{1,0:T(8,128)S(1)}, f32[1024,512,8]{1,0,2:T(8,128)}) fusion(pred[512,1024]{0,1:T(8,128)(4,1)S(1)} %fusion.36, bf16[1024,8,64]{0,2,1:T(8,128)(2,1)S(1)} %fusion.31, bf16[1024,32]{0,1:T(8,128)(2,1)S(1)} %get-tuple-element.39, bf16[1024,32]{0,1:T(8,128)(2,1)S(1)} %get-tuple-element.38), kind=kOutput, calls=%fused_computation.14 | convolution fusion | flops 545517568 | bytes 17973248 | tf_op jit(solution)/shard_map/qkrd,skd->krqs/dot_general | solution.py:85
  85.3 8.7 fusion.11
  94.0 8.8 fusion.49
  102.8 8.6 fusion.9
  111.5 8.1 fusion.52
  120.7 4.5 convolution_convert_fusion.4
  126.0 84.3 %all-reduce.8.cloned.1.call-done = bf16[1024,2048]{1,0:T(8,128)(2,1)} async-done(((bf16[1024,2048]{1,0:T(8,128)(2,1)}), bf16[1024,2048]{1,0:T(8,128)(2,1)}) %all-reduce.8.cloned.1.call-update) | async-done | bytes 4194320 | tf_op jit(solution)/shard_map/psum | solution.py:196
  210.3 5.0 multiply_reduce_fusion.1
  219.4 8.4 fusion.116
  227.8 8.6 fusion.115
  236.4 10.8 all-gather.5.cloned.1.call-done
  247.2 15.6 %multiply_convert_fusion.2 = (bf16[1024,1408]{1,0:T(8,128)(2,1)S(1)}, bf16[1024,1408]{1,0:T(8,128)(2,1)S(1)}, bf16[1024,1408]{1,0:T(8,128)(2,1)}) fusion(f32[1024,1408]{1,0:T(8,128)} %fusion.115, f32[1024,1408]{1,0:T(8,128)} %fusion.116, bf16[1024,2048]{1,0:T(8,128)(2,1)} %all-gather.5.cloned.1.call-done, bf16[1408,2048]{1,0:T(8,128)(2,1)} %param.25), kind=kOutput, calls=%fused_computation.44 | convolution fusion | flops 5928648704 | bytes 30146560 | tf_op jit(solution)/shard_map/dot_general | solution.py:23
  262.8 10.8 fusion.117
  273.6 11.0 add_convert_fusion.1
  284.8 11.1 convolution_convert_fusion.3
  295.9 73.9 %all-reduce.10.cloned.1.call-done = bf16[1024,2048]{1,0:T(8,128)(2,1)} async-done(((bf16[1024,2048]{1,0:T(8,128)(2,1)}), bf16[1024,2048]{1,0:T(8,128)(2,1)}) %all-reduce.10.cloned.1.call-update) | async-done | bytes 4194320 | tf_op jit(solution)/shard_map/psum | solution.py:218
  369.8 6.7 multiply_reduce_fusion
  376.6 12.8 %subtract_add_fusion = (f32[1024,2048]{1,0:T(8,128)}, f32[1024,2048]{1,0:T(8,128)}) fusion(bf16[1024,2048]{1,0:T(8,128)(2,1)} %all-gather.5.cloned.1.call-done, f32[1024]{0:T(1024)S(1)} %broadcast_multiply_fusion, f32[1024]{0:T(1024)S(1)} %get-tuple-element.42, bf16[1024,2048]{1,0:T(8,128)(2,1)} %all-reduce.10.cloned.1.call-done, f32[2048]{0:T(1024)S(1)} %copy-done.35, ...), kind=kLoop, calls=%fused_computation.31 | loop fusion | flops 23068672 | bytes 33574912 | tf_op jit(solution)/shard_map/add | solution.py:219
  389.4 5.9 fusion.40
  395.5 8.4 fusion
  403.9 8.7 fusion.13
  417.9 8.8 fusion.55
  427.4 8.4 fusion.3
  435.8 8.4 fusion.12
  450.1 6.2 fusion.62
  458.4 4.6 fusion.95
  463.0 8.5 fusion.70
  475.4 7.3 fusion.118
  482.8 9.2 add_convert_fusion
  493.2 7.1 convolution_convert_fusion.5
  500.4 5.9 convolution_convert_fusion.6
  506.4 10.7 convolution_convert_fusion
  517.1 11.0 convolution_convert_fusion.1
  528.2 11.2 convolution_convert_fusion.2
  540.2 6.6 convert_element_type.219
  547.6 4.3 convert_element_type.239
  553.3 44.3 %reduce-scatter.10.cloned.1.call-done = bf16[256,64]{0,1:T(8,128)(2,1)} async-done(((bf16[2048,64]{0,1:T(8,128)(2,1)}), bf16[256,64]{0,1:T(8,128)(2,1)}) %reduce-scatter.10.cloned.1.call-update) | async-done | bytes 32784 | tf_op jit(solution)/shard_map/reduce_scatter | solution.py:262
  598.9 155.4 %all-reduce.12.cloned.1.call-done = (bf16[1024,2048]{1,0:T(8,128)(2,1)}, bf16[1024,2048]{1,0:T(8,128)(2,1)}) async-done(((bf16[1024,2048]{1,0:T(8,128)(2,1)}, bf16[1024,2048]{1,0:T(8,128)(2,1)}), (bf16[1024,2048]{1,0:T(8,128)(2,1)}, bf16[1024,2048]{1,0:T(8,128)(2,1)})) %all-reduce.12.cloned.1.call-update) | async-done | bytes 8388624 | tf_op jit(solution)/shard_map/psum | solution.py:205
  756.9 4.0 multiply_reduce_fusion.3
  760.9 40.0 %all-reduce.2 = (f32[2048]{0:T(1024)S(1)}, f32[2048]{0:T(1024)S(1)}) all-reduce(f32[2048]{0:T(1024)S(1)} %get-tuple-element.11, f32[2048]{0:T(1024)S(1)} %get-tuple-element.26), channel_id=2, replica_groups=mesh['dp'=8,'tensor'=4] {'dp','tensor'}, use_global_device_ids=true, to_apply=%region_17.18.clone | all-reduce | flops 4096 | bytes 32768
  802.1 22.5 %reduce-scatter.14.cloned.1.call-done = bf16[512,256]{1,0:T(8,128)(2,1)} async-done(((bf16[512,2048]{1,0:T(8,128)(2,1)}), bf16[512,256]{1,0:T(8,128)(2,1)}) %reduce-scatter.14.cloned.1.call-update) | async-done | bytes 262160 | tf_op jit(solution)/shard_map/reduce_scatter | solution.py:268
  826.4 69.0 %reduce-scatter.8.cloned.1.call-done = bf16[256,512]{1,0:T(8,128)(2,1)} async-done(((bf16[2048,512]{1,0:T(8,128)(2,1)}), bf16[256,512]{1,0:T(8,128)(2,1)}) %reduce-scatter.8.cloned.1.call-update) | async-done | bytes 262160 | tf_op jit(solution)/shard_map/reduce_scatter | solution.py:259
  897.2 4.5 fusion.27
  901.7 108.3 %reduce-scatter.20.cloned.1.call-done = bf16[1408,256]{1,0:T(8,128)(2,1)} async-done(((bf16[1408,2048]{1,0:T(8,128)(2,1)}), bf16[1408,256]{1,0:T(8,128)(2,1)}) %reduce-scatter.20.cloned.1.call-update) | async-done | bytes 720912 | tf_op jit(solution)/shard_map/reduce_scatter | solution.py:277
  1012.4 111.1 %reduce-scatter.18.cloned.1.call-done = bf16[256,1408]{1,0:T(8,128)(2,1)} async-done(((bf16[2048,1408]{1,0:T(8,128)(2,1)}), bf16[256,1408]{1,0:T(8,128)(2,1)}) %reduce-scatter.18.cloned.1.call-update) | async-done | bytes 720912 | tf_op jit(solution)/shard_map/reduce_scatter | solution.py:274
  1125.8 111.0 %reduce-scatter.16.cloned.1.call-done = bf16[256,1408]{1,0:T(8,128)(2,1)} async-done(((bf16[2048,1408]{1,0:T(8,128)(2,1)}), bf16[256,1408]{1,0:T(8,128)(2,1)}) %reduce-scatter.16.cloned.1.call-update) | async-done | bytes 720912 | tf_op jit(solution)/shard_map/reduce_scatter | solution.py:271
  (196 shorter events, 59.8 us)
Async XLA Ops:
  7.2 113.5 %copy-start = (bf16[512,2048]{1,0:T(8,128)(2,1)S(1)}, bf16[512,2048]{1,0:T(8,128)(2,1)}, u32[]{:S(2)}) copy-start(bf16[512,2048]{1,0:T(8,128)(2,1)} %param.21) | copy-start | bytes 6291460
  7.2 42.3 %copy-start.33 = (f32[2048]{0:T(1024)S(1)}, f32[2048]{0:T(1024)}, u32[]{:S(2)}) copy-start(f32[2048]{0:T(1024)} %param.17) | copy-start | bytes 24580
  7.2 38.5 %all-gather.3.cloned.1.call-start = ((), (), s32[]{:S(2)}) async-start(), calls=%async_computation.7 | async-start | bytes 5242880 | tf_op jit(solution)/shard_map/all_gather | solution.py:170
  7.9 202.4 %all-reduce.8.cloned.1.call-start = ((), (), s32[]{:S(2)}) async-start(), calls=%async_computation.8 | async-start | bytes 8388608 | tf_op jit(solution)/shard_map/psum | solution.py:196
  8.0 45.4 %copy-start.42 = (f32[32]{0:T(128)}, f32[32]{0:T(128)S(1)}, u32[]{:S(2)}) copy-start(f32[32]{0:T(128)S(1)} %multiply_power_fusion) | copy-start | bytes 388
  8.0 45.4 %copy-start.36 = (f32[1024]{0:T(1024)}, f32[1024]{0:T(1024)S(1)}, u32[]{:S(2)}) copy-start(f32[1024]{0:T(1024)S(1)} %fusion.100) | copy-start | bytes 12292
  10.9 45.6 %copy-start.20 = (f32[1024,32]{0,1:T(8,128)}, f32[1024,32]{0,1:T(8,128)S(1)}, u32[]{:S(2)}) copy-start(f32[1024,32]{0,1:T(8,128)S(1)} %get-tuple-element.40) | copy-start | bytes 393220
  10.9 45.6 %copy-start.22 = (f32[1024,32]{0,1:T(8,128)}, f32[1024,32]{0,1:T(8,128)S(1)}, u32[]{:S(2)}) copy-start(f32[1024,32]{0,1:T(8,128)S(1)} %get-tuple-element.41) | copy-start | bytes 393220
  11.4 100.0 %copy-start.13 = (pred[512,1024]{0,1:T(8,128)(4,1)}, pred[512,1024]{0,1:T(8,128)(4,1)S(1)}, u32[]{:S(2)}) copy-start(pred[512,1024]{0,1:T(8,128)(4,1)S(1)} %fusion.36) | copy-start | bytes 1572868
  54.0 11.4 copy-start.16
  54.0 11.3 copy-start.18
  57.0 8.3 copy-start.11
  85.3 26.1 %copy-start.31 = (f32[8,512]{1,0:T(8,128)}, f32[8,512]{1,0:T(8,128)S(1)}, u32[]{:S(2)}) copy-start(f32[8,512]{1,0:T(8,128)S(1)} %get-tuple-element.50) | copy-start | bytes 49156
  111.4 8.1 copy-start.38
  111.5 8.1 copy-start.30
  125.2 90.1 %copy-start.35 = (f32[2048]{0:T(1024)S(1)}, f32[2048]{0:T(1024)}, u32[]{:S(2)}) copy-start(f32[2048]{0:T(1024)} %param.22) | copy-start | bytes 24580
  125.2 121.9 %all-gather.5.cloned.1.call-start = ((), (), s32[]{:S(2)}) async-start(), calls=%async_computation.9 | async-start | bytes 5242880 | tf_op jit(solution)/shard_map/all_gather | solution.py:171
  126.0 243.8 %all-reduce.10.cloned.1.call-start = ((), (), s32[]{:S(2)}) async-start(), calls=%async_computation.10 | async-start | bytes 8388608 | tf_op jit(solution)/shard_map/psum | solution.py:218
  210.3 9.0 slice-start.10
  215.3 161.2 %copy-start.40 = (f32[1024]{0:T(1024)}, f32[1024]{0:T(1024)S(1)}, u32[]{:S(2)}) copy-start(f32[1024]{0:T(1024)S(1)} %get-tuple-element.43) | copy-start | bytes 12292
  216.2 11.6 slice-start.8
  219.3 8.5 copy-start.15
  219.3 8.5 slice-start.9
  262.8 10.8 copy-start.45
  262.8 10.8 copy-start.46
  284.7 267.2 %reduce-scatter.12.cloned.1.call-start = ((), (), s32[]{:S(2)}) async-start(), calls=%async_computation.13 | async-start | bytes 294912 | tf_op jit(solution)/shard_map/reduce_scatter | solution.py:265
  369.8 6.8 copy-start.4
  376.6 18.8 %slice-start = ((s8[16777216]{0:T(1024)(128)(4,1)}), s8[4194304]{0:T(1024)(128)(4,1)S(1)}, s32[]{:S(2)}) async-start(s8[16777216]{0:T(1024)(128)(4,1)} %bitcast.232), calls=%async_computation.19 | async-start | bytes 8388608
  376.6 18.8 %slice-start.1 = ((s8[16777216]{0:T(1024)(128)(4,1)}), s8[4194304]{0:T(1024)(128)(4,1)S(1)}, s32[]{:S(2)}) async-start(s8[16777216]{0:T(1024)(128)(4,1)} %bitcast.232), calls=%async_computation.20 | async-start | bytes 8388608
  376.6 18.8 %slice-start.2 = ((s8[16777216]{0:T(1024)(128)(4,1)}), s8[4194304]{0:T(1024)(128)(4,1)S(1)}, s32[]{:S(2)}) async-start(s8[16777216]{0:T(1024)(128)(4,1)} %bitcast.232), calls=%async_computation.21 | async-start | bytes 8388608
  403.9 8.7 copy-start.12
  415.3 11.4 slice-start.4
  417.8 8.8 slice-start.5
  417.8 8.8 slice-start.6
  417.9 9.5 slice-start.7
  450.0 8.3 copy-start.25
  463.0 8.5 copy-start.7
  473.1 124.4 %reduce-scatter.10.cloned.1.call-start = ((), (), s32[]{:S(2)}) async-start(), calls=%async_computation.12 | async-start | bytes 294912 | tf_op jit(solution)/shard_map/reduce_scatter | solution.py:262
  475.4 7.4 copy-start.29
  482.8 271.6 %all-reduce.12.cloned.1.call-start = ((), (), s32[]{:S(2)}) async-start(), calls=%async_computation.18 | async-start | bytes 16777216 | tf_op jit(solution)/shard_map/psum | solution.py:205
  492.0 332.6 %reduce-scatter.14.cloned.1.call-start = ((), (), s32[]{:S(2)}) async-start(), calls=%async_computation.14 | async-start | bytes 2359296 | tf_op jit(solution)/shard_map/reduce_scatter | solution.py:268
  500.4 395.0 %reduce-scatter.8.cloned.1.call-start = ((), (), s32[]{:S(2)}) async-start(), calls=%async_computation.11 | async-start | bytes 2359296 | tf_op jit(solution)/shard_map/reduce_scatter | solution.py:259
  506.3 503.7 %reduce-scatter.20.cloned.1.call-start = ((), (), s32[]{:S(2)}) async-start(), calls=%async_computation.17 | async-start | bytes 6488064 | tf_op jit(solution)/shard_map/reduce_scatter | solution.py:277
  517.1 606.4 %reduce-scatter.18.cloned.1.call-start = ((), (), s32[]{:S(2)}) async-start(), calls=%async_computation.16 | async-start | bytes 6488064 | tf_op jit(solution)/shard_map/reduce_scatter | solution.py:274
  528.2 708.6 %reduce-scatter.16.cloned.1.call-start = ((), (), s32[]{:S(2)}) async-start(), calls=%async_computation.15 | async-start | bytes 6488064 | tf_op jit(solution)/shard_map/reduce_scatter | solution.py:271
  540.2 7.4 copy-start.10
  547.6 206.8 %copy-start.34 = (f32[2048]{0:T(1024)S(1)}, f32[2048]{0:T(1024)}, u32[]{:S(2)}) copy-start(f32[2048]{0:T(1024)} %param.17) | copy-start | bytes 24580
  897.2 341.9 %copy-start.1 = (bf16[512,2048]{1,0:T(8,128)(2,1)S(1)}, bf16[512,2048]{1,0:T(8,128)(2,1)}, u32[]{:S(2)}) copy-start(bf16[512,2048]{1,0:T(8,128)(2,1)} %param.21) | copy-start | bytes 6291460
  (24 other events, 87.9 us)
Sparse Core Ops, SparseCore 0:
  9.6 36.0 all-gather.2
  125.3 84.9 all-reduce.7
  211.9 35.1 all-gather.4
  284.8 84.9 all-reduce.9
  473.2 59.8 reduce-scatter.11
  536.8 60.6 reduce-scatter.9
  600.1 154.2 all-reduce.11
  757.9 66.6 reduce-scatter.13
  828.8 66.5 reduce-scatter.7
  898.9 111.0 reduce-scatter.19
  1013.7 109.7 reduce-scatter.17
  1127.0 109.7 reduce-scatter.15
where the time goes:
time: 1260 us; the launch traced here: 1250 us
  waiting for transfers between devices  826 us (66%)
  matrix products  245 us (19%)
  other arithmetic  109 us (9%)
  blocking collectives  40 us (3%)
  between operations  15.3 us (1%)
    psum x1, waiting for transfers between devices, per_device(): lax.psum(mlp_part.astype(jnp.bfloat16), 'tensor').astype(jnp.float32)  155 us
    reduce_scatter x1, waiting for transfers between devices, per_device(): lax.psum_scatter(grad_up.astype(jnp.bfloat16), 'dp', scatter_dimension=0,...  111 us
    reduce_scatter x1, waiting for transfers between devices, per_device(): lax.psum_scatter(grad_gate.astype(jnp.bfloat16), 'dp', scatter_dimension=...  111 us
    reduce_scatter x1, waiting for transfers between devices, per_device(): lax.psum_scatter(grad_down.astype(jnp.bfloat16), 'dp', scatter_dimension=...  108 us
    psum x1, waiting for transfers between devices, per_device(): lax.psum(attn_part.astype(jnp.bfloat16), 'tensor').astype(jnp.float32)  84.3 us
    psum x1, waiting for transfers between devices, per_device(): lax.psum(d_norm_part.astype(jnp.bfloat16), 'tensor').astype(jnp.float32)  73.9 us
    reduce_scatter x1, waiting for transfers between devices, per_device(): lax.psum_scatter(grad_query.astype(jnp.bfloat16), 'dp', scatter_dimension...  69 us
    dot_general x7, matrix products, contract_cols(): lax.dot_general(left, right, (((1,), (1,)), ((), ())), preferred_element_...  64.5 us
  transfers between devices with their start and end apart: 12, of which 11 were waited for; matrix products, arithmetic and copies ran while one was open for 11% of the time, Pallas kernels for 0%

commit v1 on v0

v1 whole, which is shorter than its diff:
```python
import functools

import jax
import jax.numpy as jnp
from jax import lax
from jax.experimental import pallas as pl
from jax.experimental.pallas import tpu as pltpu
from jax.sharding import PartitionSpec as P

HD = 64
SEQ = 1024
PIECE = 256
QB = 256


EPSILON = 1e-05
ROPE_BASE = 10000.0
MASKED = -1e30
VMEM_LIMIT = 48 * 2**20
NT = (((1,), (1,)), ((), ()))
TN = (((0,), (0,)), ((), ()))


def dot(left, right):
    return jnp.dot(left, right, preferred_element_type=jnp.float32)


def contract_rows(left, right):
    return lax.dot_general(left, right, TN, preferred_element_type=jnp.float32)


def contract_cols(left, right):
    return lax.dot_general(left, right, NT, preferred_element_type=jnp.float32)


def rms_inverse(resid):
    return lax.rsqrt(jnp.mean(resid * resid, axis=-1, keepdims=True) + EPSILON)


def norm_back(d_norm, resid, inverse, gain):
    scaled = d_norm * gain
    return inverse * scaled - resid * (inverse * inverse * inverse) * jnp.mean(
        scaled * resid, axis=-1, keepdims=True
    )


def rope_tables(positions):
    half_dim = HD // 2
    inverse = jnp.power(ROPE_BASE, -(jnp.arange(half_dim).astype(jnp.float32) * 2.0) / HD)
    angles = positions.astype(jnp.float32)[:, None] * inverse[None, :]
    cos, sin = jnp.cos(angles), jnp.sin(angles)
    return jnp.concatenate([cos] * 4, axis=1), jnp.concatenate([-sin, sin] * 2, axis=1)


def swap_halves(pair):
    lane = lax.broadcasted_iota(jnp.int32, pair.shape, 1)
    up = pltpu.roll(pair, 2 * HD - HD // 2, 1)
    down = pltpu.roll(pair, HD // 2, 1)
    return jnp.where(lane % HD < HD // 2, up, down)


def rotate_rows(grad, cos_tab, sin_tab):
    half = HD // 2
    swapped = jnp.concatenate([grad[:, half:], grad[:, :half]], axis=1)
    return grad * cos_tab[:, :HD] - swapped * sin_tab[:, :HD]


def project_kernel(x_ref, gain_ref, wq_ref, wkv_ref, cos_ref, sin_ref, n_ref, q_ref, k_ref, v_ref):
    resid = x_ref[...].astype(jnp.float32)
    normed = (resid * rms_inverse(resid) * gain_ref[...]).astype(jnp.bfloat16)
    n_ref[...] = normed
    cos, sin = cos_ref[...], sin_ref[...]
    query = dot(normed, wq_ref[...])
    for first in range(0, query.shape[1], 2 * HD):
        pair = query[:, first : first + 2 * HD]
        turned = (pair * cos + swap_halves(pair) * sin) * HD ** (-0.5)
        q_ref[:, first : first + 2 * HD] = turned.astype(jnp.bfloat16)
    key_value = dot(normed, wkv_ref[...])
    turned = key_value * cos + swap_halves(key_value) * sin
    k_ref[...] = turned[:, :HD].astype(jnp.bfloat16)
    v_ref[...] = key_value[:, HD:].astype(jnp.bfloat16)


def project(x, gain, w_query, w_kv, cos_tab, sin_tab):
    rows, width = x.shape
    queries = w_query.shape[1]

    def tall(cols):
        return pl.BlockSpec((QB, cols), lambda i: (i, 0))

    def whole(array):
        return pl.BlockSpec(array.shape, lambda i: (0, 0))

    return pl.pallas_call(
        project_kernel,
        grid=(rows // QB,),
        in_specs=[
            tall(width),
            pl.BlockSpec((1, width), lambda i: (0, 0)),
            whole(w_query),
            whole(w_kv),
            tall(2 * HD),
            tall(2 * HD),
        ],
        out_specs=[tall(width), tall(queries), tall(HD), tall(HD)],
        out_shape=[
            jax.ShapeDtypeStruct((rows, width), jnp.bfloat16),
            jax.ShapeDtypeStruct((rows, queries), jnp.bfloat16),
            jax.ShapeDtypeStruct((rows, HD), jnp.bfloat16),
            jax.ShapeDtypeStruct((rows, HD), jnp.bfloat16),
        ],
        compiler_params=pltpu.CompilerParams(vmem_limit_bytes=VMEM_LIMIT),
        cost_estimate=pl.CostEstimate(
            flops=2 * rows * width * (queries + 2 * HD),
            bytes_accessed=4 * rows * width + 2 * width * (queries + 2 * HD),
            transcendentals=0,
        ),
        name="project",
    )(x, gain[None, :], w_query, w_kv, cos_tab, sin_tab)


def see(qpos, kpos, starts_ref, pics):
    mask = kpos <= qpos
    for pic in range(pics):
        begin = starts_ref[pic]
        mask = mask | (
            (qpos >= begin) & (qpos < begin + PIECE) & (kpos >= begin) & (kpos < begin + PIECE)
        )
    return mask


def key_blocks(starts_ref, pics, first):
    edge = first + QB
    crossed = jnp.bool_(False)
    for pic in range(pics):
        begin = starts_ref[pic]
        crossed = crossed | ((begin < edge) & (begin + PIECE > edge))
    return edge // QB + jnp.where(crossed, 1, 0)


def forward_kernel(
    pos_ref, starts_ref, q_ref, k_ref, v_ref, o_ref, lse_ref, bias, *, heads, pics, seq
):
    first = pos_ref[pl.program_id(0)]
    count = key_blocks(starts_ref, pics, first)
    for blocks in range(1, seq // QB + 1):

        @pl.when(count == blocks)
        def _():
            ext = blocks * QB
            low = max(0, ext - 2 * QB)
            wide = ext - low
            qpos = lax.broadcasted_iota(jnp.int32, (QB, wide), 0) + first
            kpos = lax.broadcasted_iota(jnp.int32, (QB, wide), 1) + low
            bias[:, :wide] = jnp.where(see(qpos, kpos, starts_ref, pics), 0.0, MASKED)
            outs, stats = [], []
            values = jnp.concatenate([v_ref[:ext, :], jnp.ones((ext, HD), jnp.bfloat16)], axis=1)
            for head in range(heads):
                queries = q_ref[:, head * HD : (head + 1) * HD]
                scores = contract_cols(queries, k_ref[:ext, :])
                if low:
                    scores = jnp.concatenate(
                        [scores[:, :low], scores[:, low:] + bias[:, :wide]], axis=1
                    )
                else:
                    scores = scores + bias[:, :wide]
                row_max = jnp.max(scores, axis=1, keepdims=True)
                terms = jnp.exp(scores - row_max).astype(jnp.bfloat16)
                summed = dot(terms, values)
                row_sum = summed[:, HD : HD + 1]
                outs.append(summed[:, :HD] / row_sum)
                stats.append(row_max + jnp.log(row_sum))
            o_ref[...] = jnp.concatenate(outs, axis=1).astype(jnp.bfloat16)
            lse_ref[...] = jnp.concatenate(stats, axis=1)


def attend_forward(q_low, k_low, v_low, starts, positions):
    rows, width = q_low.shape
    heads, seq, pics = width // HD, k_low.shape[0], starts.shape[0]
    tall = pl.BlockSpec((QB, width), lambda i, *_: (i, 0))
    keys = pl.BlockSpec((seq, HD), lambda i, *_: (0, 0))
    return pl.pallas_call(
        functools.partial(forward_kernel, heads=heads, pics=pics, seq=seq),
        grid_spec=pltpu.PrefetchScalarGridSpec(
            num_scalar_prefetch=2,
            grid=(rows // QB,),
            in_specs=[tall, keys, keys],
            out_specs=[tall, pl.BlockSpec((QB, heads), lambda i, *_: (i, 0))],
            scratch_shapes=[pltpu.VMEM((QB, 2 * QB), jnp.float32)],
        ),
        out_shape=[
            jax.ShapeDtypeStruct((rows, width), jnp.bfloat16),
            jax.ShapeDtypeStruct((rows, heads), jnp.float32),
        ],
        compiler_params=pltpu.CompilerParams(vmem_limit_bytes=VMEM_LIMIT),
        cost_estimate=pl.CostEstimate(
            flops=16 * rows * seq * width, bytes_accessed=4 * rows * width, transcendentals=0
        ),
        name="attend_forward",
    )(positions, starts, q_low, k_low, v_low)


def in_three(value):
    top = value.astype(jnp.bfloat16)
    rest = value - top.astype(jnp.float32)
    middle = rest.astype(jnp.bfloat16)
    last = (rest - middle.astype(jnp.float32)).astype(jnp.bfloat16)
    return [top, middle, last]


def backward_kernel(
    pos_ref, starts_ref, q_ref, do_ref, o_ref, lse_ref, k_ref, v_ref, cos_ref, sin_ref,
    dq_ref, dk_ref, dv_ref, bias, *, heads, pics, seq
):
    first = pos_ref[pl.program_id(0)]
    count = key_blocks(starts_ref, pics, first)

    @pl.when(pl.program_id(0) == 0)
    def _():
        dk_ref[...] = jnp.zeros_like(dk_ref)
        dv_ref[...] = jnp.zeros_like(dv_ref)

    for blocks in range(1, seq // QB + 1):

        @pl.when(count == blocks)
        def _():
            ext = blocks * QB
            low = max(0, ext - 2 * QB)
            wide = ext - low
            kpos = lax.broadcasted_iota(jnp.int32, (wide, QB), 0) + low
            qpos = lax.broadcasted_iota(jnp.int32, (wide, QB), 1) + first
            bias[:wide, :] = jnp.where(see(qpos, kpos, starts_ref, pics), 0.0, MASKED)
            ones = jnp.ones((ext, HD), jnp.bfloat16)
            keys = jnp.concatenate([k_ref[:ext, :], ones], axis=1)
            values = jnp.concatenate([v_ref[:ext, :], ones], axis=1)
            zeros = jnp.zeros((QB, HD - 3), jnp.bfloat16)
            d_key = jnp.zeros((ext, HD), jnp.float32)
            d_val = jnp.zeros((ext, HD), jnp.float32)
            for pair in range(heads // 2):
                parts = []
                for head in (2 * pair, 2 * pair + 1):
                    cols = slice(head * HD, (head + 1) * HD)
                    queries, d_out = q_ref[:, cols], do_ref[:, cols]
                    delta = jnp.sum(
                        d_out.astype(jnp.float32) * o_ref[:, cols].astype(jnp.float32),
                        axis=1,
                        keepdims=True,
                    )
                    queries_ext = jnp.concatenate(
                        [queries] + in_three(-lse_ref[:, head : head + 1]) + [zeros], axis=1
                    )
                    d_out_ext = jnp.concatenate([d_out] + in_three(-delta) + [zeros], axis=1)
                    scores = contract_cols(keys, queries_ext)
                    if low:
                        scores = jnp.concatenate(
                            [scores[:low], scores[low:] + bias[:wide, :]], axis=0
                        )
                    else:
                        scores = scores + bias[:wide, :]
                    probs = jnp.exp(scores)
                    d_probs = contract_cols(values, d_out_ext)
                    d_scores = (probs * d_probs).astype(jnp.bfloat16)
                    d_val += dot(probs.astype(jnp.bfloat16), d_out)
                    d_key += dot(d_scores, queries)
                    parts.append(contract_rows(d_scores, k_ref[:ext, :]))
                both = jnp.concatenate(parts, axis=1) * HD ** (-0.5)
                turned = both * cos_ref[...] - swap_halves(both) * sin_ref[...]
                dq_ref[:, 2 * pair * HD : 2 * (pair + 1) * HD] = turned.astype(jnp.bfloat16)
            dk_ref[:ext, :] += d_key
            dv_ref[:ext, :] += d_val


def attend_backward(q_low, d_attn, attn_low, lse, k_low, v_low, cos_tab, sin_tab, starts, positions):
    rows, width = q_low.shape
    heads, seq, pics = width // HD, k_low.shape[0], starts.shape[0]
    tall = pl.BlockSpec((QB, width), lambda i, *_: (i, 0))
    table = pl.BlockSpec((QB, 2 * HD), lambda i, *_: (i, 0))
    keys = pl.BlockSpec((seq, HD), lambda i, *_: (0, 0))
    return pl.pallas_call(
        functools.partial(backward_kernel, heads=heads, pics=pics, seq=seq),
        grid_spec=pltpu.PrefetchScalarGridSpec(
            num_scalar_prefetch=2,
            grid=(rows // QB,),
            in_specs=[
                tall, tall, tall, pl.BlockSpec((QB, heads), lambda i, *_: (i, 0)), keys, keys, table, table
            ],
            out_specs=[tall, keys, keys],
            scratch_shapes=[pltpu.VMEM((2 * QB, QB), jnp.float32)],
        ),
        out_shape=[
            jax.ShapeDtypeStruct((rows, width), jnp.bfloat16),
            jax.ShapeDtypeStruct((seq, HD), jnp.float32),
            jax.ShapeDtypeStruct((seq, HD), jnp.float32),
        ],
        compiler_params=pltpu.CompilerParams(vmem_limit_bytes=VMEM_LIMIT),
        cost_estimate=pl.CostEstimate(
            flops=32 * rows * seq * width, bytes_accessed=8 * rows * width, transcendentals=0
        ),
        name="attend_backward",
    )(positions, starts, q_low, d_attn, attn_low, lse, k_low, v_low, cos_tab, sin_tab)


def swap_core(value):
    return lax.ppermute(value, "tensor", [(i, i ^ 1) for i in range(4)])


def swap_chip(value):
    return lax.ppermute(value, "tensor", [(i, i ^ 2) for i in range(4)])


def gather_near(own):
    return jnp.concatenate([own, swap_core(own)], axis=0)


def gather_far(own):
    far = swap_chip(own)
    return jnp.concatenate([far, swap_core(far)], axis=0)


def send_far(part):
    rows = part.shape[0] // 2
    low = part.astype(jnp.bfloat16)
    chip_sum = low[:rows].astype(jnp.float32) + swap_core(low[rows:]).astype(jnp.float32)
    return swap_chip(chip_sum.astype(jnp.bfloat16)).astype(jnp.float32)


def sum_near(part):
    rows = part.shape[0] // 2
    return part[:rows] + swap_core(part[rows:].astype(jnp.bfloat16)).astype(jnp.float32)


def block_order(bits):
    order = [0]
    for bit in reversed(bits):
        order = [item ^ bit for item in order] + order
    return order


def permuted_features(value, index, bits):
    order = block_order(bits)
    width = value.shape[1] // len(order)
    return jnp.concatenate(
        [lax.dynamic_slice_in_dim(value, (index ^ item) * width, width, 1) for item in order], axis=1
    )


def reduce(make, total, axis, bits, size):
    half = total // 2
    sent = make(0, half).astype(jnp.bfloat16)
    kept = make(half, total).astype(jnp.bfloat16)
    for step, bit in enumerate(bits):
        came = lax.ppermute(sent, "dp", [(i, i ^ bit) for i in range(size)])
        added = kept.astype(jnp.float32) + came.astype(jnp.float32)
        if step == len(bits) - 1:
            return added
        added = added.astype(jnp.bfloat16)
        half = added.shape[axis] // 2
        sent = lax.slice_in_dim(added, 0, half, axis=axis)
        kept = lax.slice_in_dim(added, half, 2 * half, axis=axis)


def per_device(
    dp_size,
    layer_input,
    cotangent,
    starts,
    pieces,
    norm_attn,
    w_query,
    w_key,
    w_value,
    w_out,
    norm_mlp,
    w_gate,
    w_up,
    w_down,
):
    rows = layer_input.shape[0]
    width = layer_input.shape[1]
    place = lax.axis_index("tensor")
    index = lax.axis_index("dp")
    bits = [1 << i for i in range(dp_size.bit_length() - 1)]
    late_bits = bits[1:] + bits[:1]
    begins = starts[0]

    block_pos = jnp.stack([(place ^ m) * rows for m in range(4)]).astype(jnp.int32)
    near_pos, far_pos = block_pos[:2], block_pos[2:]
    row_pos = (block_pos[:, None] + jnp.arange(rows, dtype=jnp.int32)[None, :]).reshape(-1)
    cos_tab, sin_tab = rope_tables(row_pos)
    w_kv = jnp.concatenate([w_key, w_value], axis=1)

    def in_sequence(value):
        return jnp.concatenate(
            [lax.dynamic_slice_in_dim(value, (place ^ b) * rows, rows, 0) for b in range(4)], axis=0
        )

    near, far = slice(0, 2 * rows), slice(2 * rows, 4 * rows)
    x_near, x_far = gather_near(layer_input), gather_far(layer_input)
    cot_near, cot_far = gather_near(cotangent), gather_far(cotangent)
    normed_n, q_n, k_n, v_n = project(x_near, norm_attn, w_query, w_kv, cos_tab[near], sin_tab[near])
    normed_f, q_f, k_f, v_f = project(x_far, norm_attn, w_query, w_kv, cos_tab[far], sin_tab[far])
    k_low = in_sequence(jnp.concatenate([k_n, k_f], axis=0))
    v_low = in_sequence(jnp.concatenate([v_n, v_f], axis=0))
    attn_f, lse_f = attend_forward(q_f, k_low, v_low, begins, far_pos)
    attn_sent = send_far(dot(attn_f, w_out))
    attn_n, lse_n = attend_forward(q_n, k_low, v_low, begins, near_pos)
    attn_total = sum_near(dot(attn_n, w_out)) + attn_sent

    resid_in = layer_input.astype(jnp.float32)
    resid_mid = resid_in + attn_total
    inv_mlp = rms_inverse(resid_mid)
    normed_own = (resid_mid * inv_mlp * norm_mlp).astype(jnp.bfloat16)

    def feed_forward(normed, cot):
        gate_val, up_val = dot(normed, w_gate), dot(normed, w_up)
        gate_sig = jax.nn.sigmoid(gate_val)
        hidden = (gate_val * gate_sig * up_val).astype(jnp.bfloat16)
        d_hidden = contract_cols(cot, w_down)
        d_gate = d_hidden * up_val * (gate_sig * (1.0 + gate_val * (1.0 - gate_sig)))
        d_up = d_hidden * gate_val * gate_sig
        return hidden, d_gate.astype(jnp.bfloat16), d_up.astype(jnp.bfloat16)

    mlp_n, mlp_f = gather_near(normed_own), gather_far(normed_own)
    hidden_n, d_gate_n, d_up_n = feed_forward(mlp_n, cot_near)
    hidden_f, d_gate_f, d_up_f = feed_forward(mlp_f, cot_far)

    def norm_part(d_gate, d_up):
        return contract_cols(d_gate, w_gate) + contract_cols(d_up, w_up)

    d_norm_sent = send_far(norm_part(d_gate_f, d_up_f))
    d_norm_mid = sum_near(norm_part(d_gate_n, d_up_n)) + d_norm_sent

    def rows_of(one, two):
        return jnp.concatenate([one, two], axis=0)

    hidden, d_gate, d_up = (
        rows_of(hidden_n, hidden_f),
        rows_of(d_gate_n, d_gate_f),
        rows_of(d_up_n, d_up_f),
    )
    cot_blocks = permuted_features(rows_of(cot_near, cot_far), index, bits)
    mlp_blocks = permuted_features(rows_of(mlp_n, mlp_f), index, bits)
    grad_down = reduce(
        lambda a, b: contract_rows(hidden, cot_blocks[:, a:b]), width, 1, bits, dp_size
    )
    grad_gate = reduce(
        lambda a, b: contract_rows(mlp_blocks[:, a:b], d_gate), width, 0, bits, dp_size
    )
    grad_up = reduce(lambda a, b: contract_rows(mlp_blocks[:, a:b], d_up), width, 0, bits, dp_size)

    mlp_sent = send_far(dot(hidden_f, w_down))
    mlp_total = sum_near(dot(hidden_n, w_down)) + mlp_sent
    block_out = (resid_mid + mlp_total).astype(jnp.bfloat16)

    d_mid = cotangent.astype(jnp.float32) + norm_back(d_norm_mid, resid_mid, inv_mlp, norm_mlp)
    d_out_own = d_mid.astype(jnp.bfloat16)
    d_out_n, d_out_f = gather_near(d_out_own), gather_far(d_out_own)
    d_attn_n = contract_cols(d_out_n, w_out).astype(jnp.bfloat16)
    d_attn_f = contract_cols(d_out_f, w_out).astype(jnp.bfloat16)
    dq_n, dk_n, dv_n = attend_backward(
        q_n, d_attn_n, attn_n, lse_n, k_low, v_low, cos_tab[near], sin_tab[near], begins, near_pos
    )
    dq_f, dk_f, dv_f = attend_backward(
        q_f, d_attn_f, attn_f, lse_f, k_low, v_low, cos_tab[far], sin_tab[far], begins, far_pos
    )
    d_key = rotate_rows(in_sequence(dk_n + dk_f), cos_tab, sin_tab)
    d_value = in_sequence(dv_n + dv_f)
    d_kv = jnp.concatenate([d_key, d_value], axis=1).astype(jnp.bfloat16)
    d_norm_in_sent = send_far(contract_cols(dq_f, w_query) + contract_cols(d_kv[far], w_kv))
    d_norm_in = (
        sum_near(contract_cols(dq_n, w_query) + contract_cols(d_kv[near], w_kv)) + d_norm_in_sent
    )
    d_out_blocks = permuted_features(rows_of(d_out_n, d_out_f), index, late_bits)
    attn_low = rows_of(attn_n, attn_f)
    grad_out = reduce(
        lambda a, b: contract_rows(attn_low, d_out_blocks[:, a:b]), width, 1, late_bits, dp_size
    )
    normed_blocks = permuted_features(rows_of(normed_n, normed_f), index, late_bits)
    d_qkv = jnp.concatenate([rows_of(dq_n, dq_f), d_kv], axis=1)
    grad_qkv = reduce(
        lambda a, b: contract_rows(normed_blocks[:, a:b], d_qkv), width, 0, late_bits, dp_size
    )
    queries = w_query.shape[1]
    grad_query = grad_qkv[:, :queries]
    grad_key = grad_qkv[:, queries : queries + HD]
    grad_value = grad_qkv[:, queries + HD :]

    x_grad = d_mid + norm_back(d_norm_in, resid_in, rms_inverse(resid_in), norm_attn)

    share = width // dp_size

    def own_features(value):
        return lax.dynamic_slice_in_dim(value, index * share, share, 0).astype(jnp.float32)

    gain_attn = (
        jnp.sum(own_features(w_query) * grad_query, axis=1)
        + jnp.sum(own_features(w_kv) * grad_qkv[:, queries:], axis=1)
    ) / own_features(norm_attn)
    gain_mlp = jnp.sum(
        own_features(w_gate) * grad_gate + own_features(w_up) * grad_up, axis=1
    ) / own_features(norm_mlp)
    gains = jnp.stack([gain_attn, gain_mlp]).reshape(2, 4, share // 4)
    gains = jnp.stack([lax.dynamic_index_in_dim(gains, place ^ m, 1, False) for m in range(4)])
    gains = gains[:2] + swap_chip(gains[2:])
    gains = gains[0] + swap_core(gains[1])

    return (
        block_out,
        x_grad,
        gains[0],
        grad_query,
        grad_key,
        grad_value,
        grad_out,
        gains[1],
        grad_gate,
        grad_up,
        grad_down,
    )


def solution(mesh):
    in_specs = (
        P(("dp", "tensor"), None),
        P(("dp", "tensor"), None),
        P("dp", None),
        P("dp"),
        P(),
        P(None, "tensor"),
        P(None, "tensor"),
        P(None, "tensor"),
        P("tensor", None),
        P(),
        P(None, "tensor"),
        P(None, "tensor"),
        P("tensor", None),
    )
    out_specs = (
        P(("dp", "tensor"), None),
        P(("dp", "tensor"), None),
        P(("dp", "tensor")),
        P("dp", "tensor"),
        P("dp", "tensor"),
        P("dp", "tensor"),
        P("tensor", "dp"),
        P(("dp", "tensor")),
        P("dp", "tensor"),
        P("dp", "tensor"),
        P("tensor", "dp"),
    )
    return jax.shard_map(
        functools.partial(per_device, mesh.shape["dp"]),
        mesh=mesh,
        in_specs=in_specs,
        out_specs=out_specs,
        check_vma=False,
    )
```

time: 1260 us -> 629 us (0.50)
  waiting for transfers between devices: 826 us -> 300 us
  matrix products: 245 us -> 124 us
  other arithmetic: 109 us -> 50.7 us
  Pallas kernels: 0 us -> 56.5 us
  blocking collectives: 40 us -> 0 us
  local copies, waits for them, and re-layouts: 11.4 us -> 49.8 us
  starting transfers between devices: 0.49 us -> 35.9 us
    reduce_scatter x7 -> x0, waiting for transfers between devices: 466 us -> none  [the longest x1 111 us: per_device(): lax.psum_scatter(grad_up.astype(jnp.bfloat16), 'dp', scatter_dimension=0,...]
    psum x3 -> x0, waiting for transfers between devices: 314 us -> none  [the longest x1 155 us: per_device(): lax.psum(mlp_part.astype(jnp.bfloat16), 'tensor').astype(jnp.float32)]
    ppermute x0 -> x41, waiting for transfers between devices: none -> 300 us  [the longest x15 225 us: reduce(): came = lax.ppermute(sent, 'dp', [(i, i ^ bit) for i in range(size)])]
    dot_general x33 -> x30, matrix products: 245 us -> 124 us  [the longest x12 53.1 us: contract_cols(): return lax.dot_general(left, right, NT, preferred_element_type=jnp.float32)]
    pallas_call x0 -> x6, Pallas kernels: none -> 56.5 us  [the longest x2 28.3 us: attend_backward(): pl.pallas_call(functools.partial(backward_kernel, heads=heads, pics=pics,...]
    all_gather x2 -> x0, waiting for transfers between devices: 44.4 us -> none  [the longest x1 33.6 us: per_device(): lax.all_gather(layer_input, 'tensor', axis=0, tiled=True)]
    unnamed x1 -> x0, blocking collectives: 40 us -> none
    ppermute x0 -> x41, starting transfers between devices: none -> 35.9 us  [the longest x15 16.6 us: reduce(): came = lax.ppermute(sent, 'dp', [(i, i ^ bit) for i in range(size)])]
  transfers between devices with their start and end apart: 12 -> 41, of which waited for: 11 -> 12; matrix products, arithmetic and copies ran while one was open for 11% -> 32% of each run, Pallas kernels for 0% -> 7%
where the time goes in v1:
time: 629 us; the launch traced here: 619 us
  waiting for transfers between devices  300 us (48%)
  matrix products  124 us (20%)
  Pallas kernels  56.5 us (9%)
  other arithmetic  50.7 us (8%)
  local copies, waits for them, and re-layouts  49.8 us (8%)
  starting transfers between devices  35.9 us (6%)
    ppermute x15, waiting for transfers between devices, reduce(): came = lax.ppermute(sent, 'dp', [(i, i ^ bit) for i in range(size)])  225 us
    ppermute x9, waiting for transfers between devices, swap_chip(): return lax.ppermute(value, 'tensor', [(i, i ^ 2) for i in range(4)])  74.6 us
    dot_general x12, matrix products, contract_cols(): return lax.dot_general(left, right, NT, preferred_element_type=jnp.float32)  53.1 us
    dot_general x10, matrix products, contract_rows(): return lax.dot_general(left, right, TN, preferred_element_type=jnp.float32)  37.5 us
    dot_general x8, matrix products, dot(): return jnp.dot(left, right, preferred_element_type=jnp.float32)  33.2 us
    pallas_call x2, Pallas kernels, attend_backward(): pl.pallas_call(functools.partial(backward_kernel, heads=heads, pics=pics,...  28.3 us
    unnamed x249, local copies, waits for them, and re-layouts  28.2 us
    pallas_call x2, Pallas kernels, attend_forward(): pl.pallas_call(functools.partial(forward_kernel, heads=heads, pics=pics,...  19.5 us
  transfers between devices with their start and end apart: 41, of which 12 were waited for; matrix products, arithmetic and copies ran while one was open for 32% of the time, Pallas kernels for 7%

profile of v1, /device:TPU:9, one launch (start us, length us, event | category | flops | bytes accessed | tf_op | source)
XLA Modules:
  0.0 619.4 jit_solution(8107826254862866672)
XLA Ops:
  3.1 3.0 fusion.99
  10.1 3.5 pad_maximum_fusion.18
  13.7 11.4 %collective-permute-done.1 = bf16[256,2048]{1,0:T(8,128)(2,1)} collective-permute-done((bf16[256,2048]{1,0:T(8,128)(2,1)}, bf16[256,2048]{1,0:T(8,128)(2,1)}, u32[]{:S(2)}, u32[]{:S(2)}) %collective-permute-start.1) | collective-permute-done | bytes 1048608 | tf_op jit(solution)/shard_map/ppermute | solution.py:308
  30.0 4.3 project.2
  34.4 2.6 pad_maximum_fusion.6.x_ref
  37.0 4.3 project.3
  42.1 10.0 %attend_forward.3 = (bf16[512,512]{1,0:T(8,128)(2,1)S(1)}, f32[512,8]{1,0:T(8,128)S(1)}) custom-call(s32[2]{0:T(128)S(1)} %get-tuple-element.146.pos_ref, s32[2]{0:T(128)S(1)} %bitcast.63, bf16[512,512]{1,0:T(8,128)(2,1)S(1)} %get-tuple-element.35.q_ref, bf16[1024,64]{1,0:T(8,128)(2,1)S(1)} %pad_maximum_fusion.26.k_ref, ...), custom_call_target="tpu_custom_call" | custom-call | flops 4294967296 | bytes 1048576 | tf_op jit(solution)/shard_map/attend_forward/pallas_call | solution.py:182
  57.7 9.5 %attend_forward.2 = (bf16[512,512]{1,0:T(8,128)(2,1)S(1)}, f32[512,8]{1,0:T(8,128)S(1)}) custom-call(s32[2]{0:T(128)S(1)} %get-tuple-element.145.pos_ref, s32[2]{0:T(128)S(1)} %bitcast.64, bf16[512,512]{1,0:T(8,128)(2,1)S(1)} %copy-done.24, bf16[1024,64]{1,0:T(8,128)(2,1)S(1)} %copy-done.15, bf16[1024,64]{1,0:T(8,128)(2,1)S(1)} %pad_maximum_fusion.27.v_ref), custom_call_target="tpu_custom_call" | custom-call | flops 4294967296 | bytes 1048576 | tf_op jit(solution)/shard_map/attend_forward/pallas_call | solution.py:182
  71.7 2.4 collective-permute-start.5
  75.5 5.3 collective-permute-done.14
  85.0 18.2 %collective-permute-done.5 = bf16[256,2048]{1,0:T(8,128)(2,1)S(1)} collective-permute-done((bf16[256,2048]{1,0:T(8,128)(2,1)S(1)}, bf16[256,2048]{1,0:T(8,128)(2,1)S(1)}, u32[]{:S(2)}, u32[]{:S(2)}) %collective-permute-start.5) | collective-permute-done | bytes 1048608 | tf_op jit(solution)/shard_map/ppermute | solution.py:308
  113.8 5.0 fusion.87
  118.8 5.0 fusion.88
  123.8 10.7 %multiply_convert_fusion.2 = (bf16[512,1408]{1,0:T(8,128)(2,1)S(1)}, bf16[512,1408]{1,0:T(8,128)(2,1)S(1)}, bf16[512,1408]{1,0:T(8,128)(2,1)}) fusion(f32[512,1408]{1,0:T(8,128)} %fusion.88, f32[512,1408]{1,0:T(8,128)} %fusion.87, bf16[1408,2048]{1,0:T(8,128)(2,1)} %param.24, bf16[256,2048]{1,0:T(8,128)(2,1)} %collective-permute-done.12, ...), kind=kOutput, calls=%fused_computation.29 | convolution fusion | flops 2968518656 | bytes 17956864 | tf_op jit(solution)/shard_map/dot_general | solution.py:33
  134.6 5.1 fusion.138
  139.7 7.1 %convolution_add_fusion.1 = f32[512,2048]{1,0:T(8,128)S(1)} fusion(f32[512,2048]{1,0:T(8,128)} %fusion.138, bf16[512,1408]{1,0:T(8,128)(2,1)S(1)} %get-tuple-element.69, bf16[2048,1408]{1,0:T(8,128)(2,1)} %param.23), kind=kOutput, calls=%fused_computation.18 | convolution fusion | flops 2953838592 | bytes 15597568 | tf_op jit(solution)/shard_map/dot_general | solution.py:33
  148.8 3.5 fusion.135
  154.6 5.0 fusion.136
  159.7 5.1 fusion.137
  164.7 10.3 %multiply_convert_fusion = (bf16[512,1408]{1,0:T(8,128)(2,1)}, bf16[512,1408]{1,0:T(8,128)(2,1)}, bf16[512,1408]{1,0:T(8,128)(2,1)}) fusion(f32[512,1408]{1,0:T(8,128)S(1)} %copy-done.107, f32[512,1408]{1,0:T(8,128)} %fusion.137, bf16[1408,2048]{1,0:T(8,128)(2,1)} %param.24, bf16[256,2048]{1,0:T(8,128)(2,1)S(1)} %copy-done.57, ...), kind=kOutput, calls=%fused_computation.27 | convolution fusion | flops 2968518656 | bytes 17956864 | tf_op jit(solution)/shard_map/dot_general | solution.py:33
  175.1 7.0 %convolution_convert_fusion.7 = bf16[512,2048]{1,0:T(8,128)(2,1)S(1)} fusion(bf16[512,1408]{1,0:T(8,128)(2,1)} %get-tuple-element.74, bf16[1408,2048]{1,0:T(8,128)(2,1)} %param.24), kind=kOutput, calls=%fused_computation.20 | convolution fusion | flops 2953838592 | bytes 9306112 | tf_op jit(solution)/shard_map/dot_general | solution.py:25
  182.2 4.8 convolution_convert_fusion
  189.2 5.5 fusion.139
  194.7 6.5 %add_convert_fusion.4 = bf16[512,2048]{1,0:T(8,128)(2,1)S(1)} fusion(f32[512,2048]{1,0:T(8,128)S(1)} %fusion.139, bf16[512,1408]{1,0:T(8,128)(2,1)} %get-tuple-element.72, bf16[2048,1408]{1,0:T(8,128)(2,1)} %param.23), kind=kOutput, calls=%fused_computation.6 | convolution fusion | flops 2954887168 | bytes 13500416 | tf_op jit(solution)/shard_map/dot_general | solution.py:33
  205.6 5.2 convolution_convert_fusion.2
  213.5 3.5 convolution_convert_fusion.4
  217.0 19.1 %collective-permute-done.17 = bf16[256,2048]{1,0:T(8,128)(2,1)S(1)} collective-permute-done((bf16[256,2048]{1,0:T(8,128)(2,1)S(1)}, bf16[256,2048]{1,0:T(8,128)(2,1)S(1)}, u32[]{:S(2)}, u32[]{:S(2)}) %collective-permute-start.17) | collective-permute-done | bytes 1048608 | tf_op jit(solution)/shard_map/ppermute | solution.py:308
  238.0 20.6 %collective-permute-done.11 = bf16[256,2048]{1,0:T(8,128)(2,1)S(1)} collective-permute-done((bf16[256,2048]{1,0:T(8,128)(2,1)S(1)}, bf16[256,2048]{1,0:T(8,128)(2,1)S(1)}, u32[]{:S(2)}, u32[]{:S(2)}) %collective-permute-start.11) | collective-permute-done | bytes 1048608 | tf_op jit(solution)/shard_map/ppermute | solution.py:308
  258.6 5.9 fusion.129
  266.2 5.6 add_convert_fusion
  273.2 39.5 %collective-permute-done.30 = bf16[1024,1408]{1,0:T(8,128)(2,1)} collective-permute-done((bf16[1024,1408]{1,0:T(8,128)(2,1)}, bf16[1024,1408]{1,0:T(8,128)(2,1)}, u32[]{:S(2)}, u32[]{:S(2)}) %collective-permute-start.30) | collective-permute-done | bytes 2883616 | tf_op jit(solution)/shard_map/ppermute | solution.py:352
  312.7 5.8 add_convert_fusion.1
  319.8 54.7 %collective-permute-done.27 = bf16[1024,1408]{1,0:T(8,128)(2,1)} collective-permute-done((bf16[1024,1408]{1,0:T(8,128)(2,1)S(1)}, bf16[1024,1408]{1,0:T(8,128)(2,1)}, u32[]{:S(2)}, u32[]{:S(2)}) %collective-permute-start.27) | collective-permute-done | bytes 2883616 | tf_op jit(solution)/shard_map/ppermute | solution.py:352
  374.5 5.4 add_convert_fusion.2
  385.6 12.6 %attend_backward.2 = (bf16[512,512]{1,0:T(8,128)(2,1)S(1)}, f32[1024,64]{1,0:T(8,128)S(1)}, f32[1024,64]{1,0:T(8,128)S(1)}) custom-call(s32[2]{0:T(128)S(1)} %get-tuple-element.145.pos_ref, s32[2]{0:T(128)S(1)} %bitcast.65, bf16[512,512]{1,0:T(8,128)(2,1)S(1)} %copy-done.25, bf16[512,512]{1,0:T(8,128)(2,1)S(1)} %fusion.92.do_ref, ...), custom_call_target="tpu_custom_call" | custom-call | flops 8589934592 | bytes 2097152 | tf_op jit(solution)/shard_map/attend_backward/pallas_call | solution.py:279
  403.6 2.2 fusion.81
  407.5 2.5 fusion.89.do_ref
  410.1 15.7 %attend_backward.3 = (bf16[512,512]{1,0:T(8,128)(2,1)S(1)}, f32[1024,64]{1,0:T(8,128)S(1)}, f32[1024,64]{1,0:T(8,128)S(1)}) custom-call(s32[2]{0:T(128)S(1)} %copy-done.20, s32[2]{0:T(128)S(1)} %bitcast.66, bf16[512,512]{1,0:T(8,128)(2,1)S(1)} %copy-done.22, bf16[512,512]{1,0:T(8,128)(2,1)S(1)} %fusion.89.do_ref, bf16[512,512]{1,0:T(8,128)(2,1)S(1)} %copy-done.13, ...), custom_call_target="tpu_custom_call" | custom-call | flops 8589934592 | bytes 2097152 | tf_op jit(solution)/shard_map/attend_backward/pallas_call | solution.py:279
  442.7 2.4 collective-permute-start.40
  449.2 32.4 %collective-permute-done.40 = bf16[1408,256]{1,0:T(8,128)(2,1)S(1)} collective-permute-done((bf16[1408,256]{1,0:T(8,128)(2,1)S(1)}, bf16[1408,256]{1,0:T(8,128)(2,1)S(1)}, u32[]{:S(2)}, u32[]{:S(2)}) %collective-permute-start.40) | collective-permute-done | bytes 720928 | tf_op jit(solution)/shard_map/ppermute | solution.py:352
  482.9 2.4 collective-permute-start.29
  490.4 74.8 %collective-permute-done.36 = bf16[512,512]{1,0:T(8,128)(2,1)S(1)} collective-permute-done((bf16[512,512]{1,0:T(8,128)(2,1)S(1)}, bf16[512,512]{1,0:T(8,128)(2,1)S(1)}, u32[]{:S(2)}, u32[]{:S(2)}) %collective-permute-start.36) | collective-permute-done | bytes 524320 | tf_op jit(solution)/shard_map/ppermute | solution.py:352
  565.2 3.1 collective-permute-start.25
  570.6 3.7 add_reduce_fusion
  577.2 18.4 %collective-permute-done.25 = bf16[512,640]{1,0:T(8,128)(2,1)} collective-permute-done((bf16[512,640]{1,0:T(8,128)(2,1)}, bf16[512,640]{1,0:T(8,128)(2,1)}, u32[]{:S(2)}, u32[]{:S(2)}) %collective-permute-start.25) | collective-permute-done | bytes 655392 | tf_op jit(solution)/shard_map/ppermute | solution.py:352
  598.4 3.0 fusion
  601.4 4.5 collective-permute-done.26
  609.3 5.0 fusion.3
  (414 shorter events, 113.2 us)
Async XLA Ops:
  0.6 51.6 %copy-start = (bf16[512,2048]{1,0:T(8,128)(2,1)S(1)}, bf16[512,2048]{1,0:T(8,128)(2,1)}, u32[]{:S(2)}) copy-start(bf16[512,2048]{1,0:T(8,128)(2,1)} %param.20) | copy-start | bytes 6291460
  0.7 24.4 %collective-permute-start.1 = (bf16[256,2048]{1,0:T(8,128)(2,1)}, bf16[256,2048]{1,0:T(8,128)(2,1)}, u32[]{:S(2)}, u32[]{:S(2)}) collective-permute-start(bf16[256,2048]{1,0:T(8,128)(2,1)} %param.13), channel_id=1, source_target_pairs={{0,2},{1,3},{2,0},{3,1},{4,6},{5,7},{6,4},{7,5},{8,10},{9,11},{10,... | collective-permute-start | bytes 3145736 | tf_op jit(solution)/shard_map/ppermute | solution.py:308
  1.9 26.2 %collective-permute-start = (bf16[256,2048]{1,0:T(8,128)(2,1)}, bf16[256,2048]{1,0:T(8,128)(2,1)}, u32[]{:S(2)}, u32[]{:S(2)}) collective-permute-start(bf16[256,2048]{1,0:T(8,128)(2,1)} %param.13), channel_id=1, source_target_pairs={{0,1},{1,0},{2,3},{3,2},{4,5},{5,4},{6,7},{7,6},{8,9},{9,8},{10,11... | collective-permute-start | bytes 3145736 | tf_op jit(solution)/shard_map/ppermute | solution.py:304
  25.1 9.4 %collective-permute-start.2 = (bf16[256,2048]{1,0:T(8,128)(2,1)}, bf16[256,2048]{1,0:T(8,128)(2,1)}, u32[]{:S(2)}, u32[]{:S(2)}) collective-permute-start(bf16[256,2048]{1,0:T(8,128)(2,1)} %collective-permute-done.1), channel_id=1, source_target_pairs={{0,1},{1,0},{2,3},{3,2},{4,5},{5,4},{6,7},{7,6},{8,9},{9,8},{10,11... | collective-permute-start | bytes 3145736 | tf_op jit(solution)/shard_map/ppermute | solution.py:304
  55.2 13.5 %collective-permute-start.4 = (bf16[256,2048]{1,0:T(8,128)(2,1)}, bf16[256,2048]{1,0:T(8,128)(2,1)}, u32[]{:S(2)}, u32[]{:S(2)}) collective-permute-start(bf16[256,2048]{1,0:T(8,128)(2,1)} %slice.253), channel_id=1, source_target_pairs={{0,1},{1,0},{2,3},{3,2},{4,5},{5,4},{6,7},{7,6},{8,9},{9,8},{10,11... | collective-permute-start | bytes 3145736 | tf_op jit(solution)/shard_map/ppermute | solution.py:304
  55.2 26.8 %collective-permute-start.12 = (bf16[256,2048]{1,0:T(8,128)(2,1)}, bf16[256,2048]{1,0:T(8,128)(2,1)}, u32[]{:S(2)}, u32[]{:S(2)}) collective-permute-start(bf16[256,2048]{1,0:T(8,128)(2,1)} %param.14), channel_id=1, source_target_pairs={{0,1},{1,0},{2,3},{3,2},{4,5},{5,4},{6,7},{7,6},{8,9},{9,8},{10,11... | collective-permute-start | bytes 3145736 | tf_op jit(solution)/shard_map/ppermute | solution.py:304
  55.7 25.1 %collective-permute-start.14 = (bf16[256,2048]{1,0:T(8,128)(2,1)}, bf16[256,2048]{1,0:T(8,128)(2,1)}, u32[]{:S(2)}, u32[]{:S(2)}) collective-permute-start(bf16[256,2048]{1,0:T(8,128)(2,1)} %param.14), channel_id=1, source_target_pairs={{0,2},{1,3},{2,0},{3,1},{4,6},{5,7},{6,4},{7,5},{8,10},{9,11},{10,... | collective-permute-start | bytes 3145736 | tf_op jit(solution)/shard_map/ppermute | solution.py:308
  68.7 16.3 %collective-permute-start.3 = (bf16[256,2048]{1,0:T(8,128)(2,1)S(1)}, bf16[256,2048]{1,0:T(8,128)(2,1)S(1)}, u32[]{:S(2)}, u32[]{:S(2)}) collective-permute-start(bf16[256,2048]{1,0:T(8,128)(2,1)S(1)} %slice.360), channel_id=1, source_target_pairs={{0,1},{1,0},{2,3},{3,2},{4,5},{5,4},{6,7},{7,6},{8,9},{9,8},{10,11... | collective-permute-start | bytes 3145736 | tf_op jit(solution)/shard_map/ppermute | solution.py:304
  71.7 31.5 %collective-permute-start.5 = (bf16[256,2048]{1,0:T(8,128)(2,1)S(1)}, bf16[256,2048]{1,0:T(8,128)(2,1)S(1)}, u32[]{:S(2)}, u32[]{:S(2)}) collective-permute-start(bf16[256,2048]{1,0:T(8,128)(2,1)S(1)} %add_convert_fusion.13), channel_id=1, source_target_pairs={{0,2},{1,3},{2,0},{3,1},{4,6},{5,7},{6,4},{7,5},{8,10},{9,11},{10,... | collective-permute-start | bytes 3145736 | tf_op jit(solution)/shard_map/ppermute | solution.py:308
  80.8 24.3 %collective-permute-start.15 = (bf16[256,2048]{1,0:T(8,128)(2,1)}, bf16[256,2048]{1,0:T(8,128)(2,1)S(1)}, u32[]{:S(2)}, u32[]{:S(2)}) collective-permute-start(bf16[256,2048]{1,0:T(8,128)(2,1)} %collective-permute-done.14), channel_id=1, source_target_pairs={{0,1},{1,0},{2,3},{3,2},{4,5},{5,4},{6,7},{7,6},{8,9},{9,8},{10,11... | collective-permute-start | bytes 3145736 | tf_op jit(solution)/shard_map/ppermute | solution.py:304
  104.2 8.3 %collective-permute-start.6 = (bf16[256,2048]{1,0:T(8,128)(2,1)S(1)}, bf16[256,2048]{1,0:T(8,128)(2,1)S(1)}, u32[]{:S(2)}, u32[]{:S(2)}) collective-permute-start(bf16[256,2048]{1,0:T(8,128)(2,1)S(1)} %multiply_convert_fusion.6), channel_id=1, source_target_pairs={{0,1},{1,0},{2,3},{3,2},{4,5},{5,4},{6,7},{7,6},{8,9},{9,8},{10,11... | collective-permute-start | bytes 3145736 | tf_op jit(solution)/shard_map/ppermute | solution.py:304
  112.3 34.5 %collective-permute-start.8 = (bf16[256,2048]{1,0:T(8,128)(2,1)S(1)}, bf16[256,2048]{1,0:T(8,128)(2,1)S(1)}, u32[]{:S(2)}, u32[]{:S(2)}) collective-permute-start(bf16[256,2048]{1,0:T(8,128)(2,1)S(1)} %multiply_convert_fusion.6), channel_id=1, source_target_pairs={{0,2},{1,3},{2,0},{3,1},{4,6},{5,7},{6,4},{7,5},{8,10},{9,11},{10,... | collective-permute-start | bytes 3145736 | tf_op jit(solution)/shard_map/ppermute | solution.py:308
  146.9 7.3 %collective-permute-start.9 = (bf16[256,2048]{1,0:T(8,128)(2,1)S(1)}, bf16[256,2048]{1,0:T(8,128)(2,1)S(1)}, u32[]{:S(2)}, u32[]{:S(2)}) collective-permute-start(bf16[256,2048]{1,0:T(8,128)(2,1)S(1)} %collective-permute-done.8), channel_id=1, source_target_pairs={{0,1},{1,0},{2,3},{3,2},{4,5},{5,4},{6,7},{7,6},{8,9},{9,8},{10,11... | collective-permute-start | bytes 3145736 | tf_op jit(solution)/shard_map/ppermute | solution.py:304
  148.8 63.5 %collective-permute-start.13 = (bf16[256,2048]{1,0:T(8,128)(2,1)}, bf16[256,2048]{1,0:T(8,128)(2,1)S(1)}, u32[]{:S(2)}, u32[]{:S(2)}) collective-permute-start(bf16[256,2048]{1,0:T(8,128)(2,1)} %slice.358), channel_id=1, source_target_pairs={{0,1},{1,0},{2,3},{3,2},{4,5},{5,4},{6,7},{7,6},{8,9},{9,8},{10,11... | collective-permute-start | bytes 3145736 | tf_op jit(solution)/shard_map/ppermute | solution.py:304
  153.6 84.4 %collective-permute-start.7 = (bf16[256,2048]{1,0:T(8,128)(2,1)}, bf16[256,2048]{1,0:T(8,128)(2,1)}, u32[]{:S(2)}, u32[]{:S(2)}) collective-permute-start(bf16[256,2048]{1,0:T(8,128)(2,1)} %slice.359), channel_id=1, source_target_pairs={{0,1},{1,0},{2,3},{3,2},{4,5},{5,4},{6,7},{7,6},{8,9},{9,8},{10,11... | collective-permute-start | bytes 3145736 | tf_op jit(solution)/shard_map/ppermute | solution.py:304
  187.0 79.2 %collective-permute-start.38 = (bf16[1408,1024]{1,0:T(8,128)(2,1)}, bf16[1408,1024]{1,0:T(8,128)(2,1)}, u32[]{:S(2)}, u32[]{:S(2)}) collective-permute-start(bf16[1408,1024]{1,0:T(8,128)(2,1)} %convolution_convert_fusion), channel_id=1, source_target_pairs={{0,4},{4,0},{8,12},{12,8},{16,20},{20,16},{24,28},{28,24},{1,5},{5... | collective-permute-start | bytes 8650760 | tf_op jit(solution)/shard_map/ppermute | solution.py:352
  188.3 23.1 %collective-permute-start.10 = (bf16[256,2048]{1,0:T(8,128)(2,1)S(1)}, bf16[256,2048]{1,0:T(8,128)(2,1)S(1)}, u32[]{:S(2)}, u32[]{:S(2)}) collective-permute-start(bf16[256,2048]{1,0:T(8,128)(2,1)S(1)} %slice.257), channel_id=1, source_target_pairs={{0,1},{1,0},{2,3},{3,2},{4,5},{5,4},{6,7},{7,6},{8,9},{9,8},{10,11... | collective-permute-start | bytes 3145736 | tf_op jit(solution)/shard_map/ppermute | solution.py:304
  201.3 9.4 %collective-permute-start.16 = (bf16[256,2048]{1,0:T(8,128)(2,1)S(1)}, bf16[256,2048]{1,0:T(8,128)(2,1)S(1)}, u32[]{:S(2)}, u32[]{:S(2)}) collective-permute-start(bf16[256,2048]{1,0:T(8,128)(2,1)S(1)} %slice.261), channel_id=1, source_target_pairs={{0,1},{1,0},{2,3},{3,2},{4,5},{5,4},{6,7},{7,6},{8,9},{9,8},{10,11... | collective-permute-start | bytes 3145736 | tf_op jit(solution)/shard_map/ppermute | solution.py:304
  210.8 101.9 %collective-permute-start.30 = (bf16[1024,1408]{1,0:T(8,128)(2,1)}, bf16[1024,1408]{1,0:T(8,128)(2,1)}, u32[]{:S(2)}, u32[]{:S(2)}) collective-permute-start(bf16[1024,1408]{1,0:T(8,128)(2,1)} %convolution_convert_fusion.2), channel_id=1, source_target_pairs={{0,4},{4,0},{8,12},{12,8},{16,20},{20,16},{24,28},{28,24},{1,5},{5... | collective-permute-start | bytes 8650760 | tf_op jit(solution)/shard_map/ppermute | solution.py:352
  211.5 24.6 %collective-permute-start.17 = (bf16[256,2048]{1,0:T(8,128)(2,1)S(1)}, bf16[256,2048]{1,0:T(8,128)(2,1)S(1)}, u32[]{:S(2)}, u32[]{:S(2)}) collective-permute-start(bf16[256,2048]{1,0:T(8,128)(2,1)S(1)} %add_convert_fusion.11), channel_id=1, source_target_pairs={{0,2},{1,3},{2,0},{3,1},{4,6},{5,7},{6,4},{7,5},{8,10},{9,11},{10,... | collective-permute-start | bytes 3145736 | tf_op jit(solution)/shard_map/ppermute | solution.py:308
  212.3 46.3 %collective-permute-start.11 = (bf16[256,2048]{1,0:T(8,128)(2,1)S(1)}, bf16[256,2048]{1,0:T(8,128)(2,1)S(1)}, u32[]{:S(2)}, u32[]{:S(2)}) collective-permute-start(bf16[256,2048]{1,0:T(8,128)(2,1)S(1)} %add_convert_fusion.12), channel_id=1, source_target_pairs={{0,2},{1,3},{2,0},{3,1},{4,6},{5,7},{6,4},{7,5},{8,10},{9,11},{10,... | collective-permute-start | bytes 3145736 | tf_op jit(solution)/shard_map/ppermute | solution.py:308
  236.1 138.4 %collective-permute-start.27 = (bf16[1024,1408]{1,0:T(8,128)(2,1)S(1)}, bf16[1024,1408]{1,0:T(8,128)(2,1)}, u32[]{:S(2)}, u32[]{:S(2)}) collective-permute-start(bf16[1024,1408]{1,0:T(8,128)(2,1)S(1)} %convolution_convert_fusion.4), channel_id=1, source_target_pairs={{0,4},{4,0},{8,12},{12,8},{16,20},{20,16},{24,28},{28,24},{1,5},{5... | collective-permute-start | bytes 8650760 | tf_op jit(solution)/shard_map/ppermute | solution.py:352
  264.5 119.7 %copy-start.42 = (bf16[256,2048]{1,0:T(8,128)(2,1)}, bf16[256,2048]{1,0:T(8,128)(2,1)S(1)}, u32[]{:S(2)}) copy-start(bf16[256,2048]{1,0:T(8,128)(2,1)S(1)} %get-tuple-element.65) | copy-start | bytes 3145732
  264.5 118.2 %collective-permute-start.19 = (bf16[256,2048]{1,0:T(8,128)(2,1)S(1)}, bf16[256,2048]{1,0:T(8,128)(2,1)S(1)}, u32[]{:S(2)}, u32[]{:S(2)}) collective-permute-start(bf16[256,2048]{1,0:T(8,128)(2,1)S(1)} %get-tuple-element.65), channel_id=1, source_target_pairs={{0,2},{1,3},{2,0},{3,1},{4,6},{5,7},{6,4},{7,5},{8,10},{9,11},{10,... | collective-permute-start | bytes 3145736 | tf_op jit(solution)/shard_map/ppermute | solution.py:308
  264.9 119.4 %collective-permute-start.18 = (bf16[256,2048]{1,0:T(8,128)(2,1)S(1)}, bf16[256,2048]{1,0:T(8,128)(2,1)S(1)}, u32[]{:S(2)}, u32[]{:S(2)}) collective-permute-start(bf16[256,2048]{1,0:T(8,128)(2,1)S(1)} %get-tuple-element.65), channel_id=1, source_target_pairs={{0,1},{1,0},{2,3},{3,2},{4,5},{5,4},{6,7},{7,6},{8,9},{9,8},{10,11... | collective-permute-start | bytes 3145736 | tf_op jit(solution)/shard_map/ppermute | solution.py:304
  271.9 46.6 %copy-start.45 = (bf16[1408,1024]{1,0:T(8,128)(2,1)}, bf16[1408,1024]{1,0:T(8,128)(2,1)S(1)}, u32[]{:S(2)}) copy-start(bf16[1408,1024]{1,0:T(8,128)(2,1)S(1)} %add_convert_fusion) | copy-start | bytes 8650756
  273.2 166.7 %collective-permute-start.39 = (bf16[1408,512]{1,0:T(8,128)(2,1)}, bf16[1408,512]{1,0:T(8,128)(2,1)}, u32[]{:S(2)}, u32[]{:S(2)}) collective-permute-start(bf16[1408,512]{1,0:T(8,128)(2,1)} %slice.293), channel_id=1, source_target_pairs={{0,8},{4,12},{8,0},{12,4},{16,24},{20,28},{24,16},{28,20},{1,9},{5... | collective-permute-start | bytes 4325384 | tf_op jit(solution)/shard_map/ppermute | solution.py:352
  318.5 61.3 %copy-start.47 = (bf16[1024,1408]{1,0:T(8,128)(2,1)}, bf16[1024,1408]{1,0:T(8,128)(2,1)S(1)}, u32[]{:S(2)}) copy-start(bf16[1024,1408]{1,0:T(8,128)(2,1)S(1)} %add_convert_fusion.1) | copy-start | bytes 8650756
  318.5 55.9 %copy-start.99 = (bf16[512,1408]{1,0:T(8,128)(2,1)S(1)}, bf16[512,1408]{1,0:T(8,128)(2,1)}, u32[]{:S(2)}) copy-start(bf16[512,1408]{1,0:T(8,128)(2,1)} %copy-done.97) | copy-start | bytes 4325380
  318.5 55.9 %copy-start.102 = (bf16[512,1408]{1,0:T(8,128)(2,1)S(1)}, bf16[512,1408]{1,0:T(8,128)(2,1)}, u32[]{:S(2)}) copy-start(bf16[512,1408]{1,0:T(8,128)(2,1)} %get-tuple-element.73) | copy-start | bytes 4325380
  319.7 122.9 %collective-permute-start.31 = (bf16[512,1408]{1,0:T(8,128)(2,1)}, bf16[512,1408]{1,0:T(8,128)(2,1)}, u32[]{:S(2)}, u32[]{:S(2)}) collective-permute-start(bf16[512,1408]{1,0:T(8,128)(2,1)} %slice.281), channel_id=1, source_target_pairs={{0,8},{4,12},{8,0},{12,4},{16,24},{20,28},{24,16},{28,20},{1,9},{5... | collective-permute-start | bytes 4325384 | tf_op jit(solution)/shard_map/ppermute | solution.py:352
  382.6 64.2 %collective-permute-start.28 = (bf16[512,1408]{1,0:T(8,128)(2,1)}, bf16[512,1408]{1,0:T(8,128)(2,1)}, u32[]{:S(2)}, u32[]{:S(2)}) collective-permute-start(bf16[512,1408]{1,0:T(8,128)(2,1)} %slice.277), channel_id=1, source_target_pairs={{0,8},{4,12},{8,0},{12,4},{16,24},{20,28},{24,16},{28,20},{1,9},{5... | collective-permute-start | bytes 4325384 | tf_op jit(solution)/shard_map/ppermute | solution.py:352
  382.7 16.8 %collective-permute-start.20 = (bf16[256,2048]{1,0:T(8,128)(2,1)S(1)}, bf16[256,2048]{1,0:T(8,128)(2,1)}, u32[]{:S(2)}, u32[]{:S(2)}) collective-permute-start(bf16[256,2048]{1,0:T(8,128)(2,1)S(1)} %collective-permute-done.19), channel_id=1, source_target_pairs={{0,1},{1,0},{2,3},{3,2},{4,5},{5,4},{6,7},{7,6},{8,9},{9,8},{10,11... | collective-permute-start | bytes 3145736 | tf_op jit(solution)/shard_map/ppermute | solution.py:304
  405.9 77.0 %collective-permute-start.35 = (bf16[512,1024]{1,0:T(8,128)(2,1)}, bf16[512,1024]{1,0:T(8,128)(2,1)S(1)}, u32[]{:S(2)}, u32[]{:S(2)}) collective-permute-start(bf16[512,1024]{1,0:T(8,128)(2,1)} %fusion.81), channel_id=1, source_target_pairs={{0,8},{4,12},{8,0},{12,4},{16,24},{20,28},{24,16},{28,20},{1,9},{5... | collective-permute-start | bytes 3145736 | tf_op jit(solution)/shard_map/ppermute | solution.py:352
  429.9 57.3 %collective-permute-start.24 = (bf16[1024,640]{1,0:T(8,128)(2,1)S(1)}, bf16[1024,640]{1,0:T(8,128)(2,1)S(1)}, u32[]{:S(2)}, u32[]{:S(2)}) collective-permute-start(bf16[1024,640]{1,0:T(8,128)(2,1)S(1)} %fusion.75), channel_id=1, source_target_pairs={{0,8},{4,12},{8,0},{12,4},{16,24},{20,28},{24,16},{28,20},{1,9},{5... | collective-permute-start | bytes 3932168 | tf_op jit(solution)/shard_map/ppermute | solution.py:352
  439.9 158.5 %collective-permute-start.21 = (bf16[256,2048]{1,0:T(8,128)(2,1)}, bf16[256,2048]{1,0:T(8,128)(2,1)}, u32[]{:S(2)}, u32[]{:S(2)}) collective-permute-start(bf16[256,2048]{1,0:T(8,128)(2,1)} %slice.357), channel_id=1, source_target_pairs={{0,1},{1,0},{2,3},{3,2},{4,5},{5,4},{6,7},{7,6},{8,9},{9,8},{10,11... | collective-permute-start | bytes 3145736 | tf_op jit(solution)/shard_map/ppermute | solution.py:304
  442.7 39.0 %collective-permute-start.40 = (bf16[1408,256]{1,0:T(8,128)(2,1)S(1)}, bf16[1408,256]{1,0:T(8,128)(2,1)S(1)}, u32[]{:S(2)}, u32[]{:S(2)}) collective-permute-start(bf16[1408,256]{1,0:T(8,128)(2,1)S(1)} %slice.295), channel_id=1, source_target_pairs={{0,16},{4,20},{8,24},{12,28},{16,0},{20,4},{24,8},{28,12},{1,17},{... | collective-permute-start | bytes 2162696 | tf_op jit(solution)/shard_map/ppermute | solution.py:352
  446.8 39.0 %collective-permute-start.22 = (bf16[256,2048]{1,0:T(8,128)(2,1)S(1)}, bf16[256,2048]{1,0:T(8,128)(2,1)S(1)}, u32[]{:S(2)}, u32[]{:S(2)}) collective-permute-start(bf16[256,2048]{1,0:T(8,128)(2,1)S(1)} %slice.269), channel_id=1, source_target_pairs={{0,1},{1,0},{2,3},{3,2},{4,5},{5,4},{6,7},{7,6},{8,9},{9,8},{10,11... | collective-permute-start | bytes 3145736 | tf_op jit(solution)/shard_map/ppermute | solution.py:304
  481.6 87.6 %collective-permute-start.32 = (bf16[256,1408]{1,0:T(8,128)(2,1)S(1)}, bf16[256,1408]{1,0:T(8,128)(2,1)S(1)}, u32[]{:S(2)}, u32[]{:S(2)}) collective-permute-start(bf16[256,1408]{1,0:T(8,128)(2,1)S(1)} %slice.283), channel_id=1, source_target_pairs={{0,16},{4,20},{8,24},{12,28},{16,0},{20,4},{24,8},{28,12},{1,17},{... | collective-permute-start | bytes 2162696 | tf_op jit(solution)/shard_map/ppermute | solution.py:352
  482.9 87.7 %collective-permute-start.29 = (bf16[256,1408]{1,0:T(8,128)(2,1)S(1)}, bf16[256,1408]{1,0:T(8,128)(2,1)S(1)}, u32[]{:S(2)}, u32[]{:S(2)}) collective-permute-start(bf16[256,1408]{1,0:T(8,128)(2,1)S(1)} %slice.279), channel_id=1, source_target_pairs={{0,16},{4,20},{8,24},{12,28},{16,0},{20,4},{24,8},{28,12},{1,17},{... | collective-permute-start | bytes 2162696 | tf_op jit(solution)/shard_map/ppermute | solution.py:352
  485.8 79.4 %collective-permute-start.36 = (bf16[512,512]{1,0:T(8,128)(2,1)S(1)}, bf16[512,512]{1,0:T(8,128)(2,1)S(1)}, u32[]{:S(2)}, u32[]{:S(2)}) collective-permute-start(bf16[512,512]{1,0:T(8,128)(2,1)S(1)} %slice.289), channel_id=1, source_target_pairs={{0,16},{4,20},{8,24},{12,28},{16,0},{20,4},{24,8},{28,12},{1,17},{... | collective-permute-start | bytes 1572872 | tf_op jit(solution)/shard_map/ppermute | solution.py:352
  487.2 111.2 %collective-permute-start.23 = (bf16[256,2048]{1,0:T(8,128)(2,1)}, bf16[256,2048]{1,0:T(8,128)(2,1)}, u32[]{:S(2)}, u32[]{:S(2)}) collective-permute-start(bf16[256,2048]{1,0:T(8,128)(2,1)} %add_convert_fusion.10), channel_id=1, source_target_pairs={{0,2},{1,3},{2,0},{3,1},{4,6},{5,7},{6,4},{7,5},{8,10},{9,11},{10,... | collective-permute-start | bytes 3145736 | tf_op jit(solution)/shard_map/ppermute | solution.py:308
  489.4 84.9 %copy-start.55 = (bf16[1024,640]{1,0:T(8,128)(2,1)}, bf16[1024,640]{1,0:T(8,128)(2,1)S(1)}, u32[]{:S(2)}) copy-start(bf16[1024,640]{1,0:T(8,128)(2,1)S(1)} %add_convert_fusion.8) | copy-start | bytes 3932164
  565.2 30.4 %collective-permute-start.25 = (bf16[512,640]{1,0:T(8,128)(2,1)}, bf16[512,640]{1,0:T(8,128)(2,1)}, u32[]{:S(2)}, u32[]{:S(2)}) collective-permute-start(bf16[512,640]{1,0:T(8,128)(2,1)} %slice.271), channel_id=1, source_target_pairs={{0,16},{4,20},{8,24},{12,28},{16,0},{20,4},{24,8},{28,12},{1,17},{... | collective-permute-start | bytes 1966088 | tf_op jit(solution)/shard_map/ppermute | solution.py:352
  569.3 6.1 collective-permute-start.37
  597.1 8.9 %collective-permute-start.26 = (bf16[256,640]{1,0:T(8,128)(2,1)S(1)}, bf16[256,640]{1,0:T(8,128)(2,1)S(1)}, u32[]{:S(2)}, u32[]{:S(2)}) collective-permute-start(bf16[256,640]{1,0:T(8,128)(2,1)S(1)} %slice.273), channel_id=1, source_target_pairs={{0,4},{4,0},{8,12},{12,8},{16,20},{20,16},{24,28},{28,24},{1,5},{5... | collective-permute-start | bytes 983048 | tf_op jit(solution)/shard_map/ppermute | solution.py:352
  608.9 5.4 collective-permute-start.33
  614.3 4.2 collective-permute-start.34
  (111 other events, 831.2 us)

commit v2 on v1

v2 whole, which is shorter than its diff:
```python
import functools

import jax
import jax.numpy as jnp
from jax import lax
from jax.experimental import pallas as pl
from jax.experimental.pallas import tpu as pltpu
from jax.sharding import PartitionSpec as P

HD = 64
SEQ = 1024
PIECE = 256
QB = 256


EPSILON = 1e-05
ROPE_BASE = 10000.0
MASKED = -1e30
VMEM_LIMIT = 48 * 2**20
PARTS = 1
PAIR = 2
NT = (((1,), (1,)), ((), ()))
TN = (((0,), (0,)), ((), ()))


def dot(left, right):
    return jnp.dot(left, right, preferred_element_type=jnp.float32)


def contract_rows(left, right):
    return lax.dot_general(left, right, TN, preferred_element_type=jnp.float32)


def contract_cols(left, right):
    return lax.dot_general(left, right, NT, preferred_element_type=jnp.float32)


def rms_inverse(resid):
    return lax.rsqrt(jnp.mean(resid * resid, axis=-1, keepdims=True) + EPSILON)


def norm_back(d_norm, resid, inverse, gain):
    scaled = d_norm * gain
    return inverse * scaled - resid * (inverse * inverse * inverse) * jnp.mean(
        scaled * resid, axis=-1, keepdims=True
    )


def rope_tables(positions):
    half_dim = HD // 2
    inverse = jnp.power(ROPE_BASE, -(jnp.arange(half_dim).astype(jnp.float32) * 2.0) / HD)
    angles = positions.astype(jnp.float32)[:, None] * inverse[None, :]
    cos, sin = jnp.cos(angles), jnp.sin(angles)
    return jnp.concatenate([cos] * 4, axis=1), jnp.concatenate([-sin, sin] * 2, axis=1)


def swap_halves(pair):
    lane = lax.broadcasted_iota(jnp.int32, pair.shape, 1)
    up = pltpu.roll(pair, 2 * HD - HD // 2, 1)
    down = pltpu.roll(pair, HD // 2, 1)
    return jnp.where(lane % HD < HD // 2, up, down)


def rotate_rows(grad, cos_tab, sin_tab):
    half = HD // 2
    swapped = jnp.concatenate([grad[:, half:], grad[:, :half]], axis=1)
    return grad * cos_tab[:, :HD] - swapped * sin_tab[:, :HD]


def either(near_refs):
    half = len(near_refs) // 2
    own, core = (
        jnp.concatenate([ref[...] for ref in refs], axis=0)
        for refs in (near_refs[:half], near_refs[half:])
    )
    return jnp.where(pl.program_id(0) == 0, own, core)


def project_kernel(*refs):
    x_refs = refs[:-9]
    gain_ref, wq_ref, wkv_ref, cos_ref, sin_ref, n_ref, q_ref, k_ref, v_ref = refs[-9:]
    resid = either(x_refs).astype(jnp.float32)
    normed = (resid * rms_inverse(resid) * gain_ref[...]).astype(jnp.bfloat16)
    n_ref[...] = normed
    cos, sin = cos_ref[...], sin_ref[...]
    query = dot(normed, wq_ref[...])
    for first in range(0, query.shape[1], 2 * HD):
        pair = query[:, first : first + 2 * HD]
        turned = (pair * cos + swap_halves(pair) * sin) * HD ** (-0.5)
        q_ref[:, first : first + 2 * HD] = turned.astype(jnp.bfloat16)
    key_value = dot(normed, wkv_ref[...])
    turned = key_value * cos + swap_halves(key_value) * sin
    k_ref[...] = turned[:, :HD].astype(jnp.bfloat16)
    v_ref[...] = key_value[:, HD:].astype(jnp.bfloat16)


def whole(array):
    return pl.BlockSpec(array.shape, lambda *_: (0,) * len(array.shape))


def params():
    return {
        "compiler_params": pltpu.CompilerParams(vmem_limit_bytes=VMEM_LIMIT),
        "cost_estimate": pl.CostEstimate(flops=1, bytes_accessed=1, transcendentals=0),
    }


def project(parts, gain, w_query, w_kv, cos_tab, sin_tab):
    rows, width = sum(part.shape[0] for part in parts) // 2, parts[0].shape[1]
    queries = w_query.shape[1]

    def tall(cols):
        return pl.BlockSpec((rows, cols), lambda i: (i, 0))

    gain = gain[None, :]
    return pl.pallas_call(
        project_kernel,
        grid=(2,),
        in_specs=[
            *(whole(item) for item in (*parts, gain, w_query, w_kv)), tall(2 * HD), tall(2 * HD)
        ],
        out_specs=[tall(width), tall(queries), tall(HD), tall(HD)],
        out_shape=[
            jax.ShapeDtypeStruct((2 * rows, width), jnp.bfloat16),
            jax.ShapeDtypeStruct((2 * rows, queries), jnp.bfloat16),
            jax.ShapeDtypeStruct((2 * rows, HD), jnp.bfloat16),
            jax.ShapeDtypeStruct((2 * rows, HD), jnp.bfloat16),
        ],
        name="project",
        **params(),
    )(*parts, gain, w_query, w_kv, cos_tab, sin_tab)


def by_rows(function, ins, consts, outs):
    flat, counts = [], []
    for item in ins:
        item = item if isinstance(item, tuple) else (item,)
        counts.append([len(flat) + sum(one is not None for one in item[:i]) if part is not None else None
                       for i, part in enumerate(item)])
        flat.extend(part for part in item if part is not None)
    rows, width = sum(flat[at].shape[0] for at in counts[0]), flat[0].shape[1]
    out_counts = [PARTS if isinstance(item, tuple) else 1 for item in outs]
    dtypes = [item[0] if isinstance(item, tuple) else item for item in outs]
    starts = [sum(out_counts[:i]) for i in range(len(outs))]
    out_places = [range(first, first + count) for first, count in zip(starts, out_counts)]
    step = 32

    def kernel(*refs):
        given = [ref[...] for ref in refs[len(flat) : len(flat) + len(consts)]]

        def views(part_refs, places, part):
            found = []
            for place in places:
                each = PARTS // len(place)
                at = place[part // each]
                ref = None if at is None else part_refs[at]
                found.append((ref, part % each * (rows // PARTS)))
            return found

        for part in range(PARTS):
            sources = views(refs, counts, part)
            targets = views(refs[len(flat) + len(consts) :], out_places, part)

            def chunk(i, _):
                def at(base):
                    return pl.ds(pl.multiple_of(base + i * step, step), step)

                values = [
                    0.0 if ref is None else ref[at(base), :].astype(jnp.float32)
                    for ref, base in sources
                ]
                for (ref, base), value in zip(targets, function(*values, *given)):
                    ref[at(base), :] = value.astype(ref.dtype)
                return 0

            lax.fori_loop(0, rows // PARTS // step, chunk, 0)

    consts = [item[None, :] for item in consts]
    shapes = []
    for count, dtype in zip(out_counts, dtypes):
        shapes.extend([jax.ShapeDtypeStruct((rows // count, width), dtype)] * count)
    results = pl.pallas_call(kernel, out_shape=shapes, name="by_rows", **params())(*flat, *consts)
    grouped, at = [], 0
    for count, item in zip(out_counts, outs):
        grouped.append(tuple(results[at : at + count]) if isinstance(item, tuple) else results[at])
        at += count
    return grouped


def see(qpos, kpos, starts_ref, pics):
    mask = kpos <= qpos
    for pic in range(pics):
        begin = starts_ref[pic]
        mask = mask | (
            (qpos >= begin) & (qpos < begin + PIECE) & (kpos >= begin) & (kpos < begin + PIECE)
        )
    return mask


def key_blocks(starts_ref, pics, first):
    edge = first + QB
    crossed = jnp.bool_(False)
    for pic in range(pics):
        begin = starts_ref[pic]
        crossed = crossed | ((begin < edge) & (begin + PIECE > edge))
    return edge // QB + jnp.where(crossed, 1, 0)


def forward_kernel(
    pos_ref, starts_ref, q_ref, k_ref, v_ref, out_ref, o_ref, lse_ref, kept_ref, *rest, heads, pics, seq
):
    *sent_refs, bias = rest
    first = pos_ref[pl.program_id(0)]
    count = key_blocks(starts_ref, pics, first)
    for blocks in range(1, seq // QB + 1):

        @pl.when(count == blocks)
        def _():
            ext = blocks * QB
            low = max(0, ext - 2 * QB)
            wide = ext - low
            qpos = lax.broadcasted_iota(jnp.int32, (QB, wide), 0) + first
            kpos = lax.broadcasted_iota(jnp.int32, (QB, wide), 1) + low
            bias[:, :wide] = jnp.where(see(qpos, kpos, starts_ref, pics), 0.0, MASKED)
            values = jnp.concatenate([v_ref[:ext, :], jnp.ones((ext, HD), jnp.bfloat16)], axis=1)
            lane = lax.broadcasted_iota(jnp.int32, (QB, heads), 1)

            def one_pair(pair, stats):
                at = pl.ds(pl.multiple_of(pair * 2 * HD, 2 * HD), 2 * HD)
                both = q_ref[:, at]
                outs = []
                for side in range(2):
                    scores = contract_cols(both[:, side * HD : (side + 1) * HD], k_ref[:ext, :])
                    if low:
                        scores = jnp.concatenate(
                            [scores[:, :low], scores[:, low:] + bias[:, :wide]], axis=1
                        )
                    else:
                        scores = scores + bias[:, :wide]
                    row_max = jnp.max(scores, axis=1, keepdims=True)
                    terms = jnp.exp(scores - row_max).astype(jnp.bfloat16)
                    summed = dot(terms, values)
                    row_sum = summed[:, HD : HD + 1]
                    outs.append(summed[:, :HD] / row_sum)
                    stats = jnp.where(lane == 2 * pair + side, row_max + jnp.log(row_sum), stats)
                o_ref[:, at] = jnp.concatenate(outs, axis=1).astype(jnp.bfloat16)
                return stats

            lse_ref[...] = lax.fori_loop(
                0, heads // 2, one_pair, jnp.zeros((QB, heads), jnp.float32)
            )

    part = dot(o_ref[...], out_ref[...]).astype(jnp.bfloat16)

    @pl.when(pl.program_id(0) == 0)
    def _():
        kept_ref[...] = part

    @pl.when(pl.program_id(0) == 1)
    def _():
        for i, ref in enumerate(sent_refs):
            ref[...] = part[i * ref.shape[0] : (i + 1) * ref.shape[0]]


def attend_forward(q_low, k_low, v_low, w_out, starts, positions):
    rows, width = q_low.shape
    heads, seq, pics = width // HD, k_low.shape[0], starts.shape[0]
    tall = pl.BlockSpec((QB, width), lambda i, *_: (i, 0))
    parts = [(QB, w_out.shape[1])] + [(QB // PARTS, w_out.shape[1])] * PARTS
    keys = pl.BlockSpec((seq, HD), lambda i, *_: (0, 0))
    return pl.pallas_call(
        functools.partial(forward_kernel, heads=heads, pics=pics, seq=seq),
        grid_spec=pltpu.PrefetchScalarGridSpec(
            num_scalar_prefetch=2,
            grid=(rows // QB,),
            in_specs=[tall, keys, keys, whole(w_out)],
            out_specs=[
                tall,
                pl.BlockSpec((QB, heads), lambda i, *_: (i, 0)),
                *(pl.BlockSpec(part, lambda i, *_: (0, 0)) for part in parts),
            ],
            scratch_shapes=[pltpu.VMEM((QB, 2 * QB), jnp.float32)],
        ),
        out_shape=[
            jax.ShapeDtypeStruct((rows, width), jnp.bfloat16),
            jax.ShapeDtypeStruct((rows, heads), jnp.float32),
            *(jax.ShapeDtypeStruct(part, jnp.bfloat16) for part in parts),
        ],
        name="attend_forward",
        **params(),
    )(positions, starts, q_low, k_low, v_low, w_out)


def in_three(value):
    top = value.astype(jnp.bfloat16)
    rest = value - top.astype(jnp.float32)
    middle = rest.astype(jnp.bfloat16)
    last = (rest - middle.astype(jnp.float32)).astype(jnp.bfloat16)
    return [top, middle, last]


def backward_kernel(
    pos_ref, starts_ref, q_ref, out_ref, o_ref, lse_ref, k_ref, v_ref, cos_ref, sin_ref,
    *rest, heads, pics, seq
):
    *d_refs, dq_ref, dk_ref, dv_ref, bias, do_ref = rest
    first = pos_ref[pl.program_id(0)]
    count = key_blocks(starts_ref, pics, first)

    @pl.when(pl.program_id(0) == 0)
    def _():
        dk_ref[...] = jnp.zeros_like(dk_ref)
        dv_ref[...] = jnp.zeros_like(dv_ref)

    do_ref[...] = contract_cols(either(d_refs), out_ref[...]).astype(jnp.bfloat16)

    for blocks in range(1, seq // QB + 1):

        @pl.when(count == blocks)
        def _():
            ext = blocks * QB
            low = max(0, ext - 2 * QB)
            wide = ext - low
            kpos = lax.broadcasted_iota(jnp.int32, (wide, QB), 0) + low
            qpos = lax.broadcasted_iota(jnp.int32, (wide, QB), 1) + first
            bias[:wide, :] = jnp.where(see(qpos, kpos, starts_ref, pics), 0.0, MASKED)
            ones = jnp.ones((ext, HD), jnp.bfloat16)
            keys = jnp.concatenate([k_ref[:ext, :], ones], axis=1)
            values = jnp.concatenate([v_ref[:ext, :], ones], axis=1)
            zeros = jnp.zeros((QB, HD - 3), jnp.bfloat16)
            lane = lax.broadcasted_iota(jnp.int32, (QB, heads), 1)

            def one_pair(pair, _):
                at = pl.ds(pl.multiple_of(pair * 2 * HD, 2 * HD), 2 * HD)
                q_both, d_both, o_both = q_ref[:, at], do_ref[:, at], o_ref[:, at]
                stats = lse_ref[...]
                d_query, d_key, d_val = [], 0.0, 0.0
                for side in range(2):
                    cols = slice(side * HD, (side + 1) * HD)
                    queries, d_out = q_both[:, cols], d_both[:, cols]
                    delta = jnp.sum(
                        d_out.astype(jnp.float32) * o_both[:, cols].astype(jnp.float32),
                        axis=1,
                        keepdims=True,
                    )
                    lse = jnp.sum(
                        jnp.where(lane == 2 * pair + side, stats, 0.0), axis=1, keepdims=True
                    )
                    queries_ext = jnp.concatenate([queries] + in_three(-lse) + [zeros], axis=1)
                    d_out_ext = jnp.concatenate([d_out] + in_three(-delta) + [zeros], axis=1)
                    scores = contract_cols(keys, queries_ext)
                    if low:
                        scores = jnp.concatenate(
                            [scores[:low], scores[low:] + bias[:wide, :]], axis=0
                        )
                    else:
                        scores = scores + bias[:wide, :]
                    probs = jnp.exp(scores)
                    d_probs = contract_cols(values, d_out_ext)
                    d_scores = (probs * d_probs).astype(jnp.bfloat16)
                    d_val += dot(probs.astype(jnp.bfloat16), d_out)
                    d_key += dot(d_scores, queries)
                    d_query.append(contract_rows(d_scores, k_ref[:ext, :]))
                dk_ref[:ext, :] += d_key
                dv_ref[:ext, :] += d_val
                turned = jnp.concatenate(d_query, axis=1) * HD ** (-0.5)
                turned = turned * cos_ref[...] - swap_halves(turned) * sin_ref[...]
                dq_ref[:, at] = turned.astype(jnp.bfloat16)
                return 0

            lax.fori_loop(0, heads // 2, one_pair, 0)


def attend_backward(
    q_low, d_parts, w_out, attn_low, lse, k_low, v_low, cos_tab, sin_tab, starts, positions
):
    rows, width = q_low.shape
    heads, seq, pics = width // HD, k_low.shape[0], starts.shape[0]
    tall = pl.BlockSpec((QB, width), lambda i, *_: (i, 0))
    table = pl.BlockSpec((QB, 2 * HD), lambda i, *_: (i, 0))
    stats = pl.BlockSpec((QB, heads), lambda i, *_: (i, 0))
    keys = whole(k_low)
    return pl.pallas_call(
        functools.partial(backward_kernel, heads=heads, pics=pics, seq=seq),
        grid_spec=pltpu.PrefetchScalarGridSpec(
            num_scalar_prefetch=2,
            grid=(rows // QB,),
            in_specs=[
                tall, whole(w_out), tall, stats, keys, keys, table, table,
                *(whole(part) for part in d_parts),
            ],
            out_specs=[tall, keys, keys],
            scratch_shapes=[
                pltpu.VMEM((2 * QB, QB), jnp.float32),
                pltpu.VMEM((QB, width), jnp.bfloat16),
            ],
        ),
        out_shape=[
            jax.ShapeDtypeStruct((rows, width), jnp.bfloat16),
            jax.ShapeDtypeStruct((seq, HD), jnp.float32),
            jax.ShapeDtypeStruct((seq, HD), jnp.float32),
        ],
        name="attend_backward",
        **params(),
    )(
        positions, starts, q_low, w_out, attn_low, lse, k_low, v_low, cos_tab, sin_tab, *d_parts
    )


def feed_kernel(*refs, counts):
    gate_ref, up_ref, down_ref, hidden_ref, d_gate_ref, d_up_ref, normed, cots = refs[sum(counts) :]

    @pl.when(pl.program_id(0) == 0)
    def _():
        for target, sources in ((normed, refs[: counts[0]]), (cots, refs[counts[0] : sum(counts)])):
            at = 0
            for ref in sources:
                target[at : at + ref.shape[0], :] = ref[...]
                at += ref.shape[0]

    gate_val, up_val = dot(normed[...], gate_ref[...]), dot(normed[...], up_ref[...])
    d_hidden = contract_cols(cots[...], down_ref[...])
    gate_sig = jax.nn.sigmoid(gate_val)
    swish = gate_val * gate_sig
    hidden_ref[...] = (swish * up_val).astype(jnp.bfloat16)
    d_gate = d_hidden * up_val * (gate_sig + swish * (1.0 - gate_sig))
    d_gate_ref[...] = d_gate.astype(jnp.bfloat16)
    d_up_ref[...] = (d_hidden * swish).astype(jnp.bfloat16)


def feed_forward(normed, cots, w_gate, w_up, w_down):
    rows, width = sum(item.shape[0] for item in normed), normed[0].shape[1]
    units, tile = w_gate.shape[1], 256
    cols = pl.BlockSpec((width, tile), lambda j: (0, j))
    out = pl.BlockSpec((rows, tile), lambda j: (0, j))
    return pl.pallas_call(
        functools.partial(feed_kernel, counts=(len(normed), len(cots))),
        grid=(pl.cdiv(units, tile),),
        in_specs=[
            *(whole(item) for item in (*normed, *cots)),
            cols,
            cols,
            pl.BlockSpec((tile, width), lambda j: (j, 0)),
        ],
        out_specs=[out] * 3,
        out_shape=[jax.ShapeDtypeStruct((rows, units), jnp.bfloat16)] * 3,
        scratch_shapes=[pltpu.VMEM((rows, width), jnp.bfloat16)] * 2,
        name="feed_forward",
        **params(),
    )(*normed, *cots, w_gate, w_up, w_down)


def share_kernel(*refs, transposed):
    count = (len(refs) - 1 - PARTS) // 2
    kept_ref, *sent_refs = refs[2 * count :]
    multiply = contract_cols if transposed else dot
    part = multiply(refs[0][...], refs[count][...])
    for left, right in zip(refs[1:count], refs[count + 1 : 2 * count]):
        part = part + multiply(left[...], right[...])
    rows = kept_ref.shape[0]
    kept_ref[...] = part[:rows].astype(jnp.bfloat16)
    for i, ref in enumerate(sent_refs):
        at = rows + i * ref.shape[0]
        ref[...] = part[at : at + ref.shape[0]].astype(jnp.bfloat16)


def row_shares(lefts, rights, transposed, rows, block):
    rows //= 2
    width, tile = rights[0].shape[0 if transposed else 1], 512

    def right_spec(item):
        if transposed:
            return pl.BlockSpec((tile, item.shape[1]), lambda j: (j, 0))
        return pl.BlockSpec((item.shape[0], tile), lambda j: (0, j))

    sizes = [rows] + [rows // PARTS] * PARTS
    return pl.pallas_call(
        functools.partial(share_kernel, transposed=transposed),
        grid=(width // tile,),
        in_specs=[
            *(pl.BlockSpec((2 * rows, item.shape[1]), lambda j: (block, 0)) for item in lefts),
            *(right_spec(item) for item in rights),
        ],
        out_specs=[pl.BlockSpec((size, tile), lambda j: (0, j)) for size in sizes],
        out_shape=[jax.ShapeDtypeStruct((size, width), jnp.bfloat16) for size in sizes],
        name="row_shares",
        **params(),
    )(*lefts, *rights)


def outer_kernel(order_ref, *refs, shape):
    refs, sent_ref, kept_ref = list(refs[:-2]), refs[-2], refs[-1]
    totals = None
    for lefts, rights in shape:
        rows = jnp.concatenate([refs.pop(0)[...] for _ in range(lefts)], axis=0)
        parts = [contract_rows(rows, refs.pop(0)[...]) for _ in range(rights)]
        totals = parts if totals is None else [a + b for a, b in zip(totals, parts)]
    total = jnp.concatenate(totals, axis=1).astype(jnp.bfloat16)
    step = pl.program_id(0)
    half = pl.num_programs(0) // 2

    @pl.when(step < half)
    def _():
        sent_ref[...] = total

    @pl.when(step >= half)
    def _():
        kept_ref[...] = total


def outer(sections, index, bits):
    width = sections[0][0][0].shape[1]
    share = width // (1 << len(bits))
    tile = 256
    if share == tile:
        blocks = jnp.stack([index ^ item for item in block_order(bits)]).astype(jnp.int32)
    else:
        blocks = jnp.arange(width // tile, dtype=jnp.int32)
        sections = [
            ([permuted_features(item, index, bits) for item in lefts], rights)
            for lefts, rights in sections
        ]
    count = width // tile
    size = sum(item.shape[1] for item in sections[0][1])
    specs, arrays = [], []
    for lefts, rights in sections:
        specs.extend(pl.BlockSpec((item.shape[0], tile), lambda j, b: (0, b[j])) for item in lefts)
        specs.extend(whole(item) for item in rights)
        arrays.extend((*lefts, *rights))
    return pl.pallas_call(
        functools.partial(
            outer_kernel, shape=[(len(lefts), len(rights)) for lefts, rights in sections]
        ),
        grid_spec=pltpu.PrefetchScalarGridSpec(
            num_scalar_prefetch=1,
            grid=(count,),
            in_specs=specs,
            out_specs=[
                pl.BlockSpec((tile, size), lambda j, _: (jnp.minimum(j, count // 2 - 1), 0)),
                pl.BlockSpec((tile, size), lambda j, _: (jnp.maximum(j - count // 2, 0), 0)),
            ],
        ),
        out_shape=[jax.ShapeDtypeStruct((width // 2, size), jnp.bfloat16)] * 2,
        name="outer",
        **params(),
    )(blocks, *arrays)


def halves_kernel(kept_a, kept_b, came_a, came_b, sent_ref, kept_ref):
    sent_ref[...] = added(kept_a[...], came_a[...])
    kept_ref[...] = added(kept_b[...], came_b[...])


def add_halves(kept, came):
    half, columns = kept.shape[0] // 2, kept.shape[1]
    block = min(256, half)
    first = pl.BlockSpec((block, columns), lambda i: (i, 0))
    second = pl.BlockSpec((block, columns), lambda i: (i + half // block, 0))
    return pl.pallas_call(
        halves_kernel,
        grid=(half // block,),
        in_specs=[first, second, first, second],
        out_specs=[first, first],
        out_shape=[jax.ShapeDtypeStruct((half, columns), jnp.bfloat16)] * 2,
        name="add_halves",
        **params(),
    )(kept, kept, came, came)


def total_kernel(kept_ref, came_ref, out_ref):
    out_ref[...] = kept_ref[...].astype(jnp.float32) + came_ref[...].astype(jnp.float32)


def add_total(kept, came):
    return pl.pallas_call(
        total_kernel,
        out_shape=jax.ShapeDtypeStruct(kept.shape, jnp.float32),
        name="add_total",
        **params(),
    )(kept, came)


def key_value_kernel(
    at_ref, dkn_ref, dkf_ref, dvn_ref, dvf_ref, cos_ref, sin_ref, near_ref, far_ref
):
    rows = dkn_ref.shape[0] // 4
    for m in range(4):
        at = pl.ds(pl.multiple_of(at_ref[m], rows), rows)
        mine = slice(m * rows, (m + 1) * rows)
        d_key = dkn_ref[at, :] + dkf_ref[at, :]
        d_val = dvn_ref[at, :] + dvf_ref[at, :]
        both = jnp.concatenate([d_key, d_val], axis=1)
        turned = both * cos_ref[mine, :] - swap_halves(both) * sin_ref[mine, :]
        both = jnp.concatenate([turned[:, :HD], d_val], axis=1).astype(jnp.bfloat16)
        target = near_ref if m < 2 else far_ref
        target[m % 2 * rows : (m % 2 + 1) * rows, :] = both


def key_value_rows(dk_n, dk_f, dv_n, dv_f, cos_tab, sin_tab, block_pos):
    shape = jax.ShapeDtypeStruct((dk_n.shape[0] // 2, 2 * HD), jnp.bfloat16)
    arrays = (dk_n, dk_f, dv_n, dv_f, cos_tab, sin_tab)
    return pl.pallas_call(
        key_value_kernel,
        grid_spec=pltpu.PrefetchScalarGridSpec(
            num_scalar_prefetch=1,
            grid=(1,),
            in_specs=[whole(item) for item in arrays],
            out_specs=[whole(shape), whole(shape)],
        ),
        out_shape=[shape, shape],
        name="key_value_rows",
        **params(),
    )(block_pos, *arrays)


def swapped(parts, flip):
    pairs = [(i, i ^ flip) for i in range(4)]
    return tuple(lax.ppermute(part, "tensor", pairs) for part in parts)


def swap_core(parts):
    return swapped(parts, 1)


def swap_chip(parts):
    return swapped(parts, 2)


def swap_pair(parts, size):
    return tuple(exchange(part, PAIR, size) for part in parts)


class Order:
    def __init__(self):
        self.last = ()

    def after(self, *values):
        tied = lax.optimization_barrier(values + (self.last,))[: len(values)]
        self.last = tied
        return tied if len(values) > 1 else tied[0]

    def done(self, *values):
        values = lax.optimization_barrier(values + (self.last,))[: len(values)]
        self.last = values
        return values if len(values) > 1 else values[0]


def wait_for(value, *others):
    return lax.optimization_barrier((value,) + others)[0]


def rows_of(one, two):
    return jnp.concatenate([one, two], axis=0)


def block_order(bits):
    order = [0]
    for bit in reversed(bits):
        order = [item ^ bit for item in order] + order
    return order


def permuted_features(value, index, bits):
    order = block_order(bits)
    width = value.shape[1] // len(order)
    return jnp.concatenate(
        [lax.dynamic_slice_in_dim(value, (index ^ item) * width, width, 1) for item in order], axis=1
    )


def rows_and_cols(one, two):
    return jnp.concatenate([one, two], axis=1)


def exchange(value, bit, size):
    return lax.ppermute(value, "dp", [(i, i ^ bit) for i in range(size)])


class Reduction:
    def __init__(self, order, sent, kept, bits, size, assemble=None):
        self.order, self.sent, self.kept, self.assemble = order, sent, kept, assemble
        self.bits, self.size, self.step = bits, size, 0
        self.total = None

    def send(self, *others):
        sent = wait_for(self.sent, *others) if others else self.sent
        self.came = exchange(sent, self.bits[self.step], self.size)
        return self

    def receive(self):
        self.came = self.order.after(self.came)
        return self

    def add(self):
        kept, came = self.kept, self.came
        self.step += 1
        if self.step == len(self.bits):
            self.total = self.order.done((self.assemble or add_total)(kept, came))
        else:
            self.sent, self.kept = self.order.done(*add_halves(kept, came))
        return self

    def advance(self):
        self.receive().add()
        if self.total is None:
            self.send()

    def finish(self):
        while self.total is None:
            self.advance()
        return self.total


def added(one, two):
    return (one.astype(jnp.float32) + two.astype(jnp.float32)).astype(jnp.bfloat16)


def per_device(
    dp_size,
    layer_input,
    cotangent,
    starts,
    pieces,
    norm_attn,
    w_query,
    w_key,
    w_value,
    w_out,
    norm_mlp,
    w_gate,
    w_up,
    w_down,
):
    rows = layer_input.shape[0]
    width = layer_input.shape[1]
    place = lax.axis_index("tensor")
    index = lax.axis_index("dp")
    bits = [1 << i for i in range(dp_size.bit_length() - 1)]
    late_bits = bits[1:] + bits[:1]
    begins = starts[0]

    block_pos = jnp.stack([(place ^ m) * rows for m in range(4)]).astype(jnp.int32)
    near_pos, far_pos = block_pos[:2], block_pos[2:]
    row_pos = (block_pos[:, None] + jnp.arange(rows, dtype=jnp.int32)[None, :]).reshape(-1)
    cos_tab, sin_tab = rope_tables(row_pos)
    w_kv = jnp.concatenate([w_key, w_value], axis=1)

    def in_sequence(value):
        return jnp.concatenate(
            [lax.dynamic_slice_in_dim(value, (place ^ b) * rows, rows, 0) for b in range(4)], axis=0
        )

    def in_two(value):
        return tuple(jnp.split(value, PARTS, axis=0))

    order = Order()
    near, far = slice(0, 2 * rows), slice(2 * rows, 4 * rows)

    def chip_sum(kept, came):
        came = order.after(came)
        return order.done(*by_rows(lambda a, b: (a + b,), (kept, came), (), ((jnp.bfloat16,),)))

    x_own, cot_own = in_two(layer_input), in_two(cotangent)
    x_chip, x_core = swap_chip(x_own), swap_core(x_own)

    side = index // PAIR % 2
    units, queries = w_gate.shape[1], w_query.shape[1]
    window = -(-units // 256) * 128
    overlap = 2 * window - units
    mine = (jnp.arange(window) >= overlap) | (side == 0)
    gate_half = lax.dynamic_slice_in_dim(w_gate, side * (units - window), window, 1)
    up_half = lax.dynamic_slice_in_dim(w_up, side * (units - window), window, 1)
    up_half = jnp.where(mine[None, :], up_half, 0).astype(jnp.bfloat16)
    down_half = lax.dynamic_slice_in_dim(w_down, side * (units - window), window, 0)
    down_half = jnp.where(mine[:, None], down_half, 0).astype(jnp.bfloat16)
    gate_half, up_half, down_half, w_kv, cos_tab, sin_tab = order.done(
        gate_half, up_half, down_half, w_kv, cos_tab, sin_tab
    )
    normed_n, q_n, k_n, v_n = order.done(
        *project((*x_own, *x_core), norm_attn, w_query, w_kv, cos_tab[near], sin_tab[near])
    )
    x_chip = order.after(x_chip)
    cot_own_ = wait_for(cot_own, x_chip)
    cot_chip, cot_core, cot_pair = (
        swap_chip(cot_own_), swap_core(cot_own_), swap_pair(cot_own_, dp_size)
    )
    normed_f, q_f, k_f, v_f = order.done(
        *project((*x_chip, *swap_core(x_chip)), norm_attn, w_query, w_kv, cos_tab[far], sin_tab[far])
    )
    k_low = in_sequence(rows_of(k_n, k_f))
    v_low = in_sequence(rows_of(v_n, v_f))
    attn_f, lse_f, kept, *sent = order.done(
        *attend_forward(q_f, k_low, v_low, w_out, begins, far_pos)
    )
    came = swap_core(sent)
    cot_chip, cot_pair = order.after(cot_chip, cot_pair)
    cot_diag, cot_other, cot_pcore = (
        swap_pair(cot_chip, dp_size), swap_core(cot_chip), swap_core(cot_pair)
    )
    attn_came = swap_chip(chip_sum(kept, came))
    cot_core, cot_other, cot_pcore, q_n = order.after(cot_core, cot_other, cot_pcore, q_n)
    attn_n, lse_n, kept, *sent = order.done(
        *attend_forward(q_n, k_low, v_low, w_out, begins, near_pos)
    )
    sum_came = swap_core(sent)
    cot_diag = order.after(cot_diag)
    cot_dcore = swap_core(cot_diag)
    attn_came = order.after(attn_came)
    sum_came, cot_dcore = order.after(sum_came, cot_dcore)

    def norm_mid(x, kept, core, chip, gain):
        resid = x + (kept + core + chip)
        return resid, resid * rms_inverse(resid) * gain

    resid_mid, mlp_own = order.done(
        *by_rows(
            norm_mid, (x_own, kept, sum_came, attn_came), (norm_mlp,), (jnp.float32, (jnp.bfloat16,))
        )
    )
    mlp_core, mlp_chip, mlp_pair = swap_core(mlp_own), swap_chip(mlp_own), swap_pair(mlp_own, dp_size)
    mlp_core = order.after(mlp_core)

    def feed(normed, cots):
        return order.done(*feed_forward(normed, cots, gate_half, up_half, down_half))

    near_hidden = feed((*mlp_own, *mlp_core), (*cot_own, *cot_core))
    mlp_chip, mlp_pair = order.after(mlp_chip, mlp_pair)
    half = rows // 2
    mlp_diag = (
        *swap_chip((mlp_pair[0][:half],)), *swap_pair((mlp_chip[0][half:],), dp_size)
    )
    mlp_other, mlp_pcore = order.after(swap_core(mlp_chip), swap_core(mlp_pair))
    side_hidden = feed(
        (*mlp_chip, *mlp_other, *mlp_pair, *mlp_pcore),
        (*cot_chip, *cot_other, *cot_pair, *cot_pcore),
    )
    mlp_diag = order.after(mlp_diag)
    mlp_dcore = order.after(swap_core(mlp_diag))
    diag_hidden = feed((*mlp_diag, *mlp_dcore), (*cot_diag, *cot_dcore))
    hiddens = (near_hidden, side_hidden, diag_hidden)

    def in_window(kept, came):
        first = jnp.where(side == 0, kept, came)
        second = jnp.where(side == 0, came, kept)
        return jnp.concatenate([first, second[:, overlap:]], axis=1).astype(jnp.float32)

    pair_bits = [bit for bit in bits if bit != PAIR] + [PAIR]
    always = begins[0] >= 0

    def fence(step):
        def inside():
            outer_last, order.last = order.last, ()
            try:
                return step()
            finally:
                order.last = outer_last

        shapes = jax.eval_shape(inside)
        taken = order.after(always)
        results = lax.cond(
            taken,
            inside,
            lambda: jax.tree.map(lambda item: jnp.zeros(item.shape, item.dtype), shapes),
        )
        leaves, tree = jax.tree.flatten(results)
        return jax.tree.unflatten(tree, order.done(tuple(leaves)))

    def gradient(sections, order_bits):
        lefts, rights = order.after([item[0] for item in sections], [item[1] for item in sections])
        return order.done(*outer(list(zip(lefts, rights)), index, order_bits))

    cots = (
        (*cot_own, *cot_core),
        (*cot_chip, *cot_other, *cot_pair, *cot_pcore),
        (*cot_diag, *cot_dcore),
    )
    mlps = (
        (*mlp_own, *mlp_core),
        (*mlp_chip, *mlp_other, *mlp_pair, *mlp_pcore),
        (*mlp_diag, *mlp_dcore),
    )

    def mlp_gradient(lefts, which):
        sections = [(left, (right[which],)) for left, right in zip(lefts, hiddens)]
        return gradient(sections, pair_bits)

    def reduction(sent_kept, order_bits, assemble=None):
        return Reduction(order, *sent_kept, order_bits, dp_size, assemble)

    def shares(lefts, rights, transposed=True, block=0):
        kept, *sent = order.done(
            *row_shares(order.after(lefts), rights, transposed, 2 * rows, block)
        )
        return kept, swap_core(sent)

    def total(*items):
        return order.done(*by_rows(lambda *values: (sum(values),), items, (), ((jnp.bfloat16,),)))

    class GroupSum:
        def __init__(self, which, rights, transposed):
            self.rest = rights, transposed
            self.near, self.sides, self.diag = (tuple(item[i] for i in which) for item in hiddens)

        def diag_sum(self):
            return chip_sum(*shares(self.diag, *self.rest))

        def side_shares(self):
            chip, chip_came = shares(self.sides, *self.rest, 0)
            pair, pair_came = shares(self.sides, *self.rest, 1)
            return (chip, *order.after(chip_came)), (pair, *order.after(pair_came))

        def own(self):
            kept, core = shares(self.near, *self.rest)
            return kept, order.after(core)

    d_norm = GroupSum((1, 2), (gate_half, up_half), True)
    block_sum = GroupSum((0,), (down_half,), False)

    down = reduction(mlp_gradient(cots, 0), pair_bits, in_window)
    down.send()
    to_pair = swap_pair(fence(d_norm.diag_sum), dp_size)
    gate, (chip_shares, pair_shares) = fence(
        lambda: (mlp_gradient(mlps, 1), d_norm.side_shares())
    )
    gate = reduction(gate, pair_bits, in_window)
    came_p = swap_pair(total(*pair_shares), dp_size)
    came_c = swap_chip(total(*chip_shares, order.after(to_pair)))
    down.receive()
    gate.send(down.came)
    down.add().send()
    (kept, core), up = fence(lambda: (d_norm.own(), mlp_gradient(mlps, 2)))
    up = reduction(up, pair_bits, in_window)
    came_c, came_p = order.after(came_c, came_p)

    def back_mid(kept, core, chip, pair, resid, cot, gain):
        d_mid = cot + norm_back(kept + core + chip + pair, resid, rms_inverse(resid), gain)
        return d_mid, d_mid

    d_mid, d_own = order.done(
        *by_rows(
            back_mid,
            (kept, core, came_c, came_p, resid_mid, cot_own),
            (norm_mlp,),
            (jnp.float32, (jnp.bfloat16,)),
        )
    )
    d_chip = swap_chip(d_own)
    gate.receive()
    up.send(gate.came)
    down.receive().add()
    down.send()
    gate.add().send()

    @fence
    def near_back():
        d_core = order.after(swap_core(d_own))
        return d_core, order.done(
            *attend_backward(
                q_n, (*d_own, *d_core), w_out, attn_n, lse_n, k_low, v_low, cos_tab[near],
                sin_tab[near], begins, near_pos,
            )
        )

    d_core, (dq_n, dk_n, dv_n) = near_back
    d_chip = order.after(d_chip)
    down.receive().add()

    @fence
    def far_back():
        d_other = order.after(swap_core(d_chip))
        dq_f, dk_f, dv_f = order.done(
            *attend_backward(
                q_f, (*d_chip, *d_other), w_out, attn_f, lse_f, k_low, v_low, cos_tab[far],
                sin_tab[far], begins, far_pos,
            )
        )
        dkv_n, dkv_f = order.done(
            *key_value_rows(dk_n, dk_f, dv_n, dv_f, cos_tab, sin_tab, block_pos)
        )
        in_sum = chip_sum(*shares((dq_f, dkv_f), (w_query, w_kv)))
        return d_other, dq_f, dkv_n, dkv_f, in_sum

    d_other, dq_f, dkv_n, dkv_f, in_sum = far_back
    d_in_came = swap_chip(in_sum)
    gate.receive()
    up.receive()
    gate.add().send()
    up.add().send()
    to_pair = swap_pair(fence(block_sum.diag_sum), dp_size)
    qkv = fence(
        lambda: gradient([((normed_n,), (dq_n, dkv_n)), ((normed_f,), (dq_f, dkv_f))], late_bits)
    )
    gate.receive().add()
    qkv = reduction(qkv, late_bits)
    qkv.send()
    wout = fence(
        lambda: gradient([((*d_own, *d_core), (attn_n,)), ((*d_chip, *d_other), (attn_f,))], bits)
    )
    wout = reduction(wout, bits)
    wout.send()

    @fence
    def near_shares():
        kept, core = shares((dq_n, dkv_n), (w_query, w_kv))
        return kept, order.after(core)

    kept_in, core_in = near_shares
    d_in_came = order.after(d_in_came)

    def back_in(kept, core, chip, resid, d_mid, gain):
        return (d_mid + norm_back(kept + core + chip, resid, rms_inverse(resid), gain),)

    (x_grad,) = by_rows(
        back_in, (kept_in, core_in, d_in_came, x_own, d_mid), (norm_attn,), (jnp.float32,)
    )
    x_grad = order.done(x_grad)
    up.receive()
    up.add().send()
    chip_shares, pair_shares = fence(block_sum.side_shares)
    to_pair = order.after(to_pair)
    up.receive()
    block_p = swap_pair(total(*pair_shares), dp_size)
    block_c = swap_chip(total(*chip_shares, to_pair))
    up.add()
    kept, core = fence(block_sum.own)
    wout.advance()
    qkv.advance()
    wout.advance()
    block_c, block_p = order.after(block_c, block_p)
    (block_out,) = by_rows(
        lambda *items: (sum(items),),
        (resid_mid, kept, core, block_c, block_p),
        (),
        (jnp.bfloat16,),
    )
    block_out = order.done(block_out)
    qkv.advance()
    for item in (down, gate, up, wout, qkv):
        item.finish()
    grad_down, grad_gate, grad_up = down.total.T, gate.total, up.total
    grad_out, grad_qkv = wout.total.T, qkv.total
    queries = w_query.shape[1]
    grad_query = grad_qkv[:, :queries]
    grad_key = grad_qkv[:, queries : queries + HD]
    grad_value = grad_qkv[:, queries + HD :]

    share = width // dp_size

    def own_features(value):
        return lax.dynamic_slice_in_dim(value, index * share, share, 0).astype(jnp.float32)

    gain_attn = (
        jnp.sum(own_features(w_query) * grad_query, axis=1)
        + jnp.sum(own_features(w_kv) * grad_qkv[:, queries:], axis=1)
    ) / own_features(norm_attn)
    gain_mlp = jnp.sum(
        own_features(w_gate) * grad_gate + own_features(w_up) * grad_up, axis=1
    ) / own_features(norm_mlp)
    gains = jnp.stack([gain_attn, gain_mlp]).reshape(2, 4, share // 4)
    gains = jnp.stack([lax.dynamic_index_in_dim(gains, place ^ m, 1, False) for m in range(4)])
    gains = gains[:2] + lax.ppermute(gains[2:], "tensor", [(i, i ^ 2) for i in range(4)])
    gains = gains[0] + lax.ppermute(gains[1], "tensor", [(i, i ^ 1) for i in range(4)])

    return (
        block_out,
        x_grad,
        gains[0],
        grad_query,
        grad_key,
        grad_value,
        grad_out,
        gains[1],
        grad_gate,
        grad_up,
        grad_down,
    )


def solution(mesh):
    in_specs = (
        P(("dp", "tensor"), None),
        P(("dp", "tensor"), None),
        P("dp", None),
        P("dp"),
        P(),
        P(None, "tensor"),
        P(None, "tensor"),
        P(None, "tensor"),
        P("tensor", None),
        P(),
        P(None, "tensor"),
        P(None, "tensor"),
        P("tensor", None),
    )
    out_specs = (
        P(("dp", "tensor"), None),
        P(("dp", "tensor"), None),
        P(("dp", "tensor")),
        P("dp", "tensor"),
        P("dp", "tensor"),
        P("dp", "tensor"),
        P("tensor", "dp"),
        P(("dp", "tensor")),
        P("dp", "tensor"),
        P("dp", "tensor"),
        P("tensor", "dp"),
    )
    return jax.shard_map(
        functools.partial(per_device, mesh.shape["dp"]),
        mesh=mesh,
        in_specs=in_specs,
        out_specs=out_specs,
        check_vma=False,
    )
```

time: 629 us -> 497 us (0.79)
  Pallas kernels: 56.5 us -> 273 us
  waiting for transfers between devices: 300 us -> 108 us
  matrix products: 124 us -> 0 us
  other arithmetic: 50.7 us -> 26.4 us
  local copies, waits for them, and re-layouts: 49.8 us -> 26.4 us
  starting transfers between devices: 35.9 us -> 53.9 us
    pallas_call x2 -> x45, Pallas kernels: 8.69 us -> 206 us  [the longest x5 58.8 us: outer(): pl.pallas_call(functools.partial(outer_kernel, shape=[(len(lefts), len(ri...]
    ppermute x41 -> x59, waiting for transfers between devices: 300 us -> 108 us  [the longest x23 64.2 us: exchange(): return lax.ppermute(value, 'dp', [(i, i ^ bit) for i in range(size)])]
    dot_general x30 -> x0, matrix products: 124 us -> none  [the longest x12 53.1 us: contract_cols(): return lax.dot_general(left, right, NT, preferred_element_type=jnp.float32)]
    ppermute x41 -> x59, starting transfers between devices: 35.9 us -> 53.9 us  [the longest x34 25.3 us: swapped(): return tuple((lax.ppermute(part, 'tensor', pairs) for part in parts))]
    select_n x0 -> x8, other arithmetic: none -> 14.8 us  [the longest x1 6.15 us: per_device(): up_half = jnp.where(mine[None, :], up_half, 0).astype(jnp.bfloat16)]
    convert_element_type x12 -> x3, other arithmetic: 17.5 us -> 3.58 us  [in_window(): jnp.concatenate([first, second[:, overlap:]], axis=1).astype(jnp.float32)]
    pallas_call x2, Pallas kernels: 28.3 us -> 39.7 us  [attend_backward(): pl.pallas_call(functools.partial(backward_kernel, heads=heads, pics=pics,...]
    unnamed x249 -> x127, local copies, waits for them, and re-layouts: 28.2 us -> 19.5 us
  transfers between devices with their start and end apart: 41 -> 59, of which waited for: 12 -> 28; matrix products, arithmetic and copies ran while one was open for 32% -> 8% of each run, Pallas kernels for 7% -> 51%
where the time goes in v2:
time: 497 us; the launch traced here: 490 us
  Pallas kernels  273 us (55%)
  waiting for transfers between devices  108 us (22%)
  starting transfers between devices  53.9 us (11%)
  other arithmetic  26.4 us (5%)
  local copies, waits for them, and re-layouts  26.4 us (5%)
    ppermute x23, waiting for transfers between devices, exchange(): return lax.ppermute(value, 'dp', [(i, i ^ bit) for i in range(size)])  64.2 us
    pallas_call x5, Pallas kernels, outer(): pl.pallas_call(functools.partial(outer_kernel, shape=[(len(lefts), len(ri...  58.8 us
    pallas_call x10, Pallas kernels, row_shares(): pl.pallas_call(functools.partial(share_kernel, transposed=transposed), gr...  48.2 us
    ppermute x34, waiting for transfers between devices, swapped(): return tuple((lax.ppermute(part, 'tensor', pairs) for part in parts))  43.4 us
    pallas_call x2, Pallas kernels, attend_backward(): pl.pallas_call(functools.partial(backward_kernel, heads=heads, pics=pics,...  39.7 us
    pallas_call x3, Pallas kernels, feed_forward(): pl.pallas_call(functools.partial(feed_kernel, counts=(len(normed), len(co...  34.2 us
    pallas_call x12, Pallas kernels, by_rows(): pl.pallas_call(kernel, out_shape=shapes, name='by_rows', **params())  31.7 us
    pallas_call x2, Pallas kernels, attend_forward(): pl.pallas_call(functools.partial(forward_kernel, heads=heads, pics=pics,...  27.5 us
  transfers between devices with their start and end apart: 59, of which 28 were waited for; matrix products, arithmetic and copies ran while one was open for 8% of the time, Pallas kernels for 51%

profile of v2, /device:TPU:9, one launch (start us, length us, event | category | flops | bytes accessed | tf_op | source)
XLA Modules:
  0.0 489.8 jit_solution(7409152332771938861)
XLA Ops:
  8.3 6.2 %dynamic-slice_select_fusion.1 = (bf16[2048,768]{1,0:T(8,128)(2,1)}, bf16[2048,768]{1,0:T(8,128)(2,1)}) fusion(bf16[2048,1408]{1,0:T(8,128)(2,1)} %param.45, s32[]{:T(128)S(6)} %select_n.91, pred[768]{0:T(1024)(128)(4,1)S(1)} %fusion.1, bf16[2048,1408]{1,0:T(8,128)(2,1)} %param.44), kind=kLoop, calls=%fused_computation.1 | loop fusion | flops 1572864 | bytes 12583684 | tf_op jit(solution)/shard_map/jit(_where)/select_n | solution.py:773
  19.1 4.1 project.2
  30.5 6.1 %project.3 = (bf16[512,2048]{1,0:T(8,128)(2,1)}, bf16[512,512]{1,0:T(8,128)(2,1)S(1)}, bf16[512,64]{1,0:T(8,128)(2,1)S(1)}, bf16[512,64]{1,0:T(8,128)(2,1)S(1)}) custom-call(bf16[256,2048]{1,0:T(8,128)(2,1)} %collective-permute-done.12.refs_0_, bf16[256,2048]{1,0:T(8,128)(2,1)} %collective-permute-done.17.refs_1_, f32[1,2048]{1,0:T(1,128)S(1)} %bitcast.74, ...), custom_call_target="tpu_custom_call" | custom-call | flops 1 | bytes 1 | tf_op jit(solution)/shard_map/project/pallas_call | solution.py:116
  38.6 14.0 %attend_forward.2 = (bf16[512,512]{1,0:T(8,128)(2,1)}, f32[512,8]{1,0:T(8,128)}, bf16[256,2048]{1,0:T(8,128)(2,1)S(1)}, bf16[256,2048]{1,0:T(8,128)(2,1)S(1)}) custom-call(s32[2]{0:T(128)S(1)} %get-tuple-element.974.pos_ref, s32[2]{0:T(128)S(1)} %bitcast.82, bf16[512,512]{1,0:T(8,128)(2,1)S(1)} %get-tuple-element.693.q_ref, ...), custom_call_target="tpu_custom_call" | custom-call | flops 1 | bytes 1 | tf_op jit(solution)/shard_map/attend_forward/pallas_call | solution.py:271
  58.3 13.5 %attend_forward.3 = (bf16[512,512]{1,0:T(8,128)(2,1)}, f32[512,8]{1,0:T(8,128)}, bf16[256,2048]{1,0:T(8,128)(2,1)S(1)}, bf16[256,2048]{1,0:T(8,128)(2,1)S(1)}) custom-call(s32[2]{0:T(128)S(1)} %get-tuple-element.973.pos_ref, s32[2]{0:T(128)S(1)} %bitcast.83, bf16[512,512]{1,0:T(8,128)(2,1)S(1)} %copy-done.58, bf16[1024,64]{1,0:T(8,128)(2,1)S(1)} %pad_maximum_fusion.3.k_ref, ...), custom_call_target="tpu_custom_call" | custom-call | flops 1 | bytes 1 | tf_op jit(solution)/shard_map/attend_forward/pallas_call | solution.py:271
  71.9 5.7 %collective-permute-done.22.refs_4_.refs_8_ = bf16[256,2048]{1,0:T(8,128)(2,1)S(1)} collective-permute-done((bf16[256,2048]{1,0:T(8,128)(2,1)S(1)}, bf16[256,2048]{1,0:T(8,128)(2,1)S(1)}, u32[]{:S(2)}, u32[]{:S(2)}) %collective-permute-start.22) | collective-permute-done | bytes 1048608 | tf_op jit(solution)/shard_map/ppermute | solution.py:676
  81.3 3.1 by_rows.16
  87.3 10.1 %feed_forward.3 = (bf16[512,768]{1,0:T(8,128)(2,1)}, bf16[512,768]{1,0:T(8,128)(2,1)}, bf16[512,768]{1,0:T(8,128)(2,1)}) custom-call(bf16[256,2048]{1,0:T(8,128)(2,1)} %get-tuple-element.728.refs_0_, bf16[256,2048]{1,0:T(8,128)(2,1)} %collective-permute-done.25.refs_1_, bf16[256,2048]{1,0:T(8,128)(2,1)S(1)} %copy-done.1, ...), custom_call_target="tpu_custom_call" | custom-call | flops 1 | bytes 1 | tf_op jit(solution)/shard_map/feed_forward/pallas_call | solution.py:436
  97.5 12.1 %collective-permute-done.26.refs_0_ = bf16[256,2048]{1,0:T(8,128)(2,1)S(1)} collective-permute-done((bf16[256,2048]{1,0:T(8,128)(2,1)}, bf16[256,2048]{1,0:T(8,128)(2,1)S(1)}, u32[]{:S(2)}, u32[]{:S(2)}) %collective-permute-start.26) | collective-permute-done | bytes 1048608 | tf_op jit(solution)/shard_map/ppermute | solution.py:618
  114.7 14.2 %feed_forward.4 = (bf16[1024,768]{1,0:T(8,128)(2,1)}, bf16[1024,768]{1,0:T(8,128)(2,1)}, bf16[1024,768]{1,0:T(8,128)(2,1)}) custom-call(bf16[256,2048]{1,0:T(8,128)(2,1)S(1)} %collective-permute-done.26.refs_0_, bf16[256,2048]{1,0:T(8,128)(2,1)S(1)} %collective-permute-done.28.refs_1_, bf16[256,2048]{1,0:T(8,128)(2,1)S(1)} %collective-permute-done.27.refs_2_, ...), custom_call_target="tpu_custom_call" | custom-call | flops 1 | bytes 1 | tf_op jit(solution)/shard_map/feed_forward/pallas_call | solution.py:436
  134.8 9.9 %feed_forward.5 = (bf16[512,768]{1,0:T(8,128)(2,1)S(1)}, bf16[512,768]{1,0:T(8,128)(2,1)}, bf16[512,768]{1,0:T(8,128)(2,1)}) custom-call(bf16[128,2048]{1,0:T(8,128)(2,1)} %collective-permute-done.30.refs_0_, bf16[128,2048]{1,0:T(8,128)(2,1)} %collective-permute-done.31.refs_1_, bf16[128,2048]{1,0:T(8,128)(2,1)} %collective-permute-done.32.refs_2_, ...), custom_call_target="tpu_custom_call" | custom-call | flops 1 | bytes 1 | tf_op jit(solution)/shard_map/feed_forward/pallas_call | solution.py:436
  144.7 12.4 %outer.9 = (bf16[1024,768]{1,0:T(8,128)(2,1)}, bf16[1024,768]{1,0:T(8,128)(2,1)}) custom-call(s32[8]{0:T(128)S(1)} %stack.195.order_ref, bf16[256,2048]{1,0:T(8,128)(2,1)S(1)} %copy-done.1, bf16[256,2048]{1,0:T(8,128)(2,1)S(1)} %copy-done.10, bf16[512,768]{1,0:T(8,128)(2,1)S(1)} %copy-done.55, bf16[256,2048]{1,0:T(8,128)(2,1)S(1)} %collective-permute-done.15.refs_4_.refs_3_, ...), custom_call_target="tpu_custom_call" | custom-call | flops 1 | bytes 1 | tf_op jit(solution)/shard_map/outer/pallas_call | solution.py:530
  158.4 9.8 %conditional.11 = (bf16[256,2048]{1,0:T(8,128)(2,1)S(1)}) conditional(s32[]{:T(128)} %convert_element_type.78, () %tuple.251, (bf16[512,768]{1,0:T(8,128)(2,1)}, bf16[512,768]{1,0:T(8,128)(2,1)}, bf16[2048,768]{1,0:T(8,128)(2,1)}, bf16[2048,768]{1,0:T(8,128)(2,1)}) %tuple.252), branch_computations={%region_0.1_spmd, %region_1.2_spmd} | conditional | flops 2 | bytes 4194354 | solution.py:860
  158.5 6.5 %row_shares.10 = (bf16[256,2048]{1,0:T(8,128)(2,1)S(1)}, bf16[256,2048]{1,0:T(8,128)(2,1)S(1)}) custom-call(bf16[512,768]{1,0:T(8,128)(2,1)} %get-tuple-element.186.refs_0_, bf16[512,768]{1,0:T(8,128)(2,1)} %get-tuple-element.187.refs_1_, bf16[2048,768]{1,0:T(8,128)(2,1)} %get-tuple-element.188.refs_2_, bf16[2048,768]{1,0:T(8,128)(2,1)} %get-tuple-element.189.refs_3_), custom_call_target="tpu_custom_call" | custom-call | flops 1 | bytes 1 | tf_op jit(solution)/shard_map/cond/branch_1_fun/row_shares/pallas_call | solution.py:477
  169.8 27.1 %conditional.12 = (bf16[1024,768]{1,0:T(8,128)(2,1)}, bf16[1024,768]{1,0:T(8,128)(2,1)}, bf16[256,2048]{1,0:T(8,128)(2,1)}, bf16[256,2048]{1,0:T(8,128)(2,1)}, b...) conditional(s32[]{:T(128)} %convert_element_type.79, () %tuple.255, (s32[]{:T(128)}, ...), branch_computations={%region_2.3_spmd, %region_3.4_spmd} | conditional | flops 10 | bytes 46137732 | solution.py:860
  169.9 14.0 %outer.5 = (bf16[1024,768]{1,0:T(8,128)(2,1)}, bf16[1024,768]{1,0:T(8,128)(2,1)}) custom-call(s32[8]{0:T(128)S(1)} %stack.127.order_ref, bf16[256,2048]{1,0:T(8,128)(2,1)} %get-tuple-element.210.refs_0_, bf16[256,2048]{1,0:T(8,128)(2,1)} %get-tuple-element.211.refs_1_, bf16[512,768]{1,0:T(8,128)(2,1)} %get-tuple-element.212.refs_2_, ...), custom_call_target="tpu_custom_call" | custom-call | flops 1 | bytes 1 | tf_op jit(solution)/shard_map/cond/branch_1_fun/outer/pallas_call | solution.py:530
  183.9 4.8 row_shares.11
  189.3 4.7 row_shares.12
  209.4 24.9 %conditional.13 = (bf16[256,2048]{1,0:T(8,128)(2,1)}, bf16[256,2048]{1,0:T(8,128)(2,1)}, bf16[1024,768]{1,0:T(8,128)(2,1)}, bf16[1024,768]{1,0:T(8,128)(2,1)}) conditional(s32[]{:T(128)} %convert_element_type.80, () %tuple.264, (bf16[512,768]{1,0:T(8,128)(2,1)}, bf16[512,768]{1,0:T(8,128)(2,1)}, bf16[2048,768]{1,0:T(8,128)(2,1)}, ...), branch_computations={%region_4.5_spmd, %region_5.6_spmd} | conditional | flops 9 | bytes 5242920 | solution.py:860
  209.4 7.2 %row_shares.13 = (bf16[256,2048]{1,0:T(8,128)(2,1)}, bf16[256,2048]{1,0:T(8,128)(2,1)}) custom-call(bf16[512,768]{1,0:T(8,128)(2,1)} %get-tuple-element.246.refs_0_, bf16[512,768]{1,0:T(8,128)(2,1)} %get-tuple-element.270.refs_1_.refs_2_, bf16[2048,768]{1,0:T(8,128)(2,1)} %get-tuple-element.248.refs_2_, bf16[2048,768]{1,0:T(8,128)(2,1)} %get-tuple-element.249.refs_3_), custom_call_target="tpu_custom_call" | custom-call | flops 1 | bytes 1 | tf_op jit(solution)/shard_map/cond/branch_1_fun/row_shares/pallas_call | solution.py:477
  220.5 13.8 %outer.6 = (bf16[1024,768]{1,0:T(8,128)(2,1)}, bf16[1024,768]{1,0:T(8,128)(2,1)}) custom-call(s32[8]{0:T(128)S(1)} %stack.136.order_ref, bf16[256,2048]{1,0:T(8,128)(2,1)} %get-tuple-element.268.refs_0_, bf16[256,2048]{1,0:T(8,128)(2,1)} %get-tuple-element.269.refs_1_, bf16[512,768]{1,0:T(8,128)(2,1)} %get-tuple-element.270.refs_1_.refs_2_, ...), custom_call_target="tpu_custom_call" | custom-call | flops 1 | bytes 1 | tf_op jit(solution)/shard_map/cond/branch_1_fun/outer/pallas_call | solution.py:530
  234.3 8.9 %collective-permute-done.38.refs_3_ = bf16[256,2048]{1,0:T(8,128)(2,1)} collective-permute-done((bf16[256,2048]{1,0:T(8,128)(2,1)}, bf16[256,2048]{1,0:T(8,128)(2,1)}, u32[]{:S(2)}, u32[]{:S(2)}) %collective-permute-start.38) | collective-permute-done | bytes 1048608 | tf_op jit(solution)/shard_map/ppermute | solution.py:676
  243.2 5.6 %by_rows.19 = (f32[256,2048]{1,0:T(8,128)S(1)}, bf16[256,2048]{1,0:T(8,128)(2,1)}) custom-call(bf16[256,2048]{1,0:T(8,128)(2,1)} %get-tuple-element.802.refs_0_, bf16[256,2048]{1,0:T(8,128)(2,1)} %get-tuple-element.803.refs_1_, bf16[256,2048]{1,0:T(8,128)(2,1)} %collective-permute-done.37.refs_2_, bf16[256,2048]{1,0:T(8,128)(2,1)} %collective-permute-done.38.refs_3_, ...), custom_call_target="tpu_custom_call" | custom-call | flops 1 | bytes 1 | tf_op jit(solution)/shard_map/by_rows/pallas_call | solution.py:182
  260.6 24.0 %conditional.14 = (bf16[256,2048]{1,0:T(8,128)(2,1)}, bf16[512,512]{1,0:T(8,128)(2,1)}, f32[1024,64]{1,0:T(8,128)}, f32[1024,64]{1,0:T(8,128)}) conditional(s32[]{:T(128)} %convert_element_type.81, () %tuple.276, (bf16[256,2048]{1,0:T(8,128)(2,1)}, f32[1024,128]{1,0:T(8,128)}, f32[1024,128]{1,0:T(8,128)}, s32[2]{0:T(128)S(1)}, s32[2]{0:T(128)S(1)}, ...), branch_computations={%region_6.7_spmd, %region_7.8_spmd} | conditional | flops 1 | bytes 5242953 | solution.py:860
  265.4 18.9 %attend_backward.2 = (bf16[512,512]{1,0:T(8,128)(2,1)}, f32[1024,64]{1,0:T(8,128)}, f32[1024,64]{1,0:T(8,128)}) custom-call(s32[2]{0:T(128)S(1)} %get-tuple-element.286.pos_ref, s32[2]{0:T(128)S(1)} %get-tuple-element.287.starts_ref, bf16[512,512]{1,0:T(8,128)(2,1)} %get-tuple-element.288.q_ref, bf16[512,2048]{1,0:T(8,128)(2,1)} %get-tuple-element.289.out_ref, ...), custom_call_target="tpu_custom_call" | custom-call | flops 1 | bytes 1 | tf_op jit(solution)/shard_map/cond/branch_1_fun/attend_backward/pallas_call | solution.py:383
  288.1 34.6 %conditional.15 = (bf16[256,2048]{1,0:T(8,128)(2,1)}, bf16[512,512]{1,0:T(8,128)(2,1)}, bf16[512,128]{1,0:T(8,128)(2,1)}, bf16[512,128]{1,0:T(8,128)(2,1)}, bf16[256,2048]{1,0:T(8,128)(2,1)}) conditional(s32[]{:T(128)} %convert_element_type.83, () %tuple.283, (bf16[256,2048]{1,0:T(8,128)(2,1)}, f32[1024,128]{1,0:T(8,128)}, f32[1024,128]{1,0:T(8,128)}, ...), branch_computations={%region_8.9_spmd, %region_9.10_spmd} | conditional | flops 4 | bytes 30408996 | solution.py:860
  290.9 20.9 %attend_backward.3 = (bf16[512,512]{1,0:T(8,128)(2,1)S(1)}, f32[1024,64]{1,0:T(8,128)S(1)}, f32[1024,64]{1,0:T(8,128)S(1)}) custom-call(s32[2]{0:T(128)S(1)} %get-tuple-element.303.pos_ref, s32[2]{0:T(128)S(1)} %get-tuple-element.304.starts_ref, bf16[512,512]{1,0:T(8,128)(2,1)} %get-tuple-element.305.q_ref, bf16[512,2048]{1,0:T(8,128)(2,1)} %get-tuple-element.306.out_ref, ...), custom_call_target="tpu_custom_call" | custom-call | flops 1 | bytes 1 | tf_op jit(solution)/shard_map/cond/branch_1_fun/attend_backward/pallas_call | solution.py:383
  311.9 3.4 key_value_rows.1
  315.3 3.4 row_shares.14
  328.6 9.0 %conditional.16 = (bf16[256,2048]{1,0:T(8,128)(2,1)}) conditional(s32[]{:T(128)} %convert_element_type.84, () %tuple.291, (bf16[512,768]{1,0:T(8,128)(2,1)}, bf16[768,2048]{1,0:T(8,128)(2,1)}) %tuple.404), branch_computations={%region_10.11_spmd, %region_11.12_spmd} | conditional | flops 2 | bytes 4194354 | solution.py:860
  328.6 4.5 row_shares.15
  338.7 9.6 %conditional.17 = ((bf16[1024,640]{1,0:T(8,128)(2,1)}, bf16[1024,640]{1,0:T(8,128)(2,1)})) conditional(s32[]{:T(128)} %convert_element_type.85, () %tuple.295, (s32[]{:T(128)}, bf16[512,2048]{1,0:T(8,128)(2,1)}, bf16[512,2048]{1,0:T(8,128)(2,1)}, bf16[512,512]{1,0:T(8,128)(2,1)}, bf16[512,128]{1,0:T(8,128)(2,1)}, ...), branch_computations={%region_12.13_spmd, %region_13.14_spmd} | conditional | flops 8 | bytes 2621468 | solution.py:860
  338.8 9.5 %outer.7 = (bf16[1024,640]{1,0:T(8,128)(2,1)}, bf16[1024,640]{1,0:T(8,128)(2,1)}) custom-call(s32[8]{0:T(128)S(1)} %stack.145.order_ref, bf16[512,2048]{1,0:T(8,128)(2,1)} %get-tuple-element.351.refs_0_, bf16[512,512]{1,0:T(8,128)(2,1)} %get-tuple-element.352.refs_1_, bf16[512,128]{1,0:T(8,128)(2,1)} %get-tuple-element.353.refs_2_, ...), custom_call_target="tpu_custom_call" | custom-call | flops 1 | bytes 1 | tf_op jit(solution)/shard_map/cond/branch_1_fun/outer/pallas_call | solution.py:530
  352.0 9.3 %conditional.18 = ((bf16[1024,512]{1,0:T(8,128)(2,1)}, bf16[1024,512]{1,0:T(8,128)(2,1)})) conditional(s32[]{:T(128)} %convert_element_type.87, () %tuple.301, (s32[]{:T(128)}, bf16[256,2048]{1,0:T(8,128)(2,1)}, bf16[256,2048]{1,0:T(8,128)(2,1)}, bf16[256,2048]{1,0:T(8,128)(2,1)}, bf16[256,2048]{1,0:T(8,128)(2,1)}, ...), branch_computations={%region_14.15_spmd, %region_15.16_spmd} | conditional | flops 8 | bytes 2097180 | solution.py:860
  352.2 9.1 %outer.8 = (bf16[1024,512]{1,0:T(8,128)(2,1)}, bf16[1024,512]{1,0:T(8,128)(2,1)}) custom-call(s32[8]{0:T(128)S(1)} %stack.154.order_ref, bf16[256,2048]{1,0:T(8,128)(2,1)} %get-tuple-element.368.refs_0_, bf16[256,2048]{1,0:T(8,128)(2,1)} %get-tuple-element.369.refs_1_, bf16[512,512]{1,0:T(8,128)(2,1)} %get-tuple-element.370.refs_2_, ...), custom_call_target="tpu_custom_call" | custom-call | flops 1 | bytes 1 | tf_op jit(solution)/shard_map/cond/branch_1_fun/outer/pallas_call | solution.py:530
  361.3 8.3 %conditional.19 = (bf16[256,2048]{1,0:T(8,128)(2,1)}, bf16[256,2048]{1,0:T(8,128)(2,1)}) conditional(s32[]{:T(128)} %convert_element_type.88, () %tuple.305, (bf16[512,512]{1,0:T(8,128)(2,1)}, bf16[512,128]{1,0:T(8,128)(2,1)S(1)}, bf16[2048,512]{1,0:T(8,128)(2,1)}, bf16[2048,128]{1,0:T(8,128)(2,1)}) %tuple.406), branch_computations={%region_16.17_spmd, %region_17.18_spmd} | conditional | flops 1 | bytes 4194361 | solution.py:860
  361.4 5.0 %row_shares.16 = (bf16[256,2048]{1,0:T(8,128)(2,1)}, bf16[256,2048]{1,0:T(8,128)(2,1)S(1)}) custom-call(bf16[512,512]{1,0:T(8,128)(2,1)} %get-tuple-element.380.refs_0_, bf16[512,128]{1,0:T(8,128)(2,1)S(1)} %get-tuple-element.381.refs_1_, bf16[2048,512]{1,0:T(8,128)(2,1)} %get-tuple-element.382.refs_2_, bf16[2048,128]{1,0:T(8,128)(2,1)} %get-tuple-element.383.refs_3_), custom_call_target="tpu_custom_call" | custom-call | flops 1 | bytes 1 | tf_op jit(solution)/shard_map/cond/branch_1_fun/row_shares/pallas_call | solution.py:477
  371.3 4.8 by_rows.20
  379.9 10.8 %conditional.20 = (bf16[256,2048]{1,0:T(8,128)(2,1)S(1)}, bf16[256,2048]{1,0:T(8,128)(2,1)}, bf16[256,2048]{1,0:T(8,128)(2,1)S(1)}, bf16[256,2048]{1,0:T(8,128)(2,1)}) conditional(s32[]{:T(128)} %convert_element_type.89, () %tuple.313, (bf16[1024,768]{1,0:T(8,128)(2,1)}, bf16[768,2048]{1,0:T(8,128)(2,1)}) %tuple.314), branch_computations={%region_18.19_spmd, %region_19.20_spmd} | conditional | flops 2 | bytes 27263144 | solution.py:860
  379.9 4.5 row_shares.17
  396.4 15.3 %collective-permute-done.47 = bf16[256,768]{1,0:T(8,128)(2,1)} collective-permute-done((bf16[256,768]{1,0:T(8,128)(2,1)}, bf16[256,768]{1,0:T(8,128)(2,1)}, u32[]{:S(2)}, u32[]{:S(2)}) %collective-permute-start.47) | collective-permute-done | bytes 393248 | tf_op jit(solution)/shard_map/ppermute | solution.py:676
  417.7 9.2 %conditional.21 = (bf16[256,2048]{1,0:T(8,128)(2,1)}, bf16[256,2048]{1,0:T(8,128)(2,1)}) conditional(s32[]{:T(128)} %convert_element_type.91, () %tuple.322, (bf16[512,768]{1,0:T(8,128)(2,1)}, bf16[768,2048]{1,0:T(8,128)(2,1)}) %tuple.323), branch_computations={%region_20.21_spmd, %region_21.22_spmd} | conditional | flops 1 | bytes 4194361 | solution.py:860
  417.7 5.0 %row_shares.19 = (bf16[256,2048]{1,0:T(8,128)(2,1)}, bf16[256,2048]{1,0:T(8,128)(2,1)S(1)}) custom-call(bf16[512,768]{1,0:T(8,128)(2,1)} %get-tuple-element.402.refs_0_, bf16[768,2048]{1,0:T(8,128)(2,1)} %get-tuple-element.403.refs_1_), custom_call_target="tpu_custom_call" | custom-call | flops 1 | bytes 1 | tf_op jit(solution)/shard_map/cond/branch_1_fun/row_shares/pallas_call | solution.py:477
  431.3 29.8 %collective-permute-done.52.came_a.came_b = bf16[512,512]{1,0:T(8,128)(2,1)} collective-permute-done((bf16[512,512]{1,0:T(8,128)(2,1)}, bf16[512,512]{1,0:T(8,128)(2,1)}, u32[]{:S(2)}, u32[]{:S(2)}) %collective-permute-start.52) | collective-permute-done | bytes 524320 | tf_op jit(solution)/shard_map/ppermute | solution.py:676
  462.9 3.9 by_rows.23
  470.3 3.8 collective-permute-done.56.came_ref
  477.9 3.5 collective-permute-start.57
  484.0 3.6 collective-permute-start.58
  (334 shorter events, 162.0 us)
Async XLA Ops:
  0.6 24.4 %collective-permute-start.12 = (bf16[256,2048]{1,0:T(8,128)(2,1)}, bf16[256,2048]{1,0:T(8,128)(2,1)}, u32[]{:S(2)}, u32[]{:S(2)}) collective-permute-start(bf16[256,2048]{1,0:T(8,128)(2,1)} %refs_3_.5), channel_id=1, source_target_pairs={{0,2},{1,3},{2,0},{3,1},{4,6},{5,7},{6,4},{7,5},{8,10},{9,11},{10,... | collective-permute-start | bytes 3145736 | tf_op jit(solution)/shard_map/ppermute | solution.py:618
  1.9 16.5 %collective-permute-start.13 = (bf16[256,2048]{1,0:T(8,128)(2,1)}, bf16[256,2048]{1,0:T(8,128)(2,1)S(1)}, u32[]{:S(2)}, u32[]{:S(2)}) collective-permute-start(bf16[256,2048]{1,0:T(8,128)(2,1)} %refs_3_.5), channel_id=1, source_target_pairs={{0,1},{1,0},{2,3},{3,2},{4,5},{5,4},{6,7},{7,6},{8,9},{9,8},{10,11... | collective-permute-start | bytes 3145736 | tf_op jit(solution)/shard_map/ppermute | solution.py:618
  25.1 4.5 collective-permute-start.17
  26.6 26.0 %collective-permute-start.15 = (bf16[256,2048]{1,0:T(8,128)(2,1)S(1)}, bf16[256,2048]{1,0:T(8,128)(2,1)S(1)}, u32[]{:S(2)}, u32[]{:S(2)}) collective-permute-start(bf16[256,2048]{1,0:T(8,128)(2,1)S(1)} %copy-done.1), channel_id=1, source_target_pairs={{0,2},{1,3},{2,0},{3,1},{4,6},{5,7},{6,4},{7,5},{8,10},{9,11},{10,... | collective-permute-start | bytes 3145736 | tf_op jit(solution)/shard_map/ppermute | solution.py:618
  27.8 24.8 %collective-permute-start.16 = (bf16[256,2048]{1,0:T(8,128)(2,1)S(1)}, bf16[256,2048]{1,0:T(8,128)(2,1)S(1)}, u32[]{:S(2)}, u32[]{:S(2)}) collective-permute-start(bf16[256,2048]{1,0:T(8,128)(2,1)S(1)} %copy-done.1), channel_id=1, source_target_pairs={{0,8},{4,12},{8,0},{12,4},{16,24},{20,28},{24,16},{28,20},{1,9},{5... | collective-permute-start | bytes 3145736 | tf_op jit(solution)/shard_map/ppermute | solution.py:676
  28.1 27.6 %collective-permute-start.14 = (bf16[256,2048]{1,0:T(8,128)(2,1)S(1)}, bf16[256,2048]{1,0:T(8,128)(2,1)S(1)}, u32[]{:S(2)}, u32[]{:S(2)}) collective-permute-start(bf16[256,2048]{1,0:T(8,128)(2,1)S(1)} %copy-done.1), channel_id=1, source_target_pairs={{0,1},{1,0},{2,3},{3,2},{4,5},{5,4},{6,7},{7,6},{8,9},{9,8},{10,11... | collective-permute-start | bytes 3145736 | tf_op jit(solution)/shard_map/ppermute | solution.py:618
  52.6 4.1 collective-permute-start.18
  53.4 4.9 collective-permute-start.19
  53.4 24.2 %collective-permute-start.22 = (bf16[256,2048]{1,0:T(8,128)(2,1)S(1)}, bf16[256,2048]{1,0:T(8,128)(2,1)S(1)}, u32[]{:S(2)}, u32[]{:S(2)}) collective-permute-start(bf16[256,2048]{1,0:T(8,128)(2,1)S(1)} %collective-permute-done.15.refs_4_.refs_3_), channel_id=1, source_target_pairs={{0,8},{4,12},{8,0},{12,4},{16,24},{20,28},{24,16},{28,20},{1,9},{5... | collective-permute-start | bytes 3145736 | tf_op jit(solution)/shard_map/ppermute | solution.py:676
  55.5 24.7 %collective-permute-start.24 = (bf16[256,2048]{1,0:T(8,128)(2,1)S(1)}, bf16[256,2048]{1,0:T(8,128)(2,1)S(1)}, u32[]{:S(2)}, u32[]{:S(2)}) collective-permute-start(bf16[256,2048]{1,0:T(8,128)(2,1)S(1)} %by_rows.15), channel_id=1, source_target_pairs={{0,2},{1,3},{2,0},{3,1},{4,6},{5,7},{6,4},{7,5},{8,10},{9,11},{10,... | collective-permute-start | bytes 3145736 | tf_op jit(solution)/shard_map/ppermute | solution.py:618
  71.8 8.4 %collective-permute-start.21 = (bf16[256,2048]{1,0:T(8,128)(2,1)S(1)}, bf16[256,2048]{1,0:T(8,128)(2,1)S(1)}, u32[]{:S(2)}, u32[]{:S(2)}) collective-permute-start(bf16[256,2048]{1,0:T(8,128)(2,1)S(1)} %get-tuple-element.718), channel_id=1, source_target_pairs={{0,1},{1,0},{2,3},{3,2},{4,5},{5,4},{6,7},{7,6},{8,9},{9,8},{10,11... | collective-permute-start | bytes 3145736 | tf_op jit(solution)/shard_map/ppermute | solution.py:618
  77.6 3.6 collective-permute-start.23
  84.7 24.8 %collective-permute-start.26 = (bf16[256,2048]{1,0:T(8,128)(2,1)}, bf16[256,2048]{1,0:T(8,128)(2,1)S(1)}, u32[]{:S(2)}, u32[]{:S(2)}) collective-permute-start(bf16[256,2048]{1,0:T(8,128)(2,1)} %get-tuple-element.728.refs_0_), channel_id=1, source_target_pairs={{0,2},{1,3},{2,0},{3,1},{4,6},{5,7},{6,4},{7,5},{8,10},{9,11},{10,... | collective-permute-start | bytes 3145736 | tf_op jit(solution)/shard_map/ppermute | solution.py:618
  85.0 24.6 %collective-permute-start.27 = (bf16[256,2048]{1,0:T(8,128)(2,1)}, bf16[256,2048]{1,0:T(8,128)(2,1)S(1)}, u32[]{:S(2)}, u32[]{:S(2)}) collective-permute-start(bf16[256,2048]{1,0:T(8,128)(2,1)} %get-tuple-element.728.refs_0_), channel_id=1, source_target_pairs={{0,8},{4,12},{8,0},{12,4},{16,24},{20,28},{24,16},{28,20},{1,9},{5... | collective-permute-start | bytes 3145736 | tf_op jit(solution)/shard_map/ppermute | solution.py:676
  109.5 4.9 %collective-permute-start.28 = (bf16[256,2048]{1,0:T(8,128)(2,1)S(1)}, bf16[256,2048]{1,0:T(8,128)(2,1)S(1)}, u32[]{:S(2)}, u32[]{:S(2)}) collective-permute-start(bf16[256,2048]{1,0:T(8,128)(2,1)S(1)} %collective-permute-done.26.refs_0_), channel_id=1, source_target_pairs={{0,1},{1,0},{2,3},{3,2},{4,5},{5,4},{6,7},{7,6},{8,9},{9,8},{10,11... | collective-permute-start | bytes 3145736 | tf_op jit(solution)/shard_map/ppermute | solution.py:618
  110.8 3.9 collective-permute-start.29
  111.6 17.3 %collective-permute-start.30 = (bf16[128,2048]{1,0:T(8,128)(2,1)}, bf16[128,2048]{1,0:T(8,128)(2,1)}, u32[]{:S(2)}, u32[]{:S(2)}) collective-permute-start(bf16[128,2048]{1,0:T(8,128)(2,1)} %slice.80), channel_id=1, source_target_pairs={{0,2},{1,3},{2,0},{3,1},{4,6},{5,7},{6,4},{7,5},{8,10},{9,11},{10,... | collective-permute-start | bytes 1572872 | tf_op jit(solution)/shard_map/ppermute | solution.py:618
  112.9 16.0 %collective-permute-start.31 = (bf16[128,2048]{1,0:T(8,128)(2,1)S(1)}, bf16[128,2048]{1,0:T(8,128)(2,1)}, u32[]{:S(2)}, u32[]{:S(2)}) collective-permute-start(bf16[128,2048]{1,0:T(8,128)(2,1)S(1)} %slice.81), channel_id=1, source_target_pairs={{0,8},{4,12},{8,0},{12,4},{16,24},{20,28},{24,16},{28,20},{1,9},{5... | collective-permute-start | bytes 1572872 | tf_op jit(solution)/shard_map/ppermute | solution.py:676
  157.2 45.6 %collective-permute-start.34 = (bf16[1024,768]{1,0:T(8,128)(2,1)}, bf16[1024,768]{1,0:T(8,128)(2,1)}, u32[]{:S(2)}, u32[]{:S(2)}) collective-permute-start(bf16[1024,768]{1,0:T(8,128)(2,1)} %get-tuple-element.770), channel_id=1, source_target_pairs={{0,4},{4,0},{8,12},{12,8},{16,20},{20,16},{24,28},{28,24},{1,5},{5... | collective-permute-start | bytes 4718600 | tf_op jit(solution)/shard_map/ppermute | solution.py:676
  169.2 30.5 %collective-permute-start.35 = (bf16[256,2048]{1,0:T(8,128)(2,1)}, bf16[256,2048]{1,0:T(8,128)(2,1)S(1)}, u32[]{:S(2)}, u32[]{:S(2)}) collective-permute-start(bf16[256,2048]{1,0:T(8,128)(2,1)} %copy-done.60), channel_id=1, source_target_pairs={{0,8},{4,12},{8,0},{12,4},{16,24},{20,28},{24,16},{28,20},{1,9},{5... | collective-permute-start | bytes 3145736 | tf_op jit(solution)/shard_map/ppermute | solution.py:676
  188.7 5.4 %collective-permute-start.1 = (bf16[256,2048]{1,0:T(8,128)(2,1)S(1)}, bf16[256,2048]{1,0:T(8,128)(2,1)}, u32[]{:S(2)}, u32[]{:S(2)}) collective-permute-start(bf16[256,2048]{1,0:T(8,128)(2,1)S(1)} %get-tuple-element.235), channel_id=1, source_target_pairs={{0,1},{1,0},{2,3},{3,2},{4,5},{5,4},{6,7},{7,6},{8,9},{9,8},{10,11... | collective-permute-start | bytes 3145736 | tf_op jit(solution)/shard_map/cond/branch_1_fun/ppermute | solution.py:618
  202.7 47.0 %collective-permute-start.36 = (bf16[1024,768]{1,0:T(8,128)(2,1)}, bf16[1024,768]{1,0:T(8,128)(2,1)}, u32[]{:S(2)}, u32[]{:S(2)}) collective-permute-start(bf16[1024,768]{1,0:T(8,128)(2,1)} %get-tuple-element.801), channel_id=1, source_target_pairs={{0,4},{4,0},{8,12},{12,8},{16,20},{20,16},{24,28},{28,24},{1,5},{5... | collective-permute-start | bytes 4718600 | tf_op jit(solution)/shard_map/ppermute | solution.py:676
  203.0 40.2 %collective-permute-start.38 = (bf16[256,2048]{1,0:T(8,128)(2,1)}, bf16[256,2048]{1,0:T(8,128)(2,1)}, u32[]{:S(2)}, u32[]{:S(2)}) collective-permute-start(bf16[256,2048]{1,0:T(8,128)(2,1)} %by_rows.17), channel_id=1, source_target_pairs={{0,8},{4,12},{8,0},{12,4},{16,24},{20,28},{24,16},{28,20},{1,9},{5... | collective-permute-start | bytes 3145736 | tf_op jit(solution)/shard_map/ppermute | solution.py:676
  203.9 39.3 %collective-permute-start.37 = (bf16[256,2048]{1,0:T(8,128)(2,1)}, bf16[256,2048]{1,0:T(8,128)(2,1)}, u32[]{:S(2)}, u32[]{:S(2)}) collective-permute-start(bf16[256,2048]{1,0:T(8,128)(2,1)} %by_rows.18), channel_id=1, source_target_pairs={{0,2},{1,3},{2,0},{3,1},{4,6},{5,7},{6,4},{7,5},{8,10},{9,11},{10,... | collective-permute-start | bytes 3145736 | tf_op jit(solution)/shard_map/ppermute | solution.py:618
  207.1 43.9 %collective-permute-start.40 = (bf16[512,768]{1,0:T(8,128)(2,1)}, bf16[512,768]{1,0:T(8,128)(2,1)}, u32[]{:S(2)}, u32[]{:S(2)}) collective-permute-start(bf16[512,768]{1,0:T(8,128)(2,1)} %get-tuple-element.792), channel_id=1, source_target_pairs={{0,16},{4,20},{8,24},{12,28},{16,0},{20,4},{24,8},{28,12},{1,17},{... | collective-permute-start | bytes 2359304 | tf_op jit(solution)/shard_map/ppermute | solution.py:676
  216.6 3.9 collective-permute-start.3
  248.8 35.8 %collective-permute-start.43 = (bf16[256,2048]{1,0:T(8,128)(2,1)}, bf16[256,2048]{1,0:T(8,128)(2,1)}, u32[]{:S(2)}, u32[]{:S(2)}) collective-permute-start(bf16[256,2048]{1,0:T(8,128)(2,1)} %get-tuple-element.809), channel_id=1, source_target_pairs={{0,2},{1,3},{2,0},{3,1},{4,6},{5,7},{6,4},{7,5},{8,10},{9,11},{10,... | collective-permute-start | bytes 3145736 | tf_op jit(solution)/shard_map/ppermute | solution.py:618
  249.7 74.9 %collective-permute-start.39 = (bf16[1024,768]{1,0:T(8,128)(2,1)}, bf16[1024,768]{1,0:T(8,128)(2,1)S(1)}, u32[]{:S(2)}, u32[]{:S(2)}) collective-permute-start(bf16[1024,768]{1,0:T(8,128)(2,1)} %get-tuple-element.811), channel_id=1, source_target_pairs={{0,4},{4,0},{8,12},{12,8},{16,20},{20,16},{24,28},{28,24},{1,5},{5... | collective-permute-start | bytes 4718600 | tf_op jit(solution)/shard_map/ppermute | solution.py:676
  253.7 30.9 %collective-permute-start.42 = (bf16[256,768]{1,0:T(8,128)(2,1)}, bf16[256,768]{1,0:T(8,128)(2,1)}, u32[]{:S(2)}, u32[]{:S(2)}) collective-permute-start(bf16[256,768]{1,0:T(8,128)(2,1)} %get-tuple-element.817), channel_id=1, source_target_pairs={{0,8},{4,12},{8,0},{12,4},{16,24},{20,28},{24,16},{28,20},{1,9},{5... | collective-permute-start | bytes 1179656 | tf_op jit(solution)/shard_map/ppermute | solution.py:676
  258.6 64.1 %collective-permute-start.41 = (bf16[512,768]{1,0:T(8,128)(2,1)}, bf16[512,768]{1,0:T(8,128)(2,1)}, u32[]{:S(2)}, u32[]{:S(2)}) collective-permute-start(bf16[512,768]{1,0:T(8,128)(2,1)} %get-tuple-element.819), channel_id=1, source_target_pairs={{0,16},{4,20},{8,24},{12,28},{16,0},{20,4},{24,8},{28,12},{1,17},{... | collective-permute-start | bytes 2359304 | tf_op jit(solution)/shard_map/ppermute | solution.py:676
  260.6 4.7 collective-permute-start.4
  324.6 24.0 %collective-permute-start.45 = (bf16[256,768]{1,0:T(8,128)(2,1)}, bf16[256,768]{1,0:T(8,128)(2,1)}, u32[]{:S(2)}, u32[]{:S(2)}) collective-permute-start(bf16[256,768]{1,0:T(8,128)(2,1)} %get-tuple-element.850), channel_id=1, source_target_pairs={{0,8},{4,12},{8,0},{12,4},{16,24},{20,28},{24,16},{28,20},{1,9},{5... | collective-permute-start | bytes 1179656 | tf_op jit(solution)/shard_map/ppermute | solution.py:676
  326.3 43.3 %collective-permute-start.46 = (bf16[256,2048]{1,0:T(8,128)(2,1)}, bf16[256,2048]{1,0:T(8,128)(2,1)}, u32[]{:S(2)}, u32[]{:S(2)}) collective-permute-start(bf16[256,2048]{1,0:T(8,128)(2,1)} %get-tuple-element.843), channel_id=1, source_target_pairs={{0,2},{1,3},{2,0},{3,1},{4,6},{5,7},{6,4},{7,5},{8,10},{9,11},{10,... | collective-permute-start | bytes 3145736 | tf_op jit(solution)/shard_map/ppermute | solution.py:618
  328.6 47.5 %collective-permute-start.44 = (bf16[512,768]{1,0:T(8,128)(2,1)}, bf16[512,768]{1,0:T(8,128)(2,1)}, u32[]{:S(2)}, u32[]{:S(2)}) collective-permute-start(bf16[512,768]{1,0:T(8,128)(2,1)} %get-tuple-element.853), channel_id=1, source_target_pairs={{0,16},{4,20},{8,24},{12,28},{16,0},{20,4},{24,8},{28,12},{1,17},{... | collective-permute-start | bytes 2359304 | tf_op jit(solution)/shard_map/ppermute | solution.py:676
  337.6 55.9 %collective-permute-start.48 = (bf16[256,2048]{1,0:T(8,128)(2,1)}, bf16[256,2048]{1,0:T(8,128)(2,1)}, u32[]{:S(2)}, u32[]{:S(2)}) collective-permute-start(bf16[256,2048]{1,0:T(8,128)(2,1)} %get-tuple-element.1042), channel_id=1, source_target_pairs={{0,8},{4,12},{8,0},{12,4},{16,24},{20,28},{24,16},{28,20},{1,9},{5... | collective-permute-start | bytes 3145736 | tf_op jit(solution)/shard_map/ppermute | solution.py:676
  348.3 80.7 %collective-permute-start.53 = (bf16[1024,640]{1,0:T(8,128)(2,1)}, bf16[1024,640]{1,0:T(8,128)(2,1)S(1)}, u32[]{:S(2)}, u32[]{:S(2)}) collective-permute-start(bf16[1024,640]{1,0:T(8,128)(2,1)} %get-tuple-element.859), channel_id=1, source_target_pairs={{0,8},{4,12},{8,0},{12,4},{16,24},{20,28},{24,16},{28,20},{1,9},{5... | collective-permute-start | bytes 3932168 | tf_op jit(solution)/shard_map/ppermute | solution.py:676
  378.7 33.0 %collective-permute-start.47 = (bf16[256,768]{1,0:T(8,128)(2,1)}, bf16[256,768]{1,0:T(8,128)(2,1)}, u32[]{:S(2)}, u32[]{:S(2)}) collective-permute-start(bf16[256,768]{1,0:T(8,128)(2,1)} %get-tuple-element.879), channel_id=1, source_target_pairs={{0,8},{4,12},{8,0},{12,4},{16,24},{20,28},{24,16},{28,20},{1,9},{5... | collective-permute-start | bytes 1179656 | tf_op jit(solution)/shard_map/ppermute | solution.py:676
  384.4 3.5 collective-permute-start.9
  390.7 36.2 %collective-permute-start.51 = (bf16[1024,512]{1,0:T(8,128)(2,1)}, bf16[1024,512]{1,0:T(8,128)(2,1)S(1)}, u32[]{:S(2)}, u32[]{:S(2)}) collective-permute-start(bf16[1024,512]{1,0:T(8,128)(2,1)} %get-tuple-element.866), channel_id=1, source_target_pairs={{0,4},{4,0},{8,12},{12,8},{16,20},{20,16},{24,28},{28,24},{1,5},{5... | collective-permute-start | bytes 3145736 | tf_op jit(solution)/shard_map/ppermute | solution.py:676
  411.7 51.2 %collective-permute-start.50 = (bf16[256,2048]{1,0:T(8,128)(2,1)}, bf16[256,2048]{1,0:T(8,128)(2,1)}, u32[]{:S(2)}, u32[]{:S(2)}) collective-permute-start(bf16[256,2048]{1,0:T(8,128)(2,1)} %by_rows.22), channel_id=1, source_target_pairs={{0,8},{4,12},{8,0},{12,4},{16,24},{20,28},{24,16},{28,20},{1,9},{5... | collective-permute-start | bytes 3145736 | tf_op jit(solution)/shard_map/ppermute | solution.py:676
  412.9 50.0 %collective-permute-start.49 = (bf16[256,2048]{1,0:T(8,128)(2,1)}, bf16[256,2048]{1,0:T(8,128)(2,1)}, u32[]{:S(2)}, u32[]{:S(2)}) collective-permute-start(bf16[256,2048]{1,0:T(8,128)(2,1)} %by_rows.21), channel_id=1, source_target_pairs={{0,2},{1,3},{2,0},{3,1},{4,6},{5,7},{6,4},{7,5},{8,10},{9,11},{10,... | collective-permute-start | bytes 3145736 | tf_op jit(solution)/shard_map/ppermute | solution.py:618
  422.7 4.2 collective-permute-start.11
  430.0 36.8 %collective-permute-start.54 = (bf16[512,640]{1,0:T(8,128)(2,1)}, bf16[512,640]{1,0:T(8,128)(2,1)}, u32[]{:S(2)}, u32[]{:S(2)}) collective-permute-start(bf16[512,640]{1,0:T(8,128)(2,1)} %get-tuple-element.907), channel_id=1, source_target_pairs={{0,16},{4,20},{8,24},{12,28},{16,0},{20,4},{24,8},{28,12},{1,17},{... | collective-permute-start | bytes 1966088 | tf_op jit(solution)/shard_map/ppermute | solution.py:676
  430.6 30.6 %collective-permute-start.52 = (bf16[512,512]{1,0:T(8,128)(2,1)}, bf16[512,512]{1,0:T(8,128)(2,1)}, u32[]{:S(2)}, u32[]{:S(2)}) collective-permute-start(bf16[512,512]{1,0:T(8,128)(2,1)} %get-tuple-element.903), channel_id=1, source_target_pairs={{0,8},{4,12},{8,0},{12,4},{16,24},{20,28},{24,16},{28,20},{1,9},{5... | collective-permute-start | bytes 1572872 | tf_op jit(solution)/shard_map/ppermute | solution.py:676
  462.9 11.2 %collective-permute-start.56 = (bf16[256,512]{1,0:T(8,128)(2,1)}, bf16[256,512]{1,0:T(8,128)(2,1)S(1)}, u32[]{:S(2)}, u32[]{:S(2)}) collective-permute-start(bf16[256,512]{1,0:T(8,128)(2,1)} %get-tuple-element.912), channel_id=1, source_target_pairs={{0,16},{4,20},{8,24},{12,28},{16,0},{20,4},{24,8},{28,12},{1,17},{... | collective-permute-start | bytes 786440 | tf_op jit(solution)/shard_map/ppermute | solution.py:676
  468.2 6.7 %collective-permute-start.55 = (bf16[256,640]{1,0:T(8,128)(2,1)S(1)}, bf16[256,640]{1,0:T(8,128)(2,1)S(1)}, u32[]{:S(2)}, u32[]{:S(2)}) collective-permute-start(bf16[256,640]{1,0:T(8,128)(2,1)S(1)} %get-tuple-element.921), channel_id=1, source_target_pairs={{0,4},{4,0},{8,12},{12,8},{16,20},{20,16},{24,28},{28,24},{1,5},{5... | collective-permute-start | bytes 983048 | tf_op jit(solution)/shard_map/ppermute | solution.py:676
  477.9 6.0 %collective-permute-start.57 = (f32[2,2,64]{2,1,0:T(2,128)S(1)}, f32[2,2,64]{2,1,0:T(2,128)S(1)}, u32[]{:S(2)}, u32[]{:S(2)}) collective-permute-start(f32[2,2,64]{2,1,0:T(2,128)S(1)} %pad_maximum_fusion.5), channel_id=1, source_target_pairs={{0,2},{1,3},{2,0},{3,1},{4,6},{5,7},{6,4},{7,5},{8,10},{9,11},{10,... | collective-permute-start | bytes 3080 | tf_op jit(solution)/shard_map/ppermute | solution.py:1061
  484.0 5.1 %collective-permute-start.58 = (f32[2,64]{1,0:T(2,128)S(1)}, f32[2,64]{1,0:T(2,128)S(1)}, u32[]{:S(2)}, u32[]{:S(2)}) collective-permute-start(f32[2,64]{1,0:T(2,128)S(1)} %slice_bitcast_fusion), channel_id=1, source_target_pairs={{0,1},{1,0},{2,3},{3,2},{4,5},{5,4},{6,7},{7,6},{8,9},{9,8},{10,11... | collective-permute-start | bytes 1544 | tf_op jit(solution)/shard_map/ppermute | solution.py:1062
  (82 other events, 882.1 us)

commit v3 on v2

--- a/solution.py
+++ b/solution.py
@@ -18,6 +18,7 @@
 MASKED = -1e30
 VMEM_LIMIT = 48 * 2**20
 PARTS = 1
+OUTER_BLOCKS = 2
 PAIR = 2
 NT = (((1,), (1,)), ((), ()))
 TN = (((0,), (0,)), ((), ()))
@@ -247,7 +248,7 @@
                 return stats
 
             lse_ref[...] = lax.fori_loop(
-                0, heads // 2, one_pair, jnp.zeros((QB, heads), jnp.float32)
+                0, heads // 2, one_pair, jnp.zeros((QB, heads), jnp.float32), unroll=4
             )
 
     part = dot(o_ref[...], out_ref[...]).astype(jnp.bfloat16)
@@ -368,7 +369,7 @@
                 dq_ref[:, at] = turned.astype(jnp.bfloat16)
                 return 0
 
-            lax.fori_loop(0, heads // 2, one_pair, 0)
+            lax.fori_loop(0, heads // 2, one_pair, 0, unroll=2)
 
 
 def attend_backward(
@@ -450,22 +451,19 @@
     )(*normed, *cots, w_gate, w_up, w_down)
 
 
-def share_kernel(*refs, transposed):
-    count = (len(refs) - 1 - PARTS) // 2
-    kept_ref, *sent_refs = refs[2 * count :]
+def share_kernel(*refs, count, transposed):
+    outs = refs[2 * count :]
     multiply = contract_cols if transposed else dot
     part = multiply(refs[0][...], refs[count][...])
     for left, right in zip(refs[1:count], refs[count + 1 : 2 * count]):
         part = part + multiply(left[...], right[...])
-    rows = kept_ref.shape[0]
-    kept_ref[...] = part[:rows].astype(jnp.bfloat16)
-    for i, ref in enumerate(sent_refs):
-        at = rows + i * ref.shape[0]
-        ref[...] = part[at : at + ref.shape[0]].astype(jnp.bfloat16)
-
-
-def row_shares(lefts, rights, transposed, rows, block):
-    rows //= 2
+    rows = outs[0].shape[0]
+    for place, ref in enumerate(outs):
+        ref[...] = part[place * rows : (place + 1) * rows].astype(jnp.bfloat16)
+
+
+def row_shares(lefts, rights, transposed, rows):
+    blocks = lefts[0].shape[0] // rows
     width, tile = rights[0].shape[0 if transposed else 1], 512
 
     def right_spec(item):
@@ -473,42 +471,45 @@
             return pl.BlockSpec((tile, item.shape[1]), lambda j: (j, 0))
         return pl.BlockSpec((item.shape[0], tile), lambda j: (0, j))
 
-    sizes = [rows] + [rows // PARTS] * PARTS
     return pl.pallas_call(
-        functools.partial(share_kernel, transposed=transposed),
+        functools.partial(share_kernel, count=len(lefts), transposed=transposed),
         grid=(width // tile,),
-        in_specs=[
-            *(pl.BlockSpec((2 * rows, item.shape[1]), lambda j: (block, 0)) for item in lefts),
-            *(right_spec(item) for item in rights),
-        ],
-        out_specs=[pl.BlockSpec((size, tile), lambda j: (0, j)) for size in sizes],
-        out_shape=[jax.ShapeDtypeStruct((size, width), jnp.bfloat16) for size in sizes],
+        in_specs=[*(whole(item) for item in lefts), *(right_spec(item) for item in rights)],
+        out_specs=[pl.BlockSpec((rows, tile), lambda j: (0, j))] * blocks,
+        out_shape=[jax.ShapeDtypeStruct((rows, width), jnp.bfloat16)] * blocks,
         name="row_shares",
         **params(),
     )(*lefts, *rights)
 
 
-def outer_kernel(order_ref, *refs, shape):
-    refs, sent_ref, kept_ref = list(refs[:-2]), refs[-2], refs[-1]
+def outer_kernel(order_ref, *refs, shape, pieces):
+    outs, refs = refs[-2 * len(pieces) :], list(refs[: -2 * len(pieces)])
     totals = None
     for lefts, rights in shape:
-        rows = jnp.concatenate([refs.pop(0)[...] for _ in range(lefts)], axis=0)
+        rows = jnp.concatenate(
+            [
+                jnp.concatenate([refs.pop(0)[...] for _ in range(OUTER_BLOCKS)], axis=1)
+                for _ in range(lefts)
+            ],
+            axis=0,
+        )
         parts = [contract_rows(rows, refs.pop(0)[...]) for _ in range(rights)]
         totals = parts if totals is None else [a + b for a, b in zip(totals, parts)]
-    total = jnp.concatenate(totals, axis=1).astype(jnp.bfloat16)
     step = pl.program_id(0)
     half = pl.num_programs(0) // 2
-
-    @pl.when(step < half)
-    def _():
-        sent_ref[...] = total
-
-    @pl.when(step >= half)
-    def _():
-        kept_ref[...] = total
-
-
-def outer(sections, index, bits):
+    for place, piece in enumerate(pieces):
+        total = jnp.concatenate(totals[piece], axis=1).astype(jnp.bfloat16)
+
+        @pl.when(step < half)
+        def _():
+            outs[2 * place][...] = total
+
+        @pl.when(step >= half)
+        def _():
+            outs[2 * place + 1][...] = total
+
+
+def outer(sections, index, bits, pieces):
     width = sections[0][0][0].shape[1]
     share = width // (1 << len(bits))
     tile = 256
@@ -520,27 +521,42 @@
             ([permuted_features(item, index, bits) for item in lefts], rights)
             for lefts, rights in sections
         ]
-    count = width // tile
-    size = sum(item.shape[1] for item in sections[0][1])
+    count = width // tile // OUTER_BLOCKS
+    sizes = [sum(item.shape[1] for item in sections[0][1][piece]) for piece in pieces]
     specs, arrays = [], []
     for lefts, rights in sections:
-        specs.extend(pl.BlockSpec((item.shape[0], tile), lambda j, b: (0, b[j])) for item in lefts)
+        for item in lefts:
+            for i in range(OUTER_BLOCKS):
+                specs.append(
+                    pl.BlockSpec(
+                        (item.shape[0], tile), lambda j, b, i=i: (0, b[j * OUTER_BLOCKS + i])
+                    )
+                )
+                arrays.append(item)
         specs.extend(whole(item) for item in rights)
-        arrays.extend((*lefts, *rights))
+        arrays.extend(rights)
     return pl.pallas_call(
         functools.partial(
-            outer_kernel, shape=[(len(lefts), len(rights)) for lefts, rights in sections]
+            outer_kernel,
+            shape=[(len(lefts), len(rights)) for lefts, rights in sections],
+            pieces=pieces,
         ),
         grid_spec=pltpu.PrefetchScalarGridSpec(
             num_scalar_prefetch=1,
             grid=(count,),
             in_specs=specs,
             out_specs=[
-                pl.BlockSpec((tile, size), lambda j, _: (jnp.minimum(j, count // 2 - 1), 0)),
-                pl.BlockSpec((tile, size), lambda j, _: (jnp.maximum(j - count // 2, 0), 0)),
+                pl.BlockSpec((tile * OUTER_BLOCKS, size), at)
+                for size in sizes
+                for at in (
+                    lambda j, _: (jnp.minimum(j, count // 2 - 1), 0),
+                    lambda j, _: (jnp.maximum(j - count // 2, 0), 0),
+                )
             ],
         ),
-        out_shape=[jax.ShapeDtypeStruct((width // 2, size), jnp.bfloat16)] * 2,
+        out_shape=[
+            jax.ShapeDtypeStruct((width // 2, size), jnp.bfloat16) for size in sizes for _ in range(2)
+        ],
         name="outer",
         **params(),
     )(blocks, *arrays)
@@ -581,24 +597,25 @@
 
 
 def key_value_kernel(
-    at_ref, dkn_ref, dkf_ref, dvn_ref, dvf_ref, cos_ref, sin_ref, near_ref, far_ref
+    at_ref, dkn_ref, dkf_ref, dvn_ref, dvf_ref, cosn_ref, sinn_ref, cosf_ref, sinf_ref, near_ref, far_ref
 ):
     rows = dkn_ref.shape[0] // 4
     for m in range(4):
         at = pl.ds(pl.multiple_of(at_ref[m], rows), rows)
-        mine = slice(m * rows, (m + 1) * rows)
+        mine = slice(m % 2 * rows, (m % 2 + 1) * rows)
+        cos_ref, sin_ref = (cosn_ref, sinn_ref) if m < 2 else (cosf_ref, sinf_ref)
         d_key = dkn_ref[at, :] + dkf_ref[at, :]
         d_val = dvn_ref[at, :] + dvf_ref[at, :]
         both = jnp.concatenate([d_key, d_val], axis=1)
         turned = both * cos_ref[mine, :] - swap_halves(both) * sin_ref[mine, :]
         both = jnp.concatenate([turned[:, :HD], d_val], axis=1).astype(jnp.bfloat16)
         target = near_ref if m < 2 else far_ref
-        target[m % 2 * rows : (m % 2 + 1) * rows, :] = both
-
-
-def key_value_rows(dk_n, dk_f, dv_n, dv_f, cos_tab, sin_tab, block_pos):
+        target[mine, :] = both
+
+
+def key_value_rows(dk_n, dk_f, dv_n, dv_f, tables, block_pos):
     shape = jax.ShapeDtypeStruct((dk_n.shape[0] // 2, 2 * HD), jnp.bfloat16)
-    arrays = (dk_n, dk_f, dv_n, dv_f, cos_tab, sin_tab)
+    arrays = (dk_n, dk_f, dv_n, dv_f, *tables)
     return pl.pallas_call(
         key_value_kernel,
         grid_spec=pltpu.PrefetchScalarGridSpec(
@@ -742,7 +759,9 @@
     block_pos = jnp.stack([(place ^ m) * rows for m in range(4)]).astype(jnp.int32)
     near_pos, far_pos = block_pos[:2], block_pos[2:]
     row_pos = (block_pos[:, None] + jnp.arange(rows, dtype=jnp.int32)[None, :]).reshape(-1)
-    cos_tab, sin_tab = rope_tables(row_pos)
+    (cos_n, sin_n), (cos_f, sin_f) = (
+        rope_tables(half) for half in (row_pos[: 2 * rows], row_pos[2 * rows :])
+    )
     w_kv = jnp.concatenate([w_key, w_value], axis=1)
 
     def in_sequence(value):
@@ -773,11 +792,11 @@
     up_half = jnp.where(mine[None, :], up_half, 0).astype(jnp.bfloat16)
     down_half = lax.dynamic_slice_in_dim(w_down, side * (units - window), window, 0)
     down_half = jnp.where(mine[:, None], down_half, 0).astype(jnp.bfloat16)
-    gate_half, up_half, down_half, w_kv, cos_tab, sin_tab = order.done(
-        gate_half, up_half, down_half, w_kv, cos_tab, sin_tab
+    gate_half, up_half, down_half, w_kv, cos_n, sin_n, cos_f, sin_f = order.done(
+        gate_half, up_half, down_half, w_kv, cos_n, sin_n, cos_f, sin_f
     )
     normed_n, q_n, k_n, v_n = order.done(
-        *project((*x_own, *x_core), norm_attn, w_query, w_kv, cos_tab[near], sin_tab[near])
+        *project((*x_own, *x_core), norm_attn, w_query, w_kv, cos_n, sin_n)
     )
     x_chip = order.after(x_chip)
     cot_own_ = wait_for(cot_own, x_chip)
@@ -785,7 +804,7 @@
         swap_chip(cot_own_), swap_core(cot_own_), swap_pair(cot_own_, dp_size)
     )
     normed_f, q_f, k_f, v_f = order.done(
-        *project((*x_chip, *swap_core(x_chip)), norm_attn, w_query, w_kv, cos_tab[far], sin_tab[far])
+        *project((*x_chip, *swap_core(x_chip)), norm_attn, w_query, w_kv, cos_f, sin_f)
     )
     k_low = in_sequence(rows_of(k_n, k_f))
     v_low = in_sequence(rows_of(v_n, v_f))
@@ -865,9 +884,9 @@
         leaves, tree = jax.tree.flatten(results)
         return jax.tree.unflatten(tree, order.done(tuple(leaves)))
 
-    def gradient(sections, order_bits):
+    def gradient(sections, order_bits, pieces=(slice(None),)):
         lefts, rights = order.after([item[0] for item in sections], [item[1] for item in sections])
-        return order.done(*outer(list(zip(lefts, rights)), index, order_bits))
+        return order.done(*outer(list(zip(lefts, rights)), index, order_bits, pieces))
 
     cots = (
         (*cot_own, *cot_core),
@@ -880,18 +899,16 @@
         (*mlp_diag, *mlp_dcore),
     )
 
-    def mlp_gradient(lefts, which):
-        sections = [(left, (right[which],)) for left, right in zip(lefts, hiddens)]
-        return gradient(sections, pair_bits)
+    def mlp_gradients(lefts, which):
+        sections = [(left, [right[i] for i in which]) for left, right in zip(lefts, hiddens)]
+        return gradient(sections, pair_bits, [slice(i, i + 1) for i in range(len(which))])
 
     def reduction(sent_kept, order_bits, assemble=None):
         return Reduction(order, *sent_kept, order_bits, dp_size, assemble)
 
-    def shares(lefts, rights, transposed=True, block=0):
-        kept, *sent = order.done(
-            *row_shares(order.after(lefts), rights, transposed, 2 * rows, block)
-        )
-        return kept, swap_core(sent)
+    def shares(lefts, rights, transposed=True):
+        parts = order.done(*row_shares(order.after(lefts), rights, transposed, rows))
+        return [(parts[i], swap_core((parts[i + 1],))) for i in range(0, len(parts), 2)]
 
     def total(*items):
         return order.done(*by_rows(lambda *values: (sum(values),), items, (), ((jnp.bfloat16,),)))
@@ -901,36 +918,65 @@
             self.rest = rights, transposed
             self.near, self.sides, self.diag = (tuple(item[i] for i in which) for item in hiddens)
 
-        def diag_sum(self):
-            return chip_sum(*shares(self.diag, *self.rest))
+        def diag_shares(self):
+            return shares(self.diag, *self.rest)[0]
 
         def side_shares(self):
-            chip, chip_came = shares(self.sides, *self.rest, 0)
-            pair, pair_came = shares(self.sides, *self.rest, 1)
-            return (chip, *order.after(chip_came)), (pair, *order.after(pair_came))
-
-        def own(self):
-            kept, core = shares(self.near, *self.rest)
-            return kept, order.after(core)
+            return shares(self.sides, *self.rest)
+
+        def own_shares(self):
+            return shares(self.near, *self.rest)[0]
 
     d_norm = GroupSum((1, 2), (gate_half, up_half), True)
     block_sum = GroupSum((0,), (down_half,), False)
 
-    down = reduction(mlp_gradient(cots, 0), pair_bits, in_window)
+    down = reduction(mlp_gradients(cots, (0,)), pair_bits, in_window)
     down.send()
-    to_pair = swap_pair(fence(d_norm.diag_sum), dp_size)
-    gate, (chip_shares, pair_shares) = fence(
-        lambda: (mlp_gradient(mlps, 1), d_norm.side_shares())
-    )
-    gate = reduction(gate, pair_bits, in_window)
-    came_p = swap_pair(total(*pair_shares), dp_size)
-    came_c = swap_chip(total(*chip_shares, order.after(to_pair)))
+
+    @fence
+    def diag_and_gradients():
+        kept, came = d_norm.diag_shares()
+        made = mlp_gradients(mlps, (1, 2))
+        return chip_sum(kept, came), made
+
+    diag, made = diag_and_gradients
+    to_pair = swap_pair(diag, dp_size)
+    gate, up = (reduction(item, pair_bits, in_window) for item in (made[:2], made[2:]))
+
+    @fence
+    def other_shares():
+        chip, pair = d_norm.side_shares()
+        own = d_norm.own_shares()
+        return order.after(chip), order.after(pair), order.after(own)
+
+    chip, pair, own = other_shares
+    came_p = swap_pair(total(pair[0], *pair[1]), dp_size)
+    to_pair = order.after(to_pair)
+    came_c = swap_chip(total(chip[0], *chip[1], to_pair))
     down.receive()
     gate.send(down.came)
-    down.add().send()
-    (kept, core), up = fence(lambda: (d_norm.own(), mlp_gradient(mlps, 2)))
-    up = reduction(up, pair_bits, in_window)
+    down.add()
+    down.send()
+
+    @fence
+    def block_shares():
+        def parts(lefts):
+            return order.done(*row_shares(order.after(lefts), *block_sum.rest, rows))
+
+        kept, sent = parts(block_sum.diag)
+        came = swap_core((sent,))
+        kept_c, sent_c, kept_p, sent_p = parts(block_sum.sides)
+        diag = chip_sum(kept, came)
+        came_c = swap_core((order.after(sent_c),))
+        kept, sent = parts(block_sum.near)
+        came_c = order.after(came_c)
+        came_p = order.after(swap_core((order.after(sent_p),)))
+        came = order.after(swap_core((order.after(sent),)))
+        return diag, (kept_c, came_c), (kept_p, came_p), (kept, came)
+
+    block_diag, block_chip, block_pair, block_own = block_shares
     came_c, came_p = order.after(came_c, came_p)
+    to_pair = swap_pair(block_diag, dp_size)
 
     def back_mid(kept, core, chip, pair, resid, cot, gain):
         d_mid = cot + norm_back(kept + core + chip + pair, resid, rms_inverse(resid), gain)
@@ -939,102 +985,109 @@
     d_mid, d_own = order.done(
         *by_rows(
             back_mid,
-            (kept, core, came_c, came_p, resid_mid, cot_own),
+            (own[0], own[1], came_c, came_p, resid_mid, cot_own),
             (norm_mlp,),
             (jnp.float32, (jnp.bfloat16,)),
         )
     )
     d_chip = swap_chip(d_own)
+
     gate.receive()
     up.send(gate.came)
-    down.receive().add()
-    down.send()
-    gate.add().send()
+    gate.add()
 
     @fence
     def near_back():
         d_core = order.after(swap_core(d_own))
         return d_core, order.done(
             *attend_backward(
-                q_n, (*d_own, *d_core), w_out, attn_n, lse_n, k_low, v_low, cos_tab[near],
-                sin_tab[near], begins, near_pos,
+                q_n, (*d_own, *d_core), w_out, attn_n, lse_n, k_low, v_low, cos_n,
+                sin_n, begins, near_pos,
             )
         )
 
     d_core, (dq_n, dk_n, dv_n) = near_back
     d_chip = order.after(d_chip)
-    down.receive().add()
+    @fence
+    def out_gradient():
+        d_other = order.after(swap_core(d_chip))
+        sections = [((*d_own, *d_core), (attn_n,)), ((*d_chip, *d_other), (attn_f,))]
+        return d_other, gradient(sections, bits)
+
+    d_other, wout = out_gradient
+    wout = reduction(wout, bits)
+    down.receive()
+    gate.send(down.came)
+    down.add().send()
+    up.receive()
+    wout.send(up.came)
+    up.add()
+    to_pair = order.after(to_pair)
+    block_c = total(block_chip[0], *block_chip[1], to_pair)
+    block_p = total(block_pair[0], *block_pair[1])
 
     @fence
     def far_back():
-        d_other = order.after(swap_core(d_chip))
-        dq_f, dk_f, dv_f = order.done(
+        return order.done(
             *attend_backward(
-                q_f, (*d_chip, *d_other), w_out, attn_f, lse_f, k_low, v_low, cos_tab[far],
-                sin_tab[far], begins, far_pos,
+                q_f, (*d_chip, *d_other), w_out, attn_f, lse_f, k_low, v_low, cos_f,
+                sin_f, begins, far_pos,
             )
         )
+
+    dq_f, dk_f, dv_f = far_back
+
+    @fence
+    def query_gradient():
         dkv_n, dkv_f = order.done(
-            *key_value_rows(dk_n, dk_f, dv_n, dv_f, cos_tab, sin_tab, block_pos)
+            *key_value_rows(dk_n, dk_f, dv_n, dv_f, (cos_n, sin_n, cos_f, sin_f), block_pos)
         )
-        in_sum = chip_sum(*shares((dq_f, dkv_f), (w_query, w_kv)))
-        return d_other, dq_f, dkv_n, dkv_f, in_sum
-
-    d_other, dq_f, dkv_n, dkv_f, in_sum = far_back
+        sections = [((normed_n,), (dq_n, dkv_n)), ((normed_f,), (dq_f, dkv_f))]
+        return dkv_n, dkv_f, gradient(sections, bits)
+
+    dkv_n, dkv_f, qkv = query_gradient
+    qkv = reduction(qkv, bits)
+    qkv.send()
+    wout.receive()
+    wout.add().send()
+    down.receive().add()
+    gate.receive()
+    up.send(gate.came)
+    gate.add().send()
+    in_sum = fence(lambda: chip_sum(*shares((dq_f, dkv_f), (w_query, w_kv))[0]))
+    gate.receive().add()
     d_in_came = swap_chip(in_sum)
-    gate.receive()
+    own = fence(lambda: order.after(shares((dq_n, dkv_n), (w_query, w_kv))[0]))
+    qkv.receive()
+    qkv.add().send()
+    wout.receive()
     up.receive()
-    gate.add().send()
     up.add().send()
-    to_pair = swap_pair(fence(block_sum.diag_sum), dp_size)
-    qkv = fence(
-        lambda: gradient([((normed_n,), (dq_n, dkv_n)), ((normed_f,), (dq_f, dkv_f))], late_bits)
-    )
-    gate.receive().add()
-    qkv = reduction(qkv, late_bits)
-    qkv.send()
-    wout = fence(
-        lambda: gradient([((*d_own, *d_core), (attn_n,)), ((*d_chip, *d_other), (attn_f,))], bits)
-    )
-    wout = reduction(wout, bits)
-    wout.send()
-
-    @fence
-    def near_shares():
-        kept, core = shares((dq_n, dkv_n), (w_query, w_kv))
-        return kept, order.after(core)
-
-    kept_in, core_in = near_shares
+    wout.add().send()
     d_in_came = order.after(d_in_came)
 
     def back_in(kept, core, chip, resid, d_mid, gain):
         return (d_mid + norm_back(kept + core + chip, resid, rms_inverse(resid), gain),)
 
     (x_grad,) = by_rows(
-        back_in, (kept_in, core_in, d_in_came, x_own, d_mid), (norm_attn,), (jnp.float32,)
+        back_in, (own[0], own[1], d_in_came, x_own, d_mid), (norm_attn,), (jnp.float32,)
     )
     x_grad = order.done(x_grad)
-    up.receive()
-    up.add().send()
-    chip_shares, pair_shares = fence(block_sum.side_shares)
-    to_pair = order.after(to_pair)
-    up.receive()
-    block_p = swap_pair(total(*pair_shares), dp_size)
-    block_c = swap_chip(total(*chip_shares, to_pair))
-    up.add()
-    kept, core = fence(block_sum.own)
-    wout.advance()
-    qkv.advance()
-    wout.advance()
+    qkv.receive()
+    block_p = swap_pair(wait_for(block_p, qkv.came), dp_size)
+    block_c = swap_chip(wait_for(block_c, qkv.came))
+    qkv.add().send()
+    up.receive().add()
+    wout.receive().add()
     block_c, block_p = order.after(block_c, block_p)
+    qkv.receive().add()
     (block_out,) = by_rows(
         lambda *items: (sum(items),),
-        (resid_mid, kept, core, block_c, block_p),
+        (resid_mid, block_own[0], block_own[1], block_c, block_p),
         (),
         (jnp.bfloat16,),
     )
     block_out = order.done(block_out)
-    qkv.advance()
     for item in (down, gate, up, wout, qkv):
         item.finish()
     grad_down, grad_gate, grad_up = down.total.T, gate.total, up.total

time: 497 us -> 472 us (0.950)
  Pallas kernels: 273 us -> 252 us
  starting transfers between devices: 53.9 us -> 46 us
    ppermute x34, waiting for transfers between devices: 43.4 us -> 60.2 us  [swapped(): return tuple((lax.ppermute(part, 'tensor', pairs) for part in parts))]
    ppermute x23, waiting for transfers between devices: 64.2 us -> 51.1 us  [exchange(): return lax.ppermute(value, 'dp', [(i, i ^ bit) for i in range(size)])]
    pallas_call x5 -> x4, Pallas kernels: 58.8 us -> 49.1 us  [outer(): pl.pallas_call(functools.partial(outer_kernel, shape=[(len(lefts), len(ri...]
    unnamed x127 -> x146, local copies, waits for them, and re-layouts: 19.5 us -> 25.2 us
    pallas_call x10 -> x8, Pallas kernels: 48.2 us -> 45.3 us  [row_shares(): pl.pallas_call(functools.partial(share_kernel, count=len(lefts), transpos...]
  transfers between devices with their start and end apart: 59 -> 59, of which waited for: 28 -> 28; matrix products, arithmetic and copies ran while one was open for 8% -> 7% of each run, Pallas kernels for 51% -> 49%
where the time goes in v3:
time: 472 us; the launch traced here: 465 us
  Pallas kernels  252 us (53%)
  waiting for transfers between devices  111 us (24%)
  starting transfers between devices  46 us (10%)
  local copies, waits for them, and re-layouts  28.4 us (6%)
  other arithmetic  25 us (5%)
    ppermute x34, waiting for transfers between devices, swapped(): return tuple((lax.ppermute(part, 'tensor', pairs) for part in parts))  60.2 us
    ppermute x23, waiting for transfers between devices, exchange(): return lax.ppermute(value, 'dp', [(i, i ^ bit) for i in range(size)])  51.1 us
    pallas_call x4, Pallas kernels, outer(): pl.pallas_call(functools.partial(outer_kernel, shape=[(len(lefts), len(ri...  49.1 us
    pallas_call x8, Pallas kernels, row_shares(): pl.pallas_call(functools.partial(share_kernel, count=len(lefts), transpos...  45.3 us
    pallas_call x2, Pallas kernels, attend_backward(): pl.pallas_call(functools.partial(backward_kernel, heads=heads, pics=pics,...  37.5 us
    pallas_call x3, Pallas kernels, feed_forward(): pl.pallas_call(functools.partial(feed_kernel, counts=(len(normed), len(co...  34 us
    pallas_call x12, Pallas kernels, by_rows(): pl.pallas_call(kernel, out_shape=shapes, name='by_rows', **params())  31.5 us
    ppermute x34, starting transfers between devices, swapped(): return tuple((lax.ppermute(part, 'tensor', pairs) for part in parts))  26.1 us
  transfers between devices with their start and end apart: 59, of which 28 were waited for; matrix products, arithmetic and copies ran while one was open for 7% of the time, Pallas kernels for 49%

profile of v3, /device:TPU:9, one launch (start us, length us, event | category | flops | bytes accessed | tf_op | source)
XLA Modules:
  0.0 464.7 jit_solution(13010941353996796413)
XLA Ops:
  11.8 6.3 %dynamic-slice_select_fusion.1 = (bf16[2048,768]{1,0:T(8,128)(2,1)}, bf16[2048,768]{1,0:T(8,128)(2,1)}) fusion(bf16[2048,1408]{1,0:T(8,128)(2,1)} %param.41, s32[]{:T(128)S(6)} %select_n.91, pred[768]{0:T(1024)(128)(4,1)S(1)} %fusion.2, bf16[2048,1408]{1,0:T(8,128)(2,1)} %param.40), kind=kLoop, calls=%fused_computation.1 | loop fusion | flops 1572864 | bytes 12583684 | tf_op jit(solution)/shard_map/jit(_where)/select_n | solution.py:792
  18.2 3.8 project.2
  22.0 3.1 collective-permute-done.12.refs_0_
  29.2 6.2 %project.3 = (bf16[512,2048]{1,0:T(8,128)(2,1)}, bf16[512,512]{1,0:T(8,128)(2,1)S(1)}, bf16[512,64]{1,0:T(8,128)(2,1)S(1)}, bf16[512,64]{1,0:T(8,128)(2,1)S(1)}) custom-call(bf16[256,2048]{1,0:T(8,128)(2,1)} %collective-permute-done.12.refs_0_, bf16[256,2048]{1,0:T(8,128)(2,1)} %collective-permute-done.17.refs_1_, f32[1,2048]{1,0:T(1,128)S(1)} %bitcast.69, ...), custom_call_target="tpu_custom_call" | custom-call | flops 1 | bytes 1 | tf_op jit(solution)/shard_map/project/pallas_call | solution.py:117
  37.4 12.2 %attend_forward.2 = (bf16[512,512]{1,0:T(8,128)(2,1)}, f32[512,8]{1,0:T(8,128)}, bf16[256,2048]{1,0:T(8,128)(2,1)S(1)}, bf16[256,2048]{1,0:T(8,128)(2,1)S(1)}) custom-call(s32[2]{0:T(128)S(1)} %get-tuple-element.956.pos_ref, s32[2]{0:T(128)S(1)} %bitcast.74, bf16[512,512]{1,0:T(8,128)(2,1)S(1)} %get-tuple-element.663.q_ref, ...), custom_call_target="tpu_custom_call" | custom-call | flops 1 | bytes 1 | tf_op jit(solution)/shard_map/attend_forward/pallas_call | solution.py:272
  57.2 11.3 %attend_forward.3 = (bf16[512,512]{1,0:T(8,128)(2,1)}, f32[512,8]{1,0:T(8,128)}, bf16[256,2048]{1,0:T(8,128)(2,1)S(1)}, bf16[256,2048]{1,0:T(8,128)(2,1)S(1)}) custom-call(s32[2]{0:T(128)S(1)} %get-tuple-element.955.pos_ref, s32[2]{0:T(128)S(1)} %bitcast.75, bf16[512,512]{1,0:T(8,128)(2,1)S(1)} %copy-done.74, bf16[1024,64]{1,0:T(8,128)(2,1)S(1)} %pad_maximum_fusion.5.k_ref, ...), custom_call_target="tpu_custom_call" | custom-call | flops 1 | bytes 1 | tf_op jit(solution)/shard_map/attend_forward/pallas_call | solution.py:272
  69.0 8.6 %collective-permute-done.22.refs_4_.refs_14_.refs_15_ = bf16[256,2048]{1,0:T(8,128)(2,1)S(1)} collective-permute-done((bf16[256,2048]{1,0:T(8,128)(2,1)S(1)}, bf16[256,2048]{1,0:T(8,128)(2,1)S(1)}, u32[]{:S(2)}, u32[]{:S(2)}) %collective-permute-start.22) | collective-permute-done | bytes 1048608 | tf_op jit(solution)/shard_map/ppermute | solution.py:693
  86.9 10.2 %feed_forward.3 = (bf16[512,768]{1,0:T(8,128)(2,1)}, bf16[512,768]{1,0:T(8,128)(2,1)}, bf16[512,768]{1,0:T(8,128)(2,1)}) custom-call(bf16[256,2048]{1,0:T(8,128)(2,1)S(1)} %get-tuple-element.698.refs_0_, bf16[256,2048]{1,0:T(8,128)(2,1)} %collective-permute-done.25.refs_1_, bf16[256,2048]{1,0:T(8,128)(2,1)S(1)} %copy-done, ...), custom_call_target="tpu_custom_call" | custom-call | flops 1 | bytes 1 | tf_op jit(solution)/shard_map/feed_forward/pallas_call | solution.py:437
  97.0 12.0 %collective-permute-done.26.refs_0_ = bf16[256,2048]{1,0:T(8,128)(2,1)S(1)} collective-permute-done((bf16[256,2048]{1,0:T(8,128)(2,1)S(1)}, bf16[256,2048]{1,0:T(8,128)(2,1)S(1)}, u32[]{:S(2)}, u32[]{:S(2)}) %collective-permute-start.26) | collective-permute-done | bytes 1048608 | tf_op jit(solution)/shard_map/ppermute | solution.py:635
  114.1 13.9 %feed_forward.4 = (bf16[1024,768]{1,0:T(8,128)(2,1)}, bf16[1024,768]{1,0:T(8,128)(2,1)}, bf16[1024,768]{1,0:T(8,128)(2,1)}) custom-call(bf16[256,2048]{1,0:T(8,128)(2,1)S(1)} %collective-permute-done.26.refs_0_, bf16[256,2048]{1,0:T(8,128)(2,1)S(1)} %collective-permute-done.28.refs_1_, bf16[256,2048]{1,0:T(8,128)(2,1)S(1)} %collective-permute-done.27.refs_2_, ...), custom_call_target="tpu_custom_call" | custom-call | flops 1 | bytes 1 | tf_op jit(solution)/shard_map/feed_forward/pallas_call | solution.py:437
  133.6 9.9 %feed_forward.5 = (bf16[512,768]{1,0:T(8,128)(2,1)S(1)}, bf16[512,768]{1,0:T(8,128)(2,1)}, bf16[512,768]{1,0:T(8,128)(2,1)}) custom-call(bf16[128,2048]{1,0:T(8,128)(2,1)} %collective-permute-done.30.refs_0_, bf16[128,2048]{1,0:T(8,128)(2,1)} %collective-permute-done.31.refs_1_, bf16[128,2048]{1,0:T(8,128)(2,1)} %collective-permute-done.32.refs_2_, ...), custom_call_target="tpu_custom_call" | custom-call | flops 1 | bytes 1 | tf_op jit(solution)/shard_map/feed_forward/pallas_call | solution.py:437
  143.6 12.0 %outer.7 = (bf16[1024,768]{1,0:T(8,128)(2,1)}, bf16[1024,768]{1,0:T(8,128)(2,1)}) custom-call(s32[8]{0:T(128)S(1)} %stack.168.order_ref, bf16[256,2048]{1,0:T(8,128)(2,1)S(1)} %copy-done, bf16[256,2048]{1,0:T(8,128)(2,1)S(1)} %copy-done, bf16[256,2048]{1,0:T(8,128)(2,1)S(1)} %copy-done.8, bf16[256,2048]{1,0:T(8,128)(2,1)S(1)} %copy-done.8, ...), custom_call_target="tpu_custom_call" | custom-call | flops 1 | bytes 1 | tf_op jit(solution)/shard_map/outer/pallas_call | solution.py:538
  156.9 33.3 %conditional.9 = (bf16[256,2048]{1,0:T(8,128)(2,1)}, bf16[1024,768]{1,0:T(8,128)(2,1)}, bf16[1024,768]{1,0:T(8,128)(2,1)}, bf16[1024,768]{1,0:T(8,128)(2,1)}, bf16[1024,768]{1,0:T(8,128)(2,1)}) conditional(s32[]{:T(128)} %convert_element_type.87, () %tuple.235, (bf16[512,768]{1,0:T(8,128)(2,1)}, bf16[512,768]{1,0:T(8,128)(2,1)}, ...), branch_computations={%region_0.1_spmd, %region_1.2_spmd} | conditional | flops 10 | bytes 12583199 | solution.py:879
  156.9 7.2 %row_shares.8 = (bf16[256,2048]{1,0:T(8,128)(2,1)S(1)}, bf16[256,2048]{1,0:T(8,128)(2,1)}) custom-call(bf16[512,768]{1,0:T(8,128)(2,1)} %get-tuple-element.202.refs_0_.refs_24_, bf16[512,768]{1,0:T(8,128)(2,1)} %get-tuple-element.203.refs_1_.refs_25_, bf16[2048,768]{1,0:T(8,128)(2,1)} %get-tuple-element.167.refs_2_, bf16[2048,768]{1,0:T(8,128)(2,1)} %get-tuple-element.168.refs_3_), custom_call_target="tpu_custom_call" | custom-call | flops 1 | bytes 1 | tf_op jit(solution)/shard_map/cond/branch_1_fun/row_shares/pallas_call | solution.py:474
  165.9 21.7 %outer.4 = (bf16[1024,768]{1,0:T(8,128)(2,1)}, bf16[1024,768]{1,0:T(8,128)(2,1)}, bf16[1024,768]{1,0:T(8,128)(2,1)}, bf16[1024,768]{1,0:T(8,128)(2,1)}) custom-call(s32[8]{0:T(128)S(1)} %stack.109.order_ref, bf16[256,2048]{1,0:T(8,128)(2,1)} %get-tuple-element.188.refs_0_.refs_1_, bf16[256,2048]{1,0:T(8,128)(2,1)} %get-tuple-element.188.refs_0_.refs_1_, ...), custom_call_target="tpu_custom_call" | custom-call | flops 1 | bytes 1 | tf_op jit(solution)/shard_map/cond/branch_1_fun/outer/pallas_call | solution.py:538
  191.3 18.3 %conditional.10 = (bf16[256,2048]{1,0:T(8,128)(2,1)S(1)}, bf16[256,2048]{1,0:T(8,128)(2,1)}, bf16[256,2048]{1,0:T(8,128)(2,1)S(1)}, bf16[256,2048]{1,0:T(8,128)(...) conditional(s32[]{:T(128)} %convert_element_type.88, () %tuple.239, (bf16[1024,768]{1,0:T(8,128)(2,1)}, ...), branch_computations={%region_2.3_spmd, %region_3.4_spmd} | conditional | flops 2 | bytes 44040472 | solution.py:879
  191.3 10.2 %row_shares.9 = (bf16[256,2048]{1,0:T(8,128)(2,1)S(1)}, bf16[256,2048]{1,0:T(8,128)(2,1)S(1)}, bf16[256,2048]{1,0:T(8,128)(2,1)S(1)}, bf16[256,2048]{1,0:T(8,128)(2,1)S(1)}) custom-call(bf16[1024,768]{1,0:T(8,128)(2,1)} %get-tuple-element.216.refs_0_, bf16[1024,768]{1,0:T(8,128)(2,1)} %get-tuple-element.217.refs_1_, ...), custom_call_target="tpu_custom_call" | custom-call | flops 1 | bytes 1 | tf_op jit(solution)/shard_map/cond/branch_1_fun/row_shares/pallas_call | solution.py:474
  202.0 4.8 %row_shares.10 = (bf16[256,2048]{1,0:T(8,128)(2,1)}, bf16[256,2048]{1,0:T(8,128)(2,1)S(1)}) custom-call(bf16[512,768]{1,0:T(8,128)(2,1)S(1)} %copy-done.71, bf16[512,768]{1,0:T(8,128)(2,1)S(1)} %copy-done.72, bf16[2048,768]{1,0:T(8,128)(2,1)S(1)} %copy-done.43, bf16[2048,768]{1,0:T(8,128)(2,1)S(1)} %copy-done.42), custom_call_target="tpu_custom_call" | custom-call | flops 1 | bytes 1 | tf_op jit(solution)/shard_map/cond/branch_1_fun/row_shares/pallas_call | solution.py:474
  212.1 3.4 collective-permute-done.35.refs_2_
  215.5 3.0 by_rows.18
  221.9 22.8 %conditional.11 = (bf16[256,2048]{1,0:T(8,128)(2,1)}, bf16[256,2048]{1,0:T(8,128)(2,1)}, bf16[256,2048]{1,0:T(8,128)(2,1)}, bf16[256,2048]{1,0:T(8,128)(2,1)}, b...) conditional(s32[]{:T(128)} %convert_element_type.89, () %tuple.248, ...), branch_computations={%region_4.5_spmd, %region_5.6_spmd} | conditional | flops 4 | bytes 32506132 | solution.py:879
  221.9 4.5 row_shares.11
  228.2 6.3 %row_shares.12 = (bf16[256,2048]{1,0:T(8,128)(2,1)}, bf16[256,2048]{1,0:T(8,128)(2,1)S(1)}, bf16[256,2048]{1,0:T(8,128)(2,1)}, bf16[256,2048]{1,0:T(8,128)(2,1)S(1)}) custom-call(bf16[1024,768]{1,0:T(8,128)(2,1)} %get-tuple-element.249.refs_0_, bf16[768,2048]{1,0:T(8,128)(2,1)S(1)} %copy-done.40), custom_call_target="tpu_custom_call" | custom-call | flops 1 | bytes 1 | tf_op jit(solution)/shard_map/cond/branch_1_fun/row_shares/pallas_call | solution.py:474
  235.8 3.3 row_shares.13
  244.8 5.3 %by_rows.19 = (f32[256,2048]{1,0:T(8,128)S(1)}, bf16[256,2048]{1,0:T(8,128)(2,1)}) custom-call(bf16[256,2048]{1,0:T(8,128)(2,1)S(1)} %copy-done.67, bf16[256,2048]{1,0:T(8,128)(2,1)} %get-tuple-element.764.refs_1_, bf16[256,2048]{1,0:T(8,128)(2,1)} %collective-permute-done.38.refs_2_, bf16[256,2048]{1,0:T(8,128)(2,1)} %collective-permute-done.39.refs_3_, ...), custom_call_target="tpu_custom_call" | custom-call | flops 1 | bytes 1 | tf_op jit(solution)/shard_map/by_rows/pallas_call | solution.py:183
  250.1 3.8 collective-permute-done.37.came_a.came_b
  260.5 22.3 %conditional.12 = (bf16[256,2048]{1,0:T(8,128)(2,1)}, bf16[512,512]{1,0:T(8,128)(2,1)}, f32[1024,64]{1,0:T(8,128)}, f32[1024,64]{1,0:T(8,128)}) conditional(s32[]{:T(128)} %convert_element_type.90, () %tuple.258, (bf16[256,2048]{1,0:T(8,128)(2,1)}, s32[2]{0:T(128)S(1)}, s32[2]{0:T(128)S(1)}, bf16[512,512]{1,0:T(8,128)(2,1)}, ...), branch_computations={%region_6.7_spmd, %region_7.8_spmd} | conditional | flops 1 | bytes 4194377 | solution.py:879
  260.5 2.8 collective-permute-start.8
  265.9 16.7 %attend_backward.2 = (bf16[512,512]{1,0:T(8,128)(2,1)}, f32[1024,64]{1,0:T(8,128)}, f32[1024,64]{1,0:T(8,128)}) custom-call(s32[2]{0:T(128)S(1)} %get-tuple-element.273.pos_ref, s32[2]{0:T(128)S(1)} %get-tuple-element.274.starts_ref, bf16[512,512]{1,0:T(8,128)(2,1)} %get-tuple-element.275.q_ref, bf16[512,2048]{1,0:T(8,128)(2,1)} %get-tuple-element.276.out_ref, ...), custom_call_target="tpu_custom_call" | custom-call | flops 1 | bytes 1 | tf_op jit(solution)/shard_map/cond/branch_1_fun/attend_backward/pallas_call | solution.py:384
  283.9 10.4 %conditional.13 = (bf16[256,2048]{1,0:T(8,128)(2,1)}, bf16[1024,512]{1,0:T(8,128)(2,1)}, bf16[1024,512]{1,0:T(8,128)(2,1)}) conditional(s32[]{:T(128)} %convert_element_type.91, () %tuple.263, (bf16[256,2048]{1,0:T(8,128)(2,1)}, s32[]{:T(128)}, bf16[256,2048]{1,0:T(8,128)(2,1)}, bf16[256,2048]{1,0:T(8,128)(2,1)}, bf16[512,512]{1,0:T(8,128)(2,1)}, ...), branch_computations={%region_8.9_spmd, %region_9.10_spmd} | conditional | flops 8 | bytes 4194517 | solution.py:879
  286.9 7.4 %outer.5 = (bf16[1024,512]{1,0:T(8,128)(2,1)}, bf16[1024,512]{1,0:T(8,128)(2,1)}) custom-call(s32[8]{0:T(128)S(1)} %stack.118.order_ref, bf16[256,2048]{1,0:T(8,128)(2,1)} %get-tuple-element.295.refs_0_.refs_1_, bf16[256,2048]{1,0:T(8,128)(2,1)} %get-tuple-element.295.refs_0_.refs_1_, bf16[256,2048]{1,0:T(8,128)(2,1)} %get-tuple-element.296.refs_2_.refs_3_, ...), custom_call_target="tpu_custom_call" | custom-call | flops 1 | bytes 1 | tf_op jit(solution)/shard_map/cond/branch_1_fun/outer/pallas_call | solution.py:538
  305.4 3.0 by_rows.20
  308.5 21.0 %conditional.14 = ((bf16[512,512]{1,0:T(8,128)(2,1)}, f32[1024,64]{1,0:T(8,128)}, f32[1024,64]{1,0:T(8,128)})) conditional(s32[]{:T(128)} %convert_element_type.92, () %tuple.274, (s32[2]{0:T(128)S(1)}, s32[2]{0:T(128)S(1)}, bf16[512,512]{1,0:T(8,128)(2,1)}, bf16[512,2048]{1,0:T(8,128)(2,1)}, bf16[512,512]{1,0:T(8,128)(2,1)}, ...), branch_computations={%region_10.11_spmd, %region_11.12_spmd} | conditional | flops 1 | bytes 1048618 | solution.py:879
  308.5 20.8 %attend_backward.3 = (bf16[512,512]{1,0:T(8,128)(2,1)}, f32[1024,64]{1,0:T(8,128)}, f32[1024,64]{1,0:T(8,128)}) custom-call(s32[2]{0:T(128)S(1)} %get-tuple-element.305.pos_ref, s32[2]{0:T(128)S(1)} %get-tuple-element.306.starts_ref, bf16[512,512]{1,0:T(8,128)(2,1)} %get-tuple-element.307.q_ref, bf16[512,2048]{1,0:T(8,128)(2,1)} %get-tuple-element.308.out_ref, ...), custom_call_target="tpu_custom_call" | custom-call | flops 1 | bytes 1 | tf_op jit(solution)/shard_map/cond/branch_1_fun/attend_backward/pallas_call | solution.py:384
  329.5 11.7 %conditional.15 = (bf16[512,128]{1,0:T(8,128)(2,1)}, bf16[512,128]{1,0:T(8,128)(2,1)}, bf16[1024,640]{1,0:T(8,128)(2,1)}, bf16[1024,640]{1,0:T(8,128)(2,1)}) conditional(s32[]{:T(128)} %convert_element_type.93, () %tuple.278, (s32[4]{0:T(128)S(1)}, f32[1024,64]{1,0:T(8,128)}, f32[1024,64]{1,0:T(8,128)}, f32[1024,64]{1,0:T(8,128)}, ...), branch_computations={%region_12.13_spmd, %region_13.14_spmd} | conditional | flops 9 | bytes 2883624 | solution.py:879
  329.5 3.6 key_value_rows.1
  333.2 8.0 %outer.6 = (bf16[1024,640]{1,0:T(8,128)(2,1)}, bf16[1024,640]{1,0:T(8,128)(2,1)}) custom-call(s32[8]{0:T(128)S(1)} %stack.127.order_ref, bf16[512,2048]{1,0:T(8,128)(2,1)} %get-tuple-element.333.refs_0_.refs_1_, bf16[512,2048]{1,0:T(8,128)(2,1)} %get-tuple-element.333.refs_0_.refs_1_, bf16[512,512]{1,0:T(8,128)(2,1)S(1)} %copy-done.62, ...), custom_call_target="tpu_custom_call" | custom-call | flops 1 | bytes 1 | tf_op jit(solution)/shard_map/cond/branch_1_fun/outer/pallas_call | solution.py:538
  350.5 9.8 %conditional.16 = (bf16[256,2048]{1,0:T(8,128)(2,1)}) conditional(s32[]{:T(128)} %convert_element_type.95, () %tuple.290, (bf16[512,512]{1,0:T(8,128)(2,1)}, bf16[512,128]{1,0:T(8,128)(2,1)}, bf16[2048,512]{1,0:T(8,128)(2,1)}, bf16[2048,128]{1,0:T(8,128)(2,1)S(1)}) %tuple.368), branch_computations={%region_14.15_spmd, %region_15.16_spmd} | conditional | flops 2 | bytes 4194354 | solution.py:879
  350.5 4.2 row_shares.14
  364.1 8.2 %conditional.17 = (bf16[256,2048]{1,0:T(8,128)(2,1)}, bf16[256,2048]{1,0:T(8,128)(2,1)}) conditional(s32[]{:T(128)} %convert_element_type.97, () %tuple.296, (bf16[512,512]{1,0:T(8,128)(2,1)}, bf16[512,128]{1,0:T(8,128)(2,1)}, bf16[2048,512]{1,0:T(8,128)(2,1)}, bf16[2048,128]{1,0:T(8,128)(2,1)}) %tuple.367), branch_computations={%region_16.17_spmd, %region_17.18_spmd} | conditional | flops 1 | bytes 4194361 | solution.py:879
  364.1 4.8 %row_shares.15 = (bf16[256,2048]{1,0:T(8,128)(2,1)}, bf16[256,2048]{1,0:T(8,128)(2,1)S(1)}) custom-call(bf16[512,512]{1,0:T(8,128)(2,1)} %get-tuple-element.357.refs_0_, bf16[512,128]{1,0:T(8,128)(2,1)} %get-tuple-element.358.refs_1_, bf16[2048,512]{1,0:T(8,128)(2,1)} %get-tuple-element.359.refs_2_, bf16[2048,128]{1,0:T(8,128)(2,1)} %get-tuple-element.360.refs_3_), custom_call_target="tpu_custom_call" | custom-call | flops 1 | bytes 1 | tf_op jit(solution)/shard_map/cond/branch_1_fun/row_shares/pallas_call | solution.py:474
  376.9 19.5 %collective-permute-done.51.came_a.came_b = bf16[512,768]{1,0:T(8,128)(2,1)S(1)} collective-permute-done((bf16[512,768]{1,0:T(8,128)(2,1)}, bf16[512,768]{1,0:T(8,128)(2,1)S(1)}, u32[]{:S(2)}, u32[]{:S(2)}) %collective-permute-start.51) | collective-permute-done | bytes 786464 | tf_op jit(solution)/shard_map/ppermute | solution.py:693
  404.9 4.8 %by_rows.22 = f32[256,2048]{1,0:T(8,128)} custom-call(bf16[256,2048]{1,0:T(8,128)(2,1)} %get-tuple-element.868.refs_0_, bf16[256,2048]{1,0:T(8,128)(2,1)} %get-tuple-element.869.refs_1_, bf16[256,2048]{1,0:T(8,128)(2,1)} %collective-permute-done.49.refs_2_, bf16[256,2048]{1,0:T(8,128)(2,1)S(1)} %copy-done.6, f32[256,2048]{1,0:T(8,128)S(1)} %copy-done.20, ...), custom_call_target="tpu_custom_call" | custom-call | flops 1 | bytes 1 | tf_op jit(solution)/shard_map/by_rows/pallas_call | solution.py:183
  418.3 15.4 %collective-permute-done.52.refs_3_ = bf16[256,2048]{1,0:T(8,128)(2,1)S(1)} collective-permute-done((bf16[256,2048]{1,0:T(8,128)(2,1)}, bf16[256,2048]{1,0:T(8,128)(2,1)S(1)}, u32[]{:S(2)}, u32[]{:S(2)}) %collective-permute-start.52) | collective-permute-done | bytes 1048608 | tf_op jit(solution)/shard_map/ppermute | solution.py:635
  433.7 8.4 %collective-permute-done.53.refs_4_ = bf16[256,2048]{1,0:T(8,128)(2,1)} collective-permute-done((bf16[256,2048]{1,0:T(8,128)(2,1)S(1)}, bf16[256,2048]{1,0:T(8,128)(2,1)}, u32[]{:S(2)}, u32[]{:S(2)}) %collective-permute-start.53) | collective-permute-done | bytes 1048608 | tf_op jit(solution)/shard_map/ppermute | solution.py:693
  442.1 3.9 collective-permute-done.56.came_ref
  451.8 3.0 copy.36
  459.1 3.4 by_rows.23
  (336 shorter events, 149.6 us)
Async XLA Ops:
  0.6 24.4 %collective-permute-start.12 = (bf16[256,2048]{1,0:T(8,128)(2,1)}, bf16[256,2048]{1,0:T(8,128)(2,1)}, u32[]{:S(2)}, u32[]{:S(2)}) collective-permute-start(bf16[256,2048]{1,0:T(8,128)(2,1)} %refs_3_.5), channel_id=1, source_target_pairs={{0,2},{1,3},{2,0},{3,1},{4,6},{5,7},{6,4},{7,5},{8,10},{9,11},{10,... | collective-permute-start | bytes 3145736 | tf_op jit(solution)/shard_map/ppermute | solution.py:635
  1.9 16.2 %collective-permute-start.13 = (bf16[256,2048]{1,0:T(8,128)(2,1)}, bf16[256,2048]{1,0:T(8,128)(2,1)S(1)}, u32[]{:S(2)}, u32[]{:S(2)}) collective-permute-start(bf16[256,2048]{1,0:T(8,128)(2,1)} %refs_3_.5), channel_id=1, source_target_pairs={{0,1},{1,0},{2,3},{3,2},{4,5},{5,4},{6,7},{7,6},{8,9},{9,8},{10,11... | collective-permute-start | bytes 3145736 | tf_op jit(solution)/shard_map/ppermute | solution.py:635
  25.1 4.2 collective-permute-start.17
  26.6 24.8 %collective-permute-start.15 = (bf16[256,2048]{1,0:T(8,128)(2,1)S(1)}, bf16[256,2048]{1,0:T(8,128)(2,1)S(1)}, u32[]{:S(2)}, u32[]{:S(2)}) collective-permute-start(bf16[256,2048]{1,0:T(8,128)(2,1)S(1)} %copy-done), channel_id=1, source_target_pairs={{0,2},{1,3},{2,0},{3,1},{4,6},{5,7},{6,4},{7,5},{8,10},{9,11},{10,... | collective-permute-start | bytes 3145736 | tf_op jit(solution)/shard_map/ppermute | solution.py:635
  27.8 24.5 %collective-permute-start.16 = (bf16[256,2048]{1,0:T(8,128)(2,1)S(1)}, bf16[256,2048]{1,0:T(8,128)(2,1)S(1)}, u32[]{:S(2)}, u32[]{:S(2)}) collective-permute-start(bf16[256,2048]{1,0:T(8,128)(2,1)S(1)} %copy-done), channel_id=1, source_target_pairs={{0,8},{4,12},{8,0},{12,4},{16,24},{20,28},{24,16},{28,20},{1,9},{5... | collective-permute-start | bytes 3145736 | tf_op jit(solution)/shard_map/ppermute | solution.py:693
  28.1 26.0 %collective-permute-start.14 = (bf16[256,2048]{1,0:T(8,128)(2,1)S(1)}, bf16[256,2048]{1,0:T(8,128)(2,1)S(1)}, u32[]{:S(2)}, u32[]{:S(2)}) collective-permute-start(bf16[256,2048]{1,0:T(8,128)(2,1)S(1)} %copy-done), channel_id=1, source_target_pairs={{0,1},{1,0},{2,3},{3,2},{4,5},{5,4},{6,7},{7,6},{8,9},{9,8},{10,11... | collective-permute-start | bytes 3145736 | tf_op jit(solution)/shard_map/ppermute | solution.py:635
  49.6 4.0 collective-permute-start.20
  53.4 3.8 collective-permute-start.19
  53.4 24.2 %collective-permute-start.22 = (bf16[256,2048]{1,0:T(8,128)(2,1)S(1)}, bf16[256,2048]{1,0:T(8,128)(2,1)S(1)}, u32[]{:S(2)}, u32[]{:S(2)}) collective-permute-start(bf16[256,2048]{1,0:T(8,128)(2,1)S(1)} %collective-permute-done.15.refs_4_.refs_5_.refs_6_), channel_id=1, source_target_pairs={{0,8},{4,12},{8,0},{12,4},{16,24},{20,28},{24,16},{28,20},{1,9},{5... | collective-permute-start | bytes 3145736 | tf_op jit(solution)/shard_map/ppermute | solution.py:693
  53.8 26.1 %collective-permute-start.24 = (bf16[256,2048]{1,0:T(8,128)(2,1)S(1)}, bf16[256,2048]{1,0:T(8,128)(2,1)S(1)}, u32[]{:S(2)}, u32[]{:S(2)}) collective-permute-start(bf16[256,2048]{1,0:T(8,128)(2,1)S(1)} %by_rows.15), channel_id=1, source_target_pairs={{0,2},{1,3},{2,0},{3,1},{4,6},{5,7},{6,4},{7,5},{8,10},{9,11},{10,... | collective-permute-start | bytes 3145736 | tf_op jit(solution)/shard_map/ppermute | solution.py:635
  68.6 11.4 %collective-permute-start.21 = (bf16[256,2048]{1,0:T(8,128)(2,1)S(1)}, bf16[256,2048]{1,0:T(8,128)(2,1)S(1)}, u32[]{:S(2)}, u32[]{:S(2)}) collective-permute-start(bf16[256,2048]{1,0:T(8,128)(2,1)S(1)} %get-tuple-element.688), channel_id=1, source_target_pairs={{0,1},{1,0},{2,3},{3,2},{4,5},{5,4},{6,7},{7,6},{8,9},{9,8},{10,11... | collective-permute-start | bytes 3145736 | tf_op jit(solution)/shard_map/ppermute | solution.py:635
  77.6 3.6 collective-permute-start.23
  84.4 24.6 %collective-permute-start.26 = (bf16[256,2048]{1,0:T(8,128)(2,1)S(1)}, bf16[256,2048]{1,0:T(8,128)(2,1)S(1)}, u32[]{:S(2)}, u32[]{:S(2)}) collective-permute-start(bf16[256,2048]{1,0:T(8,128)(2,1)S(1)} %get-tuple-element.698.refs_0_), channel_id=1, source_target_pairs={{0,2},{1,3},{2,0},{3,1},{4,6},{5,7},{6,4},{7,5},{8,10},{9,11},{10,... | collective-permute-start | bytes 3145736 | tf_op jit(solution)/shard_map/ppermute | solution.py:635
  84.7 24.4 %collective-permute-start.27 = (bf16[256,2048]{1,0:T(8,128)(2,1)S(1)}, bf16[256,2048]{1,0:T(8,128)(2,1)S(1)}, u32[]{:S(2)}, u32[]{:S(2)}) collective-permute-start(bf16[256,2048]{1,0:T(8,128)(2,1)S(1)} %get-tuple-element.698.refs_0_), channel_id=1, source_target_pairs={{0,8},{4,12},{8,0},{12,4},{16,24},{20,28},{24,16},{28,20},{1,9},{5... | collective-permute-start | bytes 3145736 | tf_op jit(solution)/shard_map/ppermute | solution.py:693
  110.3 3.8 collective-permute-start.29
  111.2 16.9 %collective-permute-start.30 = (bf16[128,2048]{1,0:T(8,128)(2,1)}, bf16[128,2048]{1,0:T(8,128)(2,1)}, u32[]{:S(2)}, u32[]{:S(2)}) collective-permute-start(bf16[128,2048]{1,0:T(8,128)(2,1)} %slice.62), channel_id=1, source_target_pairs={{0,2},{1,3},{2,0},{3,1},{4,6},{5,7},{6,4},{7,5},{8,10},{9,11},{10,... | collective-permute-start | bytes 1572872 | tf_op jit(solution)/shard_map/ppermute | solution.py:635
  112.5 15.6 %collective-permute-start.31 = (bf16[128,2048]{1,0:T(8,128)(2,1)S(1)}, bf16[128,2048]{1,0:T(8,128)(2,1)}, u32[]{:S(2)}, u32[]{:S(2)}) collective-permute-start(bf16[128,2048]{1,0:T(8,128)(2,1)S(1)} %slice.63), channel_id=1, source_target_pairs={{0,8},{4,12},{8,0},{12,4},{16,24},{20,28},{24,16},{28,20},{1,9},{5... | collective-permute-start | bytes 1572872 | tf_op jit(solution)/shard_map/ppermute | solution.py:693
  155.6 62.8 %collective-permute-start.34 = (bf16[1024,768]{1,0:T(8,128)(2,1)}, bf16[1024,768]{1,0:T(8,128)(2,1)S(1)}, u32[]{:S(2)}, u32[]{:S(2)}) collective-permute-start(bf16[1024,768]{1,0:T(8,128)(2,1)} %get-tuple-element.740), channel_id=1, source_target_pairs={{0,4},{4,0},{8,12},{12,8},{16,20},{20,16},{24,28},{28,24},{1,5},{5... | collective-permute-start | bytes 4718600 | tf_op jit(solution)/shard_map/ppermute | solution.py:693
  165.2 22.5 %collective-permute-start = (bf16[256,2048]{1,0:T(8,128)(2,1)}, bf16[256,2048]{1,0:T(8,128)(2,1)}, u32[]{:S(2)}, u32[]{:S(2)}) collective-permute-start(bf16[256,2048]{1,0:T(8,128)(2,1)} %get-tuple-element.172), channel_id=1, source_target_pairs={{0,1},{1,0},{2,3},{3,2},{4,5},{5,4},{6,7},{7,6},{8,9},{9,8},{10,11... | collective-permute-start | bytes 3145736 | tf_op jit(solution)/shard_map/cond/branch_1_fun/ppermute | solution.py:635
  190.3 25.2 %collective-permute-start.35 = (bf16[256,2048]{1,0:T(8,128)(2,1)}, bf16[256,2048]{1,0:T(8,128)(2,1)}, u32[]{:S(2)}, u32[]{:S(2)}) collective-permute-start(bf16[256,2048]{1,0:T(8,128)(2,1)} %get-tuple-element.747), channel_id=1, source_target_pairs={{0,8},{4,12},{8,0},{12,4},{16,24},{20,28},{24,16},{28,20},{1,9},{5... | collective-permute-start | bytes 3145736 | tf_op jit(solution)/shard_map/ppermute | solution.py:693
  201.5 5.6 %collective-permute-start.1 = (bf16[256,2048]{1,0:T(8,128)(2,1)S(1)}, bf16[256,2048]{1,0:T(8,128)(2,1)}, u32[]{:S(2)}, u32[]{:S(2)}) collective-permute-start(bf16[256,2048]{1,0:T(8,128)(2,1)S(1)} %get-tuple-element.225), channel_id=1, source_target_pairs={{0,1},{1,0},{2,3},{3,2},{4,5},{5,4},{6,7},{7,6},{8,9},{9,8},{10,11... | collective-permute-start | bytes 3145736 | tf_op jit(solution)/shard_map/cond/branch_1_fun/ppermute | solution.py:635
  201.8 5.3 %collective-permute-start.2 = (bf16[256,2048]{1,0:T(8,128)(2,1)S(1)}, bf16[256,2048]{1,0:T(8,128)(2,1)}, u32[]{:S(2)}, u32[]{:S(2)}) collective-permute-start(bf16[256,2048]{1,0:T(8,128)(2,1)S(1)} %get-tuple-element.229), channel_id=1, source_target_pairs={{0,1},{1,0},{2,3},{3,2},{4,5},{5,4},{6,7},{7,6},{8,9},{9,8},{10,11... | collective-permute-start | bytes 3145736 | tf_op jit(solution)/shard_map/cond/branch_1_fun/ppermute | solution.py:635
  218.4 35.4 %collective-permute-start.37 = (bf16[1024,768]{1,0:T(8,128)(2,1)}, bf16[1024,768]{1,0:T(8,128)(2,1)}, u32[]{:S(2)}, u32[]{:S(2)}) collective-permute-start(bf16[1024,768]{1,0:T(8,128)(2,1)} %get-tuple-element.786), channel_id=1, source_target_pairs={{0,4},{4,0},{8,12},{12,8},{16,20},{20,16},{24,28},{28,24},{1,5},{5... | collective-permute-start | bytes 4718600 | tf_op jit(solution)/shard_map/ppermute | solution.py:693
  218.6 26.1 %collective-permute-start.39 = (bf16[256,2048]{1,0:T(8,128)(2,1)}, bf16[256,2048]{1,0:T(8,128)(2,1)}, u32[]{:S(2)}, u32[]{:S(2)}) collective-permute-start(bf16[256,2048]{1,0:T(8,128)(2,1)} %by_rows.17), channel_id=1, source_target_pairs={{0,8},{4,12},{8,0},{12,4},{16,24},{20,28},{24,16},{28,20},{1,9},{5... | collective-permute-start | bytes 3145736 | tf_op jit(solution)/shard_map/ppermute | solution.py:693
  219.6 25.2 %collective-permute-start.38 = (bf16[256,2048]{1,0:T(8,128)(2,1)}, bf16[256,2048]{1,0:T(8,128)(2,1)}, u32[]{:S(2)}, u32[]{:S(2)}) collective-permute-start(bf16[256,2048]{1,0:T(8,128)(2,1)} %by_rows.18), channel_id=1, source_target_pairs={{0,2},{1,3},{2,0},{3,1},{4,6},{5,7},{6,4},{7,5},{8,10},{9,11},{10,... | collective-permute-start | bytes 3145736 | tf_op jit(solution)/shard_map/ppermute | solution.py:635
  226.5 8.0 %collective-permute-start.4 = (bf16[256,2048]{1,0:T(8,128)(2,1)S(1)}, bf16[256,2048]{1,0:T(8,128)(2,1)S(1)}, u32[]{:S(2)}, u32[]{:S(2)}) collective-permute-start(bf16[256,2048]{1,0:T(8,128)(2,1)S(1)} %get-tuple-element.247), channel_id=1, source_target_pairs={{0,1},{1,0},{2,3},{3,2},{4,5},{5,4},{6,7},{7,6},{8,9},{9,8},{10,11... | collective-permute-start | bytes 3145736 | tf_op jit(solution)/shard_map/cond/branch_1_fun/ppermute | solution.py:635
  253.9 43.3 %collective-permute-start.40 = (bf16[1024,768]{1,0:T(8,128)(2,1)}, bf16[1024,768]{1,0:T(8,128)(2,1)S(1)}, u32[]{:S(2)}, u32[]{:S(2)}) collective-permute-start(bf16[1024,768]{1,0:T(8,128)(2,1)} %get-tuple-element.796), channel_id=1, source_target_pairs={{0,4},{4,0},{8,12},{12,8},{16,20},{20,16},{24,28},{28,24},{1,5},{5... | collective-permute-start | bytes 4718600 | tf_op jit(solution)/shard_map/ppermute | solution.py:693
  254.1 28.7 %collective-permute-start.42 = (bf16[256,2048]{1,0:T(8,128)(2,1)}, bf16[256,2048]{1,0:T(8,128)(2,1)S(1)}, u32[]{:S(2)}, u32[]{:S(2)}) collective-permute-start(bf16[256,2048]{1,0:T(8,128)(2,1)} %get-tuple-element.794), channel_id=1, source_target_pairs={{0,2},{1,3},{2,0},{3,1},{4,6},{5,7},{6,4},{7,5},{8,10},{9,11},{10,... | collective-permute-start | bytes 3145736 | tf_op jit(solution)/shard_map/ppermute | solution.py:635
  255.3 39.0 %collective-permute-start.41 = (bf16[512,768]{1,0:T(8,128)(2,1)}, bf16[512,768]{1,0:T(8,128)(2,1)}, u32[]{:S(2)}, u32[]{:S(2)}) collective-permute-start(bf16[512,768]{1,0:T(8,128)(2,1)} %get-tuple-element.771), channel_id=1, source_target_pairs={{0,16},{4,20},{8,24},{12,28},{16,0},{20,4},{24,8},{28,12},{1,17},{... | collective-permute-start | bytes 2359304 | tf_op jit(solution)/shard_map/ppermute | solution.py:693
  257.6 47.8 %collective-permute-start.36 = (bf16[256,2048]{1,0:T(8,128)(2,1)}, bf16[256,2048]{1,0:T(8,128)(2,1)}, u32[]{:S(2)}, u32[]{:S(2)}) collective-permute-start(bf16[256,2048]{1,0:T(8,128)(2,1)} %get-tuple-element.785), channel_id=1, source_target_pairs={{0,8},{4,12},{8,0},{12,4},{16,24},{20,28},{24,16},{28,20},{1,9},{5... | collective-permute-start | bytes 3145736 | tf_op jit(solution)/shard_map/ppermute | solution.py:693
  260.5 5.4 %collective-permute-start.8 = (bf16[256,2048]{1,0:T(8,128)(2,1)}, bf16[256,2048]{1,0:T(8,128)(2,1)}, u32[]{:S(2)}, u32[]{:S(2)}) collective-permute-start(bf16[256,2048]{1,0:T(8,128)(2,1)} %get-tuple-element.272.rest_0_), channel_id=1, source_target_pairs={{0,1},{1,0},{2,3},{3,2},{4,5},{5,4},{6,7},{7,6},{8,9},{9,8},{10,11... | collective-permute-start | bytes 3145736 | tf_op jit(solution)/shard_map/cond/branch_1_fun/ppermute | solution.py:635
  297.2 44.4 %collective-permute-start.46 = (bf16[1024,512]{1,0:T(8,128)(2,1)}, bf16[1024,512]{1,0:T(8,128)(2,1)S(1)}, u32[]{:S(2)}, u32[]{:S(2)}) collective-permute-start(bf16[1024,512]{1,0:T(8,128)(2,1)} %get-tuple-element.846), channel_id=1, source_target_pairs={{0,4},{4,0},{8,12},{12,8},{16,20},{20,16},{24,28},{28,24},{1,5},{5... | collective-permute-start | bytes 3145736 | tf_op jit(solution)/shard_map/ppermute | solution.py:693
  298.4 45.1 %collective-permute-start.45 = (bf16[256,768]{1,0:T(8,128)(2,1)}, bf16[256,768]{1,0:T(8,128)(2,1)}, u32[]{:S(2)}, u32[]{:S(2)}) collective-permute-start(bf16[256,768]{1,0:T(8,128)(2,1)} %get-tuple-element.821), channel_id=1, source_target_pairs={{0,8},{4,12},{8,0},{12,4},{16,24},{20,28},{24,16},{28,20},{1,9},{5... | collective-permute-start | bytes 1179656 | tf_op jit(solution)/shard_map/ppermute | solution.py:693
  299.7 47.3 %collective-permute-start.44 = (bf16[512,768]{1,0:T(8,128)(2,1)}, bf16[512,768]{1,0:T(8,128)(2,1)}, u32[]{:S(2)}, u32[]{:S(2)}) collective-permute-start(bf16[512,768]{1,0:T(8,128)(2,1)} %get-tuple-element.845), channel_id=1, source_target_pairs={{0,16},{4,20},{8,24},{12,28},{16,0},{20,4},{24,8},{28,12},{1,17},{... | collective-permute-start | bytes 2359304 | tf_op jit(solution)/shard_map/ppermute | solution.py:693
  341.2 31.1 %collective-permute-start.43 = (bf16[1024,640]{1,0:T(8,128)(2,1)}, bf16[1024,640]{1,0:T(8,128)(2,1)S(1)}, u32[]{:S(2)}, u32[]{:S(2)}) collective-permute-start(bf16[1024,640]{1,0:T(8,128)(2,1)} %get-tuple-element.844), channel_id=1, source_target_pairs={{0,4},{4,0},{8,12},{12,8},{16,20},{20,16},{24,28},{28,24},{1,5},{5... | collective-permute-start | bytes 3932168 | tf_op jit(solution)/shard_map/ppermute | solution.py:693
  349.0 13.8 %collective-permute-start.47 = (bf16[256,768]{1,0:T(8,128)(2,1)}, bf16[256,768]{1,0:T(8,128)(2,1)S(1)}, u32[]{:S(2)}, u32[]{:S(2)}) collective-permute-start(bf16[256,768]{1,0:T(8,128)(2,1)} %get-tuple-element.860), channel_id=1, source_target_pairs={{0,8},{4,12},{8,0},{12,4},{16,24},{20,28},{24,16},{28,20},{1,9},{5... | collective-permute-start | bytes 1179656 | tf_op jit(solution)/shard_map/ppermute | solution.py:693
  349.0 27.9 %collective-permute-start.50 = (bf16[512,512]{1,0:T(8,128)(2,1)}, bf16[512,512]{1,0:T(8,128)(2,1)}, u32[]{:S(2)}, u32[]{:S(2)}) collective-permute-start(bf16[512,512]{1,0:T(8,128)(2,1)} %get-tuple-element.852), channel_id=1, source_target_pairs={{0,8},{4,12},{8,0},{12,4},{16,24},{20,28},{24,16},{28,20},{1,9},{5... | collective-permute-start | bytes 1572872 | tf_op jit(solution)/shard_map/ppermute | solution.py:693
  354.6 4.4 collective-permute-start.10
  360.3 43.1 %collective-permute-start.49 = (bf16[256,2048]{1,0:T(8,128)(2,1)}, bf16[256,2048]{1,0:T(8,128)(2,1)}, u32[]{:S(2)}, u32[]{:S(2)}) collective-permute-start(bf16[256,2048]{1,0:T(8,128)(2,1)} %get-tuple-element.1032), channel_id=1, source_target_pairs={{0,2},{1,3},{2,0},{3,1},{4,6},{5,7},{6,4},{7,5},{8,10},{9,11},{10,... | collective-permute-start | bytes 3145736 | tf_op jit(solution)/shard_map/ppermute | solution.py:635
  360.5 35.9 %collective-permute-start.51 = (bf16[512,768]{1,0:T(8,128)(2,1)}, bf16[512,768]{1,0:T(8,128)(2,1)S(1)}, u32[]{:S(2)}, u32[]{:S(2)}) collective-permute-start(bf16[512,768]{1,0:T(8,128)(2,1)} %get-tuple-element.878), channel_id=1, source_target_pairs={{0,16},{4,20},{8,24},{12,28},{16,0},{20,4},{24,8},{28,12},{1,17},{... | collective-permute-start | bytes 2359304 | tf_op jit(solution)/shard_map/ppermute | solution.py:693
  374.5 35.2 %collective-permute-start.48 = (bf16[512,640]{1,0:T(8,128)(2,1)}, bf16[512,640]{1,0:T(8,128)(2,1)S(1)}, u32[]{:S(2)}, u32[]{:S(2)}) collective-permute-start(bf16[512,640]{1,0:T(8,128)(2,1)} %get-tuple-element.873), channel_id=1, source_target_pairs={{0,8},{4,12},{8,0},{12,4},{16,24},{20,28},{24,16},{28,20},{1,9},{5... | collective-permute-start | bytes 1966088 | tf_op jit(solution)/shard_map/ppermute | solution.py:693
  398.0 15.3 %collective-permute-start.55 = (bf16[256,768]{1,0:T(8,128)(2,1)}, bf16[256,768]{1,0:T(8,128)(2,1)}, u32[]{:S(2)}, u32[]{:S(2)}) collective-permute-start(bf16[256,768]{1,0:T(8,128)(2,1)} %get-tuple-element.882), channel_id=1, source_target_pairs={{0,8},{4,12},{8,0},{12,4},{16,24},{20,28},{24,16},{28,20},{1,9},{5... | collective-permute-start | bytes 1179656 | tf_op jit(solution)/shard_map/ppermute | solution.py:693
  400.8 17.2 %collective-permute-start.54 = (bf16[256,512]{1,0:T(8,128)(2,1)S(1)}, bf16[256,512]{1,0:T(8,128)(2,1)S(1)}, u32[]{:S(2)}, u32[]{:S(2)}) collective-permute-start(bf16[256,512]{1,0:T(8,128)(2,1)S(1)} %get-tuple-element.884), channel_id=1, source_target_pairs={{0,16},{4,20},{8,24},{12,28},{16,0},{20,4},{24,8},{28,12},{1,17},{... | collective-permute-start | bytes 786440 | tf_op jit(solution)/shard_map/ppermute | solution.py:693
  410.5 23.2 %collective-permute-start.52 = (bf16[256,2048]{1,0:T(8,128)(2,1)}, bf16[256,2048]{1,0:T(8,128)(2,1)S(1)}, u32[]{:S(2)}, u32[]{:S(2)}) collective-permute-start(bf16[256,2048]{1,0:T(8,128)(2,1)} %by_rows.20), channel_id=1, source_target_pairs={{0,2},{1,3},{2,0},{3,1},{4,6},{5,7},{6,4},{7,5},{8,10},{9,11},{10,... | collective-permute-start | bytes 3145736 | tf_op jit(solution)/shard_map/ppermute | solution.py:635
  411.7 30.4 %collective-permute-start.53 = (bf16[256,2048]{1,0:T(8,128)(2,1)S(1)}, bf16[256,2048]{1,0:T(8,128)(2,1)}, u32[]{:S(2)}, u32[]{:S(2)}) collective-permute-start(bf16[256,2048]{1,0:T(8,128)(2,1)S(1)} %copy-done.28), channel_id=1, source_target_pairs={{0,8},{4,12},{8,0},{12,4},{16,24},{20,28},{24,16},{28,20},{1,9},{5... | collective-permute-start | bytes 3145736 | tf_op jit(solution)/shard_map/ppermute | solution.py:693
  413.1 32.9 %collective-permute-start.56 = (bf16[256,640]{1,0:T(8,128)(2,1)}, bf16[256,640]{1,0:T(8,128)(2,1)S(1)}, u32[]{:S(2)}, u32[]{:S(2)}) collective-permute-start(bf16[256,640]{1,0:T(8,128)(2,1)} %get-tuple-element.893), channel_id=1, source_target_pairs={{0,16},{4,20},{8,24},{12,28},{16,0},{20,4},{24,8},{28,12},{1,17},{... | collective-permute-start | bytes 983048 | tf_op jit(solution)/shard_map/ppermute | solution.py:693
  451.7 4.1 collective-permute-start.57
  455.9 8.1 %collective-permute-start.58 = (f32[2,64]{1,0:T(2,128)S(1)}, f32[2,64]{1,0:T(2,128)S(1)}, u32[]{:S(2)}, u32[]{:S(2)}) collective-permute-start(f32[2,64]{1,0:T(2,128)S(1)} %slice_bitcast_fusion), channel_id=1, source_target_pairs={{0,1},{1,0},{2,3},{3,2},{4,5},{5,4},{6,7},{7,6},{8,9},{9,8},{10,11... | collective-permute-start | bytes 1544 | tf_op jit(solution)/shard_map/ppermute | solution.py:1115
  (88 other events, 799.2 us)

commit v4 on v3

--- a/solution.py
+++ b/solution.py
@@ -408,19 +408,48 @@
     )
 
 
-def feed_kernel(*refs, counts):
-    gate_ref, up_ref, down_ref, hidden_ref, d_gate_ref, d_up_ref, normed, cots = refs[sum(counts) :]
+def hidden_kernel(*refs):
+    *parts, down_ref, out_ref, cots = refs
 
     @pl.when(pl.program_id(0) == 0)
     def _():
-        for target, sources in ((normed, refs[: counts[0]]), (cots, refs[counts[0] : sum(counts)])):
-            at = 0
-            for ref in sources:
-                target[at : at + ref.shape[0], :] = ref[...]
-                at += ref.shape[0]
+        at = 0
+        for ref in parts:
+            cots[at : at + ref.shape[0], :] = ref[...]
+            at += ref.shape[0]
+
+    out_ref[...] = contract_cols(cots[...], down_ref[...]).astype(jnp.bfloat16)
+
+
+def hidden_back(cots, w_down):
+    rows, width = sum(item.shape[0] for item in cots), cots[0].shape[1]
+    units, tile = w_down.shape[0], 256
+    return pl.pallas_call(
+        hidden_kernel,
+        grid=(pl.cdiv(units, tile),),
+        in_specs=[
+            *(whole(item) for item in cots), pl.BlockSpec((tile, width), lambda j: (j, 0))
+        ],
+        out_specs=pl.BlockSpec((rows, tile), lambda j: (0, j)),
+        out_shape=jax.ShapeDtypeStruct((rows, units), jnp.bfloat16),
+        scratch_shapes=[pltpu.VMEM((rows, width), jnp.bfloat16)],
+        name="hidden_back",
+        **params(),
+    )(*cots, w_down)
+
+
+def feed_kernel(*refs):
+    *parts, d_hidden_ref, gate_ref, up_ref, hidden_ref, d_gate_ref, d_up_ref, normed = refs
+
+    @pl.when(pl.program_id(0) == 0)
+    def _():
+        at = 0
+        for ref in parts:
+            normed[at : at + ref.shape[0], :] = ref[...]
+            at += ref.shape[0]
 
     gate_val, up_val = dot(normed[...], gate_ref[...]), dot(normed[...], up_ref[...])
-    d_hidden = contract_cols(cots[...], down_ref[...])
+    d_hidden = d_hidden_ref[...].astype(jnp.float32)
     gate_sig = jax.nn.sigmoid(gate_val)
     swish = gate_val * gate_sig
     hidden_ref[...] = (swish * up_val).astype(jnp.bfloat16)
@@ -429,26 +458,21 @@
     d_up_ref[...] = (d_hidden * swish).astype(jnp.bfloat16)
 
 
-def feed_forward(normed, cots, w_gate, w_up, w_down):
+def feed_forward(normed, d_hidden, w_gate, w_up):
     rows, width = sum(item.shape[0] for item in normed), normed[0].shape[1]
     units, tile = w_gate.shape[1], 256
     cols = pl.BlockSpec((width, tile), lambda j: (0, j))
     out = pl.BlockSpec((rows, tile), lambda j: (0, j))
     return pl.pallas_call(
-        functools.partial(feed_kernel, counts=(len(normed), len(cots))),
+        feed_kernel,
         grid=(pl.cdiv(units, tile),),
-        in_specs=[
-            *(whole(item) for item in (*normed, *cots)),
-            cols,
-            cols,
-            pl.BlockSpec((tile, width), lambda j: (j, 0)),
-        ],
+        in_specs=[*(whole(item) for item in normed), out, cols, cols],
         out_specs=[out] * 3,
         out_shape=[jax.ShapeDtypeStruct((rows, units), jnp.bfloat16)] * 3,
-        scratch_shapes=[pltpu.VMEM((rows, width), jnp.bfloat16)] * 2,
+        scratch_shapes=[pltpu.VMEM((rows, width), jnp.bfloat16)],
         name="feed_forward",
         **params(),
-    )(*normed, *cots, w_gate, w_up, w_down)
+    )(*normed, d_hidden, w_gate, w_up)
 
 
 def share_kernel(*refs, count, transposed):
@@ -822,6 +846,11 @@
         *attend_forward(q_n, k_low, v_low, w_out, begins, near_pos)
     )
     sum_came = swap_core(sent)
+
+    def cot_back(*cots):
+        return order.done(hidden_back(order.after(cots), down_half))
+
+    near_back_hidden = cot_back(*cot_own, *cot_core)
     cot_diag = order.after(cot_diag)
     cot_dcore = swap_core(cot_diag)
     attn_came = order.after(attn_came)
@@ -839,23 +868,22 @@
     mlp_core, mlp_chip, mlp_pair = swap_core(mlp_own), swap_chip(mlp_own), swap_pair(mlp_own, dp_size)
     mlp_core = order.after(mlp_core)
 
-    def feed(normed, cots):
-        return order.done(*feed_forward(normed, cots, gate_half, up_half, down_half))
-
-    near_hidden = feed((*mlp_own, *mlp_core), (*cot_own, *cot_core))
+    def feed(normed, d_hidden):
+        return order.done(*feed_forward(normed, d_hidden, gate_half, up_half))
+
+    near_hidden = feed((*mlp_own, *mlp_core), near_back_hidden)
+    side_back_hidden = cot_back(*cot_chip, *cot_other, *cot_pair, *cot_pcore)
+    diag_back_hidden = cot_back(*cot_diag, *cot_dcore)
     mlp_chip, mlp_pair = order.after(mlp_chip, mlp_pair)
     half = rows // 2
     mlp_diag = (
         *swap_chip((mlp_pair[0][:half],)), *swap_pair((mlp_chip[0][half:],), dp_size)
     )
     mlp_other, mlp_pcore = order.after(swap_core(mlp_chip), swap_core(mlp_pair))
-    side_hidden = feed(
-        (*mlp_chip, *mlp_other, *mlp_pair, *mlp_pcore),
-        (*cot_chip, *cot_other, *cot_pair, *cot_pcore),
-    )
+    side_hidden = feed((*mlp_chip, *mlp_other, *mlp_pair, *mlp_pcore), side_back_hidden)
     mlp_diag = order.after(mlp_diag)
     mlp_dcore = order.after(swap_core(mlp_diag))
-    diag_hidden = feed((*mlp_diag, *mlp_dcore), (*cot_diag, *cot_dcore))
+    diag_hidden = feed((*mlp_diag, *mlp_dcore), diag_back_hidden)
     hiddens = (near_hidden, side_hidden, diag_hidden)
 
     def in_window(kept, came):

time: 472 us -> 469 us (level)
  waiting for transfers between devices: 111 us -> 104 us
    pallas_call x3 -> x6, Pallas kernels: 34 us -> 38.3 us  [the longest x3 27.5 us: feed_forward(): pl.pallas_call(feed_kernel, grid=(pl.cdiv(units, tile),), in_specs=[*(who...]
    unnamed x146 -> x144, local copies, waits for them, and re-layouts: 25.2 us -> 23.3 us
  transfers between devices with their start and end apart: 59 -> 59, of which waited for: 28 -> 28; matrix products, arithmetic and copies ran while one was open for 7% -> 7% of each run, Pallas kernels for 49% -> 51%
where the time goes in v4:
time: 469 us; the launch traced here: 462 us
  Pallas kernels  256 us (55%)
  waiting for transfers between devices  104 us (22%)
  starting transfers between devices  46.5 us (10%)
  local copies, waits for them, and re-layouts  27.7 us (6%)
  other arithmetic  25 us (5%)
    ppermute x34, waiting for transfers between devices, swapped(): return tuple((lax.ppermute(part, 'tensor', pairs) for part in parts))  56.9 us
    pallas_call x4, Pallas kernels, outer(): pl.pallas_call(functools.partial(outer_kernel, shape=[(len(lefts), len(ri...  49.1 us
    ppermute x23, waiting for transfers between devices, exchange(): return lax.ppermute(value, 'dp', [(i, i ^ bit) for i in range(size)])  46.9 us
    pallas_call x8, Pallas kernels, row_shares(): pl.pallas_call(functools.partial(share_kernel, count=len(lefts), transpos...  45.3 us
    pallas_call x2, Pallas kernels, attend_backward(): pl.pallas_call(functools.partial(backward_kernel, heads=heads, pics=pics,...  37.5 us
    pallas_call x12, Pallas kernels, by_rows(): pl.pallas_call(kernel, out_shape=shapes, name='by_rows', **params())  31.8 us
    pallas_call x3, Pallas kernels, feed_forward(): pl.pallas_call(feed_kernel, grid=(pl.cdiv(units, tile),), in_specs=[*(who...  27.5 us
    ppermute x34, starting transfers between devices, swapped(): return tuple((lax.ppermute(part, 'tensor', pairs) for part in parts))  26 us
  transfers between devices with their start and end apart: 59, of which 28 were waited for; matrix products, arithmetic and copies ran while one was open for 7% of the time, Pallas kernels for 51%

profile of v4, /device:TPU:9, one launch (start us, length us, event | category | flops | bytes accessed | tf_op | source)
XLA Modules:
  0.0 461.6 jit_solution(10175047612897337248)
XLA Ops:
  11.8 6.3 %dynamic-slice_select_fusion.1 = (bf16[2048,768]{1,0:T(8,128)(2,1)}, bf16[2048,768]{1,0:T(8,128)(2,1)}) fusion(bf16[2048,1408]{1,0:T(8,128)(2,1)} %param.41, s32[]{:T(128)S(6)} %select_n.91, pred[768]{0:T(1024)(128)(4,1)S(1)} %fusion.2, bf16[2048,1408]{1,0:T(8,128)(2,1)} %param.40), kind=kLoop, calls=%fused_computation.1 | loop fusion | flops 1572864 | bytes 12583684 | tf_op jit(solution)/shard_map/jit(_where)/select_n | solution.py:816
  18.1 3.8 project.2
  22.0 3.1 collective-permute-done.12.refs_0_
  29.2 6.2 %project.3 = (bf16[512,2048]{1,0:T(8,128)(2,1)}, bf16[512,512]{1,0:T(8,128)(2,1)S(1)}, bf16[512,64]{1,0:T(8,128)(2,1)S(1)}, bf16[512,64]{1,0:T(8,128)(2,1)S(1)}) custom-call(bf16[256,2048]{1,0:T(8,128)(2,1)} %collective-permute-done.12.refs_0_, bf16[256,2048]{1,0:T(8,128)(2,1)} %collective-permute-done.17.refs_1_, f32[1,2048]{1,0:T(1,128)S(1)} %bitcast.69, ...), custom_call_target="tpu_custom_call" | custom-call | flops 1 | bytes 1 | tf_op jit(solution)/shard_map/project/pallas_call | solution.py:117
  37.4 12.2 %attend_forward.2 = (bf16[512,512]{1,0:T(8,128)(2,1)}, f32[512,8]{1,0:T(8,128)}, bf16[256,2048]{1,0:T(8,128)(2,1)S(1)}, bf16[256,2048]{1,0:T(8,128)(2,1)S(1)}) custom-call(s32[2]{0:T(128)S(1)} %get-tuple-element.978.pos_ref, s32[2]{0:T(128)S(1)} %bitcast.74, bf16[512,512]{1,0:T(8,128)(2,1)S(1)} %get-tuple-element.674.q_ref, ...), custom_call_target="tpu_custom_call" | custom-call | flops 1 | bytes 1 | tf_op jit(solution)/shard_map/attend_forward/pallas_call | solution.py:272
  57.2 11.4 %attend_forward.3 = (bf16[512,512]{1,0:T(8,128)(2,1)}, f32[512,8]{1,0:T(8,128)}, bf16[256,2048]{1,0:T(8,128)(2,1)S(1)}, bf16[256,2048]{1,0:T(8,128)(2,1)S(1)}) custom-call(s32[2]{0:T(128)S(1)} %get-tuple-element.977.pos_ref, s32[2]{0:T(128)S(1)} %bitcast.75, bf16[512,512]{1,0:T(8,128)(2,1)S(1)} %copy-done.73, bf16[1024,64]{1,0:T(8,128)(2,1)S(1)} %pad_maximum_fusion.5.k_ref, ...), custom_call_target="tpu_custom_call" | custom-call | flops 1 | bytes 1 | tf_op jit(solution)/shard_map/attend_forward/pallas_call | solution.py:272
  69.0 4.1 hidden_back.3.refs_2_
  73.1 4.5 collective-permute-done.22.refs_0_.refs_14_.refs_15_
  81.3 3.1 by_rows.16
  87.2 8.0 %feed_forward.3 = (bf16[512,768]{1,0:T(8,128)(2,1)}, bf16[512,768]{1,0:T(8,128)(2,1)}, bf16[512,768]{1,0:T(8,128)(2,1)}) custom-call(bf16[256,2048]{1,0:T(8,128)(2,1)} %get-tuple-element.712.refs_0_, bf16[256,2048]{1,0:T(8,128)(2,1)S(1)} %collective-permute-done.25.refs_1_, bf16[512,768]{1,0:T(8,128)(2,1)S(1)} %hidden_back.3.refs_2_, ...), custom_call_target="tpu_custom_call" | custom-call | flops 1 | bytes 1 | tf_op jit(solution)/shard_map/feed_forward/pallas_call | solution.py:466
  95.2 4.2 hidden_back.4.refs_4_
  101.9 7.7 %collective-permute-done.26.refs_0_ = bf16[256,2048]{1,0:T(8,128)(2,1)} collective-permute-done((bf16[256,2048]{1,0:T(8,128)(2,1)}, bf16[256,2048]{1,0:T(8,128)(2,1)}, u32[]{:S(2)}, u32[]{:S(2)}) %collective-permute-start.26) | collective-permute-done | bytes 1048608 | tf_op jit(solution)/shard_map/ppermute | solution.py:659
  114.8 11.7 %feed_forward.4 = (bf16[1024,768]{1,0:T(8,128)(2,1)}, bf16[1024,768]{1,0:T(8,128)(2,1)}, bf16[1024,768]{1,0:T(8,128)(2,1)}) custom-call(bf16[256,2048]{1,0:T(8,128)(2,1)} %collective-permute-done.26.refs_0_, bf16[256,2048]{1,0:T(8,128)(2,1)S(1)} %collective-permute-done.28.refs_1_, bf16[256,2048]{1,0:T(8,128)(2,1)} %collective-permute-done.27.refs_2_, ...), custom_call_target="tpu_custom_call" | custom-call | flops 1 | bytes 1 | tf_op jit(solution)/shard_map/feed_forward/pallas_call | solution.py:466
  132.5 7.8 %feed_forward.5 = (bf16[512,768]{1,0:T(8,128)(2,1)S(1)}, bf16[512,768]{1,0:T(8,128)(2,1)}, bf16[512,768]{1,0:T(8,128)(2,1)}) custom-call(bf16[128,2048]{1,0:T(8,128)(2,1)} %collective-permute-done.30.refs_0_, bf16[128,2048]{1,0:T(8,128)(2,1)} %collective-permute-done.31.refs_1_, bf16[128,2048]{1,0:T(8,128)(2,1)} %collective-permute-done.32.refs_2_, ...), custom_call_target="tpu_custom_call" | custom-call | flops 1 | bytes 1 | tf_op jit(solution)/shard_map/feed_forward/pallas_call | solution.py:466
  140.4 12.0 %outer.7 = (bf16[1024,768]{1,0:T(8,128)(2,1)}, bf16[1024,768]{1,0:T(8,128)(2,1)}) custom-call(s32[8]{0:T(128)S(1)} %stack.168.order_ref, bf16[256,2048]{1,0:T(8,128)(2,1)S(1)} %copy-done, bf16[256,2048]{1,0:T(8,128)(2,1)S(1)} %copy-done, bf16[256,2048]{1,0:T(8,128)(2,1)S(1)} %copy-done.8, bf16[256,2048]{1,0:T(8,128)(2,1)S(1)} %copy-done.8, ...), custom_call_target="tpu_custom_call" | custom-call | flops 1 | bytes 1 | tf_op jit(solution)/shard_map/outer/pallas_call | solution.py:562
  153.8 33.4 %conditional.9 = (bf16[256,2048]{1,0:T(8,128)(2,1)}, bf16[1024,768]{1,0:T(8,128)(2,1)}, bf16[1024,768]{1,0:T(8,128)(2,1)}, bf16[1024,768]{1,0:T(8,128)(2,1)}, bf16[1024,768]{1,0:T(8,128)(2,1)}) conditional(s32[]{:T(128)} %convert_element_type.87, () %tuple.247, (bf16[512,768]{1,0:T(8,128)(2,1)}, bf16[512,768]{1,0:T(8,128)(2,1)}, ...), branch_computations={%region_0.1_spmd, %region_1.2_spmd} | conditional | flops 10 | bytes 12583199 | solution.py:907
  153.8 7.2 %row_shares.8 = (bf16[256,2048]{1,0:T(8,128)(2,1)S(1)}, bf16[256,2048]{1,0:T(8,128)(2,1)}) custom-call(bf16[512,768]{1,0:T(8,128)(2,1)} %get-tuple-element.202.refs_0_.refs_24_, bf16[512,768]{1,0:T(8,128)(2,1)} %get-tuple-element.203.refs_1_.refs_25_, bf16[2048,768]{1,0:T(8,128)(2,1)} %get-tuple-element.167.refs_2_, bf16[2048,768]{1,0:T(8,128)(2,1)} %get-tuple-element.168.refs_3_), custom_call_target="tpu_custom_call" | custom-call | flops 1 | bytes 1 | tf_op jit(solution)/shard_map/cond/branch_1_fun/row_shares/pallas_call | solution.py:498
  162.7 21.7 %outer.4 = (bf16[1024,768]{1,0:T(8,128)(2,1)}, bf16[1024,768]{1,0:T(8,128)(2,1)}, bf16[1024,768]{1,0:T(8,128)(2,1)}, bf16[1024,768]{1,0:T(8,128)(2,1)}) custom-call(s32[8]{0:T(128)S(1)} %stack.109.order_ref, bf16[256,2048]{1,0:T(8,128)(2,1)} %get-tuple-element.188.refs_0_.refs_1_, bf16[256,2048]{1,0:T(8,128)(2,1)} %get-tuple-element.188.refs_0_.refs_1_, ...), custom_call_target="tpu_custom_call" | custom-call | flops 1 | bytes 1 | tf_op jit(solution)/shard_map/cond/branch_1_fun/outer/pallas_call | solution.py:562
  187.5 18.3 %conditional.10 = (bf16[256,2048]{1,0:T(8,128)(2,1)S(1)}, bf16[256,2048]{1,0:T(8,128)(2,1)}, bf16[256,2048]{1,0:T(8,128)(2,1)S(1)}, bf16[256,2048]{1,0:T(8,128)(...) conditional(s32[]{:T(128)} %convert_element_type.88, () %tuple.251, (bf16[1024,768]{1,0:T(8,128)(2,1)}, ...), branch_computations={%region_2.3_spmd, %region_3.4_spmd} | conditional | flops 2 | bytes 44040472 | solution.py:907
  187.5 10.2 %row_shares.9 = (bf16[256,2048]{1,0:T(8,128)(2,1)S(1)}, bf16[256,2048]{1,0:T(8,128)(2,1)S(1)}, bf16[256,2048]{1,0:T(8,128)(2,1)S(1)}, bf16[256,2048]{1,0:T(8,128)(2,1)S(1)}) custom-call(bf16[1024,768]{1,0:T(8,128)(2,1)} %get-tuple-element.216.refs_0_, bf16[1024,768]{1,0:T(8,128)(2,1)} %get-tuple-element.217.refs_1_, ...), custom_call_target="tpu_custom_call" | custom-call | flops 1 | bytes 1 | tf_op jit(solution)/shard_map/cond/branch_1_fun/row_shares/pallas_call | solution.py:498
  198.3 4.8 %row_shares.10 = (bf16[256,2048]{1,0:T(8,128)(2,1)}, bf16[256,2048]{1,0:T(8,128)(2,1)S(1)}) custom-call(bf16[512,768]{1,0:T(8,128)(2,1)S(1)} %copy-done.70, bf16[512,768]{1,0:T(8,128)(2,1)S(1)} %copy-done.71, bf16[2048,768]{1,0:T(8,128)(2,1)S(1)} %copy-done.44, bf16[2048,768]{1,0:T(8,128)(2,1)S(1)} %copy-done.43), custom_call_target="tpu_custom_call" | custom-call | flops 1 | bytes 1 | tf_op jit(solution)/shard_map/cond/branch_1_fun/row_shares/pallas_call | solution.py:498
  208.3 4.0 collective-permute-done.35.refs_2_
  218.0 22.8 %conditional.11 = (bf16[256,2048]{1,0:T(8,128)(2,1)}, bf16[256,2048]{1,0:T(8,128)(2,1)}, bf16[256,2048]{1,0:T(8,128)(2,1)}, bf16[256,2048]{1,0:T(8,128)(2,1)}, b...) conditional(s32[]{:T(128)} %convert_element_type.89, () %tuple.260, ...), branch_computations={%region_4.5_spmd, %region_5.6_spmd} | conditional | flops 4 | bytes 32506132 | solution.py:907
  218.0 4.5 row_shares.11
  224.2 6.3 %row_shares.12 = (bf16[256,2048]{1,0:T(8,128)(2,1)}, bf16[256,2048]{1,0:T(8,128)(2,1)S(1)}, bf16[256,2048]{1,0:T(8,128)(2,1)}, bf16[256,2048]{1,0:T(8,128)(2,1)S(1)}) custom-call(bf16[1024,768]{1,0:T(8,128)(2,1)} %get-tuple-element.249.refs_0_, bf16[768,2048]{1,0:T(8,128)(2,1)S(1)} %copy-done.41), custom_call_target="tpu_custom_call" | custom-call | flops 1 | bytes 1 | tf_op jit(solution)/shard_map/cond/branch_1_fun/row_shares/pallas_call | solution.py:498
  231.9 3.3 row_shares.13
  240.8 5.3 %by_rows.19 = (f32[256,2048]{1,0:T(8,128)S(1)}, bf16[256,2048]{1,0:T(8,128)(2,1)}) custom-call(bf16[256,2048]{1,0:T(8,128)(2,1)S(1)} %copy-done.66, bf16[256,2048]{1,0:T(8,128)(2,1)} %get-tuple-element.786.refs_1_, bf16[256,2048]{1,0:T(8,128)(2,1)} %collective-permute-done.38.refs_2_, bf16[256,2048]{1,0:T(8,128)(2,1)} %collective-permute-done.39.refs_3_, ...), custom_call_target="tpu_custom_call" | custom-call | flops 1 | bytes 1 | tf_op jit(solution)/shard_map/by_rows/pallas_call | solution.py:183
  246.1 4.6 collective-permute-done.37.came_a.came_b
  256.6 22.3 %conditional.12 = (bf16[256,2048]{1,0:T(8,128)(2,1)}, bf16[512,512]{1,0:T(8,128)(2,1)}, f32[1024,64]{1,0:T(8,128)}, f32[1024,64]{1,0:T(8,128)}) conditional(s32[]{:T(128)} %convert_element_type.90, () %tuple.270, (bf16[256,2048]{1,0:T(8,128)(2,1)}, s32[2]{0:T(128)S(1)}, s32[2]{0:T(128)S(1)}, bf16[512,512]{1,0:T(8,128)(2,1)}, ...), branch_computations={%region_6.7_spmd, %region_7.8_spmd} | conditional | flops 1 | bytes 4194377 | solution.py:907
  262.0 16.8 %attend_backward.2 = (bf16[512,512]{1,0:T(8,128)(2,1)}, f32[1024,64]{1,0:T(8,128)}, f32[1024,64]{1,0:T(8,128)}) custom-call(s32[2]{0:T(128)S(1)} %get-tuple-element.273.pos_ref, s32[2]{0:T(128)S(1)} %get-tuple-element.274.starts_ref, bf16[512,512]{1,0:T(8,128)(2,1)} %get-tuple-element.275.q_ref, bf16[512,2048]{1,0:T(8,128)(2,1)} %get-tuple-element.276.out_ref, ...), custom_call_target="tpu_custom_call" | custom-call | flops 1 | bytes 1 | tf_op jit(solution)/shard_map/cond/branch_1_fun/attend_backward/pallas_call | solution.py:384
  280.0 10.4 %conditional.13 = (bf16[256,2048]{1,0:T(8,128)(2,1)}, bf16[1024,512]{1,0:T(8,128)(2,1)}, bf16[1024,512]{1,0:T(8,128)(2,1)}) conditional(s32[]{:T(128)} %convert_element_type.91, () %tuple.275, (bf16[256,2048]{1,0:T(8,128)(2,1)}, s32[]{:T(128)}, bf16[256,2048]{1,0:T(8,128)(2,1)}, bf16[256,2048]{1,0:T(8,128)(2,1)}, bf16[512,512]{1,0:T(8,128)(2,1)}, ...), branch_computations={%region_8.9_spmd, %region_9.10_spmd} | conditional | flops 8 | bytes 4194517 | solution.py:907
  283.0 7.4 %outer.5 = (bf16[1024,512]{1,0:T(8,128)(2,1)}, bf16[1024,512]{1,0:T(8,128)(2,1)}) custom-call(s32[8]{0:T(128)S(1)} %stack.118.order_ref, bf16[256,2048]{1,0:T(8,128)(2,1)} %get-tuple-element.295.refs_0_.refs_1_, bf16[256,2048]{1,0:T(8,128)(2,1)} %get-tuple-element.295.refs_0_.refs_1_, bf16[256,2048]{1,0:T(8,128)(2,1)} %get-tuple-element.296.refs_2_.refs_3_, ...), custom_call_target="tpu_custom_call" | custom-call | flops 1 | bytes 1 | tf_op jit(solution)/shard_map/cond/branch_1_fun/outer/pallas_call | solution.py:562
  301.5 3.0 by_rows.20
  304.5 21.0 %conditional.14 = ((bf16[512,512]{1,0:T(8,128)(2,1)}, f32[1024,64]{1,0:T(8,128)}, f32[1024,64]{1,0:T(8,128)})) conditional(s32[]{:T(128)} %convert_element_type.92, () %tuple.286, (s32[2]{0:T(128)S(1)}, s32[2]{0:T(128)S(1)}, bf16[512,512]{1,0:T(8,128)(2,1)}, bf16[512,2048]{1,0:T(8,128)(2,1)}, bf16[512,512]{1,0:T(8,128)(2,1)}, ...), branch_computations={%region_10.11_spmd, %region_11.12_spmd} | conditional | flops 1 | bytes 1048618 | solution.py:907
  304.5 20.8 %attend_backward.3 = (bf16[512,512]{1,0:T(8,128)(2,1)}, f32[1024,64]{1,0:T(8,128)}, f32[1024,64]{1,0:T(8,128)}) custom-call(s32[2]{0:T(128)S(1)} %get-tuple-element.305.pos_ref, s32[2]{0:T(128)S(1)} %get-tuple-element.306.starts_ref, bf16[512,512]{1,0:T(8,128)(2,1)} %get-tuple-element.307.q_ref, bf16[512,2048]{1,0:T(8,128)(2,1)} %get-tuple-element.308.out_ref, ...), custom_call_target="tpu_custom_call" | custom-call | flops 1 | bytes 1 | tf_op jit(solution)/shard_map/cond/branch_1_fun/attend_backward/pallas_call | solution.py:384
  325.5 11.7 %conditional.15 = (bf16[512,128]{1,0:T(8,128)(2,1)}, bf16[512,128]{1,0:T(8,128)(2,1)}, bf16[1024,640]{1,0:T(8,128)(2,1)}, bf16[1024,640]{1,0:T(8,128)(2,1)}) conditional(s32[]{:T(128)} %convert_element_type.93, () %tuple.290, (s32[4]{0:T(128)S(1)}, f32[1024,64]{1,0:T(8,128)}, f32[1024,64]{1,0:T(8,128)}, f32[1024,64]{1,0:T(8,128)}, ...), branch_computations={%region_12.13_spmd, %region_13.14_spmd} | conditional | flops 9 | bytes 2883624 | solution.py:907
  325.5 3.6 key_value_rows.1
  329.2 8.0 %outer.6 = (bf16[1024,640]{1,0:T(8,128)(2,1)}, bf16[1024,640]{1,0:T(8,128)(2,1)}) custom-call(s32[8]{0:T(128)S(1)} %stack.127.order_ref, bf16[512,2048]{1,0:T(8,128)(2,1)} %get-tuple-element.333.refs_0_.refs_1_, bf16[512,2048]{1,0:T(8,128)(2,1)} %get-tuple-element.333.refs_0_.refs_1_, bf16[512,512]{1,0:T(8,128)(2,1)S(1)} %copy-done.61, ...), custom_call_target="tpu_custom_call" | custom-call | flops 1 | bytes 1 | tf_op jit(solution)/shard_map/cond/branch_1_fun/outer/pallas_call | solution.py:562
  346.5 9.8 %conditional.16 = (bf16[256,2048]{1,0:T(8,128)(2,1)}) conditional(s32[]{:T(128)} %convert_element_type.95, () %tuple.302, (bf16[512,512]{1,0:T(8,128)(2,1)}, bf16[512,128]{1,0:T(8,128)(2,1)}, bf16[2048,512]{1,0:T(8,128)(2,1)}, bf16[2048,128]{1,0:T(8,128)(2,1)S(1)}) %tuple.380), branch_computations={%region_14.15_spmd, %region_15.16_spmd} | conditional | flops 2 | bytes 4194354 | solution.py:907
  346.5 4.2 row_shares.14
  361.1 8.2 %conditional.17 = (bf16[256,2048]{1,0:T(8,128)(2,1)}, bf16[256,2048]{1,0:T(8,128)(2,1)}) conditional(s32[]{:T(128)} %convert_element_type.97, () %tuple.308, (bf16[512,512]{1,0:T(8,128)(2,1)}, bf16[512,128]{1,0:T(8,128)(2,1)}, bf16[2048,512]{1,0:T(8,128)(2,1)}, bf16[2048,128]{1,0:T(8,128)(2,1)}) %tuple.379), branch_computations={%region_16.17_spmd, %region_17.18_spmd} | conditional | flops 1 | bytes 4194361 | solution.py:907
  361.1 4.9 %row_shares.15 = (bf16[256,2048]{1,0:T(8,128)(2,1)}, bf16[256,2048]{1,0:T(8,128)(2,1)S(1)}) custom-call(bf16[512,512]{1,0:T(8,128)(2,1)} %get-tuple-element.357.refs_0_, bf16[512,128]{1,0:T(8,128)(2,1)} %get-tuple-element.358.refs_1_, bf16[2048,512]{1,0:T(8,128)(2,1)} %get-tuple-element.359.refs_2_, bf16[2048,128]{1,0:T(8,128)(2,1)} %get-tuple-element.360.refs_3_), custom_call_target="tpu_custom_call" | custom-call | flops 1 | bytes 1 | tf_op jit(solution)/shard_map/cond/branch_1_fun/row_shares/pallas_call | solution.py:498
  372.0 21.3 %collective-permute-done.51.came_a.came_b = bf16[512,768]{1,0:T(8,128)(2,1)S(1)} collective-permute-done((bf16[512,768]{1,0:T(8,128)(2,1)}, bf16[512,768]{1,0:T(8,128)(2,1)S(1)}, u32[]{:S(2)}, u32[]{:S(2)}) %collective-permute-start.51) | collective-permute-done | bytes 786464 | tf_op jit(solution)/shard_map/ppermute | solution.py:717
  401.9 4.8 %by_rows.22 = f32[256,2048]{1,0:T(8,128)} custom-call(bf16[256,2048]{1,0:T(8,128)(2,1)} %get-tuple-element.890.refs_0_, bf16[256,2048]{1,0:T(8,128)(2,1)} %get-tuple-element.891.refs_1_, bf16[256,2048]{1,0:T(8,128)(2,1)} %collective-permute-done.49.refs_2_, bf16[256,2048]{1,0:T(8,128)(2,1)S(1)} %copy-done.6, f32[256,2048]{1,0:T(8,128)S(1)} %copy-done.20, ...), custom_call_target="tpu_custom_call" | custom-call | flops 1 | bytes 1 | tf_op jit(solution)/shard_map/by_rows/pallas_call | solution.py:183
  414.3 16.3 %collective-permute-done.52.refs_3_ = bf16[256,2048]{1,0:T(8,128)(2,1)S(1)} collective-permute-done((bf16[256,2048]{1,0:T(8,128)(2,1)}, bf16[256,2048]{1,0:T(8,128)(2,1)S(1)}, u32[]{:S(2)}, u32[]{:S(2)}) %collective-permute-start.52) | collective-permute-done | bytes 1048608 | tf_op jit(solution)/shard_map/ppermute | solution.py:659
  430.6 7.7 %collective-permute-done.53.refs_4_ = bf16[256,2048]{1,0:T(8,128)(2,1)} collective-permute-done((bf16[256,2048]{1,0:T(8,128)(2,1)S(1)}, bf16[256,2048]{1,0:T(8,128)(2,1)}, u32[]{:S(2)}, u32[]{:S(2)}) %collective-permute-start.53) | collective-permute-done | bytes 1048608 | tf_op jit(solution)/shard_map/ppermute | solution.py:717
  448.9 3.0 copy.36
  456.0 3.4 by_rows.23
  (337 shorter events, 156.3 us)
Async XLA Ops:
  0.6 24.4 %collective-permute-start.12 = (bf16[256,2048]{1,0:T(8,128)(2,1)}, bf16[256,2048]{1,0:T(8,128)(2,1)}, u32[]{:S(2)}, u32[]{:S(2)}) collective-permute-start(bf16[256,2048]{1,0:T(8,128)(2,1)} %refs_3_.5), channel_id=1, source_target_pairs={{0,2},{1,3},{2,0},{3,1},{4,6},{5,7},{6,4},{7,5},{8,10},{9,11},{10,... | collective-permute-start | bytes 3145736 | tf_op jit(solution)/shard_map/ppermute | solution.py:659
  1.9 16.2 %collective-permute-start.13 = (bf16[256,2048]{1,0:T(8,128)(2,1)}, bf16[256,2048]{1,0:T(8,128)(2,1)S(1)}, u32[]{:S(2)}, u32[]{:S(2)}) collective-permute-start(bf16[256,2048]{1,0:T(8,128)(2,1)} %refs_3_.5), channel_id=1, source_target_pairs={{0,1},{1,0},{2,3},{3,2},{4,5},{5,4},{6,7},{7,6},{8,9},{9,8},{10,11... | collective-permute-start | bytes 3145736 | tf_op jit(solution)/shard_map/ppermute | solution.py:659
  25.1 4.2 collective-permute-start.17
  26.6 24.8 %collective-permute-start.15 = (bf16[256,2048]{1,0:T(8,128)(2,1)S(1)}, bf16[256,2048]{1,0:T(8,128)(2,1)S(1)}, u32[]{:S(2)}, u32[]{:S(2)}) collective-permute-start(bf16[256,2048]{1,0:T(8,128)(2,1)S(1)} %copy-done), channel_id=1, source_target_pairs={{0,2},{1,3},{2,0},{3,1},{4,6},{5,7},{6,4},{7,5},{8,10},{9,11},{10,... | collective-permute-start | bytes 3145736 | tf_op jit(solution)/shard_map/ppermute | solution.py:659
  27.8 24.5 %collective-permute-start.16 = (bf16[256,2048]{1,0:T(8,128)(2,1)S(1)}, bf16[256,2048]{1,0:T(8,128)(2,1)S(1)}, u32[]{:S(2)}, u32[]{:S(2)}) collective-permute-start(bf16[256,2048]{1,0:T(8,128)(2,1)S(1)} %copy-done), channel_id=1, source_target_pairs={{0,8},{4,12},{8,0},{12,4},{16,24},{20,28},{24,16},{28,20},{1,9},{5... | collective-permute-start | bytes 3145736 | tf_op jit(solution)/shard_map/ppermute | solution.py:717
  28.1 26.0 %collective-permute-start.14 = (bf16[256,2048]{1,0:T(8,128)(2,1)S(1)}, bf16[256,2048]{1,0:T(8,128)(2,1)S(1)}, u32[]{:S(2)}, u32[]{:S(2)}) collective-permute-start(bf16[256,2048]{1,0:T(8,128)(2,1)S(1)} %copy-done), channel_id=1, source_target_pairs={{0,1},{1,0},{2,3},{3,2},{4,5},{5,4},{6,7},{7,6},{8,9},{9,8},{10,11... | collective-permute-start | bytes 3145736 | tf_op jit(solution)/shard_map/ppermute | solution.py:659
  49.6 4.0 collective-permute-start.20
  53.4 3.8 collective-permute-start.19
  53.4 24.2 %collective-permute-start.22 = (bf16[256,2048]{1,0:T(8,128)(2,1)S(1)}, bf16[256,2048]{1,0:T(8,128)(2,1)S(1)}, u32[]{:S(2)}, u32[]{:S(2)}) collective-permute-start(bf16[256,2048]{1,0:T(8,128)(2,1)S(1)} %collective-permute-done.15.refs_0_.refs_5_.refs_6_), channel_id=1, source_target_pairs={{0,8},{4,12},{8,0},{12,4},{16,24},{20,28},{24,16},{28,20},{1,9},{5... | collective-permute-start | bytes 3145736 | tf_op jit(solution)/shard_map/ppermute | solution.py:717
  53.8 25.1 %collective-permute-start.24 = (bf16[256,2048]{1,0:T(8,128)(2,1)S(1)}, bf16[256,2048]{1,0:T(8,128)(2,1)S(1)}, u32[]{:S(2)}, u32[]{:S(2)}) collective-permute-start(bf16[256,2048]{1,0:T(8,128)(2,1)S(1)} %by_rows.15), channel_id=1, source_target_pairs={{0,2},{1,3},{2,0},{3,1},{4,6},{5,7},{6,4},{7,5},{8,10},{9,11},{10,... | collective-permute-start | bytes 3145736 | tf_op jit(solution)/shard_map/ppermute | solution.py:659
  68.6 10.4 %collective-permute-start.21 = (bf16[256,2048]{1,0:T(8,128)(2,1)S(1)}, bf16[256,2048]{1,0:T(8,128)(2,1)S(1)}, u32[]{:S(2)}, u32[]{:S(2)}) collective-permute-start(bf16[256,2048]{1,0:T(8,128)(2,1)S(1)} %get-tuple-element.699), channel_id=1, source_target_pairs={{0,1},{1,0},{2,3},{3,2},{4,5},{5,4},{6,7},{7,6},{8,9},{9,8},{10,11... | collective-permute-start | bytes 3145736 | tf_op jit(solution)/shard_map/ppermute | solution.py:659
  84.7 24.9 %collective-permute-start.26 = (bf16[256,2048]{1,0:T(8,128)(2,1)}, bf16[256,2048]{1,0:T(8,128)(2,1)}, u32[]{:S(2)}, u32[]{:S(2)}) collective-permute-start(bf16[256,2048]{1,0:T(8,128)(2,1)} %get-tuple-element.712.refs_0_), channel_id=1, source_target_pairs={{0,2},{1,3},{2,0},{3,1},{4,6},{5,7},{6,4},{7,5},{8,10},{9,11},{10,... | collective-permute-start | bytes 3145736 | tf_op jit(solution)/shard_map/ppermute | solution.py:659
  85.0 24.7 %collective-permute-start.27 = (bf16[256,2048]{1,0:T(8,128)(2,1)}, bf16[256,2048]{1,0:T(8,128)(2,1)}, u32[]{:S(2)}, u32[]{:S(2)}) collective-permute-start(bf16[256,2048]{1,0:T(8,128)(2,1)} %get-tuple-element.712.refs_0_), channel_id=1, source_target_pairs={{0,8},{4,12},{8,0},{12,4},{16,24},{20,28},{24,16},{28,20},{1,9},{5... | collective-permute-start | bytes 3145736 | tf_op jit(solution)/shard_map/ppermute | solution.py:717
  109.6 4.8 %collective-permute-start.28 = (bf16[256,2048]{1,0:T(8,128)(2,1)}, bf16[256,2048]{1,0:T(8,128)(2,1)S(1)}, u32[]{:S(2)}, u32[]{:S(2)}) collective-permute-start(bf16[256,2048]{1,0:T(8,128)(2,1)} %collective-permute-done.26.refs_0_), channel_id=1, source_target_pairs={{0,1},{1,0},{2,3},{3,2},{4,5},{5,4},{6,7},{7,6},{8,9},{9,8},{10,11... | collective-permute-start | bytes 3145736 | tf_op jit(solution)/shard_map/ppermute | solution.py:659
  110.8 4.0 collective-permute-start.29
  113.0 13.6 %collective-permute-start.30 = (bf16[128,2048]{1,0:T(8,128)(2,1)S(1)}, bf16[128,2048]{1,0:T(8,128)(2,1)}, u32[]{:S(2)}, u32[]{:S(2)}) collective-permute-start(bf16[128,2048]{1,0:T(8,128)(2,1)S(1)} %slice.62), channel_id=1, source_target_pairs={{0,2},{1,3},{2,0},{3,1},{4,6},{5,7},{6,4},{7,5},{8,10},{9,11},{10,... | collective-permute-start | bytes 1572872 | tf_op jit(solution)/shard_map/ppermute | solution.py:659
  114.3 12.8 %collective-permute-start.31 = (bf16[128,2048]{1,0:T(8,128)(2,1)S(1)}, bf16[128,2048]{1,0:T(8,128)(2,1)}, u32[]{:S(2)}, u32[]{:S(2)}) collective-permute-start(bf16[128,2048]{1,0:T(8,128)(2,1)S(1)} %slice.63), channel_id=1, source_target_pairs={{0,8},{4,12},{8,0},{12,4},{16,24},{20,28},{24,16},{28,20},{1,9},{5... | collective-permute-start | bytes 1572872 | tf_op jit(solution)/shard_map/ppermute | solution.py:717
  152.4 62.8 %collective-permute-start.34 = (bf16[1024,768]{1,0:T(8,128)(2,1)}, bf16[1024,768]{1,0:T(8,128)(2,1)S(1)}, u32[]{:S(2)}, u32[]{:S(2)}) collective-permute-start(bf16[1024,768]{1,0:T(8,128)(2,1)} %get-tuple-element.762), channel_id=1, source_target_pairs={{0,4},{4,0},{8,12},{12,8},{16,20},{20,16},{24,28},{28,24},{1,5},{5... | collective-permute-start | bytes 4718600 | tf_op jit(solution)/shard_map/ppermute | solution.py:717
  162.0 22.4 %collective-permute-start = (bf16[256,2048]{1,0:T(8,128)(2,1)}, bf16[256,2048]{1,0:T(8,128)(2,1)}, u32[]{:S(2)}, u32[]{:S(2)}) collective-permute-start(bf16[256,2048]{1,0:T(8,128)(2,1)} %get-tuple-element.172), channel_id=1, source_target_pairs={{0,1},{1,0},{2,3},{3,2},{4,5},{5,4},{6,7},{7,6},{8,9},{9,8},{10,11... | collective-permute-start | bytes 3145736 | tf_op jit(solution)/shard_map/cond/branch_1_fun/ppermute | solution.py:659
  187.1 25.2 %collective-permute-start.35 = (bf16[256,2048]{1,0:T(8,128)(2,1)}, bf16[256,2048]{1,0:T(8,128)(2,1)}, u32[]{:S(2)}, u32[]{:S(2)}) collective-permute-start(bf16[256,2048]{1,0:T(8,128)(2,1)} %get-tuple-element.769), channel_id=1, source_target_pairs={{0,8},{4,12},{8,0},{12,4},{16,24},{20,28},{24,16},{28,20},{1,9},{5... | collective-permute-start | bytes 3145736 | tf_op jit(solution)/shard_map/ppermute | solution.py:717
  197.7 5.6 %collective-permute-start.1 = (bf16[256,2048]{1,0:T(8,128)(2,1)S(1)}, bf16[256,2048]{1,0:T(8,128)(2,1)}, u32[]{:S(2)}, u32[]{:S(2)}) collective-permute-start(bf16[256,2048]{1,0:T(8,128)(2,1)S(1)} %get-tuple-element.225), channel_id=1, source_target_pairs={{0,1},{1,0},{2,3},{3,2},{4,5},{5,4},{6,7},{7,6},{8,9},{9,8},{10,11... | collective-permute-start | bytes 3145736 | tf_op jit(solution)/shard_map/cond/branch_1_fun/ppermute | solution.py:659
  198.0 5.3 %collective-permute-start.2 = (bf16[256,2048]{1,0:T(8,128)(2,1)S(1)}, bf16[256,2048]{1,0:T(8,128)(2,1)}, u32[]{:S(2)}, u32[]{:S(2)}) collective-permute-start(bf16[256,2048]{1,0:T(8,128)(2,1)S(1)} %get-tuple-element.229), channel_id=1, source_target_pairs={{0,1},{1,0},{2,3},{3,2},{4,5},{5,4},{6,7},{7,6},{8,9},{9,8},{10,11... | collective-permute-start | bytes 3145736 | tf_op jit(solution)/shard_map/cond/branch_1_fun/ppermute | solution.py:659
  215.3 35.4 %collective-permute-start.37 = (bf16[1024,768]{1,0:T(8,128)(2,1)}, bf16[1024,768]{1,0:T(8,128)(2,1)}, u32[]{:S(2)}, u32[]{:S(2)}) collective-permute-start(bf16[1024,768]{1,0:T(8,128)(2,1)} %get-tuple-element.808), channel_id=1, source_target_pairs={{0,4},{4,0},{8,12},{12,8},{16,20},{20,16},{24,28},{28,24},{1,5},{5... | collective-permute-start | bytes 4718600 | tf_op jit(solution)/shard_map/ppermute | solution.py:717
  215.5 25.3 %collective-permute-start.39 = (bf16[256,2048]{1,0:T(8,128)(2,1)}, bf16[256,2048]{1,0:T(8,128)(2,1)}, u32[]{:S(2)}, u32[]{:S(2)}) collective-permute-start(bf16[256,2048]{1,0:T(8,128)(2,1)} %by_rows.17), channel_id=1, source_target_pairs={{0,8},{4,12},{8,0},{12,4},{16,24},{20,28},{24,16},{28,20},{1,9},{5... | collective-permute-start | bytes 3145736 | tf_op jit(solution)/shard_map/ppermute | solution.py:717
  215.8 25.0 %collective-permute-start.38 = (bf16[256,2048]{1,0:T(8,128)(2,1)}, bf16[256,2048]{1,0:T(8,128)(2,1)}, u32[]{:S(2)}, u32[]{:S(2)}) collective-permute-start(bf16[256,2048]{1,0:T(8,128)(2,1)} %by_rows.18), channel_id=1, source_target_pairs={{0,2},{1,3},{2,0},{3,1},{4,6},{5,7},{6,4},{7,5},{8,10},{9,11},{10,... | collective-permute-start | bytes 3145736 | tf_op jit(solution)/shard_map/ppermute | solution.py:659
  222.6 8.0 %collective-permute-start.4 = (bf16[256,2048]{1,0:T(8,128)(2,1)S(1)}, bf16[256,2048]{1,0:T(8,128)(2,1)S(1)}, u32[]{:S(2)}, u32[]{:S(2)}) collective-permute-start(bf16[256,2048]{1,0:T(8,128)(2,1)S(1)} %get-tuple-element.247), channel_id=1, source_target_pairs={{0,1},{1,0},{2,3},{3,2},{4,5},{5,4},{6,7},{7,6},{8,9},{9,8},{10,11... | collective-permute-start | bytes 3145736 | tf_op jit(solution)/shard_map/cond/branch_1_fun/ppermute | solution.py:659
  250.7 42.5 %collective-permute-start.40 = (bf16[1024,768]{1,0:T(8,128)(2,1)}, bf16[1024,768]{1,0:T(8,128)(2,1)S(1)}, u32[]{:S(2)}, u32[]{:S(2)}) collective-permute-start(bf16[1024,768]{1,0:T(8,128)(2,1)} %get-tuple-element.818), channel_id=1, source_target_pairs={{0,4},{4,0},{8,12},{12,8},{16,20},{20,16},{24,28},{28,24},{1,5},{5... | collective-permute-start | bytes 4718600 | tf_op jit(solution)/shard_map/ppermute | solution.py:717
  251.0 27.9 %collective-permute-start.42 = (bf16[256,2048]{1,0:T(8,128)(2,1)}, bf16[256,2048]{1,0:T(8,128)(2,1)S(1)}, u32[]{:S(2)}, u32[]{:S(2)}) collective-permute-start(bf16[256,2048]{1,0:T(8,128)(2,1)} %get-tuple-element.816), channel_id=1, source_target_pairs={{0,2},{1,3},{2,0},{3,1},{4,6},{5,7},{6,4},{7,5},{8,10},{9,11},{10,... | collective-permute-start | bytes 3145736 | tf_op jit(solution)/shard_map/ppermute | solution.py:659
  251.3 39.1 %collective-permute-start.41 = (bf16[512,768]{1,0:T(8,128)(2,1)}, bf16[512,768]{1,0:T(8,128)(2,1)}, u32[]{:S(2)}, u32[]{:S(2)}) collective-permute-start(bf16[512,768]{1,0:T(8,128)(2,1)} %get-tuple-element.793), channel_id=1, source_target_pairs={{0,16},{4,20},{8,24},{12,28},{16,0},{20,4},{24,8},{28,12},{1,17},{... | collective-permute-start | bytes 2359304 | tf_op jit(solution)/shard_map/ppermute | solution.py:717
  253.6 47.9 %collective-permute-start.36 = (bf16[256,2048]{1,0:T(8,128)(2,1)}, bf16[256,2048]{1,0:T(8,128)(2,1)}, u32[]{:S(2)}, u32[]{:S(2)}) collective-permute-start(bf16[256,2048]{1,0:T(8,128)(2,1)} %get-tuple-element.807), channel_id=1, source_target_pairs={{0,8},{4,12},{8,0},{12,4},{16,24},{20,28},{24,16},{28,20},{1,9},{5... | collective-permute-start | bytes 3145736 | tf_op jit(solution)/shard_map/ppermute | solution.py:717
  256.6 5.4 %collective-permute-start.8 = (bf16[256,2048]{1,0:T(8,128)(2,1)}, bf16[256,2048]{1,0:T(8,128)(2,1)}, u32[]{:S(2)}, u32[]{:S(2)}) collective-permute-start(bf16[256,2048]{1,0:T(8,128)(2,1)} %get-tuple-element.272.rest_0_), channel_id=1, source_target_pairs={{0,1},{1,0},{2,3},{3,2},{4,5},{5,4},{6,7},{7,6},{8,9},{9,8},{10,11... | collective-permute-start | bytes 3145736 | tf_op jit(solution)/shard_map/cond/branch_1_fun/ppermute | solution.py:659
  293.2 44.3 %collective-permute-start.46 = (bf16[1024,512]{1,0:T(8,128)(2,1)}, bf16[1024,512]{1,0:T(8,128)(2,1)S(1)}, u32[]{:S(2)}, u32[]{:S(2)}) collective-permute-start(bf16[1024,512]{1,0:T(8,128)(2,1)} %get-tuple-element.868), channel_id=1, source_target_pairs={{0,4},{4,0},{8,12},{12,8},{16,20},{20,16},{24,28},{28,24},{1,5},{5... | collective-permute-start | bytes 3145736 | tf_op jit(solution)/shard_map/ppermute | solution.py:717
  294.5 45.0 %collective-permute-start.45 = (bf16[256,768]{1,0:T(8,128)(2,1)}, bf16[256,768]{1,0:T(8,128)(2,1)}, u32[]{:S(2)}, u32[]{:S(2)}) collective-permute-start(bf16[256,768]{1,0:T(8,128)(2,1)} %get-tuple-element.843), channel_id=1, source_target_pairs={{0,8},{4,12},{8,0},{12,4},{16,24},{20,28},{24,16},{28,20},{1,9},{5... | collective-permute-start | bytes 1179656 | tf_op jit(solution)/shard_map/ppermute | solution.py:717
  295.7 47.3 %collective-permute-start.44 = (bf16[512,768]{1,0:T(8,128)(2,1)}, bf16[512,768]{1,0:T(8,128)(2,1)}, u32[]{:S(2)}, u32[]{:S(2)}) collective-permute-start(bf16[512,768]{1,0:T(8,128)(2,1)} %get-tuple-element.867), channel_id=1, source_target_pairs={{0,16},{4,20},{8,24},{12,28},{16,0},{20,4},{24,8},{28,12},{1,17},{... | collective-permute-start | bytes 2359304 | tf_op jit(solution)/shard_map/ppermute | solution.py:717
  337.2 32.1 %collective-permute-start.43 = (bf16[1024,640]{1,0:T(8,128)(2,1)}, bf16[1024,640]{1,0:T(8,128)(2,1)S(1)}, u32[]{:S(2)}, u32[]{:S(2)}) collective-permute-start(bf16[1024,640]{1,0:T(8,128)(2,1)} %get-tuple-element.866), channel_id=1, source_target_pairs={{0,4},{4,0},{8,12},{12,8},{16,20},{20,16},{24,28},{28,24},{1,5},{5... | collective-permute-start | bytes 3932168 | tf_op jit(solution)/shard_map/ppermute | solution.py:717
  345.0 14.8 %collective-permute-start.47 = (bf16[256,768]{1,0:T(8,128)(2,1)}, bf16[256,768]{1,0:T(8,128)(2,1)S(1)}, u32[]{:S(2)}, u32[]{:S(2)}) collective-permute-start(bf16[256,768]{1,0:T(8,128)(2,1)} %get-tuple-element.882), channel_id=1, source_target_pairs={{0,8},{4,12},{8,0},{12,4},{16,24},{20,28},{24,16},{28,20},{1,9},{5... | collective-permute-start | bytes 1179656 | tf_op jit(solution)/shard_map/ppermute | solution.py:717
  345.0 27.0 %collective-permute-start.50 = (bf16[512,512]{1,0:T(8,128)(2,1)}, bf16[512,512]{1,0:T(8,128)(2,1)}, u32[]{:S(2)}, u32[]{:S(2)}) collective-permute-start(bf16[512,512]{1,0:T(8,128)(2,1)} %get-tuple-element.874), channel_id=1, source_target_pairs={{0,8},{4,12},{8,0},{12,4},{16,24},{20,28},{24,16},{28,20},{1,9},{5... | collective-permute-start | bytes 1572872 | tf_op jit(solution)/shard_map/ppermute | solution.py:717
  350.7 4.4 collective-permute-start.10
  356.3 44.0 %collective-permute-start.49 = (bf16[256,2048]{1,0:T(8,128)(2,1)}, bf16[256,2048]{1,0:T(8,128)(2,1)}, u32[]{:S(2)}, u32[]{:S(2)}) collective-permute-start(bf16[256,2048]{1,0:T(8,128)(2,1)} %get-tuple-element.1054), channel_id=1, source_target_pairs={{0,2},{1,3},{2,0},{3,1},{4,6},{5,7},{6,4},{7,5},{8,10},{9,11},{10,... | collective-permute-start | bytes 3145736 | tf_op jit(solution)/shard_map/ppermute | solution.py:659
  357.4 35.9 %collective-permute-start.51 = (bf16[512,768]{1,0:T(8,128)(2,1)}, bf16[512,768]{1,0:T(8,128)(2,1)S(1)}, u32[]{:S(2)}, u32[]{:S(2)}) collective-permute-start(bf16[512,768]{1,0:T(8,128)(2,1)} %get-tuple-element.900), channel_id=1, source_target_pairs={{0,16},{4,20},{8,24},{12,28},{16,0},{20,4},{24,8},{28,12},{1,17},{... | collective-permute-start | bytes 2359304 | tf_op jit(solution)/shard_map/ppermute | solution.py:717
  371.5 35.2 %collective-permute-start.48 = (bf16[512,640]{1,0:T(8,128)(2,1)}, bf16[512,640]{1,0:T(8,128)(2,1)S(1)}, u32[]{:S(2)}, u32[]{:S(2)}) collective-permute-start(bf16[512,640]{1,0:T(8,128)(2,1)} %get-tuple-element.895), channel_id=1, source_target_pairs={{0,8},{4,12},{8,0},{12,4},{16,24},{20,28},{24,16},{28,20},{1,9},{5... | collective-permute-start | bytes 1966088 | tf_op jit(solution)/shard_map/ppermute | solution.py:717
  394.9 14.4 %collective-permute-start.55 = (bf16[256,768]{1,0:T(8,128)(2,1)}, bf16[256,768]{1,0:T(8,128)(2,1)}, u32[]{:S(2)}, u32[]{:S(2)}) collective-permute-start(bf16[256,768]{1,0:T(8,128)(2,1)} %get-tuple-element.904), channel_id=1, source_target_pairs={{0,8},{4,12},{8,0},{12,4},{16,24},{20,28},{24,16},{28,20},{1,9},{5... | collective-permute-start | bytes 1179656 | tf_op jit(solution)/shard_map/ppermute | solution.py:717
  397.5 16.6 %collective-permute-start.54 = (bf16[256,512]{1,0:T(8,128)(2,1)S(1)}, bf16[256,512]{1,0:T(8,128)(2,1)S(1)}, u32[]{:S(2)}, u32[]{:S(2)}) collective-permute-start(bf16[256,512]{1,0:T(8,128)(2,1)S(1)} %get-tuple-element.906), channel_id=1, source_target_pairs={{0,16},{4,20},{8,24},{12,28},{16,0},{20,4},{24,8},{28,12},{1,17},{... | collective-permute-start | bytes 786440 | tf_op jit(solution)/shard_map/ppermute | solution.py:717
  407.4 23.1 %collective-permute-start.52 = (bf16[256,2048]{1,0:T(8,128)(2,1)}, bf16[256,2048]{1,0:T(8,128)(2,1)S(1)}, u32[]{:S(2)}, u32[]{:S(2)}) collective-permute-start(bf16[256,2048]{1,0:T(8,128)(2,1)} %by_rows.20), channel_id=1, source_target_pairs={{0,2},{1,3},{2,0},{3,1},{4,6},{5,7},{6,4},{7,5},{8,10},{9,11},{10,... | collective-permute-start | bytes 3145736 | tf_op jit(solution)/shard_map/ppermute | solution.py:659
  408.0 30.3 %collective-permute-start.53 = (bf16[256,2048]{1,0:T(8,128)(2,1)S(1)}, bf16[256,2048]{1,0:T(8,128)(2,1)}, u32[]{:S(2)}, u32[]{:S(2)}) collective-permute-start(bf16[256,2048]{1,0:T(8,128)(2,1)S(1)} %copy-done.28), channel_id=1, source_target_pairs={{0,8},{4,12},{8,0},{12,4},{16,24},{20,28},{24,16},{28,20},{1,9},{5... | collective-permute-start | bytes 3145736 | tf_op jit(solution)/shard_map/ppermute | solution.py:717
  409.3 31.8 %collective-permute-start.56 = (bf16[256,640]{1,0:T(8,128)(2,1)}, bf16[256,640]{1,0:T(8,128)(2,1)S(1)}, u32[]{:S(2)}, u32[]{:S(2)}) collective-permute-start(bf16[256,640]{1,0:T(8,128)(2,1)} %get-tuple-element.915), channel_id=1, source_target_pairs={{0,16},{4,20},{8,24},{12,28},{16,0},{20,4},{24,8},{28,12},{1,17},{... | collective-permute-start | bytes 983048 | tf_op jit(solution)/shard_map/ppermute | solution.py:717
  446.8 6.2 %collective-permute-start.57 = (f32[2,2,64]{2,1,0:T(2,128)S(1)}, f32[2,2,64]{2,1,0:T(2,128)S(1)}, u32[]{:S(2)}, u32[]{:S(2)}) collective-permute-start(f32[2,2,64]{2,1,0:T(2,128)S(1)} %pad_maximum_fusion.7), channel_id=1, source_target_pairs={{0,2},{1,3},{2,0},{3,1},{4,6},{5,7},{6,4},{7,5},{8,10},{9,11},{10,... | collective-permute-start | bytes 3080 | tf_op jit(solution)/shard_map/ppermute | solution.py:1142
  453.0 7.9 %collective-permute-start.58 = (f32[2,64]{1,0:T(2,128)S(1)}, f32[2,64]{1,0:T(2,128)S(1)}, u32[]{:S(2)}, u32[]{:S(2)}) collective-permute-start(f32[2,64]{1,0:T(2,128)S(1)} %slice_bitcast_fusion), channel_id=1, source_target_pairs={{0,1},{1,0},{2,3},{3,2},{4,5},{5,4},{6,7},{7,6},{8,9},{9,8},{10,11... | collective-permute-start | bytes 1544 | tf_op jit(solution)/shard_map/ppermute | solution.py:1143
  (87 other events, 693.1 us)

commit v5 on v4

--- a/solution.py
+++ b/solution.py
@@ -1090,6 +1090,8 @@
     qkv.add().send()
     wout.receive()
     up.receive()
+    block_p = swap_pair(wait_for(block_p, up.came), dp_size)
+    block_c = swap_chip(wait_for(block_c, up.came))
     up.add().send()
     wout.add().send()
     d_in_came = order.after(d_in_came)
@@ -1102,8 +1104,6 @@
     )
     x_grad = order.done(x_grad)
     qkv.receive()
-    block_p = swap_pair(wait_for(block_p, qkv.came), dp_size)
-    block_c = swap_chip(wait_for(block_c, qkv.came))
     qkv.add().send()
     up.receive().add()
     wout.receive().add()

time: 469 us -> 471 us (level)
  starting transfers between devices: 46.5 us -> 55.7 us
    ppermute x34, waiting for transfers between devices: 56.9 us -> 40.6 us  [swapped(): return tuple((lax.ppermute(part, 'tensor', pairs) for part in parts))]
    ppermute x23, waiting for transfers between devices: 46.9 us -> 59.4 us  [exchange(): return lax.ppermute(value, 'dp', [(i, i ^ bit) for i in range(size)])]
    ppermute x23, starting transfers between devices: 16.7 us -> 22.6 us  [exchange(): return lax.ppermute(value, 'dp', [(i, i ^ bit) for i in range(size)])]
    unnamed x144 -> x134, local copies, waits for them, and re-layouts: 23.3 us -> 21.4 us
  transfers between devices with their start and end apart: 59 -> 59, of which waited for: 28 -> 29; matrix products, arithmetic and copies ran while one was open for 7% -> 7% of each run, Pallas kernels for 51% -> 50%
where the time goes in v5:
time: 471 us; the launch traced here: 464 us
  Pallas kernels  255 us (54%)
  waiting for transfers between devices  100 us (21%)
  starting transfers between devices  55.7 us (12%)
  local copies, waits for them, and re-layouts  25.7 us (5%)
  other arithmetic  25 us (5%)
    ppermute x23, waiting for transfers between devices, exchange(): return lax.ppermute(value, 'dp', [(i, i ^ bit) for i in range(size)])  59.4 us
    pallas_call x4, Pallas kernels, outer(): pl.pallas_call(functools.partial(outer_kernel, shape=[(len(lefts), len(ri...  49.1 us
    pallas_call x8, Pallas kernels, row_shares(): pl.pallas_call(functools.partial(share_kernel, count=len(lefts), transpos...  45.4 us
    ppermute x34, waiting for transfers between devices, swapped(): return tuple((lax.ppermute(part, 'tensor', pairs) for part in parts))  40.6 us
    pallas_call x2, Pallas kernels, attend_backward(): pl.pallas_call(functools.partial(backward_kernel, heads=heads, pics=pics,...  37.5 us
    pallas_call x12, Pallas kernels, by_rows(): pl.pallas_call(kernel, out_shape=shapes, name='by_rows', **params())  30.8 us
    ppermute x34, starting transfers between devices, swapped(): return tuple((lax.ppermute(part, 'tensor', pairs) for part in parts))  30.6 us
    pallas_call x3, Pallas kernels, feed_forward(): pl.pallas_call(feed_kernel, grid=(pl.cdiv(units, tile),), in_specs=[*(who...  27.6 us
  transfers between devices with their start and end apart: 59, of which 29 were waited for; matrix products, arithmetic and copies ran while one was open for 7% of the time, Pallas kernels for 50%

profile of v5, /device:TPU:9, one launch (start us, length us, event | category | flops | bytes accessed | tf_op | source)
XLA Modules:
  0.0 463.7 jit_solution(564580088399376891)
XLA Ops:
  11.8 6.2 %dynamic-slice_select_fusion.1 = (bf16[2048,768]{1,0:T(8,128)(2,1)}, bf16[2048,768]{1,0:T(8,128)(2,1)}) fusion(bf16[2048,1408]{1,0:T(8,128)(2,1)} %param.41, s32[]{:T(128)S(6)} %select_n.91, pred[768]{0:T(1024)(128)(4,1)S(1)} %fusion.2, bf16[2048,1408]{1,0:T(8,128)(2,1)} %param.40), kind=kLoop, calls=%fused_computation.1 | loop fusion | flops 1572864 | bytes 12583684 | tf_op jit(solution)/shard_map/jit(_where)/select_n | solution.py:816
  18.1 3.8 project.2
  29.2 6.2 %project.3 = (bf16[512,2048]{1,0:T(8,128)(2,1)}, bf16[512,512]{1,0:T(8,128)(2,1)S(1)}, bf16[512,64]{1,0:T(8,128)(2,1)S(1)}, bf16[512,64]{1,0:T(8,128)(2,1)S(1)}) custom-call(bf16[256,2048]{1,0:T(8,128)(2,1)} %collective-permute-done.12.refs_0_, bf16[256,2048]{1,0:T(8,128)(2,1)} %collective-permute-done.17.refs_1_, f32[1,2048]{1,0:T(1,128)S(1)} %bitcast.69, ...), custom_call_target="tpu_custom_call" | custom-call | flops 1 | bytes 1 | tf_op jit(solution)/shard_map/project/pallas_call | solution.py:117
  37.4 12.2 %attend_forward.2 = (bf16[512,512]{1,0:T(8,128)(2,1)}, f32[512,8]{1,0:T(8,128)}, bf16[256,2048]{1,0:T(8,128)(2,1)S(1)}, bf16[256,2048]{1,0:T(8,128)(2,1)S(1)}) custom-call(s32[2]{0:T(128)S(1)} %get-tuple-element.978.pos_ref, s32[2]{0:T(128)S(1)} %bitcast.74, bf16[512,512]{1,0:T(8,128)(2,1)S(1)} %get-tuple-element.674.q_ref, ...), custom_call_target="tpu_custom_call" | custom-call | flops 1 | bytes 1 | tf_op jit(solution)/shard_map/attend_forward/pallas_call | solution.py:272
  57.2 11.3 %attend_forward.3 = (bf16[512,512]{1,0:T(8,128)(2,1)}, f32[512,8]{1,0:T(8,128)}, bf16[256,2048]{1,0:T(8,128)(2,1)S(1)}, bf16[256,2048]{1,0:T(8,128)(2,1)S(1)}) custom-call(s32[2]{0:T(128)S(1)} %get-tuple-element.977.pos_ref, s32[2]{0:T(128)S(1)} %bitcast.75, bf16[512,512]{1,0:T(8,128)(2,1)S(1)} %copy-done.68, bf16[1024,64]{1,0:T(8,128)(2,1)S(1)} %pad_maximum_fusion.5.k_ref, ...), custom_call_target="tpu_custom_call" | custom-call | flops 1 | bytes 1 | tf_op jit(solution)/shard_map/attend_forward/pallas_call | solution.py:272
  69.0 4.1 hidden_back.3.refs_2_
  73.1 4.5 collective-permute-done.22.refs_0_.refs_14_.refs_15_
  87.2 8.0 %feed_forward.3 = (bf16[512,768]{1,0:T(8,128)(2,1)}, bf16[512,768]{1,0:T(8,128)(2,1)}, bf16[512,768]{1,0:T(8,128)(2,1)}) custom-call(bf16[256,2048]{1,0:T(8,128)(2,1)} %get-tuple-element.712.refs_0_, bf16[256,2048]{1,0:T(8,128)(2,1)S(1)} %collective-permute-done.25.refs_1_, bf16[512,768]{1,0:T(8,128)(2,1)S(1)} %hidden_back.3.refs_2_, ...), custom_call_target="tpu_custom_call" | custom-call | flops 1 | bytes 1 | tf_op jit(solution)/shard_map/feed_forward/pallas_call | solution.py:466
  95.3 4.2 hidden_back.4.refs_4_
  102.0 7.6 %collective-permute-done.26.refs_0_ = bf16[256,2048]{1,0:T(8,128)(2,1)} collective-permute-done((bf16[256,2048]{1,0:T(8,128)(2,1)}, bf16[256,2048]{1,0:T(8,128)(2,1)}, u32[]{:S(2)}, u32[]{:S(2)}) %collective-permute-start.26) | collective-permute-done | bytes 1048608 | tf_op jit(solution)/shard_map/ppermute | solution.py:659
  114.8 11.7 %feed_forward.4 = (bf16[1024,768]{1,0:T(8,128)(2,1)}, bf16[1024,768]{1,0:T(8,128)(2,1)}, bf16[1024,768]{1,0:T(8,128)(2,1)}) custom-call(bf16[256,2048]{1,0:T(8,128)(2,1)} %collective-permute-done.26.refs_0_, bf16[256,2048]{1,0:T(8,128)(2,1)S(1)} %collective-permute-done.28.refs_1_, bf16[256,2048]{1,0:T(8,128)(2,1)} %collective-permute-done.27.refs_2_, ...), custom_call_target="tpu_custom_call" | custom-call | flops 1 | bytes 1 | tf_op jit(solution)/shard_map/feed_forward/pallas_call | solution.py:466
  132.5 7.9 %feed_forward.5 = (bf16[512,768]{1,0:T(8,128)(2,1)S(1)}, bf16[512,768]{1,0:T(8,128)(2,1)}, bf16[512,768]{1,0:T(8,128)(2,1)}) custom-call(bf16[128,2048]{1,0:T(8,128)(2,1)} %collective-permute-done.30.refs_0_, bf16[128,2048]{1,0:T(8,128)(2,1)} %collective-permute-done.31.refs_1_, bf16[128,2048]{1,0:T(8,128)(2,1)} %collective-permute-done.32.refs_2_, ...), custom_call_target="tpu_custom_call" | custom-call | flops 1 | bytes 1 | tf_op jit(solution)/shard_map/feed_forward/pallas_call | solution.py:466
  140.4 12.0 %outer.7 = (bf16[1024,768]{1,0:T(8,128)(2,1)}, bf16[1024,768]{1,0:T(8,128)(2,1)}) custom-call(s32[8]{0:T(128)S(1)} %stack.168.order_ref, bf16[256,2048]{1,0:T(8,128)(2,1)S(1)} %copy-done, bf16[256,2048]{1,0:T(8,128)(2,1)S(1)} %copy-done, bf16[256,2048]{1,0:T(8,128)(2,1)S(1)} %copy-done.8, bf16[256,2048]{1,0:T(8,128)(2,1)S(1)} %copy-done.8, ...), custom_call_target="tpu_custom_call" | custom-call | flops 1 | bytes 1 | tf_op jit(solution)/shard_map/outer/pallas_call | solution.py:562
  153.8 33.4 %conditional.9 = (bf16[256,2048]{1,0:T(8,128)(2,1)}, bf16[1024,768]{1,0:T(8,128)(2,1)}, bf16[1024,768]{1,0:T(8,128)(2,1)}, bf16[1024,768]{1,0:T(8,128)(2,1)}, bf16[1024,768]{1,0:T(8,128)(2,1)}) conditional(s32[]{:T(128)} %convert_element_type.87, () %tuple.247, (bf16[512,768]{1,0:T(8,128)(2,1)}, bf16[512,768]{1,0:T(8,128)(2,1)}, ...), branch_computations={%region_0.1_spmd, %region_1.2_spmd} | conditional | flops 10 | bytes 12583199 | solution.py:907
  153.8 7.3 %row_shares.8 = (bf16[256,2048]{1,0:T(8,128)(2,1)S(1)}, bf16[256,2048]{1,0:T(8,128)(2,1)}) custom-call(bf16[512,768]{1,0:T(8,128)(2,1)} %get-tuple-element.202.refs_0_.refs_24_, bf16[512,768]{1,0:T(8,128)(2,1)} %get-tuple-element.203.refs_1_.refs_25_, bf16[2048,768]{1,0:T(8,128)(2,1)} %get-tuple-element.167.refs_2_, bf16[2048,768]{1,0:T(8,128)(2,1)} %get-tuple-element.168.refs_3_), custom_call_target="tpu_custom_call" | custom-call | flops 1 | bytes 1 | tf_op jit(solution)/shard_map/cond/branch_1_fun/row_shares/pallas_call | solution.py:498
  162.8 21.7 %outer.4 = (bf16[1024,768]{1,0:T(8,128)(2,1)}, bf16[1024,768]{1,0:T(8,128)(2,1)}, bf16[1024,768]{1,0:T(8,128)(2,1)}, bf16[1024,768]{1,0:T(8,128)(2,1)}) custom-call(s32[8]{0:T(128)S(1)} %stack.109.order_ref, bf16[256,2048]{1,0:T(8,128)(2,1)} %get-tuple-element.188.refs_0_.refs_1_, bf16[256,2048]{1,0:T(8,128)(2,1)} %get-tuple-element.188.refs_0_.refs_1_, ...), custom_call_target="tpu_custom_call" | custom-call | flops 1 | bytes 1 | tf_op jit(solution)/shard_map/cond/branch_1_fun/outer/pallas_call | solution.py:562
  187.5 18.3 %conditional.10 = (bf16[256,2048]{1,0:T(8,128)(2,1)S(1)}, bf16[256,2048]{1,0:T(8,128)(2,1)}, bf16[256,2048]{1,0:T(8,128)(2,1)S(1)}, bf16[256,2048]{1,0:T(8,128)(...) conditional(s32[]{:T(128)} %convert_element_type.88, () %tuple.251, (bf16[1024,768]{1,0:T(8,128)(2,1)}, ...), branch_computations={%region_2.3_spmd, %region_3.4_spmd} | conditional | flops 2 | bytes 44040472 | solution.py:907
  187.6 10.2 %row_shares.9 = (bf16[256,2048]{1,0:T(8,128)(2,1)S(1)}, bf16[256,2048]{1,0:T(8,128)(2,1)S(1)}, bf16[256,2048]{1,0:T(8,128)(2,1)S(1)}, bf16[256,2048]{1,0:T(8,128)(2,1)S(1)}) custom-call(bf16[1024,768]{1,0:T(8,128)(2,1)} %get-tuple-element.216.refs_0_, bf16[1024,768]{1,0:T(8,128)(2,1)} %get-tuple-element.217.refs_1_, ...), custom_call_target="tpu_custom_call" | custom-call | flops 1 | bytes 1 | tf_op jit(solution)/shard_map/cond/branch_1_fun/row_shares/pallas_call | solution.py:498
  198.3 4.8 %row_shares.10 = (bf16[256,2048]{1,0:T(8,128)(2,1)}, bf16[256,2048]{1,0:T(8,128)(2,1)S(1)}) custom-call(bf16[512,768]{1,0:T(8,128)(2,1)S(1)} %copy-done.65, bf16[512,768]{1,0:T(8,128)(2,1)S(1)} %copy-done.66, bf16[2048,768]{1,0:T(8,128)(2,1)S(1)} %copy-done.40, bf16[2048,768]{1,0:T(8,128)(2,1)S(1)} %copy-done.39), custom_call_target="tpu_custom_call" | custom-call | flops 1 | bytes 1 | tf_op jit(solution)/shard_map/cond/branch_1_fun/row_shares/pallas_call | solution.py:498
  208.4 4.0 collective-permute-done.35.refs_2_
  218.0 22.9 %conditional.11 = (bf16[256,2048]{1,0:T(8,128)(2,1)}, bf16[256,2048]{1,0:T(8,128)(2,1)}, bf16[256,2048]{1,0:T(8,128)(2,1)}, bf16[256,2048]{1,0:T(8,128)(2,1)}, b...) conditional(s32[]{:T(128)} %convert_element_type.89, () %tuple.260, ...), branch_computations={%region_4.5_spmd, %region_5.6_spmd} | conditional | flops 4 | bytes 32506132 | solution.py:907
  218.0 4.5 row_shares.11
  224.2 6.3 %row_shares.12 = (bf16[256,2048]{1,0:T(8,128)(2,1)}, bf16[256,2048]{1,0:T(8,128)(2,1)S(1)}, bf16[256,2048]{1,0:T(8,128)(2,1)}, bf16[256,2048]{1,0:T(8,128)(2,1)S(1)}) custom-call(bf16[1024,768]{1,0:T(8,128)(2,1)} %get-tuple-element.249.refs_0_, bf16[768,2048]{1,0:T(8,128)(2,1)S(1)} %copy-done.37), custom_call_target="tpu_custom_call" | custom-call | flops 1 | bytes 1 | tf_op jit(solution)/shard_map/cond/branch_1_fun/row_shares/pallas_call | solution.py:498
  231.9 3.3 row_shares.13
  240.9 5.3 %by_rows.19 = (f32[256,2048]{1,0:T(8,128)S(1)}, bf16[256,2048]{1,0:T(8,128)(2,1)}) custom-call(bf16[256,2048]{1,0:T(8,128)(2,1)S(1)} %copy-done.61, bf16[256,2048]{1,0:T(8,128)(2,1)} %get-tuple-element.786.refs_1_, bf16[256,2048]{1,0:T(8,128)(2,1)} %collective-permute-done.38.refs_2_, bf16[256,2048]{1,0:T(8,128)(2,1)} %collective-permute-done.39.refs_3_, ...), custom_call_target="tpu_custom_call" | custom-call | flops 1 | bytes 1 | tf_op jit(solution)/shard_map/by_rows/pallas_call | solution.py:183
  246.2 4.6 collective-permute-done.37.came_a.came_b
  256.5 22.4 %conditional.12 = (bf16[256,2048]{1,0:T(8,128)(2,1)}, bf16[512,512]{1,0:T(8,128)(2,1)}, f32[1024,64]{1,0:T(8,128)}, f32[1024,64]{1,0:T(8,128)}) conditional(s32[]{:T(128)} %convert_element_type.90, () %tuple.270, (bf16[256,2048]{1,0:T(8,128)(2,1)}, s32[2]{0:T(128)S(1)}, s32[2]{0:T(128)S(1)}, bf16[512,512]{1,0:T(8,128)(2,1)}, ...), branch_computations={%region_6.7_spmd, %region_7.8_spmd} | conditional | flops 1 | bytes 4194377 | solution.py:907
  262.0 16.8 %attend_backward.2 = (bf16[512,512]{1,0:T(8,128)(2,1)}, f32[1024,64]{1,0:T(8,128)}, f32[1024,64]{1,0:T(8,128)}) custom-call(s32[2]{0:T(128)S(1)} %get-tuple-element.273.pos_ref, s32[2]{0:T(128)S(1)} %get-tuple-element.274.starts_ref, bf16[512,512]{1,0:T(8,128)(2,1)} %get-tuple-element.275.q_ref, bf16[512,2048]{1,0:T(8,128)(2,1)} %get-tuple-element.276.out_ref, ...), custom_call_target="tpu_custom_call" | custom-call | flops 1 | bytes 1 | tf_op jit(solution)/shard_map/cond/branch_1_fun/attend_backward/pallas_call | solution.py:384
  280.0 10.4 %conditional.13 = (bf16[256,2048]{1,0:T(8,128)(2,1)}, bf16[1024,512]{1,0:T(8,128)(2,1)}, bf16[1024,512]{1,0:T(8,128)(2,1)}) conditional(s32[]{:T(128)} %convert_element_type.91, () %tuple.275, (bf16[256,2048]{1,0:T(8,128)(2,1)}, s32[]{:T(128)}, bf16[256,2048]{1,0:T(8,128)(2,1)}, bf16[256,2048]{1,0:T(8,128)(2,1)}, bf16[512,512]{1,0:T(8,128)(2,1)}, ...), branch_computations={%region_8.9_spmd, %region_9.10_spmd} | conditional | flops 8 | bytes 4194517 | solution.py:907
  283.0 7.4 %outer.5 = (bf16[1024,512]{1,0:T(8,128)(2,1)}, bf16[1024,512]{1,0:T(8,128)(2,1)}) custom-call(s32[8]{0:T(128)S(1)} %stack.118.order_ref, bf16[256,2048]{1,0:T(8,128)(2,1)} %get-tuple-element.295.refs_0_.refs_1_, bf16[256,2048]{1,0:T(8,128)(2,1)} %get-tuple-element.295.refs_0_.refs_1_, bf16[256,2048]{1,0:T(8,128)(2,1)} %get-tuple-element.296.refs_2_.refs_3_, ...), custom_call_target="tpu_custom_call" | custom-call | flops 1 | bytes 1 | tf_op jit(solution)/shard_map/cond/branch_1_fun/outer/pallas_call | solution.py:562
  304.5 21.0 %conditional.14 = ((bf16[512,512]{1,0:T(8,128)(2,1)}, f32[1024,64]{1,0:T(8,128)}, f32[1024,64]{1,0:T(8,128)})) conditional(s32[]{:T(128)} %convert_element_type.92, () %tuple.288, (s32[2]{0:T(128)S(1)}, s32[2]{0:T(128)S(1)}, bf16[512,512]{1,0:T(8,128)(2,1)}, bf16[512,2048]{1,0:T(8,128)(2,1)}, bf16[512,512]{1,0:T(8,128)(2,1)}, ...), branch_computations={%region_10.11_spmd, %region_11.12_spmd} | conditional | flops 1 | bytes 1048618 | solution.py:907
  304.5 20.8 %attend_backward.3 = (bf16[512,512]{1,0:T(8,128)(2,1)}, f32[1024,64]{1,0:T(8,128)}, f32[1024,64]{1,0:T(8,128)}) custom-call(s32[2]{0:T(128)S(1)} %get-tuple-element.305.pos_ref, s32[2]{0:T(128)S(1)} %get-tuple-element.306.starts_ref, bf16[512,512]{1,0:T(8,128)(2,1)} %get-tuple-element.307.q_ref, bf16[512,2048]{1,0:T(8,128)(2,1)} %get-tuple-element.308.out_ref, ...), custom_call_target="tpu_custom_call" | custom-call | flops 1 | bytes 1 | tf_op jit(solution)/shard_map/cond/branch_1_fun/attend_backward/pallas_call | solution.py:384
  325.5 11.7 %conditional.15 = (bf16[512,128]{1,0:T(8,128)(2,1)}, bf16[512,128]{1,0:T(8,128)(2,1)}, bf16[1024,640]{1,0:T(8,128)(2,1)}, bf16[1024,640]{1,0:T(8,128)(2,1)}) conditional(s32[]{:T(128)} %convert_element_type.93, () %tuple.292, (s32[4]{0:T(128)S(1)}, f32[1024,64]{1,0:T(8,128)}, f32[1024,64]{1,0:T(8,128)}, f32[1024,64]{1,0:T(8,128)}, ...), branch_computations={%region_12.13_spmd, %region_13.14_spmd} | conditional | flops 9 | bytes 2883624 | solution.py:907
  325.5 3.6 key_value_rows.1
  329.2 8.0 %outer.6 = (bf16[1024,640]{1,0:T(8,128)(2,1)}, bf16[1024,640]{1,0:T(8,128)(2,1)}) custom-call(s32[8]{0:T(128)S(1)} %stack.127.order_ref, bf16[512,2048]{1,0:T(8,128)(2,1)} %get-tuple-element.333.refs_0_.refs_1_, bf16[512,2048]{1,0:T(8,128)(2,1)} %get-tuple-element.333.refs_0_.refs_1_, bf16[512,512]{1,0:T(8,128)(2,1)S(1)} %copy-done.56, ...), custom_call_target="tpu_custom_call" | custom-call | flops 1 | bytes 1 | tf_op jit(solution)/shard_map/cond/branch_1_fun/outer/pallas_call | solution.py:562
  348.7 10.2 %conditional.16 = (bf16[256,2048]{1,0:T(8,128)(2,1)}) conditional(s32[]{:T(128)} %convert_element_type.95, () %tuple.303, (bf16[512,512]{1,0:T(8,128)(2,1)}, bf16[512,128]{1,0:T(8,128)(2,1)}, bf16[2048,512]{1,0:T(8,128)(2,1)}, bf16[2048,128]{1,0:T(8,128)(2,1)}) %tuple.379), branch_computations={%region_14.15_spmd, %region_15.16_spmd} | conditional | flops 2 | bytes 4194354 | solution.py:907
  348.7 4.2 row_shares.14
  360.1 8.9 %collective-permute-done.49 = bf16[256,768]{1,0:T(8,128)(2,1)S(1)} collective-permute-done((bf16[256,768]{1,0:T(8,128)(2,1)}, bf16[256,768]{1,0:T(8,128)(2,1)S(1)}, u32[]{:S(2)}, u32[]{:S(2)}) %collective-permute-start.49) | collective-permute-done | bytes 393248 | tf_op jit(solution)/shard_map/ppermute | solution.py:717
  370.3 11.8 %conditional.17 = (bf16[256,2048]{1,0:T(8,128)(2,1)}, bf16[256,2048]{1,0:T(8,128)(2,1)}) conditional(s32[]{:T(128)} %convert_element_type.97, () %tuple.309, (bf16[512,512]{1,0:T(8,128)(2,1)}, bf16[512,128]{1,0:T(8,128)(2,1)}, bf16[2048,512]{1,0:T(8,128)(2,1)}, bf16[2048,128]{1,0:T(8,128)(2,1)}) %tuple.380), branch_computations={%region_16.17_spmd, %region_17.18_spmd} | conditional | flops 1 | bytes 4194361 | solution.py:907
  370.3 4.8 %row_shares.15 = (bf16[256,2048]{1,0:T(8,128)(2,1)}, bf16[256,2048]{1,0:T(8,128)(2,1)S(1)}) custom-call(bf16[512,512]{1,0:T(8,128)(2,1)} %get-tuple-element.357.refs_0_, bf16[512,128]{1,0:T(8,128)(2,1)} %get-tuple-element.358.refs_1_, bf16[2048,512]{1,0:T(8,128)(2,1)} %get-tuple-element.359.refs_2_, bf16[2048,128]{1,0:T(8,128)(2,1)} %get-tuple-element.360.refs_3_), custom_call_target="tpu_custom_call" | custom-call | flops 1 | bytes 1 | tf_op jit(solution)/shard_map/cond/branch_1_fun/row_shares/pallas_call | solution.py:498
  375.1 4.5 collective-permute-start.11
  396.8 4.8 %by_rows.22 = f32[256,2048]{1,0:T(8,128)} custom-call(bf16[256,2048]{1,0:T(8,128)(2,1)} %get-tuple-element.891.refs_0_, bf16[256,2048]{1,0:T(8,128)(2,1)} %get-tuple-element.892.refs_1_, bf16[256,2048]{1,0:T(8,128)(2,1)} %collective-permute-done.55.refs_2_, bf16[256,2048]{1,0:T(8,128)(2,1)S(1)} %copy-done.6, f32[256,2048]{1,0:T(8,128)S(1)} %copy-done.20, ...), custom_call_target="tpu_custom_call" | custom-call | flops 1 | bytes 1 | tf_op jit(solution)/shard_map/by_rows/pallas_call | solution.py:183
  401.6 4.4 collective-permute-done.54.came_a.came_b
  406.2 4.4 collective-permute-start.56
  410.6 10.9 %collective-permute-done.53 = bf16[256,768]{1,0:T(8,128)(2,1)} collective-permute-done((bf16[256,768]{1,0:T(8,128)(2,1)}, bf16[256,768]{1,0:T(8,128)(2,1)}, u32[]{:S(2)}, u32[]{:S(2)}) %collective-permute-start.53) | collective-permute-done | bytes 393248 | tf_op jit(solution)/shard_map/ppermute | solution.py:717
  426.2 13.9 %collective-permute-done.52.came_ref = bf16[256,512]{1,0:T(8,128)(2,1)S(1)} collective-permute-done((bf16[256,512]{1,0:T(8,128)(2,1)S(1)}, bf16[256,512]{1,0:T(8,128)(2,1)S(1)}, u32[]{:S(2)}, u32[]{:S(2)}) %collective-permute-start.52) | collective-permute-done | bytes 262176 | tf_op jit(solution)/shard_map/ppermute | solution.py:717
  440.3 3.6 collective-permute-done.51.refs_4_
  458.0 3.4 by_rows.23
  (327 shorter events, 165.1 us)
Async XLA Ops:
  0.6 24.4 %collective-permute-start.12 = (bf16[256,2048]{1,0:T(8,128)(2,1)}, bf16[256,2048]{1,0:T(8,128)(2,1)}, u32[]{:S(2)}, u32[]{:S(2)}) collective-permute-start(bf16[256,2048]{1,0:T(8,128)(2,1)} %refs_3_.5), channel_id=1, source_target_pairs={{0,2},{1,3},{2,0},{3,1},{4,6},{5,7},{6,4},{7,5},{8,10},{9,11},{10,... | collective-permute-start | bytes 3145736 | tf_op jit(solution)/shard_map/ppermute | solution.py:659
  1.9 16.1 %collective-permute-start.13 = (bf16[256,2048]{1,0:T(8,128)(2,1)}, bf16[256,2048]{1,0:T(8,128)(2,1)S(1)}, u32[]{:S(2)}, u32[]{:S(2)}) collective-permute-start(bf16[256,2048]{1,0:T(8,128)(2,1)} %refs_3_.5), channel_id=1, source_target_pairs={{0,1},{1,0},{2,3},{3,2},{4,5},{5,4},{6,7},{7,6},{8,9},{9,8},{10,11... | collective-permute-start | bytes 3145736 | tf_op jit(solution)/shard_map/ppermute | solution.py:659
  25.1 4.2 collective-permute-start.17
  26.6 24.8 %collective-permute-start.15 = (bf16[256,2048]{1,0:T(8,128)(2,1)S(1)}, bf16[256,2048]{1,0:T(8,128)(2,1)S(1)}, u32[]{:S(2)}, u32[]{:S(2)}) collective-permute-start(bf16[256,2048]{1,0:T(8,128)(2,1)S(1)} %copy-done), channel_id=1, source_target_pairs={{0,2},{1,3},{2,0},{3,1},{4,6},{5,7},{6,4},{7,5},{8,10},{9,11},{10,... | collective-permute-start | bytes 3145736 | tf_op jit(solution)/shard_map/ppermute | solution.py:659
  27.8 24.5 %collective-permute-start.16 = (bf16[256,2048]{1,0:T(8,128)(2,1)S(1)}, bf16[256,2048]{1,0:T(8,128)(2,1)S(1)}, u32[]{:S(2)}, u32[]{:S(2)}) collective-permute-start(bf16[256,2048]{1,0:T(8,128)(2,1)S(1)} %copy-done), channel_id=1, source_target_pairs={{0,8},{4,12},{8,0},{12,4},{16,24},{20,28},{24,16},{28,20},{1,9},{5... | collective-permute-start | bytes 3145736 | tf_op jit(solution)/shard_map/ppermute | solution.py:717
  28.1 26.0 %collective-permute-start.14 = (bf16[256,2048]{1,0:T(8,128)(2,1)S(1)}, bf16[256,2048]{1,0:T(8,128)(2,1)S(1)}, u32[]{:S(2)}, u32[]{:S(2)}) collective-permute-start(bf16[256,2048]{1,0:T(8,128)(2,1)S(1)} %copy-done), channel_id=1, source_target_pairs={{0,1},{1,0},{2,3},{3,2},{4,5},{5,4},{6,7},{7,6},{8,9},{9,8},{10,11... | collective-permute-start | bytes 3145736 | tf_op jit(solution)/shard_map/ppermute | solution.py:659
  49.6 4.0 collective-permute-start.20
  53.4 24.2 %collective-permute-start.22 = (bf16[256,2048]{1,0:T(8,128)(2,1)S(1)}, bf16[256,2048]{1,0:T(8,128)(2,1)S(1)}, u32[]{:S(2)}, u32[]{:S(2)}) collective-permute-start(bf16[256,2048]{1,0:T(8,128)(2,1)S(1)} %collective-permute-done.15.refs_0_.refs_5_.refs_6_), channel_id=1, source_target_pairs={{0,8},{4,12},{8,0},{12,4},{16,24},{20,28},{24,16},{28,20},{1,9},{5... | collective-permute-start | bytes 3145736 | tf_op jit(solution)/shard_map/ppermute | solution.py:717
  53.8 25.1 %collective-permute-start.24 = (bf16[256,2048]{1,0:T(8,128)(2,1)S(1)}, bf16[256,2048]{1,0:T(8,128)(2,1)S(1)}, u32[]{:S(2)}, u32[]{:S(2)}) collective-permute-start(bf16[256,2048]{1,0:T(8,128)(2,1)S(1)} %by_rows.15), channel_id=1, source_target_pairs={{0,2},{1,3},{2,0},{3,1},{4,6},{5,7},{6,4},{7,5},{8,10},{9,11},{10,... | collective-permute-start | bytes 3145736 | tf_op jit(solution)/shard_map/ppermute | solution.py:659
  68.6 10.4 %collective-permute-start.21 = (bf16[256,2048]{1,0:T(8,128)(2,1)S(1)}, bf16[256,2048]{1,0:T(8,128)(2,1)S(1)}, u32[]{:S(2)}, u32[]{:S(2)}) collective-permute-start(bf16[256,2048]{1,0:T(8,128)(2,1)S(1)} %get-tuple-element.699), channel_id=1, source_target_pairs={{0,1},{1,0},{2,3},{3,2},{4,5},{5,4},{6,7},{7,6},{8,9},{9,8},{10,11... | collective-permute-start | bytes 3145736 | tf_op jit(solution)/shard_map/ppermute | solution.py:659
  84.7 24.9 %collective-permute-start.26 = (bf16[256,2048]{1,0:T(8,128)(2,1)}, bf16[256,2048]{1,0:T(8,128)(2,1)}, u32[]{:S(2)}, u32[]{:S(2)}) collective-permute-start(bf16[256,2048]{1,0:T(8,128)(2,1)} %get-tuple-element.712.refs_0_), channel_id=1, source_target_pairs={{0,2},{1,3},{2,0},{3,1},{4,6},{5,7},{6,4},{7,5},{8,10},{9,11},{10,... | collective-permute-start | bytes 3145736 | tf_op jit(solution)/shard_map/ppermute | solution.py:659
  85.0 24.7 %collective-permute-start.27 = (bf16[256,2048]{1,0:T(8,128)(2,1)}, bf16[256,2048]{1,0:T(8,128)(2,1)}, u32[]{:S(2)}, u32[]{:S(2)}) collective-permute-start(bf16[256,2048]{1,0:T(8,128)(2,1)} %get-tuple-element.712.refs_0_), channel_id=1, source_target_pairs={{0,8},{4,12},{8,0},{12,4},{16,24},{20,28},{24,16},{28,20},{1,9},{5... | collective-permute-start | bytes 3145736 | tf_op jit(solution)/shard_map/ppermute | solution.py:717
  109.6 4.8 %collective-permute-start.28 = (bf16[256,2048]{1,0:T(8,128)(2,1)}, bf16[256,2048]{1,0:T(8,128)(2,1)S(1)}, u32[]{:S(2)}, u32[]{:S(2)}) collective-permute-start(bf16[256,2048]{1,0:T(8,128)(2,1)} %collective-permute-done.26.refs_0_), channel_id=1, source_target_pairs={{0,1},{1,0},{2,3},{3,2},{4,5},{5,4},{6,7},{7,6},{8,9},{9,8},{10,11... | collective-permute-start | bytes 3145736 | tf_op jit(solution)/shard_map/ppermute | solution.py:659
  110.8 4.0 collective-permute-start.29
  113.0 13.6 %collective-permute-start.30 = (bf16[128,2048]{1,0:T(8,128)(2,1)S(1)}, bf16[128,2048]{1,0:T(8,128)(2,1)}, u32[]{:S(2)}, u32[]{:S(2)}) collective-permute-start(bf16[128,2048]{1,0:T(8,128)(2,1)S(1)} %slice.62), channel_id=1, source_target_pairs={{0,2},{1,3},{2,0},{3,1},{4,6},{5,7},{6,4},{7,5},{8,10},{9,11},{10,... | collective-permute-start | bytes 1572872 | tf_op jit(solution)/shard_map/ppermute | solution.py:659
  114.3 12.8 %collective-permute-start.31 = (bf16[128,2048]{1,0:T(8,128)(2,1)S(1)}, bf16[128,2048]{1,0:T(8,128)(2,1)}, u32[]{:S(2)}, u32[]{:S(2)}) collective-permute-start(bf16[128,2048]{1,0:T(8,128)(2,1)S(1)} %slice.63), channel_id=1, source_target_pairs={{0,8},{4,12},{8,0},{12,4},{16,24},{20,28},{24,16},{28,20},{1,9},{5... | collective-permute-start | bytes 1572872 | tf_op jit(solution)/shard_map/ppermute | solution.py:717
  152.4 62.9 %collective-permute-start.34 = (bf16[1024,768]{1,0:T(8,128)(2,1)}, bf16[1024,768]{1,0:T(8,128)(2,1)S(1)}, u32[]{:S(2)}, u32[]{:S(2)}) collective-permute-start(bf16[1024,768]{1,0:T(8,128)(2,1)} %get-tuple-element.762), channel_id=1, source_target_pairs={{0,4},{4,0},{8,12},{12,8},{16,20},{20,16},{24,28},{28,24},{1,5},{5... | collective-permute-start | bytes 4718600 | tf_op jit(solution)/shard_map/ppermute | solution.py:717
  162.0 22.4 %collective-permute-start = (bf16[256,2048]{1,0:T(8,128)(2,1)}, bf16[256,2048]{1,0:T(8,128)(2,1)}, u32[]{:S(2)}, u32[]{:S(2)}) collective-permute-start(bf16[256,2048]{1,0:T(8,128)(2,1)} %get-tuple-element.172), channel_id=1, source_target_pairs={{0,1},{1,0},{2,3},{3,2},{4,5},{5,4},{6,7},{7,6},{8,9},{9,8},{10,11... | collective-permute-start | bytes 3145736 | tf_op jit(solution)/shard_map/cond/branch_1_fun/ppermute | solution.py:659
  187.2 25.2 %collective-permute-start.35 = (bf16[256,2048]{1,0:T(8,128)(2,1)}, bf16[256,2048]{1,0:T(8,128)(2,1)}, u32[]{:S(2)}, u32[]{:S(2)}) collective-permute-start(bf16[256,2048]{1,0:T(8,128)(2,1)} %get-tuple-element.769), channel_id=1, source_target_pairs={{0,8},{4,12},{8,0},{12,4},{16,24},{20,28},{24,16},{28,20},{1,9},{5... | collective-permute-start | bytes 3145736 | tf_op jit(solution)/shard_map/ppermute | solution.py:717
  197.7 5.6 %collective-permute-start.1 = (bf16[256,2048]{1,0:T(8,128)(2,1)S(1)}, bf16[256,2048]{1,0:T(8,128)(2,1)}, u32[]{:S(2)}, u32[]{:S(2)}) collective-permute-start(bf16[256,2048]{1,0:T(8,128)(2,1)S(1)} %get-tuple-element.225), channel_id=1, source_target_pairs={{0,1},{1,0},{2,3},{3,2},{4,5},{5,4},{6,7},{7,6},{8,9},{9,8},{10,11... | collective-permute-start | bytes 3145736 | tf_op jit(solution)/shard_map/cond/branch_1_fun/ppermute | solution.py:659
  198.1 5.3 %collective-permute-start.2 = (bf16[256,2048]{1,0:T(8,128)(2,1)S(1)}, bf16[256,2048]{1,0:T(8,128)(2,1)}, u32[]{:S(2)}, u32[]{:S(2)}) collective-permute-start(bf16[256,2048]{1,0:T(8,128)(2,1)S(1)} %get-tuple-element.229), channel_id=1, source_target_pairs={{0,1},{1,0},{2,3},{3,2},{4,5},{5,4},{6,7},{7,6},{8,9},{9,8},{10,11... | collective-permute-start | bytes 3145736 | tf_op jit(solution)/shard_map/cond/branch_1_fun/ppermute | solution.py:659
  215.3 35.4 %collective-permute-start.37 = (bf16[1024,768]{1,0:T(8,128)(2,1)}, bf16[1024,768]{1,0:T(8,128)(2,1)}, u32[]{:S(2)}, u32[]{:S(2)}) collective-permute-start(bf16[1024,768]{1,0:T(8,128)(2,1)} %get-tuple-element.808), channel_id=1, source_target_pairs={{0,4},{4,0},{8,12},{12,8},{16,20},{20,16},{24,28},{28,24},{1,5},{5... | collective-permute-start | bytes 4718600 | tf_op jit(solution)/shard_map/ppermute | solution.py:717
  215.5 25.3 %collective-permute-start.39 = (bf16[256,2048]{1,0:T(8,128)(2,1)}, bf16[256,2048]{1,0:T(8,128)(2,1)}, u32[]{:S(2)}, u32[]{:S(2)}) collective-permute-start(bf16[256,2048]{1,0:T(8,128)(2,1)} %by_rows.17), channel_id=1, source_target_pairs={{0,8},{4,12},{8,0},{12,4},{16,24},{20,28},{24,16},{28,20},{1,9},{5... | collective-permute-start | bytes 3145736 | tf_op jit(solution)/shard_map/ppermute | solution.py:717
  215.8 25.0 %collective-permute-start.38 = (bf16[256,2048]{1,0:T(8,128)(2,1)}, bf16[256,2048]{1,0:T(8,128)(2,1)}, u32[]{:S(2)}, u32[]{:S(2)}) collective-permute-start(bf16[256,2048]{1,0:T(8,128)(2,1)} %by_rows.18), channel_id=1, source_target_pairs={{0,2},{1,3},{2,0},{3,1},{4,6},{5,7},{6,4},{7,5},{8,10},{9,11},{10,... | collective-permute-start | bytes 3145736 | tf_op jit(solution)/shard_map/ppermute | solution.py:659
  222.5 8.0 %collective-permute-start.4 = (bf16[256,2048]{1,0:T(8,128)(2,1)S(1)}, bf16[256,2048]{1,0:T(8,128)(2,1)S(1)}, u32[]{:S(2)}, u32[]{:S(2)}) collective-permute-start(bf16[256,2048]{1,0:T(8,128)(2,1)S(1)} %get-tuple-element.247), channel_id=1, source_target_pairs={{0,1},{1,0},{2,3},{3,2},{4,5},{5,4},{6,7},{7,6},{8,9},{9,8},{10,11... | collective-permute-start | bytes 3145736 | tf_op jit(solution)/shard_map/cond/branch_1_fun/ppermute | solution.py:659
  250.8 42.5 %collective-permute-start.40 = (bf16[1024,768]{1,0:T(8,128)(2,1)}, bf16[1024,768]{1,0:T(8,128)(2,1)S(1)}, u32[]{:S(2)}, u32[]{:S(2)}) collective-permute-start(bf16[1024,768]{1,0:T(8,128)(2,1)} %get-tuple-element.818), channel_id=1, source_target_pairs={{0,4},{4,0},{8,12},{12,8},{16,20},{20,16},{24,28},{28,24},{1,5},{5... | collective-permute-start | bytes 4718600 | tf_op jit(solution)/shard_map/ppermute | solution.py:717
  251.0 27.9 %collective-permute-start.42 = (bf16[256,2048]{1,0:T(8,128)(2,1)}, bf16[256,2048]{1,0:T(8,128)(2,1)S(1)}, u32[]{:S(2)}, u32[]{:S(2)}) collective-permute-start(bf16[256,2048]{1,0:T(8,128)(2,1)} %get-tuple-element.816), channel_id=1, source_target_pairs={{0,2},{1,3},{2,0},{3,1},{4,6},{5,7},{6,4},{7,5},{8,10},{9,11},{10,... | collective-permute-start | bytes 3145736 | tf_op jit(solution)/shard_map/ppermute | solution.py:659
  251.2 39.1 %collective-permute-start.41 = (bf16[512,768]{1,0:T(8,128)(2,1)}, bf16[512,768]{1,0:T(8,128)(2,1)}, u32[]{:S(2)}, u32[]{:S(2)}) collective-permute-start(bf16[512,768]{1,0:T(8,128)(2,1)} %get-tuple-element.793), channel_id=1, source_target_pairs={{0,16},{4,20},{8,24},{12,28},{16,0},{20,4},{24,8},{28,12},{1,17},{... | collective-permute-start | bytes 2359304 | tf_op jit(solution)/shard_map/ppermute | solution.py:717
  253.5 47.9 %collective-permute-start.36 = (bf16[256,2048]{1,0:T(8,128)(2,1)}, bf16[256,2048]{1,0:T(8,128)(2,1)}, u32[]{:S(2)}, u32[]{:S(2)}) collective-permute-start(bf16[256,2048]{1,0:T(8,128)(2,1)} %get-tuple-element.807), channel_id=1, source_target_pairs={{0,8},{4,12},{8,0},{12,4},{16,24},{20,28},{24,16},{28,20},{1,9},{5... | collective-permute-start | bytes 3145736 | tf_op jit(solution)/shard_map/ppermute | solution.py:717
  256.5 5.4 %collective-permute-start.8 = (bf16[256,2048]{1,0:T(8,128)(2,1)}, bf16[256,2048]{1,0:T(8,128)(2,1)}, u32[]{:S(2)}, u32[]{:S(2)}) collective-permute-start(bf16[256,2048]{1,0:T(8,128)(2,1)} %get-tuple-element.272.rest_0_), channel_id=1, source_target_pairs={{0,1},{1,0},{2,3},{3,2},{4,5},{5,4},{6,7},{7,6},{8,9},{9,8},{10,11... | collective-permute-start | bytes 3145736 | tf_op jit(solution)/shard_map/cond/branch_1_fun/ppermute | solution.py:659
  293.2 44.3 %collective-permute-start.45 = (bf16[1024,512]{1,0:T(8,128)(2,1)}, bf16[1024,512]{1,0:T(8,128)(2,1)S(1)}, u32[]{:S(2)}, u32[]{:S(2)}) collective-permute-start(bf16[1024,512]{1,0:T(8,128)(2,1)} %get-tuple-element.853), channel_id=1, source_target_pairs={{0,4},{4,0},{8,12},{12,8},{16,20},{20,16},{24,28},{28,24},{1,5},{5... | collective-permute-start | bytes 3145736 | tf_op jit(solution)/shard_map/ppermute | solution.py:717
  294.5 45.0 %collective-permute-start.44 = (bf16[256,768]{1,0:T(8,128)(2,1)}, bf16[256,768]{1,0:T(8,128)(2,1)}, u32[]{:S(2)}, u32[]{:S(2)}) collective-permute-start(bf16[256,768]{1,0:T(8,128)(2,1)} %get-tuple-element.843), channel_id=1, source_target_pairs={{0,8},{4,12},{8,0},{12,4},{16,24},{20,28},{24,16},{28,20},{1,9},{5... | collective-permute-start | bytes 1179656 | tf_op jit(solution)/shard_map/ppermute | solution.py:717
  295.7 47.3 %collective-permute-start.43 = (bf16[512,768]{1,0:T(8,128)(2,1)}, bf16[512,768]{1,0:T(8,128)(2,1)}, u32[]{:S(2)}, u32[]{:S(2)}) collective-permute-start(bf16[512,768]{1,0:T(8,128)(2,1)} %get-tuple-element.852), channel_id=1, source_target_pairs={{0,16},{4,20},{8,24},{12,28},{16,0},{20,4},{24,8},{28,12},{1,17},{... | collective-permute-start | bytes 2359304 | tf_op jit(solution)/shard_map/ppermute | solution.py:717
  337.2 44.8 %collective-permute-start.48 = (bf16[1024,640]{1,0:T(8,128)(2,1)}, bf16[1024,640]{1,0:T(8,128)(2,1)S(1)}, u32[]{:S(2)}, u32[]{:S(2)}) collective-permute-start(bf16[1024,640]{1,0:T(8,128)(2,1)} %get-tuple-element.869), channel_id=1, source_target_pairs={{0,4},{4,0},{8,12},{12,8},{16,20},{20,16},{24,28},{28,24},{1,5},{5... | collective-permute-start | bytes 3932168 | tf_op jit(solution)/shard_map/ppermute | solution.py:717
  345.0 24.0 %collective-permute-start.49 = (bf16[256,768]{1,0:T(8,128)(2,1)}, bf16[256,768]{1,0:T(8,128)(2,1)S(1)}, u32[]{:S(2)}, u32[]{:S(2)}) collective-permute-start(bf16[256,768]{1,0:T(8,128)(2,1)} %get-tuple-element.883), channel_id=1, source_target_pairs={{0,8},{4,12},{8,0},{12,4},{16,24},{20,28},{24,16},{28,20},{1,9},{5... | collective-permute-start | bytes 1179656 | tf_op jit(solution)/shard_map/ppermute | solution.py:717
  345.0 41.4 %collective-permute-start.47 = (bf16[512,512]{1,0:T(8,128)(2,1)}, bf16[512,512]{1,0:T(8,128)(2,1)}, u32[]{:S(2)}, u32[]{:S(2)}) collective-permute-start(bf16[512,512]{1,0:T(8,128)(2,1)} %get-tuple-element.874), channel_id=1, source_target_pairs={{0,8},{4,12},{8,0},{12,4},{16,24},{20,28},{24,16},{28,20},{1,9},{5... | collective-permute-start | bytes 1572872 | tf_op jit(solution)/shard_map/ppermute | solution.py:717
  346.4 39.9 %collective-permute-start.46 = (bf16[512,768]{1,0:T(8,128)(2,1)}, bf16[512,768]{1,0:T(8,128)(2,1)S(1)}, u32[]{:S(2)}, u32[]{:S(2)}) collective-permute-start(bf16[512,768]{1,0:T(8,128)(2,1)} %get-tuple-element.879), channel_id=1, source_target_pairs={{0,16},{4,20},{8,24},{12,28},{16,0},{20,4},{24,8},{28,12},{1,17},{... | collective-permute-start | bytes 2359304 | tf_op jit(solution)/shard_map/ppermute | solution.py:717
  353.0 4.7 %collective-permute-start.10 = (bf16[256,2048]{1,0:T(8,128)(2,1)S(1)}, bf16[256,2048]{1,0:T(8,128)(2,1)S(1)}, u32[]{:S(2)}, u32[]{:S(2)}) collective-permute-start(bf16[256,2048]{1,0:T(8,128)(2,1)S(1)} %get-tuple-element.352), channel_id=1, source_target_pairs={{0,1},{1,0},{2,3},{3,2},{4,5},{5,4},{6,7},{7,6},{8,9},{9,8},{10,11... | collective-permute-start | bytes 3145736 | tf_op jit(solution)/shard_map/cond/branch_1_fun/ppermute | solution.py:659
  358.9 33.6 %collective-permute-start.55 = (bf16[256,2048]{1,0:T(8,128)(2,1)}, bf16[256,2048]{1,0:T(8,128)(2,1)}, u32[]{:S(2)}, u32[]{:S(2)}) collective-permute-start(bf16[256,2048]{1,0:T(8,128)(2,1)} %get-tuple-element.1054), channel_id=1, source_target_pairs={{0,2},{1,3},{2,0},{3,1},{4,6},{5,7},{6,4},{7,5},{8,10},{9,11},{10,... | collective-permute-start | bytes 3145736 | tf_op jit(solution)/shard_map/ppermute | solution.py:659
  375.1 6.9 %collective-permute-start.11 = (bf16[256,2048]{1,0:T(8,128)(2,1)S(1)}, bf16[256,2048]{1,0:T(8,128)(2,1)}, u32[]{:S(2)}, u32[]{:S(2)}) collective-permute-start(bf16[256,2048]{1,0:T(8,128)(2,1)S(1)} %get-tuple-element.364), channel_id=1, source_target_pairs={{0,1},{1,0},{2,3},{3,2},{4,5},{5,4},{6,7},{7,6},{8,9},{9,8},{10,11... | collective-permute-start | bytes 3145736 | tf_op jit(solution)/shard_map/cond/branch_1_fun/ppermute | solution.py:659
  384.2 21.8 %collective-permute-start.54 = (bf16[512,640]{1,0:T(8,128)(2,1)}, bf16[512,640]{1,0:T(8,128)(2,1)S(1)}, u32[]{:S(2)}, u32[]{:S(2)}) collective-permute-start(bf16[512,640]{1,0:T(8,128)(2,1)} %get-tuple-element.896), channel_id=1, source_target_pairs={{0,8},{4,12},{8,0},{12,4},{16,24},{20,28},{24,16},{28,20},{1,9},{5... | collective-permute-start | bytes 1966088 | tf_op jit(solution)/shard_map/ppermute | solution.py:717
  387.9 33.5 %collective-permute-start.53 = (bf16[256,768]{1,0:T(8,128)(2,1)}, bf16[256,768]{1,0:T(8,128)(2,1)}, u32[]{:S(2)}, u32[]{:S(2)}) collective-permute-start(bf16[256,768]{1,0:T(8,128)(2,1)} %get-tuple-element.906), channel_id=1, source_target_pairs={{0,8},{4,12},{8,0},{12,4},{16,24},{20,28},{24,16},{28,20},{1,9},{5... | collective-permute-start | bytes 1179656 | tf_op jit(solution)/shard_map/ppermute | solution.py:717
  390.2 50.1 %collective-permute-start.50 = (bf16[256,2048]{1,0:T(8,128)(2,1)}, bf16[256,2048]{1,0:T(8,128)(2,1)S(1)}, u32[]{:S(2)}, u32[]{:S(2)}) collective-permute-start(bf16[256,2048]{1,0:T(8,128)(2,1)} %copy-done.32), channel_id=1, source_target_pairs={{0,2},{1,3},{2,0},{3,1},{4,6},{5,7},{6,4},{7,5},{8,10},{9,11},{10,... | collective-permute-start | bytes 3145736 | tf_op jit(solution)/shard_map/ppermute | solution.py:659
  391.2 52.8 %collective-permute-start.51 = (bf16[256,2048]{1,0:T(8,128)(2,1)}, bf16[256,2048]{1,0:T(8,128)(2,1)}, u32[]{:S(2)}, u32[]{:S(2)}) collective-permute-start(bf16[256,2048]{1,0:T(8,128)(2,1)} %copy-done.27), channel_id=1, source_target_pairs={{0,8},{4,12},{8,0},{12,4},{16,24},{20,28},{24,16},{28,20},{1,9},{5... | collective-permute-start | bytes 3145736 | tf_op jit(solution)/shard_map/ppermute | solution.py:717
  392.5 47.6 %collective-permute-start.52 = (bf16[256,512]{1,0:T(8,128)(2,1)S(1)}, bf16[256,512]{1,0:T(8,128)(2,1)S(1)}, u32[]{:S(2)}, u32[]{:S(2)}) collective-permute-start(bf16[256,512]{1,0:T(8,128)(2,1)S(1)} %get-tuple-element.909), channel_id=1, source_target_pairs={{0,16},{4,20},{8,24},{12,28},{16,0},{20,4},{24,8},{28,12},{1,17},{... | collective-permute-start | bytes 786440 | tf_op jit(solution)/shard_map/ppermute | solution.py:717
  406.2 41.0 %collective-permute-start.56 = (bf16[256,640]{1,0:T(8,128)(2,1)S(1)}, bf16[256,640]{1,0:T(8,128)(2,1)S(1)}, u32[]{:S(2)}, u32[]{:S(2)}) collective-permute-start(bf16[256,640]{1,0:T(8,128)(2,1)S(1)} %get-tuple-element.915), channel_id=1, source_target_pairs={{0,16},{4,20},{8,24},{12,28},{16,0},{20,4},{24,8},{28,12},{1,17},{... | collective-permute-start | bytes 983048 | tf_op jit(solution)/shard_map/ppermute | solution.py:717
  450.1 5.3 %collective-permute-start.57 = (f32[2,2,64]{2,1,0:T(2,128)S(1)}, f32[2,2,64]{2,1,0:T(2,128)S(1)}, u32[]{:S(2)}, u32[]{:S(2)}) collective-permute-start(f32[2,2,64]{2,1,0:T(2,128)S(1)} %pad_maximum_fusion.7), channel_id=1, source_target_pairs={{0,2},{1,3},{2,0},{3,1},{4,6},{5,7},{6,4},{7,5},{8,10},{9,11},{10,... | collective-permute-start | bytes 3080 | tf_op jit(solution)/shard_map/ppermute | solution.py:1142
  455.5 7.4 %collective-permute-start.58 = (f32[2,64]{1,0:T(2,128)S(1)}, f32[2,64]{1,0:T(2,128)S(1)}, u32[]{:S(2)}, u32[]{:S(2)}) collective-permute-start(f32[2,64]{1,0:T(2,128)S(1)} %slice_bitcast_fusion), channel_id=1, source_target_pairs={{0,1},{1,0},{2,3},{3,2},{4,5},{5,4},{6,7},{7,6},{8,9},{9,8},{10,11... | collective-permute-start | bytes 1544 | tf_op jit(solution)/shard_map/ppermute | solution.py:1143
  (82 other events, 674.7 us)

commit v6 on v4

--- a/solution.py
+++ b/solution.py
@@ -1139,7 +1139,8 @@
     ) / own_features(norm_mlp)
     gains = jnp.stack([gain_attn, gain_mlp]).reshape(2, 4, share // 4)
     gains = jnp.stack([lax.dynamic_index_in_dim(gains, place ^ m, 1, False) for m in range(4)])
-    gains = gains[:2] + lax.ppermute(gains[2:], "tensor", [(i, i ^ 2) for i in range(4)])
+    came = lax.ppermute(gains[2:], "tensor", [(i, i ^ 2) for i in range(4)])
+    gains = gains[:2] + wait_for(came, block_out)
     gains = gains[0] + lax.ppermute(gains[1], "tensor", [(i, i ^ 1) for i in range(4)])
 
     return (

time: 469 us -> 469 us (level)
  no operation moved by 1% of the time
where the time goes in v6:
time: 469 us; the launch traced here: 462 us
  Pallas kernels  256 us (55%)
  waiting for transfers between devices  104 us (22%)
  starting transfers between devices  46.5 us (10%)
  local copies, waits for them, and re-layouts  27.7 us (6%)
  other arithmetic  25 us (5%)
    ppermute x34, waiting for transfers between devices, swapped(): return tuple((lax.ppermute(part, 'tensor', pairs) for part in parts))  56.9 us
    pallas_call x4, Pallas kernels, outer(): pl.pallas_call(functools.partial(outer_kernel, shape=[(len(lefts), len(ri...  49.1 us
    ppermute x23, waiting for transfers between devices, exchange(): return lax.ppermute(value, 'dp', [(i, i ^ bit) for i in range(size)])  46.9 us
    pallas_call x8, Pallas kernels, row_shares(): pl.pallas_call(functools.partial(share_kernel, count=len(lefts), transpos...  45.3 us
    pallas_call x2, Pallas kernels, attend_backward(): pl.pallas_call(functools.partial(backward_kernel, heads=heads, pics=pics,...  37.5 us
    pallas_call x12, Pallas kernels, by_rows(): pl.pallas_call(kernel, out_shape=shapes, name='by_rows', **params())  31.8 us
    pallas_call x3, Pallas kernels, feed_forward(): pl.pallas_call(feed_kernel, grid=(pl.cdiv(units, tile),), in_specs=[*(who...  27.5 us
    ppermute x34, starting transfers between devices, swapped(): return tuple((lax.ppermute(part, 'tensor', pairs) for part in parts))  26 us
  transfers between devices with their start and end apart: 59, of which 28 were waited for; matrix products, arithmetic and copies ran while one was open for 7% of the time, Pallas kernels for 51%

profile of v6, /device:TPU:9, one launch (start us, length us, event | category | flops | bytes accessed | tf_op | source)
XLA Modules:
  0.0 461.6 jit_solution(15999449180358250886)
XLA Ops:
  11.8 6.3 %dynamic-slice_select_fusion.1 = (bf16[2048,768]{1,0:T(8,128)(2,1)}, bf16[2048,768]{1,0:T(8,128)(2,1)}) fusion(bf16[2048,1408]{1,0:T(8,128)(2,1)} %param.41, s32[]{:T(128)S(6)} %select_n.91, pred[768]{0:T(1024)(128)(4,1)S(1)} %fusion.2, bf16[2048,1408]{1,0:T(8,128)(2,1)} %param.40), kind=kLoop, calls=%fused_computation.1 | loop fusion | flops 1572864 | bytes 12583684 | tf_op jit(solution)/shard_map/jit(_where)/select_n | solution.py:816
  18.1 3.8 project.2
  22.0 3.1 collective-permute-done.12.refs_0_
  29.2 6.2 %project.3 = (bf16[512,2048]{1,0:T(8,128)(2,1)}, bf16[512,512]{1,0:T(8,128)(2,1)S(1)}, bf16[512,64]{1,0:T(8,128)(2,1)S(1)}, bf16[512,64]{1,0:T(8,128)(2,1)S(1)}) custom-call(bf16[256,2048]{1,0:T(8,128)(2,1)} %collective-permute-done.12.refs_0_, bf16[256,2048]{1,0:T(8,128)(2,1)} %collective-permute-done.17.refs_1_, f32[1,2048]{1,0:T(1,128)S(1)} %bitcast.69, ...), custom_call_target="tpu_custom_call" | custom-call | flops 1 | bytes 1 | tf_op jit(solution)/shard_map/project/pallas_call | solution.py:117
  37.4 12.2 %attend_forward.2 = (bf16[512,512]{1,0:T(8,128)(2,1)}, f32[512,8]{1,0:T(8,128)}, bf16[256,2048]{1,0:T(8,128)(2,1)S(1)}, bf16[256,2048]{1,0:T(8,128)(2,1)S(1)}) custom-call(s32[2]{0:T(128)S(1)} %get-tuple-element.980.pos_ref, s32[2]{0:T(128)S(1)} %bitcast.74, bf16[512,512]{1,0:T(8,128)(2,1)S(1)} %get-tuple-element.675.q_ref, ...), custom_call_target="tpu_custom_call" | custom-call | flops 1 | bytes 1 | tf_op jit(solution)/shard_map/attend_forward/pallas_call | solution.py:272
  57.2 11.4 %attend_forward.3 = (bf16[512,512]{1,0:T(8,128)(2,1)}, f32[512,8]{1,0:T(8,128)}, bf16[256,2048]{1,0:T(8,128)(2,1)S(1)}, bf16[256,2048]{1,0:T(8,128)(2,1)S(1)}) custom-call(s32[2]{0:T(128)S(1)} %get-tuple-element.979.pos_ref, s32[2]{0:T(128)S(1)} %bitcast.75, bf16[512,512]{1,0:T(8,128)(2,1)S(1)} %copy-done.73, bf16[1024,64]{1,0:T(8,128)(2,1)S(1)} %pad_maximum_fusion.5.k_ref, ...), custom_call_target="tpu_custom_call" | custom-call | flops 1 | bytes 1 | tf_op jit(solution)/shard_map/attend_forward/pallas_call | solution.py:272
  69.0 4.1 hidden_back.3.refs_2_
  73.1 4.5 collective-permute-done.22.refs_0_.refs_14_.refs_15_
  81.3 3.1 by_rows.16
  87.2 8.0 %feed_forward.3 = (bf16[512,768]{1,0:T(8,128)(2,1)}, bf16[512,768]{1,0:T(8,128)(2,1)}, bf16[512,768]{1,0:T(8,128)(2,1)}) custom-call(bf16[256,2048]{1,0:T(8,128)(2,1)} %get-tuple-element.713.refs_0_, bf16[256,2048]{1,0:T(8,128)(2,1)S(1)} %collective-permute-done.25.refs_1_, bf16[512,768]{1,0:T(8,128)(2,1)S(1)} %hidden_back.3.refs_2_, ...), custom_call_target="tpu_custom_call" | custom-call | flops 1 | bytes 1 | tf_op jit(solution)/shard_map/feed_forward/pallas_call | solution.py:466
  95.2 4.2 hidden_back.4.refs_4_
  101.9 7.7 %collective-permute-done.26.refs_0_ = bf16[256,2048]{1,0:T(8,128)(2,1)} collective-permute-done((bf16[256,2048]{1,0:T(8,128)(2,1)}, bf16[256,2048]{1,0:T(8,128)(2,1)}, u32[]{:S(2)}, u32[]{:S(2)}) %collective-permute-start.26) | collective-permute-done | bytes 1048608 | tf_op jit(solution)/shard_map/ppermute | solution.py:659
  114.8 11.7 %feed_forward.4 = (bf16[1024,768]{1,0:T(8,128)(2,1)}, bf16[1024,768]{1,0:T(8,128)(2,1)}, bf16[1024,768]{1,0:T(8,128)(2,1)}) custom-call(bf16[256,2048]{1,0:T(8,128)(2,1)} %collective-permute-done.26.refs_0_, bf16[256,2048]{1,0:T(8,128)(2,1)S(1)} %collective-permute-done.28.refs_1_, bf16[256,2048]{1,0:T(8,128)(2,1)} %collective-permute-done.27.refs_2_, ...), custom_call_target="tpu_custom_call" | custom-call | flops 1 | bytes 1 | tf_op jit(solution)/shard_map/feed_forward/pallas_call | solution.py:466
  132.5 7.8 %feed_forward.5 = (bf16[512,768]{1,0:T(8,128)(2,1)S(1)}, bf16[512,768]{1,0:T(8,128)(2,1)}, bf16[512,768]{1,0:T(8,128)(2,1)}) custom-call(bf16[128,2048]{1,0:T(8,128)(2,1)} %collective-permute-done.30.refs_0_, bf16[128,2048]{1,0:T(8,128)(2,1)} %collective-permute-done.31.refs_1_, bf16[128,2048]{1,0:T(8,128)(2,1)} %collective-permute-done.32.refs_2_, ...), custom_call_target="tpu_custom_call" | custom-call | flops 1 | bytes 1 | tf_op jit(solution)/shard_map/feed_forward/pallas_call | solution.py:466
  140.4 12.0 %outer.7 = (bf16[1024,768]{1,0:T(8,128)(2,1)}, bf16[1024,768]{1,0:T(8,128)(2,1)}) custom-call(s32[8]{0:T(128)S(1)} %stack.168.order_ref, bf16[256,2048]{1,0:T(8,128)(2,1)S(1)} %copy-done, bf16[256,2048]{1,0:T(8,128)(2,1)S(1)} %copy-done, bf16[256,2048]{1,0:T(8,128)(2,1)S(1)} %copy-done.8, bf16[256,2048]{1,0:T(8,128)(2,1)S(1)} %copy-done.8, ...), custom_call_target="tpu_custom_call" | custom-call | flops 1 | bytes 1 | tf_op jit(solution)/shard_map/outer/pallas_call | solution.py:562
  153.8 33.4 %conditional.9 = (bf16[256,2048]{1,0:T(8,128)(2,1)}, bf16[1024,768]{1,0:T(8,128)(2,1)}, bf16[1024,768]{1,0:T(8,128)(2,1)}, bf16[1024,768]{1,0:T(8,128)(2,1)}, bf16[1024,768]{1,0:T(8,128)(2,1)}) conditional(s32[]{:T(128)} %convert_element_type.87, () %tuple.248, (bf16[512,768]{1,0:T(8,128)(2,1)}, bf16[512,768]{1,0:T(8,128)(2,1)}, ...), branch_computations={%region_0.1_spmd, %region_1.2_spmd} | conditional | flops 10 | bytes 12583199 | solution.py:907
  153.8 7.2 %row_shares.8 = (bf16[256,2048]{1,0:T(8,128)(2,1)S(1)}, bf16[256,2048]{1,0:T(8,128)(2,1)}) custom-call(bf16[512,768]{1,0:T(8,128)(2,1)} %get-tuple-element.202.refs_0_.refs_24_, bf16[512,768]{1,0:T(8,128)(2,1)} %get-tuple-element.203.refs_1_.refs_25_, bf16[2048,768]{1,0:T(8,128)(2,1)} %get-tuple-element.167.refs_2_, bf16[2048,768]{1,0:T(8,128)(2,1)} %get-tuple-element.168.refs_3_), custom_call_target="tpu_custom_call" | custom-call | flops 1 | bytes 1 | tf_op jit(solution)/shard_map/cond/branch_1_fun/row_shares/pallas_call | solution.py:498
  162.7 21.7 %outer.4 = (bf16[1024,768]{1,0:T(8,128)(2,1)}, bf16[1024,768]{1,0:T(8,128)(2,1)}, bf16[1024,768]{1,0:T(8,128)(2,1)}, bf16[1024,768]{1,0:T(8,128)(2,1)}) custom-call(s32[8]{0:T(128)S(1)} %stack.109.order_ref, bf16[256,2048]{1,0:T(8,128)(2,1)} %get-tuple-element.188.refs_0_.refs_1_, bf16[256,2048]{1,0:T(8,128)(2,1)} %get-tuple-element.188.refs_0_.refs_1_, ...), custom_call_target="tpu_custom_call" | custom-call | flops 1 | bytes 1 | tf_op jit(solution)/shard_map/cond/branch_1_fun/outer/pallas_call | solution.py:562
  187.5 18.3 %conditional.10 = (bf16[256,2048]{1,0:T(8,128)(2,1)S(1)}, bf16[256,2048]{1,0:T(8,128)(2,1)}, bf16[256,2048]{1,0:T(8,128)(2,1)S(1)}, bf16[256,2048]{1,0:T(8,128)(...) conditional(s32[]{:T(128)} %convert_element_type.88, () %tuple.252, (bf16[1024,768]{1,0:T(8,128)(2,1)}, ...), branch_computations={%region_2.3_spmd, %region_3.4_spmd} | conditional | flops 2 | bytes 44040472 | solution.py:907
  187.5 10.2 %row_shares.9 = (bf16[256,2048]{1,0:T(8,128)(2,1)S(1)}, bf16[256,2048]{1,0:T(8,128)(2,1)S(1)}, bf16[256,2048]{1,0:T(8,128)(2,1)S(1)}, bf16[256,2048]{1,0:T(8,128)(2,1)S(1)}) custom-call(bf16[1024,768]{1,0:T(8,128)(2,1)} %get-tuple-element.216.refs_0_, bf16[1024,768]{1,0:T(8,128)(2,1)} %get-tuple-element.217.refs_1_, ...), custom_call_target="tpu_custom_call" | custom-call | flops 1 | bytes 1 | tf_op jit(solution)/shard_map/cond/branch_1_fun/row_shares/pallas_call | solution.py:498
  198.3 4.8 %row_shares.10 = (bf16[256,2048]{1,0:T(8,128)(2,1)}, bf16[256,2048]{1,0:T(8,128)(2,1)S(1)}) custom-call(bf16[512,768]{1,0:T(8,128)(2,1)S(1)} %copy-done.70, bf16[512,768]{1,0:T(8,128)(2,1)S(1)} %copy-done.71, bf16[2048,768]{1,0:T(8,128)(2,1)S(1)} %copy-done.44, bf16[2048,768]{1,0:T(8,128)(2,1)S(1)} %copy-done.43), custom_call_target="tpu_custom_call" | custom-call | flops 1 | bytes 1 | tf_op jit(solution)/shard_map/cond/branch_1_fun/row_shares/pallas_call | solution.py:498
  208.3 4.0 collective-permute-done.35.refs_2_
  218.0 22.8 %conditional.11 = (bf16[256,2048]{1,0:T(8,128)(2,1)}, bf16[256,2048]{1,0:T(8,128)(2,1)}, bf16[256,2048]{1,0:T(8,128)(2,1)}, bf16[256,2048]{1,0:T(8,128)(2,1)}, b...) conditional(s32[]{:T(128)} %convert_element_type.89, () %tuple.261, ...), branch_computations={%region_4.5_spmd, %region_5.6_spmd} | conditional | flops 4 | bytes 32506132 | solution.py:907
  218.0 4.5 row_shares.11
  224.2 6.3 %row_shares.12 = (bf16[256,2048]{1,0:T(8,128)(2,1)}, bf16[256,2048]{1,0:T(8,128)(2,1)S(1)}, bf16[256,2048]{1,0:T(8,128)(2,1)}, bf16[256,2048]{1,0:T(8,128)(2,1)S(1)}) custom-call(bf16[1024,768]{1,0:T(8,128)(2,1)} %get-tuple-element.249.refs_0_, bf16[768,2048]{1,0:T(8,128)(2,1)S(1)} %copy-done.41), custom_call_target="tpu_custom_call" | custom-call | flops 1 | bytes 1 | tf_op jit(solution)/shard_map/cond/branch_1_fun/row_shares/pallas_call | solution.py:498
  231.9 3.3 row_shares.13
  240.8 5.3 %by_rows.19 = (f32[256,2048]{1,0:T(8,128)S(1)}, bf16[256,2048]{1,0:T(8,128)(2,1)}) custom-call(bf16[256,2048]{1,0:T(8,128)(2,1)S(1)} %copy-done.66, bf16[256,2048]{1,0:T(8,128)(2,1)} %get-tuple-element.787.refs_1_, bf16[256,2048]{1,0:T(8,128)(2,1)} %collective-permute-done.38.refs_2_, bf16[256,2048]{1,0:T(8,128)(2,1)} %collective-permute-done.39.refs_3_, ...), custom_call_target="tpu_custom_call" | custom-call | flops 1 | bytes 1 | tf_op jit(solution)/shard_map/by_rows/pallas_call | solution.py:183
  246.1 4.6 collective-permute-done.37.came_a.came_b
  256.6 22.3 %conditional.12 = (bf16[256,2048]{1,0:T(8,128)(2,1)}, bf16[512,512]{1,0:T(8,128)(2,1)}, f32[1024,64]{1,0:T(8,128)}, f32[1024,64]{1,0:T(8,128)}) conditional(s32[]{:T(128)} %convert_element_type.90, () %tuple.271, (bf16[256,2048]{1,0:T(8,128)(2,1)}, s32[2]{0:T(128)S(1)}, s32[2]{0:T(128)S(1)}, bf16[512,512]{1,0:T(8,128)(2,1)}, ...), branch_computations={%region_6.7_spmd, %region_7.8_spmd} | conditional | flops 1 | bytes 4194377 | solution.py:907
  262.0 16.8 %attend_backward.2 = (bf16[512,512]{1,0:T(8,128)(2,1)}, f32[1024,64]{1,0:T(8,128)}, f32[1024,64]{1,0:T(8,128)}) custom-call(s32[2]{0:T(128)S(1)} %get-tuple-element.273.pos_ref, s32[2]{0:T(128)S(1)} %get-tuple-element.274.starts_ref, bf16[512,512]{1,0:T(8,128)(2,1)} %get-tuple-element.275.q_ref, bf16[512,2048]{1,0:T(8,128)(2,1)} %get-tuple-element.276.out_ref, ...), custom_call_target="tpu_custom_call" | custom-call | flops 1 | bytes 1 | tf_op jit(solution)/shard_map/cond/branch_1_fun/attend_backward/pallas_call | solution.py:384
  280.0 10.4 %conditional.13 = (bf16[256,2048]{1,0:T(8,128)(2,1)}, bf16[1024,512]{1,0:T(8,128)(2,1)}, bf16[1024,512]{1,0:T(8,128)(2,1)}) conditional(s32[]{:T(128)} %convert_element_type.91, () %tuple.276, (bf16[256,2048]{1,0:T(8,128)(2,1)}, s32[]{:T(128)}, bf16[256,2048]{1,0:T(8,128)(2,1)}, bf16[256,2048]{1,0:T(8,128)(2,1)}, bf16[512,512]{1,0:T(8,128)(2,1)}, ...), branch_computations={%region_8.9_spmd, %region_9.10_spmd} | conditional | flops 8 | bytes 4194517 | solution.py:907
  283.0 7.4 %outer.5 = (bf16[1024,512]{1,0:T(8,128)(2,1)}, bf16[1024,512]{1,0:T(8,128)(2,1)}) custom-call(s32[8]{0:T(128)S(1)} %stack.118.order_ref, bf16[256,2048]{1,0:T(8,128)(2,1)} %get-tuple-element.295.refs_0_.refs_1_, bf16[256,2048]{1,0:T(8,128)(2,1)} %get-tuple-element.295.refs_0_.refs_1_, bf16[256,2048]{1,0:T(8,128)(2,1)} %get-tuple-element.296.refs_2_.refs_3_, ...), custom_call_target="tpu_custom_call" | custom-call | flops 1 | bytes 1 | tf_op jit(solution)/shard_map/cond/branch_1_fun/outer/pallas_call | solution.py:562
  301.5 3.0 by_rows.20
  304.5 21.0 %conditional.14 = ((bf16[512,512]{1,0:T(8,128)(2,1)}, f32[1024,64]{1,0:T(8,128)}, f32[1024,64]{1,0:T(8,128)})) conditional(s32[]{:T(128)} %convert_element_type.92, () %tuple.287, (s32[2]{0:T(128)S(1)}, s32[2]{0:T(128)S(1)}, bf16[512,512]{1,0:T(8,128)(2,1)}, bf16[512,2048]{1,0:T(8,128)(2,1)}, bf16[512,512]{1,0:T(8,128)(2,1)}, ...), branch_computations={%region_10.11_spmd, %region_11.12_spmd} | conditional | flops 1 | bytes 1048618 | solution.py:907
  304.5 20.8 %attend_backward.3 = (bf16[512,512]{1,0:T(8,128)(2,1)}, f32[1024,64]{1,0:T(8,128)}, f32[1024,64]{1,0:T(8,128)}) custom-call(s32[2]{0:T(128)S(1)} %get-tuple-element.305.pos_ref, s32[2]{0:T(128)S(1)} %get-tuple-element.306.starts_ref, bf16[512,512]{1,0:T(8,128)(2,1)} %get-tuple-element.307.q_ref, bf16[512,2048]{1,0:T(8,128)(2,1)} %get-tuple-element.308.out_ref, ...), custom_call_target="tpu_custom_call" | custom-call | flops 1 | bytes 1 | tf_op jit(solution)/shard_map/cond/branch_1_fun/attend_backward/pallas_call | solution.py:384
  325.5 11.7 %conditional.15 = (bf16[512,128]{1,0:T(8,128)(2,1)}, bf16[512,128]{1,0:T(8,128)(2,1)}, bf16[1024,640]{1,0:T(8,128)(2,1)}, bf16[1024,640]{1,0:T(8,128)(2,1)}) conditional(s32[]{:T(128)} %convert_element_type.93, () %tuple.291, (s32[4]{0:T(128)S(1)}, f32[1024,64]{1,0:T(8,128)}, f32[1024,64]{1,0:T(8,128)}, f32[1024,64]{1,0:T(8,128)}, ...), branch_computations={%region_12.13_spmd, %region_13.14_spmd} | conditional | flops 9 | bytes 2883624 | solution.py:907
  325.5 3.6 key_value_rows.1
  329.2 8.0 %outer.6 = (bf16[1024,640]{1,0:T(8,128)(2,1)}, bf16[1024,640]{1,0:T(8,128)(2,1)}) custom-call(s32[8]{0:T(128)S(1)} %stack.127.order_ref, bf16[512,2048]{1,0:T(8,128)(2,1)} %get-tuple-element.333.refs_0_.refs_1_, bf16[512,2048]{1,0:T(8,128)(2,1)} %get-tuple-element.333.refs_0_.refs_1_, bf16[512,512]{1,0:T(8,128)(2,1)S(1)} %copy-done.61, ...), custom_call_target="tpu_custom_call" | custom-call | flops 1 | bytes 1 | tf_op jit(solution)/shard_map/cond/branch_1_fun/outer/pallas_call | solution.py:562
  346.5 9.8 %conditional.16 = (bf16[256,2048]{1,0:T(8,128)(2,1)}) conditional(s32[]{:T(128)} %convert_element_type.95, () %tuple.303, (bf16[512,512]{1,0:T(8,128)(2,1)}, bf16[512,128]{1,0:T(8,128)(2,1)}, bf16[2048,512]{1,0:T(8,128)(2,1)}, bf16[2048,128]{1,0:T(8,128)(2,1)S(1)}) %tuple.382), branch_computations={%region_14.15_spmd, %region_15.16_spmd} | conditional | flops 2 | bytes 4194354 | solution.py:907
  346.5 4.2 row_shares.14
  361.1 8.2 %conditional.17 = (bf16[256,2048]{1,0:T(8,128)(2,1)}, bf16[256,2048]{1,0:T(8,128)(2,1)}) conditional(s32[]{:T(128)} %convert_element_type.97, () %tuple.309, (bf16[512,512]{1,0:T(8,128)(2,1)}, bf16[512,128]{1,0:T(8,128)(2,1)}, bf16[2048,512]{1,0:T(8,128)(2,1)}, bf16[2048,128]{1,0:T(8,128)(2,1)}) %tuple.381), branch_computations={%region_16.17_spmd, %region_17.18_spmd} | conditional | flops 1 | bytes 4194361 | solution.py:907
  361.1 4.9 %row_shares.15 = (bf16[256,2048]{1,0:T(8,128)(2,1)}, bf16[256,2048]{1,0:T(8,128)(2,1)S(1)}) custom-call(bf16[512,512]{1,0:T(8,128)(2,1)} %get-tuple-element.357.refs_0_, bf16[512,128]{1,0:T(8,128)(2,1)} %get-tuple-element.358.refs_1_, bf16[2048,512]{1,0:T(8,128)(2,1)} %get-tuple-element.359.refs_2_, bf16[2048,128]{1,0:T(8,128)(2,1)} %get-tuple-element.360.refs_3_), custom_call_target="tpu_custom_call" | custom-call | flops 1 | bytes 1 | tf_op jit(solution)/shard_map/cond/branch_1_fun/row_shares/pallas_call | solution.py:498
  372.0 21.3 %collective-permute-done.51.came_a.came_b = bf16[512,768]{1,0:T(8,128)(2,1)S(1)} collective-permute-done((bf16[512,768]{1,0:T(8,128)(2,1)}, bf16[512,768]{1,0:T(8,128)(2,1)S(1)}, u32[]{:S(2)}, u32[]{:S(2)}) %collective-permute-start.51) | collective-permute-done | bytes 786464 | tf_op jit(solution)/shard_map/ppermute | solution.py:717
  401.9 4.8 %by_rows.22 = f32[256,2048]{1,0:T(8,128)} custom-call(bf16[256,2048]{1,0:T(8,128)(2,1)} %get-tuple-element.891.refs_0_, bf16[256,2048]{1,0:T(8,128)(2,1)} %get-tuple-element.892.refs_1_, bf16[256,2048]{1,0:T(8,128)(2,1)} %collective-permute-done.49.refs_2_, bf16[256,2048]{1,0:T(8,128)(2,1)S(1)} %copy-done.6, f32[256,2048]{1,0:T(8,128)S(1)} %copy-done.20, ...), custom_call_target="tpu_custom_call" | custom-call | flops 1 | bytes 1 | tf_op jit(solution)/shard_map/by_rows/pallas_call | solution.py:183
  414.3 16.3 %collective-permute-done.52.refs_3_ = bf16[256,2048]{1,0:T(8,128)(2,1)S(1)} collective-permute-done((bf16[256,2048]{1,0:T(8,128)(2,1)}, bf16[256,2048]{1,0:T(8,128)(2,1)S(1)}, u32[]{:S(2)}, u32[]{:S(2)}) %collective-permute-start.52) | collective-permute-done | bytes 1048608 | tf_op jit(solution)/shard_map/ppermute | solution.py:659
  430.6 7.7 %collective-permute-done.53.refs_4_ = bf16[256,2048]{1,0:T(8,128)(2,1)} collective-permute-done((bf16[256,2048]{1,0:T(8,128)(2,1)S(1)}, bf16[256,2048]{1,0:T(8,128)(2,1)}, u32[]{:S(2)}, u32[]{:S(2)}) %collective-permute-start.53) | collective-permute-done | bytes 1048608 | tf_op jit(solution)/shard_map/ppermute | solution.py:717
  448.9 3.0 copy.36
  454.2 3.4 by_rows.23
  (337 shorter events, 156.3 us)
Async XLA Ops:
  0.6 24.4 %collective-permute-start.12 = (bf16[256,2048]{1,0:T(8,128)(2,1)}, bf16[256,2048]{1,0:T(8,128)(2,1)}, u32[]{:S(2)}, u32[]{:S(2)}) collective-permute-start(bf16[256,2048]{1,0:T(8,128)(2,1)} %refs_3_.5), channel_id=1, source_target_pairs={{0,2},{1,3},{2,0},{3,1},{4,6},{5,7},{6,4},{7,5},{8,10},{9,11},{10,... | collective-permute-start | bytes 3145736 | tf_op jit(solution)/shard_map/ppermute | solution.py:659
  1.9 16.2 %collective-permute-start.13 = (bf16[256,2048]{1,0:T(8,128)(2,1)}, bf16[256,2048]{1,0:T(8,128)(2,1)S(1)}, u32[]{:S(2)}, u32[]{:S(2)}) collective-permute-start(bf16[256,2048]{1,0:T(8,128)(2,1)} %refs_3_.5), channel_id=1, source_target_pairs={{0,1},{1,0},{2,3},{3,2},{4,5},{5,4},{6,7},{7,6},{8,9},{9,8},{10,11... | collective-permute-start | bytes 3145736 | tf_op jit(solution)/shard_map/ppermute | solution.py:659
  25.1 4.2 collective-permute-start.17
  26.6 24.8 %collective-permute-start.15 = (bf16[256,2048]{1,0:T(8,128)(2,1)S(1)}, bf16[256,2048]{1,0:T(8,128)(2,1)S(1)}, u32[]{:S(2)}, u32[]{:S(2)}) collective-permute-start(bf16[256,2048]{1,0:T(8,128)(2,1)S(1)} %copy-done), channel_id=1, source_target_pairs={{0,2},{1,3},{2,0},{3,1},{4,6},{5,7},{6,4},{7,5},{8,10},{9,11},{10,... | collective-permute-start | bytes 3145736 | tf_op jit(solution)/shard_map/ppermute | solution.py:659
  27.8 24.5 %collective-permute-start.16 = (bf16[256,2048]{1,0:T(8,128)(2,1)S(1)}, bf16[256,2048]{1,0:T(8,128)(2,1)S(1)}, u32[]{:S(2)}, u32[]{:S(2)}) collective-permute-start(bf16[256,2048]{1,0:T(8,128)(2,1)S(1)} %copy-done), channel_id=1, source_target_pairs={{0,8},{4,12},{8,0},{12,4},{16,24},{20,28},{24,16},{28,20},{1,9},{5... | collective-permute-start | bytes 3145736 | tf_op jit(solution)/shard_map/ppermute | solution.py:717
  28.1 26.0 %collective-permute-start.14 = (bf16[256,2048]{1,0:T(8,128)(2,1)S(1)}, bf16[256,2048]{1,0:T(8,128)(2,1)S(1)}, u32[]{:S(2)}, u32[]{:S(2)}) collective-permute-start(bf16[256,2048]{1,0:T(8,128)(2,1)S(1)} %copy-done), channel_id=1, source_target_pairs={{0,1},{1,0},{2,3},{3,2},{4,5},{5,4},{6,7},{7,6},{8,9},{9,8},{10,11... | collective-permute-start | bytes 3145736 | tf_op jit(solution)/shard_map/ppermute | solution.py:659
  49.6 4.0 collective-permute-start.20
  53.4 3.8 collective-permute-start.19
  53.4 24.2 %collective-permute-start.22 = (bf16[256,2048]{1,0:T(8,128)(2,1)S(1)}, bf16[256,2048]{1,0:T(8,128)(2,1)S(1)}, u32[]{:S(2)}, u32[]{:S(2)}) collective-permute-start(bf16[256,2048]{1,0:T(8,128)(2,1)S(1)} %collective-permute-done.15.refs_0_.refs_5_.refs_6_), channel_id=1, source_target_pairs={{0,8},{4,12},{8,0},{12,4},{16,24},{20,28},{24,16},{28,20},{1,9},{5... | collective-permute-start | bytes 3145736 | tf_op jit(solution)/shard_map/ppermute | solution.py:717
  53.8 25.1 %collective-permute-start.24 = (bf16[256,2048]{1,0:T(8,128)(2,1)S(1)}, bf16[256,2048]{1,0:T(8,128)(2,1)S(1)}, u32[]{:S(2)}, u32[]{:S(2)}) collective-permute-start(bf16[256,2048]{1,0:T(8,128)(2,1)S(1)} %by_rows.15), channel_id=1, source_target_pairs={{0,2},{1,3},{2,0},{3,1},{4,6},{5,7},{6,4},{7,5},{8,10},{9,11},{10,... | collective-permute-start | bytes 3145736 | tf_op jit(solution)/shard_map/ppermute | solution.py:659
  68.6 10.4 %collective-permute-start.21 = (bf16[256,2048]{1,0:T(8,128)(2,1)S(1)}, bf16[256,2048]{1,0:T(8,128)(2,1)S(1)}, u32[]{:S(2)}, u32[]{:S(2)}) collective-permute-start(bf16[256,2048]{1,0:T(8,128)(2,1)S(1)} %get-tuple-element.700), channel_id=1, source_target_pairs={{0,1},{1,0},{2,3},{3,2},{4,5},{5,4},{6,7},{7,6},{8,9},{9,8},{10,11... | collective-permute-start | bytes 3145736 | tf_op jit(solution)/shard_map/ppermute | solution.py:659
  77.6 3.6 collective-permute-start.23
  84.7 24.9 %collective-permute-start.26 = (bf16[256,2048]{1,0:T(8,128)(2,1)}, bf16[256,2048]{1,0:T(8,128)(2,1)}, u32[]{:S(2)}, u32[]{:S(2)}) collective-permute-start(bf16[256,2048]{1,0:T(8,128)(2,1)} %get-tuple-element.713.refs_0_), channel_id=1, source_target_pairs={{0,2},{1,3},{2,0},{3,1},{4,6},{5,7},{6,4},{7,5},{8,10},{9,11},{10,... | collective-permute-start | bytes 3145736 | tf_op jit(solution)/shard_map/ppermute | solution.py:659
  85.0 24.7 %collective-permute-start.27 = (bf16[256,2048]{1,0:T(8,128)(2,1)}, bf16[256,2048]{1,0:T(8,128)(2,1)}, u32[]{:S(2)}, u32[]{:S(2)}) collective-permute-start(bf16[256,2048]{1,0:T(8,128)(2,1)} %get-tuple-element.713.refs_0_), channel_id=1, source_target_pairs={{0,8},{4,12},{8,0},{12,4},{16,24},{20,28},{24,16},{28,20},{1,9},{5... | collective-permute-start | bytes 3145736 | tf_op jit(solution)/shard_map/ppermute | solution.py:717
  109.6 4.8 %collective-permute-start.28 = (bf16[256,2048]{1,0:T(8,128)(2,1)}, bf16[256,2048]{1,0:T(8,128)(2,1)S(1)}, u32[]{:S(2)}, u32[]{:S(2)}) collective-permute-start(bf16[256,2048]{1,0:T(8,128)(2,1)} %collective-permute-done.26.refs_0_), channel_id=1, source_target_pairs={{0,1},{1,0},{2,3},{3,2},{4,5},{5,4},{6,7},{7,6},{8,9},{9,8},{10,11... | collective-permute-start | bytes 3145736 | tf_op jit(solution)/shard_map/ppermute | solution.py:659
  110.8 4.0 collective-permute-start.29
  113.0 13.6 %collective-permute-start.30 = (bf16[128,2048]{1,0:T(8,128)(2,1)S(1)}, bf16[128,2048]{1,0:T(8,128)(2,1)}, u32[]{:S(2)}, u32[]{:S(2)}) collective-permute-start(bf16[128,2048]{1,0:T(8,128)(2,1)S(1)} %slice.62), channel_id=1, source_target_pairs={{0,2},{1,3},{2,0},{3,1},{4,6},{5,7},{6,4},{7,5},{8,10},{9,11},{10,... | collective-permute-start | bytes 1572872 | tf_op jit(solution)/shard_map/ppermute | solution.py:659
  114.3 12.8 %collective-permute-start.31 = (bf16[128,2048]{1,0:T(8,128)(2,1)S(1)}, bf16[128,2048]{1,0:T(8,128)(2,1)}, u32[]{:S(2)}, u32[]{:S(2)}) collective-permute-start(bf16[128,2048]{1,0:T(8,128)(2,1)S(1)} %slice.63), channel_id=1, source_target_pairs={{0,8},{4,12},{8,0},{12,4},{16,24},{20,28},{24,16},{28,20},{1,9},{5... | collective-permute-start | bytes 1572872 | tf_op jit(solution)/shard_map/ppermute | solution.py:717
  152.4 62.8 %collective-permute-start.34 = (bf16[1024,768]{1,0:T(8,128)(2,1)}, bf16[1024,768]{1,0:T(8,128)(2,1)S(1)}, u32[]{:S(2)}, u32[]{:S(2)}) collective-permute-start(bf16[1024,768]{1,0:T(8,128)(2,1)} %get-tuple-element.763), channel_id=1, source_target_pairs={{0,4},{4,0},{8,12},{12,8},{16,20},{20,16},{24,28},{28,24},{1,5},{5... | collective-permute-start | bytes 4718600 | tf_op jit(solution)/shard_map/ppermute | solution.py:717
  162.0 22.4 %collective-permute-start = (bf16[256,2048]{1,0:T(8,128)(2,1)}, bf16[256,2048]{1,0:T(8,128)(2,1)}, u32[]{:S(2)}, u32[]{:S(2)}) collective-permute-start(bf16[256,2048]{1,0:T(8,128)(2,1)} %get-tuple-element.172), channel_id=1, source_target_pairs={{0,1},{1,0},{2,3},{3,2},{4,5},{5,4},{6,7},{7,6},{8,9},{9,8},{10,11... | collective-permute-start | bytes 3145736 | tf_op jit(solution)/shard_map/cond/branch_1_fun/ppermute | solution.py:659
  187.1 25.2 %collective-permute-start.35 = (bf16[256,2048]{1,0:T(8,128)(2,1)}, bf16[256,2048]{1,0:T(8,128)(2,1)}, u32[]{:S(2)}, u32[]{:S(2)}) collective-permute-start(bf16[256,2048]{1,0:T(8,128)(2,1)} %get-tuple-element.770), channel_id=1, source_target_pairs={{0,8},{4,12},{8,0},{12,4},{16,24},{20,28},{24,16},{28,20},{1,9},{5... | collective-permute-start | bytes 3145736 | tf_op jit(solution)/shard_map/ppermute | solution.py:717
  197.7 5.6 %collective-permute-start.1 = (bf16[256,2048]{1,0:T(8,128)(2,1)S(1)}, bf16[256,2048]{1,0:T(8,128)(2,1)}, u32[]{:S(2)}, u32[]{:S(2)}) collective-permute-start(bf16[256,2048]{1,0:T(8,128)(2,1)S(1)} %get-tuple-element.225), channel_id=1, source_target_pairs={{0,1},{1,0},{2,3},{3,2},{4,5},{5,4},{6,7},{7,6},{8,9},{9,8},{10,11... | collective-permute-start | bytes 3145736 | tf_op jit(solution)/shard_map/cond/branch_1_fun/ppermute | solution.py:659
  198.0 5.3 %collective-permute-start.2 = (bf16[256,2048]{1,0:T(8,128)(2,1)S(1)}, bf16[256,2048]{1,0:T(8,128)(2,1)}, u32[]{:S(2)}, u32[]{:S(2)}) collective-permute-start(bf16[256,2048]{1,0:T(8,128)(2,1)S(1)} %get-tuple-element.229), channel_id=1, source_target_pairs={{0,1},{1,0},{2,3},{3,2},{4,5},{5,4},{6,7},{7,6},{8,9},{9,8},{10,11... | collective-permute-start | bytes 3145736 | tf_op jit(solution)/shard_map/cond/branch_1_fun/ppermute | solution.py:659
  215.3 35.4 %collective-permute-start.37 = (bf16[1024,768]{1,0:T(8,128)(2,1)}, bf16[1024,768]{1,0:T(8,128)(2,1)}, u32[]{:S(2)}, u32[]{:S(2)}) collective-permute-start(bf16[1024,768]{1,0:T(8,128)(2,1)} %get-tuple-element.809), channel_id=1, source_target_pairs={{0,4},{4,0},{8,12},{12,8},{16,20},{20,16},{24,28},{28,24},{1,5},{5... | collective-permute-start | bytes 4718600 | tf_op jit(solution)/shard_map/ppermute | solution.py:717
  215.5 25.3 %collective-permute-start.39 = (bf16[256,2048]{1,0:T(8,128)(2,1)}, bf16[256,2048]{1,0:T(8,128)(2,1)}, u32[]{:S(2)}, u32[]{:S(2)}) collective-permute-start(bf16[256,2048]{1,0:T(8,128)(2,1)} %by_rows.17), channel_id=1, source_target_pairs={{0,8},{4,12},{8,0},{12,4},{16,24},{20,28},{24,16},{28,20},{1,9},{5... | collective-permute-start | bytes 3145736 | tf_op jit(solution)/shard_map/ppermute | solution.py:717
  215.8 25.0 %collective-permute-start.38 = (bf16[256,2048]{1,0:T(8,128)(2,1)}, bf16[256,2048]{1,0:T(8,128)(2,1)}, u32[]{:S(2)}, u32[]{:S(2)}) collective-permute-start(bf16[256,2048]{1,0:T(8,128)(2,1)} %by_rows.18), channel_id=1, source_target_pairs={{0,2},{1,3},{2,0},{3,1},{4,6},{5,7},{6,4},{7,5},{8,10},{9,11},{10,... | collective-permute-start | bytes 3145736 | tf_op jit(solution)/shard_map/ppermute | solution.py:659
  222.6 8.0 %collective-permute-start.4 = (bf16[256,2048]{1,0:T(8,128)(2,1)S(1)}, bf16[256,2048]{1,0:T(8,128)(2,1)S(1)}, u32[]{:S(2)}, u32[]{:S(2)}) collective-permute-start(bf16[256,2048]{1,0:T(8,128)(2,1)S(1)} %get-tuple-element.247), channel_id=1, source_target_pairs={{0,1},{1,0},{2,3},{3,2},{4,5},{5,4},{6,7},{7,6},{8,9},{9,8},{10,11... | collective-permute-start | bytes 3145736 | tf_op jit(solution)/shard_map/cond/branch_1_fun/ppermute | solution.py:659
  250.7 42.5 %collective-permute-start.40 = (bf16[1024,768]{1,0:T(8,128)(2,1)}, bf16[1024,768]{1,0:T(8,128)(2,1)S(1)}, u32[]{:S(2)}, u32[]{:S(2)}) collective-permute-start(bf16[1024,768]{1,0:T(8,128)(2,1)} %get-tuple-element.819), channel_id=1, source_target_pairs={{0,4},{4,0},{8,12},{12,8},{16,20},{20,16},{24,28},{28,24},{1,5},{5... | collective-permute-start | bytes 4718600 | tf_op jit(solution)/shard_map/ppermute | solution.py:717
  251.0 27.9 %collective-permute-start.42 = (bf16[256,2048]{1,0:T(8,128)(2,1)}, bf16[256,2048]{1,0:T(8,128)(2,1)S(1)}, u32[]{:S(2)}, u32[]{:S(2)}) collective-permute-start(bf16[256,2048]{1,0:T(8,128)(2,1)} %get-tuple-element.817), channel_id=1, source_target_pairs={{0,2},{1,3},{2,0},{3,1},{4,6},{5,7},{6,4},{7,5},{8,10},{9,11},{10,... | collective-permute-start | bytes 3145736 | tf_op jit(solution)/shard_map/ppermute | solution.py:659
  251.3 39.1 %collective-permute-start.41 = (bf16[512,768]{1,0:T(8,128)(2,1)}, bf16[512,768]{1,0:T(8,128)(2,1)}, u32[]{:S(2)}, u32[]{:S(2)}) collective-permute-start(bf16[512,768]{1,0:T(8,128)(2,1)} %get-tuple-element.794), channel_id=1, source_target_pairs={{0,16},{4,20},{8,24},{12,28},{16,0},{20,4},{24,8},{28,12},{1,17},{... | collective-permute-start | bytes 2359304 | tf_op jit(solution)/shard_map/ppermute | solution.py:717
  253.6 47.9 %collective-permute-start.36 = (bf16[256,2048]{1,0:T(8,128)(2,1)}, bf16[256,2048]{1,0:T(8,128)(2,1)}, u32[]{:S(2)}, u32[]{:S(2)}) collective-permute-start(bf16[256,2048]{1,0:T(8,128)(2,1)} %get-tuple-element.808), channel_id=1, source_target_pairs={{0,8},{4,12},{8,0},{12,4},{16,24},{20,28},{24,16},{28,20},{1,9},{5... | collective-permute-start | bytes 3145736 | tf_op jit(solution)/shard_map/ppermute | solution.py:717
  256.6 5.4 %collective-permute-start.8 = (bf16[256,2048]{1,0:T(8,128)(2,1)}, bf16[256,2048]{1,0:T(8,128)(2,1)}, u32[]{:S(2)}, u32[]{:S(2)}) collective-permute-start(bf16[256,2048]{1,0:T(8,128)(2,1)} %get-tuple-element.272.rest_0_), channel_id=1, source_target_pairs={{0,1},{1,0},{2,3},{3,2},{4,5},{5,4},{6,7},{7,6},{8,9},{9,8},{10,11... | collective-permute-start | bytes 3145736 | tf_op jit(solution)/shard_map/cond/branch_1_fun/ppermute | solution.py:659
  293.2 44.3 %collective-permute-start.46 = (bf16[1024,512]{1,0:T(8,128)(2,1)}, bf16[1024,512]{1,0:T(8,128)(2,1)S(1)}, u32[]{:S(2)}, u32[]{:S(2)}) collective-permute-start(bf16[1024,512]{1,0:T(8,128)(2,1)} %get-tuple-element.869), channel_id=1, source_target_pairs={{0,4},{4,0},{8,12},{12,8},{16,20},{20,16},{24,28},{28,24},{1,5},{5... | collective-permute-start | bytes 3145736 | tf_op jit(solution)/shard_map/ppermute | solution.py:717
  294.5 45.0 %collective-permute-start.45 = (bf16[256,768]{1,0:T(8,128)(2,1)}, bf16[256,768]{1,0:T(8,128)(2,1)}, u32[]{:S(2)}, u32[]{:S(2)}) collective-permute-start(bf16[256,768]{1,0:T(8,128)(2,1)} %get-tuple-element.844), channel_id=1, source_target_pairs={{0,8},{4,12},{8,0},{12,4},{16,24},{20,28},{24,16},{28,20},{1,9},{5... | collective-permute-start | bytes 1179656 | tf_op jit(solution)/shard_map/ppermute | solution.py:717
  295.7 47.3 %collective-permute-start.44 = (bf16[512,768]{1,0:T(8,128)(2,1)}, bf16[512,768]{1,0:T(8,128)(2,1)}, u32[]{:S(2)}, u32[]{:S(2)}) collective-permute-start(bf16[512,768]{1,0:T(8,128)(2,1)} %get-tuple-element.868), channel_id=1, source_target_pairs={{0,16},{4,20},{8,24},{12,28},{16,0},{20,4},{24,8},{28,12},{1,17},{... | collective-permute-start | bytes 2359304 | tf_op jit(solution)/shard_map/ppermute | solution.py:717
  337.2 32.1 %collective-permute-start.43 = (bf16[1024,640]{1,0:T(8,128)(2,1)}, bf16[1024,640]{1,0:T(8,128)(2,1)S(1)}, u32[]{:S(2)}, u32[]{:S(2)}) collective-permute-start(bf16[1024,640]{1,0:T(8,128)(2,1)} %get-tuple-element.867), channel_id=1, source_target_pairs={{0,4},{4,0},{8,12},{12,8},{16,20},{20,16},{24,28},{28,24},{1,5},{5... | collective-permute-start | bytes 3932168 | tf_op jit(solution)/shard_map/ppermute | solution.py:717
  345.0 14.8 %collective-permute-start.47 = (bf16[256,768]{1,0:T(8,128)(2,1)}, bf16[256,768]{1,0:T(8,128)(2,1)S(1)}, u32[]{:S(2)}, u32[]{:S(2)}) collective-permute-start(bf16[256,768]{1,0:T(8,128)(2,1)} %get-tuple-element.883), channel_id=1, source_target_pairs={{0,8},{4,12},{8,0},{12,4},{16,24},{20,28},{24,16},{28,20},{1,9},{5... | collective-permute-start | bytes 1179656 | tf_op jit(solution)/shard_map/ppermute | solution.py:717
  345.0 27.0 %collective-permute-start.50 = (bf16[512,512]{1,0:T(8,128)(2,1)}, bf16[512,512]{1,0:T(8,128)(2,1)}, u32[]{:S(2)}, u32[]{:S(2)}) collective-permute-start(bf16[512,512]{1,0:T(8,128)(2,1)} %get-tuple-element.875), channel_id=1, source_target_pairs={{0,8},{4,12},{8,0},{12,4},{16,24},{20,28},{24,16},{28,20},{1,9},{5... | collective-permute-start | bytes 1572872 | tf_op jit(solution)/shard_map/ppermute | solution.py:717
  350.7 4.4 collective-permute-start.10
  356.3 44.0 %collective-permute-start.49 = (bf16[256,2048]{1,0:T(8,128)(2,1)}, bf16[256,2048]{1,0:T(8,128)(2,1)}, u32[]{:S(2)}, u32[]{:S(2)}) collective-permute-start(bf16[256,2048]{1,0:T(8,128)(2,1)} %get-tuple-element.1056), channel_id=1, source_target_pairs={{0,2},{1,3},{2,0},{3,1},{4,6},{5,7},{6,4},{7,5},{8,10},{9,11},{10,... | collective-permute-start | bytes 3145736 | tf_op jit(solution)/shard_map/ppermute | solution.py:659
  357.4 35.9 %collective-permute-start.51 = (bf16[512,768]{1,0:T(8,128)(2,1)}, bf16[512,768]{1,0:T(8,128)(2,1)S(1)}, u32[]{:S(2)}, u32[]{:S(2)}) collective-permute-start(bf16[512,768]{1,0:T(8,128)(2,1)} %get-tuple-element.901), channel_id=1, source_target_pairs={{0,16},{4,20},{8,24},{12,28},{16,0},{20,4},{24,8},{28,12},{1,17},{... | collective-permute-start | bytes 2359304 | tf_op jit(solution)/shard_map/ppermute | solution.py:717
  371.5 35.2 %collective-permute-start.48 = (bf16[512,640]{1,0:T(8,128)(2,1)}, bf16[512,640]{1,0:T(8,128)(2,1)S(1)}, u32[]{:S(2)}, u32[]{:S(2)}) collective-permute-start(bf16[512,640]{1,0:T(8,128)(2,1)} %get-tuple-element.896), channel_id=1, source_target_pairs={{0,8},{4,12},{8,0},{12,4},{16,24},{20,28},{24,16},{28,20},{1,9},{5... | collective-permute-start | bytes 1966088 | tf_op jit(solution)/shard_map/ppermute | solution.py:717
  394.9 14.4 %collective-permute-start.55 = (bf16[256,768]{1,0:T(8,128)(2,1)}, bf16[256,768]{1,0:T(8,128)(2,1)}, u32[]{:S(2)}, u32[]{:S(2)}) collective-permute-start(bf16[256,768]{1,0:T(8,128)(2,1)} %get-tuple-element.905), channel_id=1, source_target_pairs={{0,8},{4,12},{8,0},{12,4},{16,24},{20,28},{24,16},{28,20},{1,9},{5... | collective-permute-start | bytes 1179656 | tf_op jit(solution)/shard_map/ppermute | solution.py:717
  397.5 16.6 %collective-permute-start.54 = (bf16[256,512]{1,0:T(8,128)(2,1)S(1)}, bf16[256,512]{1,0:T(8,128)(2,1)S(1)}, u32[]{:S(2)}, u32[]{:S(2)}) collective-permute-start(bf16[256,512]{1,0:T(8,128)(2,1)S(1)} %get-tuple-element.907), channel_id=1, source_target_pairs={{0,16},{4,20},{8,24},{12,28},{16,0},{20,4},{24,8},{28,12},{1,17},{... | collective-permute-start | bytes 786440 | tf_op jit(solution)/shard_map/ppermute | solution.py:717
  407.4 23.1 %collective-permute-start.52 = (bf16[256,2048]{1,0:T(8,128)(2,1)}, bf16[256,2048]{1,0:T(8,128)(2,1)S(1)}, u32[]{:S(2)}, u32[]{:S(2)}) collective-permute-start(bf16[256,2048]{1,0:T(8,128)(2,1)} %by_rows.20), channel_id=1, source_target_pairs={{0,2},{1,3},{2,0},{3,1},{4,6},{5,7},{6,4},{7,5},{8,10},{9,11},{10,... | collective-permute-start | bytes 3145736 | tf_op jit(solution)/shard_map/ppermute | solution.py:659
  408.0 30.3 %collective-permute-start.53 = (bf16[256,2048]{1,0:T(8,128)(2,1)S(1)}, bf16[256,2048]{1,0:T(8,128)(2,1)}, u32[]{:S(2)}, u32[]{:S(2)}) collective-permute-start(bf16[256,2048]{1,0:T(8,128)(2,1)S(1)} %copy-done.28), channel_id=1, source_target_pairs={{0,8},{4,12},{8,0},{12,4},{16,24},{20,28},{24,16},{28,20},{1,9},{5... | collective-permute-start | bytes 3145736 | tf_op jit(solution)/shard_map/ppermute | solution.py:717
  409.3 31.8 %collective-permute-start.56 = (bf16[256,640]{1,0:T(8,128)(2,1)}, bf16[256,640]{1,0:T(8,128)(2,1)S(1)}, u32[]{:S(2)}, u32[]{:S(2)}) collective-permute-start(bf16[256,640]{1,0:T(8,128)(2,1)} %get-tuple-element.916), channel_id=1, source_target_pairs={{0,16},{4,20},{8,24},{12,28},{16,0},{20,4},{24,8},{28,12},{1,17},{... | collective-permute-start | bytes 983048 | tf_op jit(solution)/shard_map/ppermute | solution.py:717
  446.8 10.9 %collective-permute-start.57 = (f32[2,2,64]{2,1,0:T(2,128)S(1)}, f32[2,2,64]{2,1,0:T(2,128)S(1)}, u32[]{:S(2)}, u32[]{:S(2)}) collective-permute-start(f32[2,2,64]{2,1,0:T(2,128)S(1)} %pad_maximum_fusion.7), channel_id=1, source_target_pairs={{0,2},{1,3},{2,0},{3,1},{4,6},{5,7},{6,4},{7,5},{8,10},{9,11},{10,... | collective-permute-start | bytes 3080 | tf_op jit(solution)/shard_map/ppermute | solution.py:1142
  (87 other events, 690.8 us)

commit v7 on v4

--- a/solution.py
+++ b/solution.py
@@ -133,59 +133,38 @@
 
 
 def by_rows(function, ins, consts, outs):
-    flat, counts = [], []
-    for item in ins:
-        item = item if isinstance(item, tuple) else (item,)
-        counts.append([len(flat) + sum(one is not None for one in item[:i]) if part is not None else None
-                       for i, part in enumerate(item)])
-        flat.extend(part for part in item if part is not None)
-    rows, width = sum(flat[at].shape[0] for at in counts[0]), flat[0].shape[1]
-    out_counts = [PARTS if isinstance(item, tuple) else 1 for item in outs]
+    flat = [item[0] if isinstance(item, tuple) else item for item in ins]
     dtypes = [item[0] if isinstance(item, tuple) else item for item in outs]
-    starts = [sum(out_counts[:i]) for i in range(len(outs))]
-    out_places = [range(first, first + count) for first, count in zip(starts, out_counts)]
-    step = 32
+    consts = [item[None, :] for item in consts]
+    rows, width = flat[0].shape
+    block, step = rows // 2, 32
 
     def kernel(*refs):
         given = [ref[...] for ref in refs[len(flat) : len(flat) + len(consts)]]
-
-        def views(part_refs, places, part):
-            found = []
-            for place in places:
-                each = PARTS // len(place)
-                at = place[part // each]
-                ref = None if at is None else part_refs[at]
-                found.append((ref, part % each * (rows // PARTS)))
-            return found
-
-        for part in range(PARTS):
-            sources = views(refs, counts, part)
-            targets = views(refs[len(flat) + len(consts) :], out_places, part)
-
-            def chunk(i, _):
-                def at(base):
-                    return pl.ds(pl.multiple_of(base + i * step, step), step)
-
-                values = [
-                    0.0 if ref is None else ref[at(base), :].astype(jnp.float32)
-                    for ref, base in sources
-                ]
-                for (ref, base), value in zip(targets, function(*values, *given)):
-                    ref[at(base), :] = value.astype(ref.dtype)
-                return 0
-
-            lax.fori_loop(0, rows // PARTS // step, chunk, 0)
-
-    consts = [item[None, :] for item in consts]
-    shapes = []
-    for count, dtype in zip(out_counts, dtypes):
-        shapes.extend([jax.ShapeDtypeStruct((rows // count, width), dtype)] * count)
-    results = pl.pallas_call(kernel, out_shape=shapes, name="by_rows", **params())(*flat, *consts)
-    grouped, at = [], 0
-    for count, item in zip(out_counts, outs):
-        grouped.append(tuple(results[at : at + count]) if isinstance(item, tuple) else results[at])
-        at += count
-    return grouped
+        targets = refs[len(flat) + len(consts) :]
+
+        def chunk(i, _):
+            at = pl.ds(pl.multiple_of(i * step, step), step)
+            values = [ref[at, :].astype(jnp.float32) for ref in refs[: len(flat)]]
+            for ref, value in zip(targets, function(*values, *given)):
+                ref[at, :] = value.astype(ref.dtype)
+            return 0
+
+        lax.fori_loop(0, block // step, chunk, 0)
+
+    tall = pl.BlockSpec((block, width), lambda i: (i, 0))
+    results = pl.pallas_call(
+        kernel,
+        grid=(2,),
+        in_specs=[tall] * len(flat) + [whole(item) for item in consts],
+        out_specs=[tall] * len(dtypes),
+        out_shape=[jax.ShapeDtypeStruct((rows, width), dtype) for dtype in dtypes],
+        name="by_rows",
+        **params(),
+    )(*flat, *consts)
+    return [
+        (result,) if isinstance(item, tuple) else result for result, item in zip(results, outs)
+    ]
 
 
 def see(qpos, kpos, starts_ref, pics):

time: 469 us -> 467 us (level)
  transfers between devices with their start and end apart: 59 -> 59, of which waited for: 28 -> 29; matrix products, arithmetic and copies ran while one was open for 7% -> 7% of each run, Pallas kernels for 51% -> 50%
where the time goes in v7:
time: 467 us; the launch traced here: 459 us
  Pallas kernels  252 us (54%)
  waiting for transfers between devices  106 us (23%)
  starting transfers between devices  46.2 us (10%)
  local copies, waits for them, and re-layouts  27.8 us (6%)
  other arithmetic  25 us (5%)
    ppermute x34, waiting for transfers between devices, swapped(): return tuple((lax.ppermute(part, 'tensor', pairs) for part in parts))  56.6 us
    ppermute x23, waiting for transfers between devices, exchange(): return lax.ppermute(value, 'dp', [(i, i ^ bit) for i in range(size)])  49.6 us
    pallas_call x4, Pallas kernels, outer(): pl.pallas_call(functools.partial(outer_kernel, shape=[(len(lefts), len(ri...  49.1 us
    pallas_call x8, Pallas kernels, row_shares(): pl.pallas_call(functools.partial(share_kernel, count=len(lefts), transpos...  45.3 us
    pallas_call x2, Pallas kernels, attend_backward(): pl.pallas_call(functools.partial(backward_kernel, heads=heads, pics=pics,...  37.5 us
    pallas_call x3, Pallas kernels, feed_forward(): pl.pallas_call(feed_kernel, grid=(pl.cdiv(units, tile),), in_specs=[*(who...  27.5 us
    pallas_call x12, Pallas kernels, by_rows(): pl.pallas_call(kernel, grid=(2,), in_specs=[tall] * len(flat) + [whole(it...  27.3 us
    ppermute x34, starting transfers between devices, swapped(): return tuple((lax.ppermute(part, 'tensor', pairs) for part in parts))  25.9 us
  transfers between devices with their start and end apart: 59, of which 29 were waited for; matrix products, arithmetic and copies ran while one was open for 7% of the time, Pallas kernels for 50%

profile of v7, /device:TPU:9, one launch (start us, length us, event | category | flops | bytes accessed | tf_op | source)
XLA Modules:
  0.0 459.5 jit_solution(6669808118681853139)
XLA Ops:
  11.8 6.3 %dynamic-slice_select_fusion.1 = (bf16[2048,768]{1,0:T(8,128)(2,1)}, bf16[2048,768]{1,0:T(8,128)(2,1)}) fusion(bf16[2048,1408]{1,0:T(8,128)(2,1)} %param.41, s32[]{:T(128)S(6)} %select_n.91, pred[768]{0:T(1024)(128)(4,1)S(1)} %fusion.2, bf16[2048,1408]{1,0:T(8,128)(2,1)} %param.40), kind=kLoop, calls=%fused_computation.1 | loop fusion | flops 1572864 | bytes 12583684 | tf_op jit(solution)/shard_map/jit(_where)/select_n | solution.py:795
  18.1 3.8 project.2
  22.0 3.1 collective-permute-done.12.refs_0_
  29.2 6.2 %project.3 = (bf16[512,2048]{1,0:T(8,128)(2,1)}, bf16[512,512]{1,0:T(8,128)(2,1)S(1)}, bf16[512,64]{1,0:T(8,128)(2,1)S(1)}, bf16[512,64]{1,0:T(8,128)(2,1)S(1)}) custom-call(bf16[256,2048]{1,0:T(8,128)(2,1)} %collective-permute-done.12.refs_0_, bf16[256,2048]{1,0:T(8,128)(2,1)} %collective-permute-done.17.refs_1_, f32[1,2048]{1,0:T(1,128)S(1)} %bitcast.69, ...), custom_call_target="tpu_custom_call" | custom-call | flops 1 | bytes 1 | tf_op jit(solution)/shard_map/project/pallas_call | solution.py:117
  37.4 12.2 %attend_forward.2 = (bf16[512,512]{1,0:T(8,128)(2,1)}, f32[512,8]{1,0:T(8,128)}, bf16[256,2048]{1,0:T(8,128)(2,1)S(1)}, bf16[256,2048]{1,0:T(8,128)(2,1)S(1)}) custom-call(s32[2]{0:T(128)S(1)} %get-tuple-element.978.pos_ref, s32[2]{0:T(128)S(1)} %bitcast.74, bf16[512,512]{1,0:T(8,128)(2,1)S(1)} %get-tuple-element.674.q_ref, ...), custom_call_target="tpu_custom_call" | custom-call | flops 1 | bytes 1 | tf_op jit(solution)/shard_map/attend_forward/pallas_call | solution.py:251
  57.2 11.4 %attend_forward.3 = (bf16[512,512]{1,0:T(8,128)(2,1)}, f32[512,8]{1,0:T(8,128)}, bf16[256,2048]{1,0:T(8,128)(2,1)S(1)}, bf16[256,2048]{1,0:T(8,128)(2,1)S(1)}) custom-call(s32[2]{0:T(128)S(1)} %get-tuple-element.977.pos_ref, s32[2]{0:T(128)S(1)} %bitcast.75, bf16[512,512]{1,0:T(8,128)(2,1)S(1)} %copy-done.73, bf16[1024,64]{1,0:T(8,128)(2,1)S(1)} %pad_maximum_fusion.5.k_ref, ...), custom_call_target="tpu_custom_call" | custom-call | flops 1 | bytes 1 | tf_op jit(solution)/shard_map/attend_forward/pallas_call | solution.py:251
  69.0 4.1 hidden_back.3.refs_2_
  73.1 4.5 collective-permute-done.22.refs_0_.refs_14_.refs_15_
  86.8 8.0 %feed_forward.3 = (bf16[512,768]{1,0:T(8,128)(2,1)}, bf16[512,768]{1,0:T(8,128)(2,1)}, bf16[512,768]{1,0:T(8,128)(2,1)}) custom-call(bf16[256,2048]{1,0:T(8,128)(2,1)} %get-tuple-element.712.refs_0_, bf16[256,2048]{1,0:T(8,128)(2,1)S(1)} %collective-permute-done.25.refs_1_, bf16[512,768]{1,0:T(8,128)(2,1)S(1)} %hidden_back.3.refs_2_, ...), custom_call_target="tpu_custom_call" | custom-call | flops 1 | bytes 1 | tf_op jit(solution)/shard_map/feed_forward/pallas_call | solution.py:445
  94.8 4.2 hidden_back.4.refs_4_
  101.5 7.7 %collective-permute-done.26.refs_0_ = bf16[256,2048]{1,0:T(8,128)(2,1)} collective-permute-done((bf16[256,2048]{1,0:T(8,128)(2,1)}, bf16[256,2048]{1,0:T(8,128)(2,1)}, u32[]{:S(2)}, u32[]{:S(2)}) %collective-permute-start.26) | collective-permute-done | bytes 1048608 | tf_op jit(solution)/shard_map/ppermute | solution.py:638
  114.4 11.7 %feed_forward.4 = (bf16[1024,768]{1,0:T(8,128)(2,1)}, bf16[1024,768]{1,0:T(8,128)(2,1)}, bf16[1024,768]{1,0:T(8,128)(2,1)}) custom-call(bf16[256,2048]{1,0:T(8,128)(2,1)} %collective-permute-done.26.refs_0_, bf16[256,2048]{1,0:T(8,128)(2,1)S(1)} %collective-permute-done.28.refs_1_, bf16[256,2048]{1,0:T(8,128)(2,1)} %collective-permute-done.27.refs_2_, ...), custom_call_target="tpu_custom_call" | custom-call | flops 1 | bytes 1 | tf_op jit(solution)/shard_map/feed_forward/pallas_call | solution.py:445
  132.1 7.8 %feed_forward.5 = (bf16[512,768]{1,0:T(8,128)(2,1)S(1)}, bf16[512,768]{1,0:T(8,128)(2,1)}, bf16[512,768]{1,0:T(8,128)(2,1)}) custom-call(bf16[128,2048]{1,0:T(8,128)(2,1)} %collective-permute-done.30.refs_0_, bf16[128,2048]{1,0:T(8,128)(2,1)} %collective-permute-done.31.refs_1_, bf16[128,2048]{1,0:T(8,128)(2,1)} %collective-permute-done.32.refs_2_, ...), custom_call_target="tpu_custom_call" | custom-call | flops 1 | bytes 1 | tf_op jit(solution)/shard_map/feed_forward/pallas_call | solution.py:445
  140.0 12.0 %outer.7 = (bf16[1024,768]{1,0:T(8,128)(2,1)}, bf16[1024,768]{1,0:T(8,128)(2,1)}) custom-call(s32[8]{0:T(128)S(1)} %stack.168.order_ref, bf16[256,2048]{1,0:T(8,128)(2,1)S(1)} %copy-done, bf16[256,2048]{1,0:T(8,128)(2,1)S(1)} %copy-done, bf16[256,2048]{1,0:T(8,128)(2,1)S(1)} %copy-done.8, bf16[256,2048]{1,0:T(8,128)(2,1)S(1)} %copy-done.8, ...), custom_call_target="tpu_custom_call" | custom-call | flops 1 | bytes 1 | tf_op jit(solution)/shard_map/outer/pallas_call | solution.py:541
  153.4 33.1 %conditional.9 = (bf16[256,2048]{1,0:T(8,128)(2,1)}, bf16[1024,768]{1,0:T(8,128)(2,1)}, bf16[1024,768]{1,0:T(8,128)(2,1)}, bf16[1024,768]{1,0:T(8,128)(2,1)}, bf16[1024,768]{1,0:T(8,128)(2,1)}) conditional(s32[]{:T(128)} %convert_element_type.87, () %tuple.247, (bf16[512,768]{1,0:T(8,128)(2,1)}, bf16[512,768]{1,0:T(8,128)(2,1)}, ...), branch_computations={%region_0.1_spmd, %region_1.2_spmd} | conditional | flops 10 | bytes 12583199 | solution.py:886
  153.4 7.2 %row_shares.8 = (bf16[256,2048]{1,0:T(8,128)(2,1)S(1)}, bf16[256,2048]{1,0:T(8,128)(2,1)}) custom-call(bf16[512,768]{1,0:T(8,128)(2,1)} %get-tuple-element.202.refs_0_.refs_24_, bf16[512,768]{1,0:T(8,128)(2,1)} %get-tuple-element.203.refs_1_.refs_25_, bf16[2048,768]{1,0:T(8,128)(2,1)} %get-tuple-element.167.refs_2_, bf16[2048,768]{1,0:T(8,128)(2,1)} %get-tuple-element.168.refs_3_), custom_call_target="tpu_custom_call" | custom-call | flops 1 | bytes 1 | tf_op jit(solution)/shard_map/cond/branch_1_fun/row_shares/pallas_call | solution.py:477
  162.3 21.7 %outer.4 = (bf16[1024,768]{1,0:T(8,128)(2,1)}, bf16[1024,768]{1,0:T(8,128)(2,1)}, bf16[1024,768]{1,0:T(8,128)(2,1)}, bf16[1024,768]{1,0:T(8,128)(2,1)}) custom-call(s32[8]{0:T(128)S(1)} %stack.109.order_ref, bf16[256,2048]{1,0:T(8,128)(2,1)} %get-tuple-element.188.refs_0_.refs_1_, bf16[256,2048]{1,0:T(8,128)(2,1)} %get-tuple-element.188.refs_0_.refs_1_, ...), custom_call_target="tpu_custom_call" | custom-call | flops 1 | bytes 1 | tf_op jit(solution)/shard_map/cond/branch_1_fun/outer/pallas_call | solution.py:541
  186.8 18.3 %conditional.10 = (bf16[256,2048]{1,0:T(8,128)(2,1)S(1)}, bf16[256,2048]{1,0:T(8,128)(2,1)}, bf16[256,2048]{1,0:T(8,128)(2,1)S(1)}, bf16[256,2048]{1,0:T(8,128)(...) conditional(s32[]{:T(128)} %convert_element_type.88, () %tuple.251, (bf16[1024,768]{1,0:T(8,128)(2,1)}, ...), branch_computations={%region_2.3_spmd, %region_3.4_spmd} | conditional | flops 2 | bytes 44040472 | solution.py:886
  186.8 10.2 %row_shares.9 = (bf16[256,2048]{1,0:T(8,128)(2,1)S(1)}, bf16[256,2048]{1,0:T(8,128)(2,1)S(1)}, bf16[256,2048]{1,0:T(8,128)(2,1)S(1)}, bf16[256,2048]{1,0:T(8,128)(2,1)S(1)}) custom-call(bf16[1024,768]{1,0:T(8,128)(2,1)} %get-tuple-element.216.refs_0_, bf16[1024,768]{1,0:T(8,128)(2,1)} %get-tuple-element.217.refs_1_, ...), custom_call_target="tpu_custom_call" | custom-call | flops 1 | bytes 1 | tf_op jit(solution)/shard_map/cond/branch_1_fun/row_shares/pallas_call | solution.py:477
  197.6 4.8 %row_shares.10 = (bf16[256,2048]{1,0:T(8,128)(2,1)}, bf16[256,2048]{1,0:T(8,128)(2,1)S(1)}) custom-call(bf16[512,768]{1,0:T(8,128)(2,1)S(1)} %copy-done.70, bf16[512,768]{1,0:T(8,128)(2,1)S(1)} %copy-done.71, bf16[2048,768]{1,0:T(8,128)(2,1)S(1)} %copy-done.44, bf16[2048,768]{1,0:T(8,128)(2,1)S(1)} %copy-done.43), custom_call_target="tpu_custom_call" | custom-call | flops 1 | bytes 1 | tf_op jit(solution)/shard_map/cond/branch_1_fun/row_shares/pallas_call | solution.py:477
  207.3 4.4 collective-permute-done.35.refs_2_
  216.9 22.7 %conditional.11 = (bf16[256,2048]{1,0:T(8,128)(2,1)}, bf16[256,2048]{1,0:T(8,128)(2,1)}, bf16[256,2048]{1,0:T(8,128)(2,1)}, bf16[256,2048]{1,0:T(8,128)(2,1)}, b...) conditional(s32[]{:T(128)} %convert_element_type.89, () %tuple.260, ...), branch_computations={%region_4.5_spmd, %region_5.6_spmd} | conditional | flops 4 | bytes 32506132 | solution.py:886
  216.9 4.5 row_shares.11
  223.1 6.3 %row_shares.12 = (bf16[256,2048]{1,0:T(8,128)(2,1)}, bf16[256,2048]{1,0:T(8,128)(2,1)S(1)}, bf16[256,2048]{1,0:T(8,128)(2,1)}, bf16[256,2048]{1,0:T(8,128)(2,1)S(1)}) custom-call(bf16[1024,768]{1,0:T(8,128)(2,1)} %get-tuple-element.249.refs_0_, bf16[768,2048]{1,0:T(8,128)(2,1)S(1)} %copy-done.41), custom_call_target="tpu_custom_call" | custom-call | flops 1 | bytes 1 | tf_op jit(solution)/shard_map/cond/branch_1_fun/row_shares/pallas_call | solution.py:477
  230.7 3.3 row_shares.13
  239.6 4.3 by_rows.19
  243.9 5.7 %collective-permute-done.37.came_a.came_b = bf16[1024,768]{1,0:T(8,128)(2,1)} collective-permute-done((bf16[1024,768]{1,0:T(8,128)(2,1)}, bf16[1024,768]{1,0:T(8,128)(2,1)}, u32[]{:S(2)}, u32[]{:S(2)}) %collective-permute-start.37) | collective-permute-done | bytes 1572896 | tf_op jit(solution)/shard_map/ppermute | solution.py:696
  255.4 22.3 %conditional.12 = (bf16[256,2048]{1,0:T(8,128)(2,1)}, bf16[512,512]{1,0:T(8,128)(2,1)}, f32[1024,64]{1,0:T(8,128)}, f32[1024,64]{1,0:T(8,128)}) conditional(s32[]{:T(128)} %convert_element_type.90, () %tuple.270, (bf16[256,2048]{1,0:T(8,128)(2,1)}, s32[2]{0:T(128)S(1)}, s32[2]{0:T(128)S(1)}, bf16[512,512]{1,0:T(8,128)(2,1)}, ...), branch_computations={%region_6.7_spmd, %region_7.8_spmd} | conditional | flops 1 | bytes 4194377 | solution.py:886
  255.4 2.8 collective-permute-start.8
  260.8 16.7 %attend_backward.2 = (bf16[512,512]{1,0:T(8,128)(2,1)}, f32[1024,64]{1,0:T(8,128)}, f32[1024,64]{1,0:T(8,128)}) custom-call(s32[2]{0:T(128)S(1)} %get-tuple-element.273.pos_ref, s32[2]{0:T(128)S(1)} %get-tuple-element.274.starts_ref, bf16[512,512]{1,0:T(8,128)(2,1)} %get-tuple-element.275.q_ref, bf16[512,2048]{1,0:T(8,128)(2,1)} %get-tuple-element.276.out_ref, ...), custom_call_target="tpu_custom_call" | custom-call | flops 1 | bytes 1 | tf_op jit(solution)/shard_map/cond/branch_1_fun/attend_backward/pallas_call | solution.py:363
  278.8 10.4 %conditional.13 = (bf16[256,2048]{1,0:T(8,128)(2,1)}, bf16[1024,512]{1,0:T(8,128)(2,1)}, bf16[1024,512]{1,0:T(8,128)(2,1)}) conditional(s32[]{:T(128)} %convert_element_type.91, () %tuple.275, (bf16[256,2048]{1,0:T(8,128)(2,1)}, s32[]{:T(128)}, bf16[256,2048]{1,0:T(8,128)(2,1)}, bf16[256,2048]{1,0:T(8,128)(2,1)}, bf16[512,512]{1,0:T(8,128)(2,1)}, ...), branch_computations={%region_8.9_spmd, %region_9.10_spmd} | conditional | flops 8 | bytes 4194517 | solution.py:886
  281.8 7.4 %outer.5 = (bf16[1024,512]{1,0:T(8,128)(2,1)}, bf16[1024,512]{1,0:T(8,128)(2,1)}) custom-call(s32[8]{0:T(128)S(1)} %stack.118.order_ref, bf16[256,2048]{1,0:T(8,128)(2,1)} %get-tuple-element.295.refs_0_.refs_1_, bf16[256,2048]{1,0:T(8,128)(2,1)} %get-tuple-element.295.refs_0_.refs_1_, bf16[256,2048]{1,0:T(8,128)(2,1)} %get-tuple-element.296.refs_2_.refs_3_, ...), custom_call_target="tpu_custom_call" | custom-call | flops 1 | bytes 1 | tf_op jit(solution)/shard_map/cond/branch_1_fun/outer/pallas_call | solution.py:541
  302.8 21.0 %conditional.14 = ((bf16[512,512]{1,0:T(8,128)(2,1)}, f32[1024,64]{1,0:T(8,128)}, f32[1024,64]{1,0:T(8,128)})) conditional(s32[]{:T(128)} %convert_element_type.92, () %tuple.286, (s32[2]{0:T(128)S(1)}, s32[2]{0:T(128)S(1)}, bf16[512,512]{1,0:T(8,128)(2,1)}, bf16[512,2048]{1,0:T(8,128)(2,1)}, bf16[512,512]{1,0:T(8,128)(2,1)}, ...), branch_computations={%region_10.11_spmd, %region_11.12_spmd} | conditional | flops 1 | bytes 1048618 | solution.py:886
  302.8 20.8 %attend_backward.3 = (bf16[512,512]{1,0:T(8,128)(2,1)}, f32[1024,64]{1,0:T(8,128)}, f32[1024,64]{1,0:T(8,128)}) custom-call(s32[2]{0:T(128)S(1)} %get-tuple-element.305.pos_ref, s32[2]{0:T(128)S(1)} %get-tuple-element.306.starts_ref, bf16[512,512]{1,0:T(8,128)(2,1)} %get-tuple-element.307.q_ref, bf16[512,2048]{1,0:T(8,128)(2,1)} %get-tuple-element.308.out_ref, ...), custom_call_target="tpu_custom_call" | custom-call | flops 1 | bytes 1 | tf_op jit(solution)/shard_map/cond/branch_1_fun/attend_backward/pallas_call | solution.py:363
  323.8 11.7 %conditional.15 = (bf16[512,128]{1,0:T(8,128)(2,1)}, bf16[512,128]{1,0:T(8,128)(2,1)}, bf16[1024,640]{1,0:T(8,128)(2,1)}, bf16[1024,640]{1,0:T(8,128)(2,1)}) conditional(s32[]{:T(128)} %convert_element_type.93, () %tuple.290, (s32[4]{0:T(128)S(1)}, f32[1024,64]{1,0:T(8,128)}, f32[1024,64]{1,0:T(8,128)}, f32[1024,64]{1,0:T(8,128)}, ...), branch_computations={%region_12.13_spmd, %region_13.14_spmd} | conditional | flops 9 | bytes 2883624 | solution.py:886
  323.8 3.6 key_value_rows.1
  327.5 8.0 %outer.6 = (bf16[1024,640]{1,0:T(8,128)(2,1)}, bf16[1024,640]{1,0:T(8,128)(2,1)}) custom-call(s32[8]{0:T(128)S(1)} %stack.127.order_ref, bf16[512,2048]{1,0:T(8,128)(2,1)} %get-tuple-element.333.refs_0_.refs_1_, bf16[512,2048]{1,0:T(8,128)(2,1)} %get-tuple-element.333.refs_0_.refs_1_, bf16[512,512]{1,0:T(8,128)(2,1)S(1)} %copy-done.61, ...), custom_call_target="tpu_custom_call" | custom-call | flops 1 | bytes 1 | tf_op jit(solution)/shard_map/cond/branch_1_fun/outer/pallas_call | solution.py:541
  344.8 9.7 %conditional.16 = (bf16[256,2048]{1,0:T(8,128)(2,1)}) conditional(s32[]{:T(128)} %convert_element_type.95, () %tuple.302, (bf16[512,512]{1,0:T(8,128)(2,1)}, bf16[512,128]{1,0:T(8,128)(2,1)}, bf16[2048,512]{1,0:T(8,128)(2,1)}, bf16[2048,128]{1,0:T(8,128)(2,1)S(1)}) %tuple.380), branch_computations={%region_14.15_spmd, %region_15.16_spmd} | conditional | flops 2 | bytes 4194354 | solution.py:886
  344.8 4.2 row_shares.14
  359.3 8.2 %conditional.17 = (bf16[256,2048]{1,0:T(8,128)(2,1)}, bf16[256,2048]{1,0:T(8,128)(2,1)}) conditional(s32[]{:T(128)} %convert_element_type.97, () %tuple.308, (bf16[512,512]{1,0:T(8,128)(2,1)}, bf16[512,128]{1,0:T(8,128)(2,1)}, bf16[2048,512]{1,0:T(8,128)(2,1)}, bf16[2048,128]{1,0:T(8,128)(2,1)}) %tuple.379), branch_computations={%region_16.17_spmd, %region_17.18_spmd} | conditional | flops 1 | bytes 4194361 | solution.py:886
  359.3 4.9 %row_shares.15 = (bf16[256,2048]{1,0:T(8,128)(2,1)}, bf16[256,2048]{1,0:T(8,128)(2,1)S(1)}) custom-call(bf16[512,512]{1,0:T(8,128)(2,1)} %get-tuple-element.357.refs_0_, bf16[512,128]{1,0:T(8,128)(2,1)} %get-tuple-element.358.refs_1_, bf16[2048,512]{1,0:T(8,128)(2,1)} %get-tuple-element.359.refs_2_, bf16[2048,128]{1,0:T(8,128)(2,1)} %get-tuple-element.360.refs_3_), custom_call_target="tpu_custom_call" | custom-call | flops 1 | bytes 1 | tf_op jit(solution)/shard_map/cond/branch_1_fun/row_shares/pallas_call | solution.py:477
  370.8 20.7 %collective-permute-done.51.came_a.came_b = bf16[512,768]{1,0:T(8,128)(2,1)S(1)} collective-permute-done((bf16[512,768]{1,0:T(8,128)(2,1)}, bf16[512,768]{1,0:T(8,128)(2,1)S(1)}, u32[]{:S(2)}, u32[]{:S(2)}) %collective-permute-start.51) | collective-permute-done | bytes 786464 | tf_op jit(solution)/shard_map/ppermute | solution.py:696
  400.1 3.9 by_rows.22
  412.0 16.0 %collective-permute-done.52.refs_3_ = bf16[256,2048]{1,0:T(8,128)(2,1)S(1)} collective-permute-done((bf16[256,2048]{1,0:T(8,128)(2,1)}, bf16[256,2048]{1,0:T(8,128)(2,1)S(1)}, u32[]{:S(2)}, u32[]{:S(2)}) %collective-permute-start.52) | collective-permute-done | bytes 1048608 | tf_op jit(solution)/shard_map/ppermute | solution.py:638
  428.0 8.8 %collective-permute-done.53.refs_4_ = bf16[256,2048]{1,0:T(8,128)(2,1)} collective-permute-done((bf16[256,2048]{1,0:T(8,128)(2,1)S(1)}, bf16[256,2048]{1,0:T(8,128)(2,1)}, u32[]{:S(2)}, u32[]{:S(2)}) %collective-permute-start.53) | collective-permute-done | bytes 1048608 | tf_op jit(solution)/shard_map/ppermute | solution.py:696
  436.8 2.7 collective-permute-done.56.came_ref
  447.2 3.0 copy.36
  454.3 3.0 by_rows.23
  (337 shorter events, 155.2 us)
Async XLA Ops:
  0.6 24.4 %collective-permute-start.12 = (bf16[256,2048]{1,0:T(8,128)(2,1)}, bf16[256,2048]{1,0:T(8,128)(2,1)}, u32[]{:S(2)}, u32[]{:S(2)}) collective-permute-start(bf16[256,2048]{1,0:T(8,128)(2,1)} %refs_3_.5), channel_id=1, source_target_pairs={{0,2},{1,3},{2,0},{3,1},{4,6},{5,7},{6,4},{7,5},{8,10},{9,11},{10,... | collective-permute-start | bytes 3145736 | tf_op jit(solution)/shard_map/ppermute | solution.py:638
  1.9 16.2 %collective-permute-start.13 = (bf16[256,2048]{1,0:T(8,128)(2,1)}, bf16[256,2048]{1,0:T(8,128)(2,1)S(1)}, u32[]{:S(2)}, u32[]{:S(2)}) collective-permute-start(bf16[256,2048]{1,0:T(8,128)(2,1)} %refs_3_.5), channel_id=1, source_target_pairs={{0,1},{1,0},{2,3},{3,2},{4,5},{5,4},{6,7},{7,6},{8,9},{9,8},{10,11... | collective-permute-start | bytes 3145736 | tf_op jit(solution)/shard_map/ppermute | solution.py:638
  25.1 4.2 collective-permute-start.17
  26.6 24.8 %collective-permute-start.15 = (bf16[256,2048]{1,0:T(8,128)(2,1)S(1)}, bf16[256,2048]{1,0:T(8,128)(2,1)S(1)}, u32[]{:S(2)}, u32[]{:S(2)}) collective-permute-start(bf16[256,2048]{1,0:T(8,128)(2,1)S(1)} %copy-done), channel_id=1, source_target_pairs={{0,2},{1,3},{2,0},{3,1},{4,6},{5,7},{6,4},{7,5},{8,10},{9,11},{10,... | collective-permute-start | bytes 3145736 | tf_op jit(solution)/shard_map/ppermute | solution.py:638
  27.8 24.5 %collective-permute-start.16 = (bf16[256,2048]{1,0:T(8,128)(2,1)S(1)}, bf16[256,2048]{1,0:T(8,128)(2,1)S(1)}, u32[]{:S(2)}, u32[]{:S(2)}) collective-permute-start(bf16[256,2048]{1,0:T(8,128)(2,1)S(1)} %copy-done), channel_id=1, source_target_pairs={{0,8},{4,12},{8,0},{12,4},{16,24},{20,28},{24,16},{28,20},{1,9},{5... | collective-permute-start | bytes 3145736 | tf_op jit(solution)/shard_map/ppermute | solution.py:696
  28.1 26.0 %collective-permute-start.14 = (bf16[256,2048]{1,0:T(8,128)(2,1)S(1)}, bf16[256,2048]{1,0:T(8,128)(2,1)S(1)}, u32[]{:S(2)}, u32[]{:S(2)}) collective-permute-start(bf16[256,2048]{1,0:T(8,128)(2,1)S(1)} %copy-done), channel_id=1, source_target_pairs={{0,1},{1,0},{2,3},{3,2},{4,5},{5,4},{6,7},{7,6},{8,9},{9,8},{10,11... | collective-permute-start | bytes 3145736 | tf_op jit(solution)/shard_map/ppermute | solution.py:638
  49.6 4.0 collective-permute-start.20
  53.4 3.8 collective-permute-start.19
  53.4 24.2 %collective-permute-start.22 = (bf16[256,2048]{1,0:T(8,128)(2,1)S(1)}, bf16[256,2048]{1,0:T(8,128)(2,1)S(1)}, u32[]{:S(2)}, u32[]{:S(2)}) collective-permute-start(bf16[256,2048]{1,0:T(8,128)(2,1)S(1)} %collective-permute-done.15.refs_0_.refs_5_.refs_6_), channel_id=1, source_target_pairs={{0,8},{4,12},{8,0},{12,4},{16,24},{20,28},{24,16},{28,20},{1,9},{5... | collective-permute-start | bytes 3145736 | tf_op jit(solution)/shard_map/ppermute | solution.py:696
  53.9 25.1 %collective-permute-start.24 = (bf16[256,2048]{1,0:T(8,128)(2,1)S(1)}, bf16[256,2048]{1,0:T(8,128)(2,1)S(1)}, u32[]{:S(2)}, u32[]{:S(2)}) collective-permute-start(bf16[256,2048]{1,0:T(8,128)(2,1)S(1)} %by_rows.15), channel_id=1, source_target_pairs={{0,2},{1,3},{2,0},{3,1},{4,6},{5,7},{6,4},{7,5},{8,10},{9,11},{10,... | collective-permute-start | bytes 3145736 | tf_op jit(solution)/shard_map/ppermute | solution.py:638
  68.6 10.4 %collective-permute-start.21 = (bf16[256,2048]{1,0:T(8,128)(2,1)S(1)}, bf16[256,2048]{1,0:T(8,128)(2,1)S(1)}, u32[]{:S(2)}, u32[]{:S(2)}) collective-permute-start(bf16[256,2048]{1,0:T(8,128)(2,1)S(1)} %get-tuple-element.699), channel_id=1, source_target_pairs={{0,1},{1,0},{2,3},{3,2},{4,5},{5,4},{6,7},{7,6},{8,9},{9,8},{10,11... | collective-permute-start | bytes 3145736 | tf_op jit(solution)/shard_map/ppermute | solution.py:638
  84.3 24.9 %collective-permute-start.26 = (bf16[256,2048]{1,0:T(8,128)(2,1)}, bf16[256,2048]{1,0:T(8,128)(2,1)}, u32[]{:S(2)}, u32[]{:S(2)}) collective-permute-start(bf16[256,2048]{1,0:T(8,128)(2,1)} %get-tuple-element.712.refs_0_), channel_id=1, source_target_pairs={{0,2},{1,3},{2,0},{3,1},{4,6},{5,7},{6,4},{7,5},{8,10},{9,11},{10,... | collective-permute-start | bytes 3145736 | tf_op jit(solution)/shard_map/ppermute | solution.py:638
  84.6 24.7 %collective-permute-start.27 = (bf16[256,2048]{1,0:T(8,128)(2,1)}, bf16[256,2048]{1,0:T(8,128)(2,1)}, u32[]{:S(2)}, u32[]{:S(2)}) collective-permute-start(bf16[256,2048]{1,0:T(8,128)(2,1)} %get-tuple-element.712.refs_0_), channel_id=1, source_target_pairs={{0,8},{4,12},{8,0},{12,4},{16,24},{20,28},{24,16},{28,20},{1,9},{5... | collective-permute-start | bytes 3145736 | tf_op jit(solution)/shard_map/ppermute | solution.py:696
  109.2 4.8 %collective-permute-start.28 = (bf16[256,2048]{1,0:T(8,128)(2,1)}, bf16[256,2048]{1,0:T(8,128)(2,1)S(1)}, u32[]{:S(2)}, u32[]{:S(2)}) collective-permute-start(bf16[256,2048]{1,0:T(8,128)(2,1)} %collective-permute-done.26.refs_0_), channel_id=1, source_target_pairs={{0,1},{1,0},{2,3},{3,2},{4,5},{5,4},{6,7},{7,6},{8,9},{9,8},{10,11... | collective-permute-start | bytes 3145736 | tf_op jit(solution)/shard_map/ppermute | solution.py:638
  110.4 4.0 collective-permute-start.29
  112.6 13.6 %collective-permute-start.30 = (bf16[128,2048]{1,0:T(8,128)(2,1)S(1)}, bf16[128,2048]{1,0:T(8,128)(2,1)}, u32[]{:S(2)}, u32[]{:S(2)}) collective-permute-start(bf16[128,2048]{1,0:T(8,128)(2,1)S(1)} %slice.62), channel_id=1, source_target_pairs={{0,2},{1,3},{2,0},{3,1},{4,6},{5,7},{6,4},{7,5},{8,10},{9,11},{10,... | collective-permute-start | bytes 1572872 | tf_op jit(solution)/shard_map/ppermute | solution.py:638
  113.9 12.8 %collective-permute-start.31 = (bf16[128,2048]{1,0:T(8,128)(2,1)S(1)}, bf16[128,2048]{1,0:T(8,128)(2,1)}, u32[]{:S(2)}, u32[]{:S(2)}) collective-permute-start(bf16[128,2048]{1,0:T(8,128)(2,1)S(1)} %slice.63), channel_id=1, source_target_pairs={{0,8},{4,12},{8,0},{12,4},{16,24},{20,28},{24,16},{28,20},{1,9},{5... | collective-permute-start | bytes 1572872 | tf_op jit(solution)/shard_map/ppermute | solution.py:696
  152.0 62.2 %collective-permute-start.34 = (bf16[1024,768]{1,0:T(8,128)(2,1)}, bf16[1024,768]{1,0:T(8,128)(2,1)S(1)}, u32[]{:S(2)}, u32[]{:S(2)}) collective-permute-start(bf16[1024,768]{1,0:T(8,128)(2,1)} %get-tuple-element.762), channel_id=1, source_target_pairs={{0,4},{4,0},{8,12},{12,8},{16,20},{20,16},{24,28},{28,24},{1,5},{5... | collective-permute-start | bytes 4718600 | tf_op jit(solution)/shard_map/ppermute | solution.py:696
  161.6 22.5 %collective-permute-start = (bf16[256,2048]{1,0:T(8,128)(2,1)}, bf16[256,2048]{1,0:T(8,128)(2,1)}, u32[]{:S(2)}, u32[]{:S(2)}) collective-permute-start(bf16[256,2048]{1,0:T(8,128)(2,1)} %get-tuple-element.172), channel_id=1, source_target_pairs={{0,1},{1,0},{2,3},{3,2},{4,5},{5,4},{6,7},{7,6},{8,9},{9,8},{10,11... | collective-permute-start | bytes 3145736 | tf_op jit(solution)/shard_map/cond/branch_1_fun/ppermute | solution.py:638
  186.4 25.2 %collective-permute-start.35 = (bf16[256,2048]{1,0:T(8,128)(2,1)}, bf16[256,2048]{1,0:T(8,128)(2,1)}, u32[]{:S(2)}, u32[]{:S(2)}) collective-permute-start(bf16[256,2048]{1,0:T(8,128)(2,1)} %get-tuple-element.769), channel_id=1, source_target_pairs={{0,8},{4,12},{8,0},{12,4},{16,24},{20,28},{24,16},{28,20},{1,9},{5... | collective-permute-start | bytes 3145736 | tf_op jit(solution)/shard_map/ppermute | solution.py:696
  197.0 5.6 %collective-permute-start.1 = (bf16[256,2048]{1,0:T(8,128)(2,1)S(1)}, bf16[256,2048]{1,0:T(8,128)(2,1)}, u32[]{:S(2)}, u32[]{:S(2)}) collective-permute-start(bf16[256,2048]{1,0:T(8,128)(2,1)S(1)} %get-tuple-element.225), channel_id=1, source_target_pairs={{0,1},{1,0},{2,3},{3,2},{4,5},{5,4},{6,7},{7,6},{8,9},{9,8},{10,11... | collective-permute-start | bytes 3145736 | tf_op jit(solution)/shard_map/cond/branch_1_fun/ppermute | solution.py:638
  197.3 5.3 %collective-permute-start.2 = (bf16[256,2048]{1,0:T(8,128)(2,1)S(1)}, bf16[256,2048]{1,0:T(8,128)(2,1)}, u32[]{:S(2)}, u32[]{:S(2)}) collective-permute-start(bf16[256,2048]{1,0:T(8,128)(2,1)S(1)} %get-tuple-element.229), channel_id=1, source_target_pairs={{0,1},{1,0},{2,3},{3,2},{4,5},{5,4},{6,7},{7,6},{8,9},{9,8},{10,11... | collective-permute-start | bytes 3145736 | tf_op jit(solution)/shard_map/cond/branch_1_fun/ppermute | solution.py:638
  214.2 35.5 %collective-permute-start.37 = (bf16[1024,768]{1,0:T(8,128)(2,1)}, bf16[1024,768]{1,0:T(8,128)(2,1)}, u32[]{:S(2)}, u32[]{:S(2)}) collective-permute-start(bf16[1024,768]{1,0:T(8,128)(2,1)} %get-tuple-element.808), channel_id=1, source_target_pairs={{0,4},{4,0},{8,12},{12,8},{16,20},{20,16},{24,28},{28,24},{1,5},{5... | collective-permute-start | bytes 4718600 | tf_op jit(solution)/shard_map/ppermute | solution.py:696
  214.4 25.2 %collective-permute-start.39 = (bf16[256,2048]{1,0:T(8,128)(2,1)}, bf16[256,2048]{1,0:T(8,128)(2,1)}, u32[]{:S(2)}, u32[]{:S(2)}) collective-permute-start(bf16[256,2048]{1,0:T(8,128)(2,1)} %by_rows.17), channel_id=1, source_target_pairs={{0,8},{4,12},{8,0},{12,4},{16,24},{20,28},{24,16},{28,20},{1,9},{5... | collective-permute-start | bytes 3145736 | tf_op jit(solution)/shard_map/ppermute | solution.py:696
  214.7 24.9 %collective-permute-start.38 = (bf16[256,2048]{1,0:T(8,128)(2,1)}, bf16[256,2048]{1,0:T(8,128)(2,1)}, u32[]{:S(2)}, u32[]{:S(2)}) collective-permute-start(bf16[256,2048]{1,0:T(8,128)(2,1)} %by_rows.18), channel_id=1, source_target_pairs={{0,2},{1,3},{2,0},{3,1},{4,6},{5,7},{6,4},{7,5},{8,10},{9,11},{10,... | collective-permute-start | bytes 3145736 | tf_op jit(solution)/shard_map/ppermute | solution.py:638
  221.4 8.0 %collective-permute-start.4 = (bf16[256,2048]{1,0:T(8,128)(2,1)S(1)}, bf16[256,2048]{1,0:T(8,128)(2,1)S(1)}, u32[]{:S(2)}, u32[]{:S(2)}) collective-permute-start(bf16[256,2048]{1,0:T(8,128)(2,1)S(1)} %get-tuple-element.247), channel_id=1, source_target_pairs={{0,1},{1,0},{2,3},{3,2},{4,5},{5,4},{6,7},{7,6},{8,9},{9,8},{10,11... | collective-permute-start | bytes 3145736 | tf_op jit(solution)/shard_map/cond/branch_1_fun/ppermute | solution.py:638
  249.7 42.5 %collective-permute-start.40 = (bf16[1024,768]{1,0:T(8,128)(2,1)}, bf16[1024,768]{1,0:T(8,128)(2,1)S(1)}, u32[]{:S(2)}, u32[]{:S(2)}) collective-permute-start(bf16[1024,768]{1,0:T(8,128)(2,1)} %get-tuple-element.818), channel_id=1, source_target_pairs={{0,4},{4,0},{8,12},{12,8},{16,20},{20,16},{24,28},{28,24},{1,5},{5... | collective-permute-start | bytes 4718600 | tf_op jit(solution)/shard_map/ppermute | solution.py:696
  249.9 27.9 %collective-permute-start.42 = (bf16[256,2048]{1,0:T(8,128)(2,1)}, bf16[256,2048]{1,0:T(8,128)(2,1)S(1)}, u32[]{:S(2)}, u32[]{:S(2)}) collective-permute-start(bf16[256,2048]{1,0:T(8,128)(2,1)} %get-tuple-element.816), channel_id=1, source_target_pairs={{0,2},{1,3},{2,0},{3,1},{4,6},{5,7},{6,4},{7,5},{8,10},{9,11},{10,... | collective-permute-start | bytes 3145736 | tf_op jit(solution)/shard_map/ppermute | solution.py:638
  250.1 39.1 %collective-permute-start.41 = (bf16[512,768]{1,0:T(8,128)(2,1)}, bf16[512,768]{1,0:T(8,128)(2,1)}, u32[]{:S(2)}, u32[]{:S(2)}) collective-permute-start(bf16[512,768]{1,0:T(8,128)(2,1)} %get-tuple-element.793), channel_id=1, source_target_pairs={{0,16},{4,20},{8,24},{12,28},{16,0},{20,4},{24,8},{28,12},{1,17},{... | collective-permute-start | bytes 2359304 | tf_op jit(solution)/shard_map/ppermute | solution.py:696
  252.4 47.7 %collective-permute-start.36 = (bf16[256,2048]{1,0:T(8,128)(2,1)}, bf16[256,2048]{1,0:T(8,128)(2,1)}, u32[]{:S(2)}, u32[]{:S(2)}) collective-permute-start(bf16[256,2048]{1,0:T(8,128)(2,1)} %get-tuple-element.807), channel_id=1, source_target_pairs={{0,8},{4,12},{8,0},{12,4},{16,24},{20,28},{24,16},{28,20},{1,9},{5... | collective-permute-start | bytes 3145736 | tf_op jit(solution)/shard_map/ppermute | solution.py:696
  255.4 5.4 %collective-permute-start.8 = (bf16[256,2048]{1,0:T(8,128)(2,1)}, bf16[256,2048]{1,0:T(8,128)(2,1)}, u32[]{:S(2)}, u32[]{:S(2)}) collective-permute-start(bf16[256,2048]{1,0:T(8,128)(2,1)} %get-tuple-element.272.rest_0_), channel_id=1, source_target_pairs={{0,1},{1,0},{2,3},{3,2},{4,5},{5,4},{6,7},{7,6},{8,9},{9,8},{10,11... | collective-permute-start | bytes 3145736 | tf_op jit(solution)/shard_map/cond/branch_1_fun/ppermute | solution.py:638
  292.1 43.7 %collective-permute-start.46 = (bf16[1024,512]{1,0:T(8,128)(2,1)}, bf16[1024,512]{1,0:T(8,128)(2,1)S(1)}, u32[]{:S(2)}, u32[]{:S(2)}) collective-permute-start(bf16[1024,512]{1,0:T(8,128)(2,1)} %get-tuple-element.868), channel_id=1, source_target_pairs={{0,4},{4,0},{8,12},{12,8},{16,20},{20,16},{24,28},{28,24},{1,5},{5... | collective-permute-start | bytes 3145736 | tf_op jit(solution)/shard_map/ppermute | solution.py:696
  293.4 44.4 %collective-permute-start.45 = (bf16[256,768]{1,0:T(8,128)(2,1)}, bf16[256,768]{1,0:T(8,128)(2,1)}, u32[]{:S(2)}, u32[]{:S(2)}) collective-permute-start(bf16[256,768]{1,0:T(8,128)(2,1)} %get-tuple-element.843), channel_id=1, source_target_pairs={{0,8},{4,12},{8,0},{12,4},{16,24},{20,28},{24,16},{28,20},{1,9},{5... | collective-permute-start | bytes 1179656 | tf_op jit(solution)/shard_map/ppermute | solution.py:696
  294.5 46.8 %collective-permute-start.44 = (bf16[512,768]{1,0:T(8,128)(2,1)}, bf16[512,768]{1,0:T(8,128)(2,1)}, u32[]{:S(2)}, u32[]{:S(2)}) collective-permute-start(bf16[512,768]{1,0:T(8,128)(2,1)} %get-tuple-element.867), channel_id=1, source_target_pairs={{0,16},{4,20},{8,24},{12,28},{16,0},{20,4},{24,8},{28,12},{1,17},{... | collective-permute-start | bytes 2359304 | tf_op jit(solution)/shard_map/ppermute | solution.py:696
  335.5 32.0 %collective-permute-start.43 = (bf16[1024,640]{1,0:T(8,128)(2,1)}, bf16[1024,640]{1,0:T(8,128)(2,1)S(1)}, u32[]{:S(2)}, u32[]{:S(2)}) collective-permute-start(bf16[1024,640]{1,0:T(8,128)(2,1)} %get-tuple-element.866), channel_id=1, source_target_pairs={{0,4},{4,0},{8,12},{12,8},{16,20},{20,16},{24,28},{28,24},{1,5},{5... | collective-permute-start | bytes 3932168 | tf_op jit(solution)/shard_map/ppermute | solution.py:696
  343.3 14.7 %collective-permute-start.47 = (bf16[256,768]{1,0:T(8,128)(2,1)}, bf16[256,768]{1,0:T(8,128)(2,1)S(1)}, u32[]{:S(2)}, u32[]{:S(2)}) collective-permute-start(bf16[256,768]{1,0:T(8,128)(2,1)} %get-tuple-element.882), channel_id=1, source_target_pairs={{0,8},{4,12},{8,0},{12,4},{16,24},{20,28},{24,16},{28,20},{1,9},{5... | collective-permute-start | bytes 1179656 | tf_op jit(solution)/shard_map/ppermute | solution.py:696
  343.3 27.5 %collective-permute-start.50 = (bf16[512,512]{1,0:T(8,128)(2,1)}, bf16[512,512]{1,0:T(8,128)(2,1)}, u32[]{:S(2)}, u32[]{:S(2)}) collective-permute-start(bf16[512,512]{1,0:T(8,128)(2,1)} %get-tuple-element.874), channel_id=1, source_target_pairs={{0,8},{4,12},{8,0},{12,4},{16,24},{20,28},{24,16},{28,20},{1,9},{5... | collective-permute-start | bytes 1572872 | tf_op jit(solution)/shard_map/ppermute | solution.py:696
  349.0 4.4 collective-permute-start.10
  354.5 44.0 %collective-permute-start.49 = (bf16[256,2048]{1,0:T(8,128)(2,1)}, bf16[256,2048]{1,0:T(8,128)(2,1)}, u32[]{:S(2)}, u32[]{:S(2)}) collective-permute-start(bf16[256,2048]{1,0:T(8,128)(2,1)} %get-tuple-element.1054), channel_id=1, source_target_pairs={{0,2},{1,3},{2,0},{3,1},{4,6},{5,7},{6,4},{7,5},{8,10},{9,11},{10,... | collective-permute-start | bytes 3145736 | tf_op jit(solution)/shard_map/ppermute | solution.py:638
  355.7 35.8 %collective-permute-start.51 = (bf16[512,768]{1,0:T(8,128)(2,1)}, bf16[512,768]{1,0:T(8,128)(2,1)S(1)}, u32[]{:S(2)}, u32[]{:S(2)}) collective-permute-start(bf16[512,768]{1,0:T(8,128)(2,1)} %get-tuple-element.900), channel_id=1, source_target_pairs={{0,16},{4,20},{8,24},{12,28},{16,0},{20,4},{24,8},{28,12},{1,17},{... | collective-permute-start | bytes 2359304 | tf_op jit(solution)/shard_map/ppermute | solution.py:696
  369.6 34.4 %collective-permute-start.48 = (bf16[512,640]{1,0:T(8,128)(2,1)}, bf16[512,640]{1,0:T(8,128)(2,1)S(1)}, u32[]{:S(2)}, u32[]{:S(2)}) collective-permute-start(bf16[512,640]{1,0:T(8,128)(2,1)} %get-tuple-element.895), channel_id=1, source_target_pairs={{0,8},{4,12},{8,0},{12,4},{16,24},{20,28},{24,16},{28,20},{1,9},{5... | collective-permute-start | bytes 1966088 | tf_op jit(solution)/shard_map/ppermute | solution.py:696
  393.1 13.9 %collective-permute-start.55 = (bf16[256,768]{1,0:T(8,128)(2,1)}, bf16[256,768]{1,0:T(8,128)(2,1)}, u32[]{:S(2)}, u32[]{:S(2)}) collective-permute-start(bf16[256,768]{1,0:T(8,128)(2,1)} %get-tuple-element.904), channel_id=1, source_target_pairs={{0,8},{4,12},{8,0},{12,4},{16,24},{20,28},{24,16},{28,20},{1,9},{5... | collective-permute-start | bytes 1179656 | tf_op jit(solution)/shard_map/ppermute | solution.py:696
  395.8 16.0 %collective-permute-start.54 = (bf16[256,512]{1,0:T(8,128)(2,1)S(1)}, bf16[256,512]{1,0:T(8,128)(2,1)S(1)}, u32[]{:S(2)}, u32[]{:S(2)}) collective-permute-start(bf16[256,512]{1,0:T(8,128)(2,1)S(1)} %get-tuple-element.906), channel_id=1, source_target_pairs={{0,16},{4,20},{8,24},{12,28},{16,0},{20,4},{24,8},{28,12},{1,17},{... | collective-permute-start | bytes 786440 | tf_op jit(solution)/shard_map/ppermute | solution.py:696
  404.8 23.1 %collective-permute-start.52 = (bf16[256,2048]{1,0:T(8,128)(2,1)}, bf16[256,2048]{1,0:T(8,128)(2,1)S(1)}, u32[]{:S(2)}, u32[]{:S(2)}) collective-permute-start(bf16[256,2048]{1,0:T(8,128)(2,1)} %by_rows.20), channel_id=1, source_target_pairs={{0,2},{1,3},{2,0},{3,1},{4,6},{5,7},{6,4},{7,5},{8,10},{9,11},{10,... | collective-permute-start | bytes 3145736 | tf_op jit(solution)/shard_map/ppermute | solution.py:638
  405.3 31.4 %collective-permute-start.53 = (bf16[256,2048]{1,0:T(8,128)(2,1)S(1)}, bf16[256,2048]{1,0:T(8,128)(2,1)}, u32[]{:S(2)}, u32[]{:S(2)}) collective-permute-start(bf16[256,2048]{1,0:T(8,128)(2,1)S(1)} %copy-done.28), channel_id=1, source_target_pairs={{0,8},{4,12},{8,0},{12,4},{16,24},{20,28},{24,16},{28,20},{1,9},{5... | collective-permute-start | bytes 3145736 | tf_op jit(solution)/shard_map/ppermute | solution.py:696
  406.7 32.8 %collective-permute-start.56 = (bf16[256,640]{1,0:T(8,128)(2,1)}, bf16[256,640]{1,0:T(8,128)(2,1)S(1)}, u32[]{:S(2)}, u32[]{:S(2)}) collective-permute-start(bf16[256,640]{1,0:T(8,128)(2,1)} %get-tuple-element.915), channel_id=1, source_target_pairs={{0,16},{4,20},{8,24},{12,28},{16,0},{20,4},{24,8},{28,12},{1,17},{... | collective-permute-start | bytes 983048 | tf_op jit(solution)/shard_map/ppermute | solution.py:696
  445.2 6.0 %collective-permute-start.57 = (f32[2,2,64]{2,1,0:T(2,128)S(1)}, f32[2,2,64]{2,1,0:T(2,128)S(1)}, u32[]{:S(2)}, u32[]{:S(2)}) collective-permute-start(f32[2,2,64]{2,1,0:T(2,128)S(1)} %pad_maximum_fusion.7), channel_id=1, source_target_pairs={{0,2},{1,3},{2,0},{3,1},{4,6},{5,7},{6,4},{7,5},{8,10},{9,11},{10,... | collective-permute-start | bytes 3080 | tf_op jit(solution)/shard_map/ppermute | solution.py:1121
  451.2 7.5 %collective-permute-start.58 = (f32[2,64]{1,0:T(2,128)S(1)}, f32[2,64]{1,0:T(2,128)S(1)}, u32[]{:S(2)}, u32[]{:S(2)}) collective-permute-start(f32[2,64]{1,0:T(2,128)S(1)} %slice_bitcast_fusion), channel_id=1, source_target_pairs={{0,1},{1,0},{2,3},{3,2},{4,5},{5,4},{6,7},{7,6},{8,9},{9,8},{10,11... | collective-permute-start | bytes 1544 | tf_op jit(solution)/shard_map/ppermute | solution.py:1122
  (87 other events, 692.5 us)
